TPU v7x, 32 devices: a whole 2x2x4 slice. The times are simulated.
32 devices in a mesh: tm: 4 (over y, x), space: 8 (over z, core).
Axes of the slice: x: 2, y: 2, z: 4, core: 2. Of those that a mesh axis runs over, the one named last changes fastest.
Arguments:
- frames_in: bfloat16 [16, 32, 64, 512], P('tm', 'space'), may hold values from -6 to 6
- spatial_kernel: bfloat16 [3, 3, 512, 512], replicated, may hold values from -0.09375 to 0.09375
- temporal_kernel: bfloat16 [3, 512, 512], replicated, may hold values from -0.15625 to 0.15625
- norm_gain: float32 [512], replicated, may hold values from 0.1 to 1.9
- query_weight: bfloat16 [512, 512], replicated, may hold values from -2 to 2
- key_weight: bfloat16 [512, 512], replicated, may hold values from -2 to 2
- value_weight: bfloat16 [512, 512], replicated, may hold values from -0.25 to 0.25
- out_weight: bfloat16 [512, 512], replicated, may hold values from -0.25 to 0.25
- cotangent: bfloat16 [16, 32, 64, 512], P('tm', 'space'), may hold values from -6 to 6
Outputs:
- encoded: bfloat16 [16, 32, 64, 512], P('tm', 'space')
- kernel_grad: float32 [3, 512, 512], P(None, 'tm', 'space')
All inputs are finite; a program needn't handle non-finite values.
Results may differ from a plain program's by a relative error of at most 0.007.
Values may be sent and summed in bfloat16 or wider, within the bound.
No kernel may reach another device: no remote copies, remote signals or barrier semaphores. Data moves between devices by JAX's collectives and lax.ppermute only.
A program may use at most 128 MiB of HBM per device.

v0:
```python
import jax
import jax.numpy as jnp
from jax import lax
from jax.sharding import PartitionSpec as P


def extended_2(cells, sides, width):
    for axis, dim in sides:
        count = lax.axis_size(axis)
        ends = count - 1
        head = lax.slice_in_dim(cells, 0, width, axis=dim)
        tail = lax.slice_in_dim(cells, cells.shape[dim] - width, cells.shape[dim], axis=dim)
        cells = jnp.concatenate(
            [
                lax.ppermute(tail, axis, [(i, (i + 1) % count) for i in range(ends)]),
                cells,
                lax.ppermute(head, axis, [((i + 1) % count, i) for i in range(ends)]),
            ],
            axis=dim,
        )
    return cells


def from_behind(value, axis, steps):
    count = lax.axis_size(axis)
    first, last = (max(0, -steps), min(count, count - steps))
    return lax.ppermute(value, axis, [(source, source + steps) for source in range(first, last)])


def project_all(normed, query_weight, key_weight, value_weight, lead, positions, chans):
    query = (
        jnp.dot(normed, query_weight, preferred_element_type=jnp.float32)
        .astype(jnp.bfloat16)
        .reshape(lead, positions, chans)
    )
    key = (
        jnp.dot(normed, key_weight, preferred_element_type=jnp.float32)
        .astype(jnp.bfloat16)
        .reshape(lead, positions, chans)
    )
    value = (
        jnp.dot(normed, value_weight, preferred_element_type=jnp.float32)
        .astype(jnp.bfloat16)
        .reshape(lead, positions, chans)
    )
    return (query, key, value)


def on_device(
    frames_in,
    spatial_kernel,
    temporal_kernel,
    norm_gain,
    query_weight,
    key_weight,
    value_weight,
    out_weight,
    cotangent,
):
    frames, rows, cols, chans = frames_in.shape
    padded = extended_2(frames_in, (("space", 1),), 1)
    padded = jnp.pad(padded, ((0, 0), (0, 0), (1, 1), (0, 0)))
    spatial = jnp.zeros((frames * rows * cols, chans), jnp.float32)
    for di in range(3):
        for dj in range(3):
            piece = padded[:, di : di + rows, dj : dj + cols, :].reshape(-1, chans)
            spatial = spatial + jnp.dot(
                piece, spatial_kernel[di, dj], preferred_element_type=jnp.float32
            )
    act = jax.nn.silu(spatial).astype(jnp.bfloat16).reshape(frames, rows, cols, chans)
    earlier = from_behind(act[frames - 2 :], "tm", 1)
    extended = jnp.concatenate([earlier, act], axis=0)
    temporal = jnp.zeros((frames * rows * cols, chans), jnp.float32)
    flat_grad = cotangent.reshape(-1, chans)
    grads = []
    for tap in range(3):
        shifted = extended[2 - tap : 2 - tap + frames].reshape(-1, chans)
        temporal = temporal + jnp.dot(
            shifted, temporal_kernel[tap], preferred_element_type=jnp.float32
        )
        grads.append(
            jnp.einsum("nc,nd->cd", shifted, flat_grad, preferred_element_type=jnp.float32)
        )
    partial_grad = jnp.stack(grads, axis=0)
    hidden = (frames_in.reshape(-1, chans).astype(jnp.float32) + temporal).astype(jnp.bfloat16)
    wide = hidden.astype(jnp.float32)
    normed = (
        wide / jnp.sqrt(jnp.mean(wide * wide, axis=1, keepdims=True) + 1e-06) * norm_gain
    ).astype(jnp.bfloat16)
    positions = rows * cols
    query, key, value = project_all(
        normed, query_weight, key_weight, value_weight, frames, positions, chans
    )
    first_frame = lax.axis_index("tm") * frames
    query_frames = first_frame + jnp.arange(frames)
    scale = 1.0 / jnp.sqrt(jnp.float32(chans))
    running_max = jnp.full((frames, positions), -1e30, jnp.float32)
    key_piece = lax.all_gather(key, "tm", axis=0, tiled=True)
    value_piece = lax.all_gather(value, "tm", axis=0, tiled=True)
    scores = (
        jnp.einsum("anc,bnc->abn", query, key_piece, preferred_element_type=jnp.float32) * scale
    )
    key_frames = jnp.arange(key_piece.shape[0])
    allowed = (key_frames[None, :] <= query_frames[:, None])[:, :, None]
    masked = jnp.where(allowed, scores, jnp.float32(-1e30))
    new_max = jnp.maximum(running_max, jnp.max(masked, axis=1))
    expon = jnp.where(allowed, jnp.exp(scores - new_max[:, None, :]), jnp.float32(0.0))
    new_sum = jnp.sum(expon, axis=1)
    new_acc = jnp.einsum("abn,bnc->anc", expon, value_piece.astype(jnp.float32))
    attended = (new_acc / new_sum[:, :, None]).astype(jnp.bfloat16)
    encoded = (
        wide + jnp.dot(attended.reshape(-1, chans), out_weight, preferred_element_type=jnp.float32)
    ).astype(jnp.bfloat16)
    section = lax.psum_scatter(partial_grad, "space", scatter_dimension=2, tiled=True)
    kernel_grad = lax.psum_scatter(section, "tm", scatter_dimension=1, tiled=True)
    return (encoded.reshape(frames, rows, cols, chans), kernel_grad)


def solution(mesh):
    in_specs = (
        P("tm", "space", None, None),
        P(),
        P(),
        P(),
        P(),
        P(),
        P(),
        P(),
        P("tm", "space", None, None),
    )
    out_specs = (P("tm", "space", None, None), P(None, "tm", "space"))
    return jax.shard_map(
        on_device, mesh=mesh, in_specs=in_specs, out_specs=out_specs, check_vma=False
    )
```

profile of v0, /device:TPU:0, one launch (start us, length us, event | category | flops | bytes accessed | tf_op | source)
XLA Modules:
  0.0 327.8 jit_solution(11937465625691930124)
XLA Ops:
  7.2 1.1 fusion.74
  8.4 2.5 collective-permute-start
  10.9 1.3 collective-permute-start.1
  12.2 2.1 fusion.41
  14.3 2.2 collective-permute-done.1
  16.5 0.9 fusion.14
  17.5 1.3 fusion.73
  18.8 0.2 slice-done.1
  19.0 0.7 fusion.37
  19.7 0.7 fusion.39
  20.5 0.7 fusion.43
  21.2 0.7 fusion.45
  21.9 0.7 fusion.49
  22.7 0.7 fusion.35
  23.4 0.7 fusion.47
  24.1 1.6 multiply_convert_fusion
  25.8 3.4 %collective-permute-start.2 = (bf16[2,4,64,512]{3,2,1,0:T(8,128)(2,1)S(1)}, bf16[2,4,64,512]{3,2,1,0:T(8,128)(2,1)S(1)}, u32[]{:S(2)}, u32[]{:S(2)}) collective-permute-start(bf16[2,4,64,512]{3,2,1,0:T(8,128)(2,1)S(1)} %bitcast.127), channel_id=1, source_target_pairs={{0,8},{8,16},{16,24},{1,9},{9,17},{17,25},{2,10},{10,18},{18,26},{... | collective-permute-start | bytes 1572872 | tf_op jit(solution)/shard_map/ppermute | solution.py:27
  29.2 0.7 convolution_bitcast_fusion
  30.0 7.7 %collective-permute-done.2 = bf16[2,4,64,512]{3,2,1,0:T(8,128)(2,1)S(1)} collective-permute-done((bf16[2,4,64,512]{3,2,1,0:T(8,128)(2,1)S(1)}, bf16[2,4,64,512]{3,2,1,0:T(8,128)(2,1)S(1)}, u32[]{:S(2)}, u32[]{:S(2)}) %collective-permute-start.2) | collective-permute-done | bytes 524320 | tf_op jit(solution)/shard_map/ppermute | solution.py:27
  37.6 0.7 convolution_bitcast_fusion.2
  38.4 0.7 convolution_bitcast_fusion.1
  39.2 2.0 pad_maximum_fusion
  41.2 5.1 %copy.30 = f32[3,512,512]{1,0,2:T(4,128)} copy(f32[3,512,512]{2,1,0:T(8,128)} %pad_maximum_fusion) | data formatting | bytes 6291456 | tf_op jit(solution)/shard_map/stack | solution.py:84
  46.3 0.2 reduce-scatter.4.cloned.1.call-start
  46.5 0.4 copy-done.10
  46.9 0.6 dynamic-slice
  48.1 3.1 fusion.29
  51.2 1.3 fusion.24
  52.5 3.1 fusion.27
  55.6 94.9 %all-reduce.4.cloned.1.call-done = f32[3,512,512]{1,0,2:T(4,128)} async-done(((f32[3,512,512]{1,0,2:T(4,128)}), f32[3,512,512]{1,0,2:T(4,128)}) %all-reduce.4.cloned.1.call-update) | async-done | bytes 3145744
  150.4 1.1 constant_dynamic-slice_fusion
  151.6 13.7 %copy.34 = f32[3,512,64]{0,2,1:T(8,128)} copy(f32[3,512,64]{1,0,2:T(4,128)S(1)} %constant_dynamic-slice_fusion) | data formatting | bytes 786432
  165.3 13.3 %reshape.117 = f32[512,192]{1,0:T(8,128)} reshape(f32[512,64,3]{2,1,0:T(8,128)} %bitcast.105) | data formatting | bytes 786432
  178.7 3.4 %fusion.5 = (f32[1024]{0:T(1024)S(1)}, bf16[1024,512]{1,0:T(8,128)(2,1)S(1)}) fusion(bf16[1024,512]{1,0:T(8,128)(2,1)S(1)} %bitcast.114, bf16[3,512,512]{2,1,0:T(8,128)(2,1)} %param.11, f32[1024,512]{1,0:T(8,128)} %fusion.29, f32[1024,512]{1,0:T(8,128)} %fusion.27, bf16[1024,512]{1,0:T(8,128)(2,1)S(1)} %bitcast.107), kind=kOutput, calls=%fused_computation.14 | convolution fusion | flops 541064192 | bytes 7868416 | tf_op jit(solution)/shard_map/dot_general | solution.py:78
  182.1 1.8 convolution_convert_fusion.1
  184.0 1.7 convolution_convert_fusion.2
  185.9 1.8 convolution_convert_fusion
  187.7 16.0 %reduce-scatter.4.cloned.1.call-done = f32[128,192]{1,0:T(8,128)} async-done(((f32[512,192]{1,0:T(8,128)}), f32[128,192]{1,0:T(8,128)}) %reduce-scatter.4.cloned.1.call-update) | async-done | bytes 98320
  203.6 6.4 %reshape.118 = f32[128,64,3]{2,1,0:T(8,128)} reshape(f32[128,192]{1,0:T(8,128)} %reduce-scatter.4.cloned.1.call-done) | data formatting | bytes 196608
  210.0 4.5 %copy.31 = f32[3,128,64]{1,2,0:T(8,128)} copy(f32[3,128,64]{0,2,1:T(8,128)} %bitcast.108) | data formatting | bytes 196608
  214.5 43.8 %all-gather.5.cloned.1.call-done = bf16[16,256,512]{2,1,0:T(8,128)(2,1)} async-done(((bf16[4,256,512]{2,1,0:T(8,128)(2,1)}), bf16[16,256,512]{2,1,0:T(8,128)(2,1)}) %all-gather.5.cloned.1.call-update) | async-done | bytes 4194320 | tf_op jit(solution)/shard_map/all_gather | solution.py:98
  258.4 5.4 %select_reduce_fusion = (f32[4,256]{0,1:T(8,128)S(1)}, f32[4,16,256]{1,0,2:T(4,128)S(1)}) fusion(pred[4,16]{1,0:T(4,128)(4,1)S(1)} %iota_compare_fusion.2, bf16[4,256,512]{2,1,0:T(8,128)(2,1)S(1)} %bitcast.128, bf16[16,256,512]{2,1,0:T(8,128)(2,1)} %all-gather.5.cloned.1.call-done), kind=kOutput, calls=%fused_computation.66 | convolution fusion | flops 16825344 | bytes 5312576 | tf_op jit(solution)/shard_map/anc,bnc->abn/dot_general | solution.py:101
  263.7 0.7 fusion.63
  264.4 49.1 %all-gather.3.cloned.1.call-done = bf16[16,256,512]{2,1,0:T(8,128)(2,1)} async-done(((bf16[4,256,512]{2,1,0:T(8,128)(2,1)}), bf16[16,256,512]{2,1,0:T(8,128)(2,1)}) %all-gather.3.cloned.1.call-update) | async-done | bytes 4194320 | tf_op jit(solution)/shard_map/all_gather | solution.py:99
  313.5 5.1 %fusion.9 = bf16[4,256,512]{2,0,1:T(4,128)(2,1)S(1)} fusion(bf16[16,256,512]{2,1,0:T(8,128)(2,1)} %all-gather.3.cloned.1.call-done, f32[4,256]{0,1:T(8,128)S(1)} %fusion.63, f32[4,16,256]{1,0,2:T(4,128)S(1)} %get-tuple-element.25, f32[4,256]{0,1:T(8,128)S(1)} %broadcast_maximum_fusion, pred[4,16]{1,0:T(4,128)(4,1)S(1)} %iota_compare_fusion.2), kind=kOutput, calls=%fused_computation.21 | convolution fusion | flops 17858560 | bytes 5316672 | tf_op jit(solution)/shard_map/abn,bnc->anc/dot_general | solution.py:109
  318.6 0.2 copy.29
  318.8 0.8 copy-done.7
  319.6 1.7 fusion.8
  (38 shorter events, 0.6 us)
Async XLA Ops:
  7.2 22.1 %copy-start = (bf16[4,4,64,512]{3,2,1,0:T(8,128)(2,1)S(1)}, bf16[4,4,64,512]{3,2,1,0:T(8,128)(2,1)}, u32[]{:S(2)}) copy-start(bf16[4,4,64,512]{3,2,1,0:T(8,128)(2,1)} %param.17) | copy-start | bytes 3145732
  7.2 143.3 %all-reduce.4.cloned.1.call-start = ((), (), s32[]{:S(2)}) async-start(), calls=%async_computation.4 | async-start | bytes 8388608
  8.4 8.1 %copy-start.2 = (bf16[4,4,64,512]{3,2,1,0:T(8,128)(2,1)S(1)}, bf16[4,4,64,512]{3,2,1,0:T(8,128)(2,1)}, u32[]{:S(2)}) copy-start(bf16[4,4,64,512]{3,2,1,0:T(8,128)(2,1)} %param.9) | copy-start | bytes 3145732
  8.4 5.9 %collective-permute-start = (bf16[4,1,64,512]{3,2,1,0:T(8,128)(2,1)S(1)}, bf16[4,1,64,512]{3,2,1,0:T(8,128)(2,1)S(1)}, u32[]{:S(2)}, u32[]{:S(2)}) collective-permute-start(bf16[4,1,64,512]{3,2,1,0:T(8,128)(2,1)S(1)} %get-tuple-element.20), channel_id=1, source_target_pairs={{0,1},{1,2},{2,3},{3,4},{4,5},{5,6},{6,7},{8,9},{9,10},{10,11},{11... | collective-permute-start | bytes 786440 | tf_op jit(solution)/shard_map/ppermute | solution.py:15
  10.9 5.6 %collective-permute-start.1 = (bf16[4,1,64,512]{3,2,1,0:T(8,128)(2,1)S(1)}, bf16[4,1,64,512]{3,2,1,0:T(8,128)(2,1)S(1)}, u32[]{:S(2)}, u32[]{:S(2)}) collective-permute-start(bf16[4,1,64,512]{3,2,1,0:T(8,128)(2,1)S(1)} %get-tuple-element.21), channel_id=1, source_target_pairs={{1,0},{2,1},{3,2},{4,3},{5,4},{6,5},{7,6},{9,8},{10,9},{11,10},{12... | collective-permute-start | bytes 786440 | tf_op jit(solution)/shard_map/ppermute | solution.py:17
  16.5 2.3 slice-start
  17.5 1.6 slice-start.1
  25.8 11.8 %collective-permute-start.2 = (bf16[2,4,64,512]{3,2,1,0:T(8,128)(2,1)S(1)}, bf16[2,4,64,512]{3,2,1,0:T(8,128)(2,1)S(1)}, u32[]{:S(2)}, u32[]{:S(2)}) collective-permute-start(bf16[2,4,64,512]{3,2,1,0:T(8,128)(2,1)S(1)} %bitcast.127), channel_id=1, source_target_pairs={{0,8},{8,16},{16,24},{1,9},{9,17},{17,25},{2,10},{10,18},{18,26},{... | collective-permute-start | bytes 1572872 | tf_op jit(solution)/shard_map/ppermute | solution.py:27
  37.6 0.8 copy-start.3
  46.3 0.7 copy-start.10
  46.3 157.3 %reduce-scatter.4.cloned.1.call-start = ((), (), s32[]{:S(2)}) async-start(), calls=%async_computation.3 | async-start | bytes 655360
  178.6 79.7 %all-gather.5.cloned.1.call-start = ((), (), s32[]{:S(2)}) async-start(), calls=%async_computation.2 | async-start | bytes 5242880 | tf_op jit(solution)/shard_map/all_gather | solution.py:98
  178.7 3.4 %copy-start.4 = (bf16[512,512]{1,0:T(8,128)(2,1)S(1)}, bf16[512,512]{1,0:T(8,128)(2,1)}, u32[]{:S(2)}) copy-start(bf16[512,512]{1,0:T(8,128)(2,1)} %param.14) | copy-start | bytes 1572868
  178.7 3.4 %copy-start.8 = (f32[512]{0:T(512)S(1)}, f32[512]{0:T(512)}, u32[]{:S(2)}) copy-start(f32[512]{0:T(512)} %param.12) | copy-start | bytes 6148
  182.1 1.9 copy-start.5
  184.0 1.9 copy-start.6
  184.0 129.5 %all-gather.3.cloned.1.call-start = ((), (), s32[]{:S(2)}) async-start(), calls=%async_computation.1 | async-start | bytes 5242880 | tf_op jit(solution)/shard_map/all_gather | solution.py:99
  210.0 48.3 %copy-start.9 = (bf16[1024,512]{1,0:T(8,128)(2,1)S(1)}, bf16[1024,512]{1,0:T(8,128)(2,1)}, u32[]{:S(2)}) copy-start(bf16[1024,512]{1,0:T(8,128)(2,1)} %convolution_convert_fusion) | copy-start | bytes 3145732
  318.6 1.0 copy-start.7
  318.6 2.7 copy-start.1
Sparse Core Ops, SparseCore 0:
  46.4 103.9 all-reduce.3
  178.7 24.8 reduce-scatter.3
  205.6 52.6 all-gather.4
  260.8 52.6 all-gather.2
where the time goes:
time: 329 us; the launch traced here: 328 us
  waiting for transfers between devices  214 us (65%)
  local copies, waits for them, and re-layouts  49 us (15%)
  matrix products  37.7 us (11%)
  between operations  14.7 us (4%)
  starting transfers between devices  7.57 us (2%)
  other arithmetic  5.18 us (2%)
    unnamed x6, waiting for transfers between devices  111 us
    all_gather x1, waiting for transfers between devices, on_device(): value_piece = lax.all_gather(value, 'tm', axis=0, tiled=True)  49.1 us
    all_gather x1, waiting for transfers between devices, on_device(): key_piece = lax.all_gather(key, 'tm', axis=0, tiled=True)  43.8 us
    unnamed x32, local copies, waits for them, and re-layouts  41.2 us
    dot_general x3, matrix products, on_device(): jnp.dot(shifted, temporal_kernel[tap], preferred_element_type=jnp.float32)  9.51 us
    dot_general x9, matrix products, on_device(): jnp.dot(piece, spatial_kernel[di, dj], preferred_element_type=jnp.float32)  8.59 us
    ppermute x1, waiting for transfers between devices, from_behind(): lax.ppermute(value, axis, [(source, source + steps) for source in range(f...  7.65 us
  transfers between devices with their start and end apart: 7, of which 6 were waited for; matrix products, arithmetic and copies ran while one was open for 11% of the time, Pallas kernels for 0%

commit v1 on v0

v1 whole, which is shorter than its diff:
```python
import functools

import jax
import jax.numpy as jnp
from jax import lax
from jax.experimental import pallas as pl
from jax.experimental.pallas import tpu as pltpu
from jax.sharding import PartitionSpec as P

BF = jnp.bfloat16
F32 = jnp.float32
VMEM = pl.BlockSpec(memory_space=pltpu.VMEM)
SMEM = pl.BlockSpec(memory_space=pltpu.SMEM)


def call(kernel, outs, *args, flops=0, scratch=()):
    moved = sum(a.size * a.dtype.itemsize for a in args)
    moved += sum(o.size * o.dtype.itemsize for o in outs)
    return pl.pallas_call(
        kernel,
        out_shape=tuple(outs),
        in_specs=[SMEM if a.dtype == jnp.int32 else VMEM for a in args],
        out_specs=tuple(VMEM for _ in outs),
        scratch_shapes=scratch,
        compiler_params=pltpu.CompilerParams(vmem_limit_bytes=40 * 2**20),
        cost_estimate=pl.CostEstimate(flops=flops, bytes_accessed=moved, transcendentals=0),
    )(*args)


def shape(dims, kind=BF):
    return jax.ShapeDtypeStruct(dims, kind)


def chooser(rows, cols, source):
    q = lax.broadcasted_iota(jnp.int32, (rows, cols), 0)
    m = lax.broadcasted_iota(jnp.int32, (rows, cols), 1)
    return jnp.where(source(q) == m, 1.0, 0.0).astype(BF)


def moved(matrix, rows):
    return jnp.dot(matrix, rows, preferred_element_type=F32).astype(BF)


class Sizes:
    def __init__(self, count, frames, rows, cols, chans):
        self.n, self.fl, self.r, self.w, self.c = count, frames, rows, cols, chans
        self.f = count * frames
        self.wc = cols // count
        self.block = self.f * self.wc
        self.piece = frames * self.wc
        self.main = rows * self.piece
        self.sides = 2 * rows * frames


def pack_kernel(z, halo, me_ref, x_ref, *outs):
    me = me_ref[0]

    def source(q):
        k = q // z.piece
        f = q % z.piece // z.wc
        return f * z.w + (me ^ k) * z.wc + q % z.wc

    matrix = chooser(z.n * z.piece, z.fl * z.w, source)
    for r in range(z.r):
        rows = x_ref[:, r].reshape(z.fl * z.w, z.c)
        cut = moved(matrix, rows)
        for k in range(z.n):
            outs[k][r * z.piece : (r + 1) * z.piece] = cut[k * z.piece : (k + 1) * z.piece]
    if not halo:
        return

    def edge(q):
        k = q // z.sides
        side = q % z.sides // (z.r * z.fl)
        r = q % (z.r * z.fl) // z.fl
        f = q % z.fl
        col = (me ^ k) * z.wc - 1 + side * (z.wc + 1)
        inside = (col >= 0) & (col < z.w)
        return jnp.where(inside, (f * z.r + r) * z.w + col, -1)

    total = z.fl * z.r * z.w
    cut = moved(chooser(z.n * z.sides, total, edge), x_ref[...].reshape(total, z.c))
    for k in range(z.n):
        outs[k][z.main : z.main + z.sides] = cut[k * z.sides : (k + 1) * z.sides]


def gather_matrix(z, me):
    def source(q):
        s = q % z.f // z.fl
        return ((me ^ s) * z.fl + q % z.fl) * z.wc + q // z.f

    return chooser(z.block, z.block, source)


def assemble_kernel(z, me_ref, *refs):
    parts, (out, top, bottom) = refs[: z.n], refs[z.n :]
    me = me_ref[0]
    matrix = gather_matrix(z, me)

    def edge(q):
        head = q // z.f
        s = q % z.f // z.fl
        return ((me ^ s) * 2 * z.r + head) * z.fl + q % z.fl

    count = z.n * z.sides
    tails = jnp.concatenate([p[z.main : z.main + z.sides] for p in parts], axis=0)
    tails = moved(chooser(count, count, edge), tails)
    last = z.f + z.block
    for r in range(z.r):
        rows = jnp.concatenate([p[r * z.piece : (r + 1) * z.piece] for p in parts], axis=0)
        rows = moved(matrix, rows)
        left = tails[r * z.f : (r + 1) * z.f]
        right = tails[(z.r + r) * z.f : (z.r + r + 1) * z.f]
        copies = [out.at[r]]
        if r == 0:
            copies.append(top)
        if r == z.r - 1:
            copies.append(bottom)
        for ref in copies:
            ref[0 : z.f] = left
            ref[z.f : last] = rows
            ref[last : last + z.f] = right


def inner_kernel(z, x_ref, w_ref, out):
    for r in range(z.r):
        total = jnp.zeros((z.block, z.c), F32)
        for di in range(3):
            if not 0 <= r + di - 1 < z.r:
                continue
            for dj in range(3):
                total += jnp.dot(
                    x_ref[r + di - 1, dj * z.f : dj * z.f + z.block],
                    w_ref[di, dj],
                    preferred_element_type=F32,
                )
        out[r] = total


def act_kernel(z, part_ref, up_ref, down_ref, w_ref, out):
    frame = lax.broadcasted_iota(jnp.int32, (z.block, z.c), 0) % z.f
    for r in range(z.r):
        total = part_ref[r]
        for edge, di, ref in ((0, 0, up_ref), (z.r - 1, 2, down_ref)):
            if r == edge:
                for dj in range(3):
                    total += jnp.dot(
                        ref[dj * z.f : dj * z.f + z.block],
                        w_ref[di, dj],
                        preferred_element_type=F32,
                    )
        act = (total / (1.0 + jnp.exp(-total))).astype(BF)
        out[r, :, 0 : z.c] = act
        wide = act.astype(F32)
        for k in (1, 2):
            late = jnp.where(frame >= k, pltpu.roll(wide, k, 0), 0.0)
            out[r, :, k * z.c : (k + 1) * z.c] = late.astype(BF)


def main_kernel(z, x_ref, act_ref, t_ref, gain_ref, q_ref, k_ref, v_ref, o_ref, out):
    a = lax.broadcasted_iota(jnp.int32, (z.block, z.block), 0)
    b = lax.broadcasted_iota(jnp.int32, (z.block, z.block), 1)
    allowed = (a // z.f == b // z.f) & (b % z.f <= a % z.f)
    scale = float(z.c) ** -0.5
    back = chooser(z.block, z.block, lambda q: q % z.wc * z.f + q // z.wc)
    gain = gain_ref[...]
    for r in range(z.r):
        temporal = jnp.dot(act_ref[r], t_ref[...], preferred_element_type=F32)
        hidden = (x_ref[r, z.f : z.f + z.block].astype(F32) + temporal).astype(BF)
        wide = hidden.astype(F32)
        mean = jnp.mean(wide * wide, axis=1, keepdims=True)
        normed = (wide / jnp.sqrt(mean + 1e-06) * gain).astype(BF)
        query = jnp.dot(normed, q_ref[...], preferred_element_type=F32).astype(BF)
        key = jnp.dot(normed, k_ref[...], preferred_element_type=F32).astype(BF)
        value = jnp.dot(normed, v_ref[...], preferred_element_type=F32).astype(BF)
        scores = lax.dot_general(
            query, key, (((1,), (1,)), ((), ())), preferred_element_type=F32
        )
        scores = jnp.where(allowed, scores * scale, -1e30)
        top = jnp.max(scores, axis=1, keepdims=True)
        expon = jnp.where(allowed, jnp.exp(scores - top), 0.0)
        total = jnp.sum(expon, axis=1, keepdims=True)
        mixed = jnp.dot(expon.astype(BF), value, preferred_element_type=F32)
        attended = (mixed / total).astype(BF)
        encoded = wide + jnp.dot(attended, o_ref[...], preferred_element_type=F32)
        encoded = moved(back, encoded.astype(BF))
        for i in range(z.n):
            out[i, r] = encoded[i * z.piece : (i + 1) * z.piece]


def grad_kernel(z, width, me_ref, *refs):
    parts, (act_ref, keep, send, cot) = refs[: z.n], refs[z.n :]
    matrix = gather_matrix(z, me_ref[0])
    mine = me_ref[1] == 0
    for r in range(z.r):
        rows = jnp.concatenate([p[r * z.piece : (r + 1) * z.piece] for p in parts], axis=0)
        cot[r * z.block : (r + 1) * z.block] = moved(matrix, rows)
    flat = cot[...]
    for k in range(3):
        lanes = slice(k * z.c, (k + 1) * z.c)
        grad = lax.dot_general(
            flat,
            act_ref[:, :, lanes].reshape(z.r * z.block, z.c),
            (((0,), (0,)), ((), ())),
            preferred_element_type=F32,
        )
        for i in range(z.c // (2 * width)):
            low = grad[2 * i * width : (2 * i + 1) * width]
            high = grad[(2 * i + 1) * width : (2 * i + 2) * width]
            keep[i * width : (i + 1) * width, lanes] = jnp.where(mine, low, high)
            send[i * width : (i + 1) * width, lanes] = jnp.where(mine, high, low).astype(BF)


def split_kernel(z, me_ref, keep_ref, got_ref, *outs):
    me = me_ref[0]
    wide = z.c // z.n
    for tap in range(3):
        place = slice(tap * wide, (tap + 1) * wide)
        if wide % 128 == 0:
            for k in range(z.n):
                lanes = pl.ds(pl.multiple_of(tap * z.c + (me ^ k) * wide, 128), wide)
                total = keep_ref[:, lanes] + got_ref[:, lanes].astype(F32)
                outs[k][:, place] = total.astype(outs[k].dtype)
            continue
        lanes = slice(tap * z.c, (tap + 1) * z.c)
        total = keep_ref[:, lanes] + got_ref[:, lanes].astype(F32)
        for k in range(z.n):
            cut = total[:, 0:wide]
            for i in range(1, z.n):
                cut = jnp.where((me ^ k) == i, total[:, i * wide : (i + 1) * wide], cut)
            outs[k][:, place] = cut.astype(outs[k].dtype)


def swap(value, axis, k):
    count = lax.axis_size(axis)
    return lax.ppermute(value, axis, [(i, i ^ k) for i in range(count)])


def on_device(frames_in, spatial, temporal, gain, q_w, k_w, v_w, o_w, cotangent):
    n = lax.axis_size("tm")
    space = lax.axis_size("space")
    z = Sizes(n, *frames_in.shape)
    me = lax.axis_index("tm")
    here = lax.axis_index("space")
    ids = jnp.stack([me, here % 2]).astype(jnp.int32)
    part = [shape((z.main + z.sides, z.c))] * n
    packed = call(functools.partial(pack_kernel, z, True), part, ids, frames_in)
    got = [packed[0]] + [swap(packed[k], "tm", k) for k in range(1, n)]
    line = z.block + 2 * z.f
    x, top, bottom = call(
        functools.partial(assemble_kernel, z),
        [shape((z.r, line, z.c)), shape((line, z.c)), shape((line, z.c))],
        ids,
        *got,
    )
    up = lax.ppermute(bottom, "space", [(i, i + 1) for i in range(space - 1)])
    down = lax.ppermute(top, "space", [(i + 1, i) for i in range(space - 1)])
    part = [shape((z.main, z.c))] * n
    cot = call(functools.partial(pack_kernel, z, False), part, ids, cotangent)
    cot = [cot[0]] + [swap(cot[k], "tm", k) for k in range(1, n)]
    one = 2 * z.r * z.block * z.c * z.c
    (inner,) = call(
        functools.partial(inner_kernel, z),
        [shape((z.r, z.block, z.c), F32)],
        x,
        spatial,
        flops=9 * one * (3 * z.r - 2) // (3 * z.r),
    )
    (acts,) = call(
        functools.partial(act_kernel, z),
        [shape((z.r, z.block, 3 * z.c))],
        inner,
        up,
        down,
        spatial,
        flops=6 * one // z.r,
    )
    width = z.c // space
    keep, send = call(
        functools.partial(grad_kernel, z, width),
        [shape((z.c // 2, 3 * z.c), F32), shape((z.c // 2, 3 * z.c))],
        ids,
        *cot,
        acts,
        flops=3 * one,
        scratch=[pltpu.VMEM((z.r * z.block, z.c), BF)],
    )
    other = swap(send, "space", 1)
    (encoded,) = call(
        functools.partial(main_kernel, z),
        [shape((n, z.r, z.piece, z.c))],
        x,
        acts,
        temporal.reshape(3 * z.c, z.c),
        gain.reshape(1, z.c),
        q_w,
        k_w,
        v_w,
        o_w,
        flops=8 * one,
    )
    wide = z.c // n
    pieces = call(
        functools.partial(split_kernel, z),
        [shape((z.c // 2, 3 * wide), F32)] + [shape((z.c // 2, 3 * wide))] * (n - 1),
        ids,
        keep,
        other,
    )
    back = [lax.dynamic_index_in_dim(encoded, me ^ k, 0, False) for k in range(n)]
    back = [back[0]] + [swap(back[k], "tm", k) for k in range(1, n)]
    total = pieces[0]
    for k in range(1, n):
        total = total + swap(pieces[k], "tm", k).astype(F32)
    chips = space // 2
    total = total.reshape(chips, width, 3 * wide)
    sums = lax.dynamic_index_in_dim(total, here // 2, 0, False)
    total = total.astype(BF)
    for k in range(1, chips):
        mine = lax.dynamic_index_in_dim(total, here // 2 ^ k, 0, False)
        sums = sums + swap(mine, "space", 2 * k).astype(F32)
    kernel_grad = sums.reshape(width, 3, wide).transpose(1, 2, 0)
    whole = jnp.zeros((z.fl, z.r, n, z.wc, z.c), BF)
    for k in range(n):
        rows = back[k].reshape(z.r, z.fl, 1, z.wc, z.c).transpose(1, 0, 2, 3, 4)
        whole = lax.dynamic_update_slice_in_dim(whole, rows, me ^ k, 2)
    return whole.reshape(frames_in.shape), kernel_grad


def solution(mesh):
    tiles = P("tm", "space", None, None)
    return jax.shard_map(
        on_device,
        mesh=mesh,
        in_specs=(tiles,) + (P(),) * 7 + (tiles,),
        out_specs=(tiles, P(None, "tm", "space")),
        check_vma=False,
    )
```

time: 329 us -> 91.3 us (0.28)
  waiting for transfers between devices: 214 us -> 27.4 us
  matrix products: 37.7 us -> 0 us
  local copies, waits for them, and re-layouts: 49 us -> 13.8 us
  Pallas kernels: 0 us -> 21.4 us
  starting transfers between devices: 7.57 us -> 27.3 us
  between operations: 14.7 us -> 0.88 us
  other arithmetic: 5.18 us -> 0.22 us
    unnamed x6 -> x0, waiting for transfers between devices: 111 us -> none
    all_gather x2 -> x0, waiting for transfers between devices: 92.9 us -> none  [the longest x1 49.1 us: on_device(): value_piece = lax.all_gather(value, 'tm', axis=0, tiled=True)]
    dot_general x21 -> x0, matrix products: 37.7 us -> none  [the longest x3 9.51 us: on_device(): jnp.dot(shifted, temporal_kernel[tap], preferred_element_type=jnp.float32)]
    unnamed x32 -> x29, local copies, waits for them, and re-layouts: 41.2 us -> 7.82 us
    pallas_call x0 -> x8, Pallas kernels: none -> 21.4 us  [call(): pl.pallas_call(kernel, out_shape=tuple(outs), in_specs=[SMEM if a.dtype =...]
    ppermute x3 -> x18, starting transfers between devices: 7.22 us -> 27.3 us  [the longest x16 24.7 us: swap(): return lax.ppermute(value, axis, [(i, i ^ k) for i in range(count)])]
    ppermute x3 -> x18, waiting for transfers between devices: 9.89 us -> 27.4 us  [the longest x16 27.4 us: swap(): return lax.ppermute(value, axis, [(i, i ^ k) for i in range(count)])]
    another operation x1 -> x0, local copies, waits for them, and re-layouts: 5.09 us -> none  [on_device(): partial_grad = jnp.stack(grads, axis=0)]
  transfers between devices with their start and end apart: 7 -> 18, of which waited for: 6 -> 7; matrix products, arithmetic and copies ran while one was open for 11% -> 7% of each run, Pallas kernels for 0% -> 19%
where the time goes in v1:
time: 91.3 us; the launch traced here: 91 us
  waiting for transfers between devices  27.4 us (30%)
  starting transfers between devices  27.3 us (30%)
  Pallas kernels  21.4 us (23%)
  local copies, waits for them, and re-layouts  13.8 us (15%)
    ppermute x16, waiting for transfers between devices, swap(): return lax.ppermute(value, axis, [(i, i ^ k) for i in range(count)])  27.4 us
    ppermute x16, starting transfers between devices, swap(): return lax.ppermute(value, axis, [(i, i ^ k) for i in range(count)])  24.7 us
    pallas_call x8, Pallas kernels, call(): pl.pallas_call(kernel, out_shape=tuple(outs), in_specs=[SMEM if a.dtype =...  21.4 us
    unnamed x29, local copies, waits for them, and re-layouts  7.82 us
    dynamic_update_slice x4, local copies, waits for them, and re-layouts, on_device(): whole = lax.dynamic_update_slice_in_dim(whole, rows, me ^ k, 2)  3.83 us
  transfers between devices with their start and end apart: 18, of which 7 were waited for; matrix products, arithmetic and copies ran while one was open for 7% of the time, Pallas kernels for 19%

profile of v1, /device:TPU:0, one launch (start us, length us, event | category | flops | bytes accessed | tf_op | source)
XLA Modules:
  0.0 91.0 jit_solution(14805374188236621598)
XLA Ops:
  0.6 0.1 pad_add_fusion.me_ref
  0.7 1.2 %copy-done.1 = bf16[4,4,64,512]{3,2,1,0:T(8,128)(2,1)S(1)} copy-done((bf16[4,4,64,512]{3,2,1,0:T(8,128)(2,1)S(1)}, bf16[4,4,64,512]{3,2,1,0:T(8,128)(2,1)}, u32[]{:S(2)}) %copy-start.1) | copy-done | bytes 1048600
  1.9 1.1 %shard_map.104 = (bf16[288,512]{1,0:T(8,128)(2,1)S(1)}, bf16[288,512]{1,0:T(8,128)(2,1)S(1)}, bf16[288,512]{1,0:T(8,128)(2,1)S(1)}, bf16[288,512]{1,0:T(8,128)(2,1)S(1)}) custom-call(s32[2]{0:T(128)S(1)} %pad_add_fusion.me_ref, bf16[4,4,64,512]{3,2,1,0:T(8,128)(2,1)S(1)} %copy-done.1), custom_call_target="tpu_custom_call" | custom-call | bytes 2228232 | tf_op jit(solution)/shard_map/pallas_call | solution.py:19
  3.1 3.0 %collective-permute-start = (bf16[288,512]{1,0:T(8,128)(2,1)S(1)}, bf16[288,512]{1,0:T(8,128)(2,1)S(1)}, u32[]{:S(2)}, u32[]{:S(2)}) collective-permute-start(bf16[288,512]{1,0:T(8,128)(2,1)S(1)} %get-tuple-element.20), channel_id=1, source_target_pairs={{0,8},{8,0},{16,24},{24,16},{1,9},{9,1},{17,25},{25,17},{2,10},{10... | collective-permute-start | bytes 884744 | tf_op jit(solution)/shard_map/ppermute | solution.py:236
  6.1 1.5 %collective-permute-start.1 = (bf16[288,512]{1,0:T(8,128)(2,1)S(1)}, bf16[288,512]{1,0:T(8,128)(2,1)S(1)}, u32[]{:S(2)}, u32[]{:S(2)}) collective-permute-start(bf16[288,512]{1,0:T(8,128)(2,1)S(1)} %get-tuple-element.21), channel_id=1, source_target_pairs={{0,16},{8,24},{16,0},{24,8},{1,17},{9,25},{17,1},{25,9},{2,18},{10... | collective-permute-start | bytes 884744 | tf_op jit(solution)/shard_map/ppermute | solution.py:236
  7.6 0.0 collective-permute-start.2
  7.6 1.2 %copy-done.2 = bf16[4,4,64,512]{3,2,1,0:T(8,128)(2,1)S(1)} copy-done((bf16[4,4,64,512]{3,2,1,0:T(8,128)(2,1)S(1)}, bf16[4,4,64,512]{3,2,1,0:T(8,128)(2,1)}, u32[]{:S(2)}) %copy-start.2) | copy-done | bytes 1048600
  8.8 1.7 %shard_map.109 = (bf16[256,512]{1,0:T(8,128)(2,1)S(1)}, bf16[256,512]{1,0:T(8,128)(2,1)}, bf16[256,512]{1,0:T(8,128)(2,1)S(1)}, bf16[256,512]{1,0:T(8,128)(2,1)}) custom-call(s32[2]{0:T(128)S(1)} %pad_add_fusion.me_ref, bf16[4,4,64,512]{3,2,1,0:T(8,128)(2,1)S(1)} %copy-done.2), custom_call_target="tpu_custom_call" | custom-call | bytes 2097160 | tf_op jit(solution)/shard_map/pallas_call | solution.py:19
  10.6 0.7 copy-done.10
  11.3 2.9 %collective-permute-start.10 = (bf16[256,512]{1,0:T(8,128)(2,1)}, bf16[256,512]{1,0:T(8,128)(2,1)S(1)}, u32[]{:S(2)}, u32[]{:S(2)}) collective-permute-start(bf16[256,512]{1,0:T(8,128)(2,1)} %get-tuple-element.29), channel_id=1, source_target_pairs={{0,24},{8,16},{16,8},{24,0},{1,25},{9,17},{17,9},{25,1},{2,26},{10... | collective-permute-start | bytes 786440 | tf_op jit(solution)/shard_map/ppermute | solution.py:236
  14.2 0.5 collective-permute-start.8
  14.7 1.3 %collective-permute-start.9 = (bf16[256,512]{1,0:T(8,128)(2,1)}, bf16[256,512]{1,0:T(8,128)(2,1)S(1)}, u32[]{:S(2)}, u32[]{:S(2)}) collective-permute-start(bf16[256,512]{1,0:T(8,128)(2,1)} %copy-done.10), channel_id=1, source_target_pairs={{0,16},{8,24},{16,0},{24,8},{1,17},{9,25},{17,1},{25,9},{2,18},{10... | collective-permute-start | bytes 786440 | tf_op jit(solution)/shard_map/ppermute | solution.py:236
  16.0 10.9 %collective-permute-done.1.refs_2_ = bf16[288,512]{1,0:T(8,128)(2,1)S(1)} collective-permute-done((bf16[288,512]{1,0:T(8,128)(2,1)S(1)}, bf16[288,512]{1,0:T(8,128)(2,1)S(1)}, u32[]{:S(2)}, u32[]{:S(2)}) %collective-permute-start.1) | collective-permute-done | bytes 294944 | tf_op jit(solution)/shard_map/ppermute | solution.py:236
  26.9 1.0 %shard_map.105 = (bf16[4,288,512]{2,1,0:T(8,128)(2,1)S(1)}, bf16[288,512]{1,0:T(8,128)(2,1)S(1)}, bf16[288,512]{1,0:T(8,128)(2,1)S(1)}) custom-call(s32[2]{0:T(128)S(1)} %pad_add_fusion.me_ref, bf16[288,512]{1,0:T(8,128)(2,1)S(1)} %get-tuple-element.19.refs_0_, bf16[288,512]{1,0:T(8,128)(2,1)S(1)} %collective-permute-done.refs_1_, ...), custom_call_target="tpu_custom_call" | custom-call | bytes 2949128 | tf_op jit(solution)/shard_map/pallas_call | solution.py:19
  27.9 1.3 %collective-permute-start.3 = (bf16[288,512]{1,0:T(8,128)(2,1)S(1)}, bf16[288,512]{1,0:T(8,128)(2,1)S(1)}, u32[]{:S(2)}, u32[]{:S(2)}) collective-permute-start(bf16[288,512]{1,0:T(8,128)(2,1)S(1)} %get-tuple-element.24), channel_id=1, source_target_pairs={{0,1},{1,2},{2,3},{3,4},{4,5},{5,6},{6,7},{8,9},{9,10},{10,11},{11... | collective-permute-start | bytes 884744 | tf_op jit(solution)/shard_map/ppermute | solution.py:256
  29.2 1.3 %collective-permute-start.4 = (bf16[288,512]{1,0:T(8,128)(2,1)S(1)}, bf16[288,512]{1,0:T(8,128)(2,1)S(1)}, u32[]{:S(2)}, u32[]{:S(2)}) collective-permute-start(bf16[288,512]{1,0:T(8,128)(2,1)S(1)} %get-tuple-element.25), channel_id=1, source_target_pairs={{1,0},{2,1},{3,2},{4,3},{5,4},{6,5},{7,6},{9,8},{10,9},{11,10},{12... | collective-permute-start | bytes 884744 | tf_op jit(solution)/shard_map/ppermute | solution.py:257
  30.5 0.0 copy-start
  30.5 2.3 %copy-done = bf16[3,3,512,512]{3,2,1,0:T(8,128)(2,1)S(1)} copy-done((bf16[3,3,512,512]{3,2,1,0:T(8,128)(2,1)S(1)}, bf16[3,3,512,512]{3,2,1,0:T(8,128)(2,1)}, u32[]{:S(2)}) %copy-start) | copy-done | bytes 4718616
  32.8 4.2 %shard_map.106.part_ref = f32[4,256,512]{2,1,0:T(8,128)S(1)} custom-call(bf16[4,288,512]{2,1,0:T(8,128)(2,1)S(1)} %get-tuple-element.23.x_ref, bf16[3,3,512,512]{3,2,1,0:T(8,128)(2,1)S(1)} %copy-done), custom_call_target="tpu_custom_call" | custom-call | flops 4026531840 | bytes 7995392 | tf_op jit(solution)/shard_map/pallas_call | solution.py:19
  37.1 1.8 %shard_map.107.act_ref.refs_4_ = bf16[4,256,1536]{2,1,0:T(8,128)(2,1)S(1)} custom-call(f32[4,256,512]{2,1,0:T(8,128)S(1)} %shard_map.106.part_ref, bf16[288,512]{1,0:T(8,128)(2,1)S(1)} %collective-permute-done.3.up_ref, bf16[288,512]{1,0:T(8,128)(2,1)S(1)} %collective-permute-done.4.down_ref, bf16[3,3,512,512]{3,2,1,0:T(8,128)(2,1)S(1)} %bitcast.38), custom_call_target="tpu_custom_call" | custom-call | flops 805306368 | bytes 10551296 | tf_op jit(solution)/shard_map/pallas_call | solution.py:19
  38.9 0.7 copy-done.8
  39.6 0.9 %copy-done.9 = bf16[256,512]{1,0:T(8,128)(2,1)S(1)} copy-done((bf16[256,512]{1,0:T(8,128)(2,1)S(1)}, bf16[256,512]{1,0:T(8,128)(2,1)}, u32[]{:S(2)}) %copy-start.9) | copy-done | bytes 262168
  40.6 0.0 copy-start.7
  40.6 3.2 %shard_map.110 = (f32[256,1536]{1,0:T(8,128)S(1)}, bf16[256,1536]{1,0:T(8,128)(2,1)S(1)}) custom-call(s32[2]{0:T(128)S(1)} %pad_add_fusion.me_ref, bf16[256,512]{1,0:T(8,128)(2,1)S(1)} %get-tuple-element.26.refs_0_, bf16[256,512]{1,0:T(8,128)(2,1)} %collective-permute-done.8.refs_1_, bf16[256,512]{1,0:T(8,128)(2,1)S(1)} %collective-permute-done.9.refs_2_, ...), custom_call_target="tpu_custom_call" | custom-call | flops 1610612736 | bytes 6553608 | tf_op jit(solution)/shard_map/pallas_call | solution.py:19
  43.9 2.7 %collective-permute-start.11 = (bf16[256,1536]{1,0:T(8,128)(2,1)S(1)}, bf16[256,1536]{1,0:T(8,128)(2,1)S(1)}, u32[]{:S(2)}, u32[]{:S(2)}) collective-permute-start(bf16[256,1536]{1,0:T(8,128)(2,1)S(1)} %get-tuple-element.31), channel_id=1, source_target_pairs={{0,1},{1,0},{2,3},{3,2},{4,5},{5,4},{6,7},{7,6},{8,9},{9,8},{10,11... | collective-permute-start | bytes 2359304 | tf_op jit(solution)/shard_map/ppermute | solution.py:236
  46.6 7.5 %shard_map.108 = bf16[4,4,64,512]{3,2,1,0:T(8,128)(2,1)S(1)} custom-call(bf16[4,288,512]{2,1,0:T(8,128)(2,1)S(1)} %get-tuple-element.23.x_ref, bf16[4,256,1536]{2,1,0:T(8,128)(2,1)S(1)} %shard_map.107.act_ref.refs_4_, bf16[1536,512]{1,0:T(8,128)(2,1)S(1)} %bitcast.39, f32[1,512]{1,0:T(1,128)S(1)} %bitcast.40, bf16[512,512]{1,0:T(8,128)(2,1)S(1)} %copy-done.4, ...), custom_call_target="tpu_custom_call" | custom-call | flops 4294967296 | bytes 9046016 | tf_op jit(solution)/shard_map/pallas_call | solution.py:19
  54.1 0.9 %dynamic-slice_bitcast_fusion = (bf16[4,64,512]{2,1,0:T(8,128)(2,1)}, bf16[4,64,512]{2,1,0:T(8,128)(2,1)}, bf16[4,64,512]{2,1,0:T(8,128)(2,1)}, bf16[1,4,64,512]{3,2,1,0:T(8,128)(2,1)S(1)}) fusion(bf16[4,4,64,512]{3,2,1,0:T(8,128)(2,1)S(1)} %shard_map.108, s32[]{:T(128)S(6)} %select_n.49, s32[]{:T(128)S(6)} %select_n.48, s32[]{:T(128)S(6)} %select_n.47, ...), kind=kLoop, calls=%fused_computation.5 | loop fusion | bytes 2097168 | tf_op jit(solution)/shard_map/jit(dynamic_index_in_dim)/squeeze | solution.py:310
  55.0 2.5 %collective-permute-start.6 = (bf16[4,64,512]{2,1,0:T(8,128)(2,1)}, bf16[4,64,512]{2,1,0:T(8,128)(2,1)S(1)}, u32[]{:S(2)}, u32[]{:S(2)}) collective-permute-start(bf16[4,64,512]{2,1,0:T(8,128)(2,1)} %get-tuple-element.39), channel_id=1, source_target_pairs={{0,16},{8,24},{16,0},{24,8},{1,17},{9,25},{17,1},{25,9},{2,18},{10... | collective-permute-start | bytes 786440 | tf_op jit(solution)/shard_map/ppermute | solution.py:236
  57.5 1.5 %collective-permute-start.7 = (bf16[4,64,512]{2,1,0:T(8,128)(2,1)}, bf16[4,64,512]{2,1,0:T(8,128)(2,1)S(1)}, u32[]{:S(2)}, u32[]{:S(2)}) collective-permute-start(bf16[4,64,512]{2,1,0:T(8,128)(2,1)} %get-tuple-element.38), channel_id=1, source_target_pairs={{0,24},{8,16},{16,8},{24,0},{1,25},{9,17},{17,9},{25,1},{2,26},{10... | collective-permute-start | bytes 786440 | tf_op jit(solution)/shard_map/ppermute | solution.py:236
  59.0 1.1 %broadcast_in_dim.3 = bf16[4,4,4,16,512]{4,3,2,1,0:T(8,128)(2,1)} broadcast(bf16[]{:T(256)} %constant.59.clone.1), dimensions={} | broadcast | bytes 1048578 | tf_op jit(solution)/shard_map/broadcast_in_dim | solution.py:323
  60.1 0.7 copy_dynamic-update-slice_fusion.3
  60.8 3.7 %collective-permute-done.5 = bf16[4,64,512]{2,1,0:T(8,128)(2,1)} collective-permute-done((bf16[4,64,512]{2,1,0:T(8,128)(2,1)}, bf16[4,64,512]{2,1,0:T(8,128)(2,1)}, u32[]{:S(2)}, u32[]{:S(2)}) %collective-permute-start.5) | collective-permute-done | bytes 262176 | tf_op jit(solution)/shard_map/ppermute | solution.py:236
  64.5 1.7 %copy_dynamic-update-slice_fusion.2 = bf16[4,4,4,16,512]{4,3,2,1,0:T(8,128)(2,1)} fusion(bf16[4,4,4,16,512]{4,3,2,1,0:T(8,128)(2,1)} %copy_dynamic-update-slice_fusion.3, s32[]{:T(128)S(6)} %select_n.47, bf16[4,4,1,16,512]{4,3,0,1,2:T(8,128)(2,1)} %bitcast.8), kind=kLoop, calls=%fused_computation.3 | loop fusion | bytes 524292 | tf_op jit(solution)/shard_map/dynamic_update_slice | solution.py:326
  66.2 0.9 shard_map.111
  67.1 0.1 collective-permute-start.12
  67.1 2.6 %collective-permute-start.13 = (bf16[256,384]{1,0:T(8,128)(2,1)S(1)}, bf16[256,384]{1,0:T(8,128)(2,1)S(1)}, u32[]{:S(2)}, u32[]{:S(2)}) collective-permute-start(bf16[256,384]{1,0:T(8,128)(2,1)S(1)} %get-tuple-element.34), channel_id=1, source_target_pairs={{0,16},{8,24},{16,0},{24,8},{1,17},{9,25},{17,1},{25,9},{2,18},{10... | collective-permute-start | bytes 589832 | tf_op jit(solution)/shard_map/ppermute | solution.py:236
  69.7 1.4 %collective-permute-start.14 = (bf16[256,384]{1,0:T(8,128)(2,1)S(1)}, bf16[256,384]{1,0:T(8,128)(2,1)S(1)}, u32[]{:S(2)}, u32[]{:S(2)}) collective-permute-start(bf16[256,384]{1,0:T(8,128)(2,1)S(1)} %get-tuple-element.35), channel_id=1, source_target_pairs={{0,24},{8,16},{16,8},{24,0},{1,25},{9,17},{17,9},{25,1},{2,26},{10... | collective-permute-start | bytes 589832 | tf_op jit(solution)/shard_map/ppermute | solution.py:236
  71.1 0.7 copy_dynamic-update-slice_fusion.1
  71.8 3.2 %collective-permute-done.12 = bf16[256,384]{1,0:T(8,128)(2,1)S(1)} collective-permute-done((bf16[256,384]{1,0:T(8,128)(2,1)S(1)}, bf16[256,384]{1,0:T(8,128)(2,1)S(1)}, u32[]{:S(2)}, u32[]{:S(2)}) %collective-permute-start.12) | collective-permute-done | bytes 196640 | tf_op jit(solution)/shard_map/ppermute | solution.py:236
  75.0 2.6 %collective-permute-done.13 = bf16[256,384]{1,0:T(8,128)(2,1)S(1)} collective-permute-done((bf16[256,384]{1,0:T(8,128)(2,1)S(1)}, bf16[256,384]{1,0:T(8,128)(2,1)S(1)}, u32[]{:S(2)}, u32[]{:S(2)}) %collective-permute-start.13) | collective-permute-done | bytes 196640 | tf_op jit(solution)/shard_map/ppermute | solution.py:236
  77.6 1.9 %collective-permute-done.14 = bf16[256,384]{1,0:T(8,128)(2,1)S(1)} collective-permute-done((bf16[256,384]{1,0:T(8,128)(2,1)S(1)}, bf16[256,384]{1,0:T(8,128)(2,1)S(1)}, u32[]{:S(2)}, u32[]{:S(2)}) %collective-permute-start.14) | collective-permute-done | bytes 196640 | tf_op jit(solution)/shard_map/ppermute | solution.py:236
  79.5 0.1 convert_add_fusion
  79.6 2.2 %collective-permute-start.15 = (bf16[64,384]{1,0:T(8,128)(2,1)S(1)}, bf16[64,384]{1,0:T(8,128)(2,1)S(1)}, u32[]{:S(2)}, u32[]{:S(2)}) collective-permute-start(bf16[64,384]{1,0:T(8,128)(2,1)S(1)} %get-tuple-element.42), channel_id=1, source_target_pairs={{0,2},{1,3},{2,0},{3,1},{4,6},{5,7},{6,4},{7,5},{8,10},{9,11},{10,... | collective-permute-start | bytes 147464 | tf_op jit(solution)/shard_map/ppermute | solution.py:236
  81.8 2.6 %collective-permute-start.16 = (bf16[64,384]{1,0:T(8,128)(2,1)S(1)}, bf16[64,384]{1,0:T(8,128)(2,1)S(1)}, u32[]{:S(2)}, u32[]{:S(2)}) collective-permute-start(bf16[64,384]{1,0:T(8,128)(2,1)S(1)} %get-tuple-element.44), channel_id=1, source_target_pairs={{0,4},{1,5},{2,6},{3,7},{4,0},{5,1},{6,2},{7,3},{8,12},{9,13},{10,... | collective-permute-start | bytes 147464 | tf_op jit(solution)/shard_map/ppermute | solution.py:236
  84.4 0.7 copy_dynamic-update-slice_fusion
  85.1 2.7 %collective-permute-done.16 = bf16[64,384]{1,0:T(8,128)(2,1)S(1)} collective-permute-done((bf16[64,384]{1,0:T(8,128)(2,1)S(1)}, bf16[64,384]{1,0:T(8,128)(2,1)S(1)}, u32[]{:S(2)}, u32[]{:S(2)}) %collective-permute-start.16) | collective-permute-done | bytes 49184 | tf_op jit(solution)/shard_map/ppermute | solution.py:236
  87.8 2.4 %collective-permute-done.17 = bf16[64,384]{1,0:T(8,128)(2,1)S(1)} collective-permute-done((bf16[64,384]{1,0:T(8,128)(2,1)S(1)}, bf16[64,384]{1,0:T(8,128)(2,1)S(1)}, u32[]{:S(2)}, u32[]{:S(2)}) %collective-permute-start.17) | collective-permute-done | bytes 49184 | tf_op jit(solution)/shard_map/ppermute | solution.py:236
  90.4 0.6 copy.15
  (38 shorter events, 0.2 us)
Async XLA Ops:
  0.7 1.2 %copy-start.1 = (bf16[4,4,64,512]{3,2,1,0:T(8,128)(2,1)S(1)}, bf16[4,4,64,512]{3,2,1,0:T(8,128)(2,1)}, u32[]{:S(2)}) copy-start(bf16[4,4,64,512]{3,2,1,0:T(8,128)(2,1)} %x_ref.2) | copy-start | bytes 3145732
  3.1 11.7 %collective-permute-start = (bf16[288,512]{1,0:T(8,128)(2,1)S(1)}, bf16[288,512]{1,0:T(8,128)(2,1)S(1)}, u32[]{:S(2)}, u32[]{:S(2)}) collective-permute-start(bf16[288,512]{1,0:T(8,128)(2,1)S(1)} %get-tuple-element.20), channel_id=1, source_target_pairs={{0,8},{8,0},{16,24},{24,16},{1,9},{9,1},{17,25},{25,17},{2,10},{10... | collective-permute-start | bytes 884744 | tf_op jit(solution)/shard_map/ppermute | solution.py:236
  6.1 20.8 %collective-permute-start.1 = (bf16[288,512]{1,0:T(8,128)(2,1)S(1)}, bf16[288,512]{1,0:T(8,128)(2,1)S(1)}, u32[]{:S(2)}, u32[]{:S(2)}) collective-permute-start(bf16[288,512]{1,0:T(8,128)(2,1)S(1)} %get-tuple-element.21), channel_id=1, source_target_pairs={{0,16},{8,24},{16,0},{24,8},{1,17},{9,25},{17,1},{25,9},{2,18},{10... | collective-permute-start | bytes 884744 | tf_op jit(solution)/shard_map/ppermute | solution.py:236
  7.6 19.3 %collective-permute-start.2 = (bf16[288,512]{1,0:T(8,128)(2,1)S(1)}, bf16[288,512]{1,0:T(8,128)(2,1)S(1)}, u32[]{:S(2)}, u32[]{:S(2)}) collective-permute-start(bf16[288,512]{1,0:T(8,128)(2,1)S(1)} %get-tuple-element.22), channel_id=1, source_target_pairs={{0,24},{8,16},{16,8},{24,0},{1,25},{9,17},{17,9},{25,1},{2,26},{10... | collective-permute-start | bytes 884744 | tf_op jit(solution)/shard_map/ppermute | solution.py:236
  7.6 1.2 %copy-start.2 = (bf16[4,4,64,512]{3,2,1,0:T(8,128)(2,1)S(1)}, bf16[4,4,64,512]{3,2,1,0:T(8,128)(2,1)}, u32[]{:S(2)}) copy-start(bf16[4,4,64,512]{3,2,1,0:T(8,128)(2,1)} %x_ref.3) | copy-start | bytes 3145732
  8.8 28.2 %slice-start = ((s8[4718592]{0:T(1024)(128)(4,1)}), s8[524288]{0:T(1024)(128)(4,1)S(1)}, s32[]{:S(2)}) async-start(s8[4718592]{0:T(1024)(128)(4,1)} %bitcast.37), calls=%async_computation | async-start | bytes 1048576
  10.6 0.7 copy-start.10
  11.3 27.6 %collective-permute-start.10 = (bf16[256,512]{1,0:T(8,128)(2,1)}, bf16[256,512]{1,0:T(8,128)(2,1)S(1)}, u32[]{:S(2)}, u32[]{:S(2)}) collective-permute-start(bf16[256,512]{1,0:T(8,128)(2,1)} %get-tuple-element.29), channel_id=1, source_target_pairs={{0,24},{8,16},{16,8},{24,0},{1,25},{9,17},{17,9},{25,1},{2,26},{10... | collective-permute-start | bytes 786440 | tf_op jit(solution)/shard_map/ppermute | solution.py:236
  14.2 25.5 %collective-permute-start.8 = (bf16[256,512]{1,0:T(8,128)(2,1)}, bf16[256,512]{1,0:T(8,128)(2,1)}, u32[]{:S(2)}, u32[]{:S(2)}) collective-permute-start(bf16[256,512]{1,0:T(8,128)(2,1)} %get-tuple-element.27), channel_id=1, source_target_pairs={{0,8},{8,0},{16,24},{24,16},{1,9},{9,1},{17,25},{25,17},{2,10},{10... | collective-permute-start | bytes 786440 | tf_op jit(solution)/shard_map/ppermute | solution.py:236
  14.7 24.9 %collective-permute-start.9 = (bf16[256,512]{1,0:T(8,128)(2,1)}, bf16[256,512]{1,0:T(8,128)(2,1)S(1)}, u32[]{:S(2)}, u32[]{:S(2)}) collective-permute-start(bf16[256,512]{1,0:T(8,128)(2,1)} %copy-done.10), channel_id=1, source_target_pairs={{0,16},{8,24},{16,0},{24,8},{1,17},{9,25},{17,1},{25,9},{2,18},{10... | collective-permute-start | bytes 786440 | tf_op jit(solution)/shard_map/ppermute | solution.py:236
  27.9 9.2 %collective-permute-start.3 = (bf16[288,512]{1,0:T(8,128)(2,1)S(1)}, bf16[288,512]{1,0:T(8,128)(2,1)S(1)}, u32[]{:S(2)}, u32[]{:S(2)}) collective-permute-start(bf16[288,512]{1,0:T(8,128)(2,1)S(1)} %get-tuple-element.24), channel_id=1, source_target_pairs={{0,1},{1,2},{2,3},{3,4},{4,5},{5,6},{6,7},{8,9},{9,10},{10,11},{11... | collective-permute-start | bytes 884744 | tf_op jit(solution)/shard_map/ppermute | solution.py:256
  29.2 7.9 %collective-permute-start.4 = (bf16[288,512]{1,0:T(8,128)(2,1)S(1)}, bf16[288,512]{1,0:T(8,128)(2,1)S(1)}, u32[]{:S(2)}, u32[]{:S(2)}) collective-permute-start(bf16[288,512]{1,0:T(8,128)(2,1)S(1)} %get-tuple-element.25), channel_id=1, source_target_pairs={{1,0},{2,1},{3,2},{4,3},{5,4},{6,5},{7,6},{9,8},{10,9},{11,10},{12... | collective-permute-start | bytes 884744 | tf_op jit(solution)/shard_map/ppermute | solution.py:257
  30.5 2.3 %copy-start = (bf16[3,3,512,512]{3,2,1,0:T(8,128)(2,1)S(1)}, bf16[3,3,512,512]{3,2,1,0:T(8,128)(2,1)}, u32[]{:S(2)}) copy-start(bf16[3,3,512,512]{3,2,1,0:T(8,128)(2,1)} %w_ref.3) | copy-start | bytes 14155780
  32.8 4.2 %slice-start.1 = ((s8[4718592]{0:T(1024)(128)(4,1)}), s8[4194304]{0:T(1024)(128)(4,1)S(1)}, s32[]{:S(2)}) async-start(s8[4718592]{0:T(1024)(128)(4,1)} %bitcast.37), calls=%async_computation.1 | async-start | bytes 8388608
  38.9 0.7 copy-start.8
  39.6 1.0 %copy-start.9 = (bf16[256,512]{1,0:T(8,128)(2,1)S(1)}, bf16[256,512]{1,0:T(8,128)(2,1)}, u32[]{:S(2)}) copy-start(bf16[256,512]{1,0:T(8,128)(2,1)} %copy-done.8) | copy-start | bytes 786436
  40.6 6.0 %copy-start.3 = (bf16[3,512,512]{2,1,0:T(8,128)(2,1)S(1)}, bf16[3,512,512]{2,1,0:T(8,128)(2,1)}, u32[]{:S(2)}) copy-start(bf16[3,512,512]{2,1,0:T(8,128)(2,1)} %param.11) | copy-start | bytes 4718596
  40.6 6.0 %copy-start.4 = (bf16[512,512]{1,0:T(8,128)(2,1)S(1)}, bf16[512,512]{1,0:T(8,128)(2,1)}, u32[]{:S(2)}) copy-start(bf16[512,512]{1,0:T(8,128)(2,1)} %q_ref.1) | copy-start | bytes 1572868
  40.6 6.0 %copy-start.5 = (bf16[512,512]{1,0:T(8,128)(2,1)S(1)}, bf16[512,512]{1,0:T(8,128)(2,1)}, u32[]{:S(2)}) copy-start(bf16[512,512]{1,0:T(8,128)(2,1)} %k_ref.1) | copy-start | bytes 1572868
  40.6 6.0 %copy-start.6 = (bf16[512,512]{1,0:T(8,128)(2,1)S(1)}, bf16[512,512]{1,0:T(8,128)(2,1)}, u32[]{:S(2)}) copy-start(bf16[512,512]{1,0:T(8,128)(2,1)} %v_ref.1) | copy-start | bytes 1572868
  40.6 6.0 %copy-start.7 = (bf16[512,512]{1,0:T(8,128)(2,1)S(1)}, bf16[512,512]{1,0:T(8,128)(2,1)}, u32[]{:S(2)}) copy-start(bf16[512,512]{1,0:T(8,128)(2,1)} %o_ref.1) | copy-start | bytes 1572868
  40.6 6.0 %copy-start.11 = (f32[512]{0:T(512)S(1)}, f32[512]{0:T(512)}, u32[]{:S(2)}) copy-start(f32[512]{0:T(512)} %param.12) | copy-start | bytes 6148
  43.9 22.4 %collective-permute-start.11 = (bf16[256,1536]{1,0:T(8,128)(2,1)S(1)}, bf16[256,1536]{1,0:T(8,128)(2,1)S(1)}, u32[]{:S(2)}, u32[]{:S(2)}) collective-permute-start(bf16[256,1536]{1,0:T(8,128)(2,1)S(1)} %get-tuple-element.31), channel_id=1, source_target_pairs={{0,1},{1,0},{2,3},{3,2},{4,5},{5,4},{6,7},{7,6},{8,9},{9,8},{10,11... | collective-permute-start | bytes 2359304 | tf_op jit(solution)/shard_map/ppermute | solution.py:236
  55.0 9.5 %collective-permute-start.5 = (bf16[4,64,512]{2,1,0:T(8,128)(2,1)}, bf16[4,64,512]{2,1,0:T(8,128)(2,1)}, u32[]{:S(2)}, u32[]{:S(2)}) collective-permute-start(bf16[4,64,512]{2,1,0:T(8,128)(2,1)} %get-tuple-element.40), channel_id=1, source_target_pairs={{0,8},{8,0},{16,24},{24,16},{1,9},{9,1},{17,25},{25,17},{2,10},{10... | collective-permute-start | bytes 786440 | tf_op jit(solution)/shard_map/ppermute | solution.py:236
  55.0 16.0 %collective-permute-start.6 = (bf16[4,64,512]{2,1,0:T(8,128)(2,1)}, bf16[4,64,512]{2,1,0:T(8,128)(2,1)S(1)}, u32[]{:S(2)}, u32[]{:S(2)}) collective-permute-start(bf16[4,64,512]{2,1,0:T(8,128)(2,1)} %get-tuple-element.39), channel_id=1, source_target_pairs={{0,16},{8,24},{16,0},{24,8},{1,17},{9,25},{17,1},{25,9},{2,18},{10... | collective-permute-start | bytes 786440 | tf_op jit(solution)/shard_map/ppermute | solution.py:236
  57.5 26.9 %collective-permute-start.7 = (bf16[4,64,512]{2,1,0:T(8,128)(2,1)}, bf16[4,64,512]{2,1,0:T(8,128)(2,1)S(1)}, u32[]{:S(2)}, u32[]{:S(2)}) collective-permute-start(bf16[4,64,512]{2,1,0:T(8,128)(2,1)} %get-tuple-element.38), channel_id=1, source_target_pairs={{0,24},{8,16},{16,8},{24,0},{1,25},{9,17},{17,9},{25,1},{2,26},{10... | collective-permute-start | bytes 786440 | tf_op jit(solution)/shard_map/ppermute | solution.py:236
  67.1 7.9 %collective-permute-start.12 = (bf16[256,384]{1,0:T(8,128)(2,1)S(1)}, bf16[256,384]{1,0:T(8,128)(2,1)S(1)}, u32[]{:S(2)}, u32[]{:S(2)}) collective-permute-start(bf16[256,384]{1,0:T(8,128)(2,1)S(1)} %get-tuple-element.33), channel_id=1, source_target_pairs={{0,8},{8,0},{16,24},{24,16},{1,9},{9,1},{17,25},{25,17},{2,10},{10... | collective-permute-start | bytes 589832 | tf_op jit(solution)/shard_map/ppermute | solution.py:236
  67.1 10.4 %collective-permute-start.13 = (bf16[256,384]{1,0:T(8,128)(2,1)S(1)}, bf16[256,384]{1,0:T(8,128)(2,1)S(1)}, u32[]{:S(2)}, u32[]{:S(2)}) collective-permute-start(bf16[256,384]{1,0:T(8,128)(2,1)S(1)} %get-tuple-element.34), channel_id=1, source_target_pairs={{0,16},{8,24},{16,0},{24,8},{1,17},{9,25},{17,1},{25,9},{2,18},{10... | collective-permute-start | bytes 589832 | tf_op jit(solution)/shard_map/ppermute | solution.py:236
  69.7 9.8 %collective-permute-start.14 = (bf16[256,384]{1,0:T(8,128)(2,1)S(1)}, bf16[256,384]{1,0:T(8,128)(2,1)S(1)}, u32[]{:S(2)}, u32[]{:S(2)}) collective-permute-start(bf16[256,384]{1,0:T(8,128)(2,1)S(1)} %get-tuple-element.35), channel_id=1, source_target_pairs={{0,24},{8,16},{16,8},{24,0},{1,25},{9,17},{17,9},{25,1},{2,26},{10... | collective-permute-start | bytes 589832 | tf_op jit(solution)/shard_map/ppermute | solution.py:236
  79.6 5.5 %collective-permute-start.15 = (bf16[64,384]{1,0:T(8,128)(2,1)S(1)}, bf16[64,384]{1,0:T(8,128)(2,1)S(1)}, u32[]{:S(2)}, u32[]{:S(2)}) collective-permute-start(bf16[64,384]{1,0:T(8,128)(2,1)S(1)} %get-tuple-element.42), channel_id=1, source_target_pairs={{0,2},{1,3},{2,0},{3,1},{4,6},{5,7},{6,4},{7,5},{8,10},{9,11},{10,... | collective-permute-start | bytes 147464 | tf_op jit(solution)/shard_map/ppermute | solution.py:236
  81.8 6.0 %collective-permute-start.16 = (bf16[64,384]{1,0:T(8,128)(2,1)S(1)}, bf16[64,384]{1,0:T(8,128)(2,1)S(1)}, u32[]{:S(2)}, u32[]{:S(2)}) collective-permute-start(bf16[64,384]{1,0:T(8,128)(2,1)S(1)} %get-tuple-element.44), channel_id=1, source_target_pairs={{0,4},{1,5},{2,6},{3,7},{4,0},{5,1},{6,2},{7,3},{8,12},{9,13},{10,... | collective-permute-start | bytes 147464 | tf_op jit(solution)/shard_map/ppermute | solution.py:236
  84.4 5.9 %collective-permute-start.17 = (bf16[64,384]{1,0:T(8,128)(2,1)S(1)}, bf16[64,384]{1,0:T(8,128)(2,1)S(1)}, u32[]{:S(2)}, u32[]{:S(2)}) collective-permute-start(bf16[64,384]{1,0:T(8,128)(2,1)S(1)} %get-tuple-element.43), channel_id=1, source_target_pairs={{0,6},{1,7},{2,4},{3,5},{4,2},{5,3},{6,0},{7,1},{8,14},{9,15},{10,... | collective-permute-start | bytes 147464 | tf_op jit(solution)/shard_map/ppermute | solution.py:236

commit v2 on v1

--- a/solution.py
+++ b/solution.py
@@ -52,7 +52,7 @@
         self.sides = 2 * rows * frames
 
 
-def pack_kernel(z, halo, me_ref, x_ref, *outs):
+def pack_kernel(z, halo, me_ref, x_ref, outs):
     me = me_ref[0]
 
     def source(q):
@@ -65,7 +65,7 @@
         rows = x_ref[:, r].reshape(z.fl * z.w, z.c)
         cut = moved(matrix, rows)
         for k in range(z.n):
-            outs[k][r * z.piece : (r + 1) * z.piece] = cut[k * z.piece : (k + 1) * z.piece]
+            outs[k, r * z.piece : (r + 1) * z.piece] = cut[k * z.piece : (k + 1) * z.piece]
     if not halo:
         return
 
@@ -81,7 +81,7 @@
     total = z.fl * z.r * z.w
     cut = moved(chooser(z.n * z.sides, total, edge), x_ref[...].reshape(total, z.c))
     for k in range(z.n):
-        outs[k][z.main : z.main + z.sides] = cut[k * z.sides : (k + 1) * z.sides]
+        outs[k, z.main : z.main + z.sides] = cut[k * z.sides : (k + 1) * z.sides]
 
 
 def gather_matrix(z, me):
@@ -92,8 +92,7 @@
     return chooser(z.block, z.block, source)
 
 
-def assemble_kernel(z, me_ref, *refs):
-    parts, (out, top, bottom) = refs[: z.n], refs[z.n :]
+def assemble_kernel(z, me_ref, parts, out, top, bottom):
     me = me_ref[0]
     matrix = gather_matrix(z, me)
 
@@ -103,11 +102,12 @@
         return ((me ^ s) * 2 * z.r + head) * z.fl + q % z.fl
 
     count = z.n * z.sides
-    tails = jnp.concatenate([p[z.main : z.main + z.sides] for p in parts], axis=0)
+    tails = jnp.concatenate([parts[k, z.main : z.main + z.sides] for k in range(z.n)], axis=0)
     tails = moved(chooser(count, count, edge), tails)
     last = z.f + z.block
     for r in range(z.r):
-        rows = jnp.concatenate([p[r * z.piece : (r + 1) * z.piece] for p in parts], axis=0)
+        cut = slice(r * z.piece, (r + 1) * z.piece)
+        rows = jnp.concatenate([parts[k, cut] for k in range(z.n)], axis=0)
         rows = moved(matrix, rows)
         left = tails[r * z.f : (r + 1) * z.f]
         right = tails[(z.r + r) * z.f : (z.r + r + 1) * z.f]
@@ -188,12 +188,12 @@
             out[i, r] = encoded[i * z.piece : (i + 1) * z.piece]
 
 
-def grad_kernel(z, width, me_ref, *refs):
-    parts, (act_ref, keep, send, cot) = refs[: z.n], refs[z.n :]
+def grad_kernel(z, width, me_ref, parts, act_ref, keep, send, cot):
     matrix = gather_matrix(z, me_ref[0])
     mine = me_ref[1] == 0
     for r in range(z.r):
-        rows = jnp.concatenate([p[r * z.piece : (r + 1) * z.piece] for p in parts], axis=0)
+        cut = slice(r * z.piece, (r + 1) * z.piece)
+        rows = jnp.concatenate([parts[k, cut] for k in range(z.n)], axis=0)
         cot[r * z.block : (r + 1) * z.block] = moved(matrix, rows)
     flat = cot[...]
     for k in range(3):
@@ -211,24 +211,25 @@
             send[i * width : (i + 1) * width, lanes] = jnp.where(mine, high, low).astype(BF)
 
 
-def split_kernel(z, me_ref, keep_ref, got_ref, *outs):
-    me = me_ref[0]
+def split_kernel(z, keep_ref, got_ref, out):
     wide = z.c // z.n
     for tap in range(3):
-        place = slice(tap * wide, (tap + 1) * wide)
-        if wide % 128 == 0:
-            for k in range(z.n):
-                lanes = pl.ds(pl.multiple_of(tap * z.c + (me ^ k) * wide, 128), wide)
-                total = keep_ref[:, lanes] + got_ref[:, lanes].astype(F32)
-                outs[k][:, place] = total.astype(outs[k].dtype)
-            continue
         lanes = slice(tap * z.c, (tap + 1) * z.c)
-        total = keep_ref[:, lanes] + got_ref[:, lanes].astype(F32)
+        total = (keep_ref[:, lanes] + got_ref[:, lanes].astype(F32)).astype(BF)
         for k in range(z.n):
-            cut = total[:, 0:wide]
-            for i in range(1, z.n):
-                cut = jnp.where((me ^ k) == i, total[:, i * wide : (i + 1) * wide], cut)
-            outs[k][:, place] = cut.astype(outs[k].dtype)
+            out[k, :, tap * wide : (tap + 1) * wide] = total[:, k * wide : (k + 1) * wide]
+
+
+def load_kernel(count, after_ref, *refs):
+    sources, places, sem = refs[:count], refs[count : 2 * count], refs[2 * count]
+    copies = [
+        pltpu.make_async_copy(source, place, sem.at[i])
+        for i, (source, place) in enumerate(zip(sources, places))
+    ]
+    for copy in copies:
+        copy.start()
+    for copy in copies:
+        copy.wait()
 
 
 def swap(value, axis, k):
@@ -240,24 +241,47 @@
     n = lax.axis_size("tm")
     space = lax.axis_size("space")
     z = Sizes(n, *frames_in.shape)
-    me = lax.axis_index("tm")
     here = lax.axis_index("space")
-    ids = jnp.stack([me, here % 2]).astype(jnp.int32)
-    part = [shape((z.main + z.sides, z.c))] * n
-    packed = call(functools.partial(pack_kernel, z, True), part, ids, frames_in)
-    got = [packed[0]] + [swap(packed[k], "tm", k) for k in range(1, n)]
+    ids = jnp.stack([0 * here, here % 2]).astype(jnp.int32)
+    temporal = temporal.reshape(3 * z.c, z.c)
+
+    def exchange(value):
+        return lax.all_to_all(value, "tm", 0, 0, tiled=True)
+
+    (packed,) = call(
+        functools.partial(pack_kernel, z, True),
+        [shape((n, z.main + z.sides, z.c))],
+        ids,
+        frames_in,
+    )
+    got = exchange(packed)
+    weights = (spatial, temporal, q_w, k_w, v_w, o_w)
+    spatial, temporal, q_w, k_w, v_w, o_w = pl.pallas_call(
+        functools.partial(load_kernel, len(weights)),
+        out_shape=tuple(shape(w.shape) for w in weights),
+        in_specs=[pl.BlockSpec(memory_space=pl.ANY)] * (1 + len(weights)),
+        out_specs=tuple(VMEM for _ in weights),
+        scratch_shapes=[pltpu.SemaphoreType.DMA((len(weights),))],
+        compiler_params=pltpu.CompilerParams(vmem_limit_bytes=40 * 2**20),
+        cost_estimate=pl.CostEstimate(flops=0, bytes_accessed=16 * 2**20, transcendentals=0),
+    )(packed, *weights)
     line = z.block + 2 * z.f
     x, top, bottom = call(
         functools.partial(assemble_kernel, z),
         [shape((z.r, line, z.c)), shape((line, z.c)), shape((line, z.c))],
         ids,
-        *got,
+        got,
     )
     up = lax.ppermute(bottom, "space", [(i, i + 1) for i in range(space - 1)])
     down = lax.ppermute(top, "space", [(i + 1, i) for i in range(space - 1)])
-    part = [shape((z.main, z.c))] * n
-    cot = call(functools.partial(pack_kernel, z, False), part, ids, cotangent)
-    cot = [cot[0]] + [swap(cot[k], "tm", k) for k in range(1, n)]
+    (cot,) = call(
+        functools.partial(pack_kernel, z, False),
+        [shape((n, z.main, z.c))],
+        ids,
+        cotangent,
+    )
+    cot, x = lax.optimization_barrier((cot, x))
+    cot = exchange(cot)
     one = 2 * z.r * z.block * z.c * z.c
     (inner,) = call(
         functools.partial(inner_kernel, z),
@@ -280,18 +304,18 @@
         functools.partial(grad_kernel, z, width),
         [shape((z.c // 2, 3 * z.c), F32), shape((z.c // 2, 3 * z.c))],
         ids,
-        *cot,
+        cot,
         acts,
         flops=3 * one,
         scratch=[pltpu.VMEM((z.r * z.block, z.c), BF)],
     )
-    other = swap(send, "space", 1)
+    other = lax.ppermute(send, "space", [(i, i ^ 1) for i in range(space)])
     (encoded,) = call(
         functools.partial(main_kernel, z),
         [shape((n, z.r, z.piece, z.c))],
         x,
         acts,
-        temporal.reshape(3 * z.c, z.c),
+        temporal,
         gain.reshape(1, z.c),
         q_w,
         k_w,
@@ -300,30 +324,23 @@
         flops=8 * one,
     )
     wide = z.c // n
-    pieces = call(
-        functools.partial(split_kernel, z),
-        [shape((z.c // 2, 3 * wide), F32)] + [shape((z.c // 2, 3 * wide))] * (n - 1),
-        ids,
-        keep,
-        other,
-    )
-    back = [lax.dynamic_index_in_dim(encoded, me ^ k, 0, False) for k in range(n)]
-    back = [back[0]] + [swap(back[k], "tm", k) for k in range(1, n)]
-    total = pieces[0]
-    for k in range(1, n):
-        total = total + swap(pieces[k], "tm", k).astype(F32)
+    (pieces,) = call(
+        functools.partial(split_kernel, z), [shape((n, z.c // 2, 3 * wide))], keep, other
+    )
+    back = exchange(encoded)
     chips = space // 2
-    total = total.reshape(chips, width, 3 * wide)
-    sums = lax.dynamic_index_in_dim(total, here // 2, 0, False)
-    total = total.astype(BF)
-    for k in range(1, chips):
-        mine = lax.dynamic_index_in_dim(total, here // 2 ^ k, 0, False)
-        sums = sums + swap(mine, "space", 2 * k).astype(F32)
+    total = jnp.sum(exchange(pieces).astype(F32), axis=0).astype(BF)
+    total = lax.all_to_all(
+        total.reshape(chips, width, 3 * wide),
+        "space",
+        0,
+        0,
+        axis_index_groups=[list(range(i, space, 2)) for i in range(2)],
+        tiled=True,
+    )
+    sums = jnp.sum(total.astype(F32), axis=0)
     kernel_grad = sums.reshape(width, 3, wide).transpose(1, 2, 0)
-    whole = jnp.zeros((z.fl, z.r, n, z.wc, z.c), BF)
-    for k in range(n):
-        rows = back[k].reshape(z.r, z.fl, 1, z.wc, z.c).transpose(1, 0, 2, 3, 4)
-        whole = lax.dynamic_update_slice_in_dim(whole, rows, me ^ k, 2)
+    whole = back.reshape(n, z.r, z.fl, z.wc, z.c).transpose(2, 1, 0, 3, 4)
     return whole.reshape(frames_in.shape), kernel_grad
 
 

time: 91.3 us -> 109 us (1.19)
  waiting for transfers between devices: 27.4 us -> 32.9 us
  Pallas kernels: 21.4 us -> 25.4 us
  local copies, waits for them, and re-layouts: 13.8 us -> 17.1 us
  starting transfers between devices: 27.3 us -> 29.7 us
  other arithmetic: 0.22 us -> 2.07 us
    all_to_all x0 -> x5, waiting for transfers between devices: none -> 30.9 us  [the longest x4 25.3 us: exchange(): return lax.all_to_all(value, 'tm', 0, 0, tiled=True)]
    ppermute x16 -> x1, waiting for transfers between devices: 27.4 us -> 1.91 us  [on_device(): other = lax.ppermute(send, 'space', [(i, i ^ 1) for i in range(space)])]
    all_to_all x0 -> x5, starting transfers between devices: none -> 22.2 us  [the longest x4 18.3 us: exchange(): return lax.all_to_all(value, 'tm', 0, 0, tiled=True)]
    ppermute x16 -> x1, starting transfers between devices: 24.7 us -> 4.89 us  [on_device(): other = lax.ppermute(send, 'space', [(i, i ^ 1) for i in range(space)])]
    unnamed x29 -> x53, local copies, waits for them, and re-layouts: 7.82 us -> 16 us
    dynamic_update_slice x4 -> x0, local copies, waits for them, and re-layouts: 3.83 us -> none  [on_device(): whole = lax.dynamic_update_slice_in_dim(whole, rows, me ^ k, 2)]
    pallas_call x0 -> x1, Pallas kernels: none -> 2.53 us  [on_device(): pl.pallas_call(functools.partial(load_kernel, len(weights)), out_shape=tu...]
    reduce_sum x0 -> x2, other arithmetic: none -> 2 us  [the longest x1 1.97 us: on_device(): total = jnp.sum(exchange(pieces).astype(F32), axis=0).astype(BF)]
  transfers between devices with their start and end apart: 18 -> 8, of which waited for: 7 -> 4; matrix products, arithmetic and copies ran while one was open for 7% -> 3% of each run, Pallas kernels for 19% -> 17%
where the time goes in v2:
time: 109 us; the launch traced here: 108 us
  waiting for transfers between devices  32.9 us (30%)
  starting transfers between devices  29.7 us (27%)
  Pallas kernels  25.4 us (23%)
  local copies, waits for them, and re-layouts  17.1 us (16%)
  other arithmetic  2.07 us (2%)
    all_to_all x4, waiting for transfers between devices, exchange(): return lax.all_to_all(value, 'tm', 0, 0, tiled=True)  25.3 us
    pallas_call x8, Pallas kernels, call(): pl.pallas_call(kernel, out_shape=tuple(outs), in_specs=[SMEM if a.dtype =...  22.9 us
    all_to_all x4, starting transfers between devices, exchange(): return lax.all_to_all(value, 'tm', 0, 0, tiled=True)  18.3 us
    unnamed x53, local copies, waits for them, and re-layouts  16 us
    all_to_all x1, waiting for transfers between devices, on_device(): lax.all_to_all(total.reshape(chips, width, 3 * wide), 'space', 0, 0, axis...  5.66 us
    ppermute x1, starting transfers between devices, on_device(): other = lax.ppermute(send, 'space', [(i, i ^ 1) for i in range(space)])  4.89 us
    all_to_all x1, starting transfers between devices, on_device(): lax.all_to_all(total.reshape(chips, width, 3 * wide), 'space', 0, 0, axis...  3.84 us
    pallas_call x1, Pallas kernels, on_device(): pl.pallas_call(functools.partial(load_kernel, len(weights)), out_shape=tu...  2.53 us
  transfers between devices with their start and end apart: 8, of which 4 were waited for; matrix products, arithmetic and copies ran while one was open for 3% of the time, Pallas kernels for 17%

profile of v2, /device:TPU:0, one launch (start us, length us, event | category | flops | bytes accessed | tf_op | source)
XLA Modules:
  0.0 108.0 jit_solution(931700391162769069)
XLA Ops:
  0.6 0.1 pad_add_fusion.me_ref
  0.7 1.2 %copy-done.1 = bf16[4,4,64,512]{3,2,1,0:T(8,128)(2,1)S(1)} copy-done((bf16[4,4,64,512]{3,2,1,0:T(8,128)(2,1)S(1)}, bf16[4,4,64,512]{3,2,1,0:T(8,128)(2,1)}, u32[]{:S(2)}) %copy-start.1) | copy-done | bytes 1048600
  1.9 2.1 %shard_map.105.after_ref = bf16[4,288,512]{2,1,0:T(8,128)(2,1)} custom-call(s32[2]{0:T(128)S(1)} %pad_add_fusion.me_ref, bf16[4,4,64,512]{3,2,1,0:T(8,128)(2,1)S(1)} %copy-done.1), custom_call_target="tpu_custom_call" | custom-call | bytes 2228232 | tf_op jit(solution)/shard_map/pallas_call | solution.py:19
  4.1 5.3 %all-to-all-start = ((bf16[4,288,512]{2,1,0:T(8,128)(2,1)}), bf16[4,288,512]{2,1,0:T(8,128)(2,1)S(1)}, u32[]{:S(2)}, u32[]{:S(2)}) async-start(bf16[4,288,512]{2,1,0:T(8,128)(2,1)} %shard_map.105.after_ref), calls=%async_computation | async-start | bytes 2359296 | tf_op jit(solution)/shard_map/all_to_all | solution.py:249
  9.4 1.9 %shard_map.104 = bf16[4,256,512]{2,1,0:T(8,128)(2,1)} custom-call(s32[2]{0:T(128)S(1)} %pad_add_fusion.me_ref, bf16[4,4,64,512]{3,2,1,0:T(8,128)(2,1)S(1)} %copy-done.2), custom_call_target="tpu_custom_call" | custom-call | bytes 2097160 | tf_op jit(solution)/shard_map/pallas_call | solution.py:19
  11.3 13.1 %all-to-all-done.parts = bf16[4,288,512]{2,1,0:T(8,128)(2,1)S(1)} async-done(((bf16[4,288,512]{2,1,0:T(8,128)(2,1)}), bf16[4,288,512]{2,1,0:T(8,128)(2,1)S(1)}, u32[]{:S(2)}, u32[]{:S(2)}) %all-to-all-start) | async-done | bytes 1179680 | tf_op jit(solution)/shard_map/all_to_all | solution.py:249
  24.4 1.0 shard_map.106
  25.5 1.0 copy-done.10
  26.5 0.7 copy-done.21
  27.2 0.7 copy-done.23
  27.9 4.4 %all-to-all-start.2 = ((bf16[4,256,512]{2,1,0:T(8,128)(2,1)}), bf16[4,256,512]{2,1,0:T(8,128)(2,1)}, u32[]{:S(2)}, u32[]{:S(2)}) async-start(bf16[4,256,512]{2,1,0:T(8,128)(2,1)} %shard_map.104), calls=%async_computation.2 | async-start | bytes 2097152 | tf_op jit(solution)/shard_map/all_to_all | solution.py:249
  32.4 0.0 copy-start.7
  32.4 1.0 copy-done.7
  33.4 2.5 %shard_map.107 = (bf16[3,3,512,512]{3,2,1,0:T(8,128)(2,1)S(1)}, bf16[1536,512]{1,0:T(8,128)(2,1)S(1)}, bf16[512,512]{1,0:T(8,128)(2,1)S(1)}, bf16[512,512]{1,0:T...) custom-call(bf16[4,288,512]{2,1,0:T(8,128)(2,1)} %shard_map.105.after_ref, ...), custom_call_target="tpu_custom_call" | custom-call | bytes 16777216 | tf_op jit(solution)/shard_map/pallas_call | solution.py:259
  36.0 0.0 copy-start.8
  36.0 1.1 %copy-done.8 = bf16[1536,512]{1,0:T(8,128)(2,1)} copy-done((bf16[1536,512]{1,0:T(8,128)(2,1)}, bf16[1536,512]{1,0:T(8,128)(2,1)S(1)}, u32[]{:S(2)}) %copy-start.8) | copy-done | bytes 1572888
  37.1 0.8 copy-done.13
  37.9 0.8 copy-done.15
  38.8 1.3 %collective-permute-start = (bf16[288,512]{1,0:T(8,128)(2,1)S(1)}, bf16[288,512]{1,0:T(8,128)(2,1)S(1)}, u32[]{:S(2)}, u32[]{:S(2)}) collective-permute-start(bf16[288,512]{1,0:T(8,128)(2,1)S(1)} %copy-done.24), channel_id=1, source_target_pairs={{0,1},{1,2},{2,3},{3,4},{4,5},{5,6},{6,7},{8,9},{9,10},{10,11},{11... | collective-permute-start | bytes 884744 | tf_op jit(solution)/shard_map/ppermute | solution.py:275
  40.1 1.3 %collective-permute-start.1 = (bf16[288,512]{1,0:T(8,128)(2,1)S(1)}, bf16[288,512]{1,0:T(8,128)(2,1)S(1)}, u32[]{:S(2)}, u32[]{:S(2)}) collective-permute-start(bf16[288,512]{1,0:T(8,128)(2,1)S(1)} %copy-done.22), channel_id=1, source_target_pairs={{1,0},{2,1},{3,2},{4,3},{5,4},{6,5},{7,6},{9,8},{10,9},{11,10},{12... | collective-permute-start | bytes 884744 | tf_op jit(solution)/shard_map/ppermute | solution.py:276
  41.4 4.2 %shard_map.108.part_ref = f32[4,256,512]{2,1,0:T(8,128)S(1)} custom-call(bf16[4,288,512]{2,1,0:T(8,128)(2,1)S(1)} %copy-done.11, bf16[3,3,512,512]{3,2,1,0:T(8,128)(2,1)S(1)} %get-tuple-element.17.w_ref), custom_call_target="tpu_custom_call" | custom-call | flops 4026531840 | bytes 7995392 | tf_op jit(solution)/shard_map/pallas_call | solution.py:19
  45.6 0.0 copy-done.17
  45.6 0.0 collective-permute-done.up_ref
  45.6 0.0 collective-permute-done.1.down_ref
  45.6 1.8 %shard_map.109.act_ref = bf16[4,256,1536]{2,1,0:T(8,128)(2,1)S(1)} custom-call(f32[4,256,512]{2,1,0:T(8,128)S(1)} %shard_map.108.part_ref, bf16[288,512]{1,0:T(8,128)(2,1)S(1)} %collective-permute-done.up_ref, bf16[288,512]{1,0:T(8,128)(2,1)S(1)} %collective-permute-done.1.down_ref, bf16[3,3,512,512]{3,2,1,0:T(8,128)(2,1)S(1)} %get-tuple-element.17.w_ref), custom_call_target="tpu_custom_call" | custom-call | flops 805306368 | bytes 10551296 | tf_op jit(solution)/shard_map/pallas_call | solution.py:19
  47.4 0.0 all-to-all-done.2.parts
  47.4 3.3 %shard_map.111 = (f32[256,1536]{1,0:T(8,128)S(1)}, bf16[256,1536]{1,0:T(8,128)(2,1)S(1)}) custom-call(s32[2]{0:T(128)S(1)} %pad_add_fusion.me_ref, bf16[4,256,512]{2,1,0:T(8,128)(2,1)} %all-to-all-done.2.parts, bf16[4,256,1536]{2,1,0:T(8,128)(2,1)S(1)} %shard_map.109.act_ref), custom_call_target="tpu_custom_call" | custom-call | flops 1610612736 | bytes 6553608 | tf_op jit(solution)/shard_map/pallas_call | solution.py:19
  50.8 4.9 %collective-permute-start.2 = (bf16[256,1536]{1,0:T(8,128)(2,1)S(1)}, bf16[256,1536]{1,0:T(8,128)(2,1)S(1)}, u32[]{:S(2)}, u32[]{:S(2)}) collective-permute-start(bf16[256,1536]{1,0:T(8,128)(2,1)S(1)} %get-tuple-element.27), channel_id=1, source_target_pairs={{0,1},{1,0},{2,3},{3,2},{4,5},{5,4},{6,7},{7,6},{8,9},{9,8},{10,11... | collective-permute-start | bytes 2359304 | tf_op jit(solution)/shard_map/ppermute | solution.py:312
  55.6 1.9 %collective-permute-done.2.got_ref = bf16[256,1536]{1,0:T(8,128)(2,1)S(1)} collective-permute-done((bf16[256,1536]{1,0:T(8,128)(2,1)S(1)}, bf16[256,1536]{1,0:T(8,128)(2,1)S(1)}, u32[]{:S(2)}, u32[]{:S(2)}) %collective-permute-start.2) | collective-permute-done | bytes 786464 | tf_op jit(solution)/shard_map/ppermute | solution.py:312
  57.6 1.1 shard_map.112
  58.6 4.5 %all-to-all-start.3 = ((bf16[4,256,384]{2,1,0:T(8,128)(2,1)}), bf16[4,256,384]{2,1,0:T(8,128)(2,1)}, u32[]{:S(2)}, u32[]{:S(2)}) async-start(bf16[4,256,384]{2,1,0:T(8,128)(2,1)} %shard_map.112), calls=%async_computation.3 | async-start | bytes 1572864 | tf_op jit(solution)/shard_map/all_to_all | solution.py:249
  63.2 1.4 %copy-done.9 = bf16[1536,512]{1,0:T(8,128)(2,1)S(1)} copy-done((bf16[1536,512]{1,0:T(8,128)(2,1)S(1)}, bf16[1536,512]{1,0:T(8,128)(2,1)}, u32[]{:S(2)}) %copy-start.9) | copy-done | bytes 1572888
  64.6 1.3 %copy-done.12 = bf16[4,288,512]{2,1,0:T(8,128)(2,1)S(1)} copy-done((bf16[4,288,512]{2,1,0:T(8,128)(2,1)S(1)}, bf16[4,288,512]{2,1,0:T(8,128)(2,1)}, u32[]{:S(2)}) %copy-start.12) | copy-done | bytes 1179672
  65.9 1.0 copy-done.14
  66.9 1.0 copy-done.16
  67.9 1.0 copy-done.18
  69.0 1.0 copy-done.20
  70.0 7.4 %shard_map.110 = bf16[4,4,64,512]{3,2,1,0:T(8,128)(2,1)S(1)} custom-call(bf16[4,288,512]{2,1,0:T(8,128)(2,1)S(1)} %copy-done.12, bf16[4,256,1536]{2,1,0:T(8,128)(2,1)S(1)} %shard_map.109.act_ref, bf16[1536,512]{1,0:T(8,128)(2,1)S(1)} %copy-done.9, f32[1,512]{1,0:T(1,128)S(1)} %bitcast.10, bf16[512,512]{1,0:T(8,128)(2,1)S(1)} %copy-done.14, ...), custom_call_target="tpu_custom_call" | custom-call | flops 4294967296 | bytes 9046016 | tf_op jit(solution)/shard_map/pallas_call | solution.py:19
  77.5 0.0 copy-start.3
  77.5 1.0 copy-done.3
  78.4 0.0 all-to-all-done.3
  78.4 4.1 %all-to-all-start.1 = ((bf16[4,4,64,512]{3,2,1,0:T(8,128)(2,1)}), bf16[4,4,64,512]{3,2,1,0:T(8,128)(2,1)S(1)}, u32[]{:S(2)}, u32[]{:S(2)}) async-start(bf16[4,4,64,512]{3,2,1,0:T(8,128)(2,1)} %copy-done.3), calls=%async_computation.1 | async-start | bytes 2097152 | tf_op jit(solution)/shard_map/all_to_all | solution.py:249
  82.6 2.0 %reduce_sum.21 = bf16[256,384]{1,0:T(8,128)(2,1)} reduce(bf16[4,256,384]{2,1,0:T(8,128)(2,1)} %all-to-all-done.3, bf16[]{:T(256)} %constant.21.clone.1), dimensions={0}, to_apply=%region_0.1 | reduce | flops 294912 | bytes 983042 | tf_op jit(solution)/shard_map/reduce_sum | solution.py:332
  84.5 12.2 %all-to-all-done.1 = bf16[4,4,64,512]{3,2,1,0:T(8,128)(2,1)S(1)} async-done(((bf16[4,4,64,512]{3,2,1,0:T(8,128)(2,1)}), bf16[4,4,64,512]{3,2,1,0:T(8,128)(2,1)S(1)}, u32[]{:S(2)}, u32[]{:S(2)}) %all-to-all-start.1) | async-done | bytes 1048608 | tf_op jit(solution)/shard_map/all_to_all | solution.py:249
  96.7 3.8 %all-to-all-start.4 = ((bf16[4,64,384]{2,1,0:T(8,128)(2,1)}), bf16[4,64,384]{2,1,0:T(8,128)(2,1)S(1)}, u32[]{:S(2)}, u32[]{:S(2)}) async-start(bf16[4,64,384]{2,1,0:T(8,128)(2,1)} %bitcast.6), calls=%async_computation.4 | async-start | bytes 393216 | tf_op jit(solution)/shard_map/all_to_all | solution.py:333
  100.6 1.1 copy.14
  101.6 5.7 %all-to-all-done.4 = bf16[4,64,384]{2,1,0:T(8,128)(2,1)S(1)} async-done(((bf16[4,64,384]{2,1,0:T(8,128)(2,1)}), bf16[4,64,384]{2,1,0:T(8,128)(2,1)S(1)}, u32[]{:S(2)}, u32[]{:S(2)}) %all-to-all-start.4) | async-done | bytes 196640 | tf_op jit(solution)/shard_map/all_to_all | solution.py:333
  107.4 0.6 copy.15
  (35 shorter events, 0.1 us)
Async XLA Ops:
  0.7 1.2 %copy-start.1 = (bf16[4,4,64,512]{3,2,1,0:T(8,128)(2,1)S(1)}, bf16[4,4,64,512]{3,2,1,0:T(8,128)(2,1)}, u32[]{:S(2)}) copy-start(bf16[4,4,64,512]{3,2,1,0:T(8,128)(2,1)} %x_ref.3) | copy-start | bytes 3145732
  4.1 5.3 %copy-start.2 = (bf16[4,4,64,512]{3,2,1,0:T(8,128)(2,1)S(1)}, bf16[4,4,64,512]{3,2,1,0:T(8,128)(2,1)}, u32[]{:S(2)}) copy-start(bf16[4,4,64,512]{3,2,1,0:T(8,128)(2,1)} %x_ref.2) | copy-start | bytes 3145732
  4.1 20.3 %all-to-all-start = ((bf16[4,288,512]{2,1,0:T(8,128)(2,1)}), bf16[4,288,512]{2,1,0:T(8,128)(2,1)S(1)}, u32[]{:S(2)}, u32[]{:S(2)}) async-start(bf16[4,288,512]{2,1,0:T(8,128)(2,1)} %shard_map.105.after_ref), calls=%async_computation | async-start | bytes 2359296 | tf_op jit(solution)/shard_map/all_to_all | solution.py:249
  11.3 21.0 %copy-start = (bf16[3,512,512]{2,1,0:T(8,128)(2,1)S(1)}, bf16[3,512,512]{2,1,0:T(8,128)(2,1)}, u32[]{:S(2)}) copy-start(bf16[3,512,512]{2,1,0:T(8,128)(2,1)} %param.11) | copy-start | bytes 4718596
  11.3 21.0 %copy-start.4 = (bf16[512,512]{1,0:T(8,128)(2,1)S(1)}, bf16[512,512]{1,0:T(8,128)(2,1)}, u32[]{:S(2)}) copy-start(bf16[512,512]{1,0:T(8,128)(2,1)} %refs_2_.1) | copy-start | bytes 1572868
  25.4 1.0 copy-start.10
  26.5 0.7 copy-start.21
  27.2 0.7 copy-start.23
  27.9 4.4 %copy-start.5 = (bf16[512,512]{1,0:T(8,128)(2,1)S(1)}, bf16[512,512]{1,0:T(8,128)(2,1)}, u32[]{:S(2)}) copy-start(bf16[512,512]{1,0:T(8,128)(2,1)} %refs_3_.1) | copy-start | bytes 1572868
  27.9 4.4 %copy-start.6 = (bf16[512,512]{1,0:T(8,128)(2,1)S(1)}, bf16[512,512]{1,0:T(8,128)(2,1)}, u32[]{:S(2)}) copy-start(bf16[512,512]{1,0:T(8,128)(2,1)} %refs_4_.1) | copy-start | bytes 1572868
  27.9 19.5 %all-to-all-start.2 = ((bf16[4,256,512]{2,1,0:T(8,128)(2,1)}), bf16[4,256,512]{2,1,0:T(8,128)(2,1)}, u32[]{:S(2)}, u32[]{:S(2)}) async-start(bf16[4,256,512]{2,1,0:T(8,128)(2,1)} %shard_map.104), calls=%async_computation.2 | async-start | bytes 2097152 | tf_op jit(solution)/shard_map/all_to_all | solution.py:249
  32.4 1.0 copy-start.7
  33.4 5.3 %copy-start.24 = (bf16[288,512]{1,0:T(8,128)(2,1)S(1)}, bf16[288,512]{1,0:T(8,128)(2,1)}, u32[]{:S(2)}) copy-start(bf16[288,512]{1,0:T(8,128)(2,1)} %copy-done.23) | copy-start | bytes 884740
  33.4 6.6 %copy-start.22 = (bf16[288,512]{1,0:T(8,128)(2,1)S(1)}, bf16[288,512]{1,0:T(8,128)(2,1)}, u32[]{:S(2)}) copy-start(bf16[288,512]{1,0:T(8,128)(2,1)} %copy-done.21) | copy-start | bytes 884740
  33.4 7.9 %copy-start.11 = (bf16[4,288,512]{2,1,0:T(8,128)(2,1)S(1)}, bf16[4,288,512]{2,1,0:T(8,128)(2,1)}, u32[]{:S(2)}) copy-start(bf16[4,288,512]{2,1,0:T(8,128)(2,1)} %copy-done.10) | copy-start | bytes 3538948
  36.0 1.2 %copy-start.8 = (bf16[1536,512]{1,0:T(8,128)(2,1)}, bf16[1536,512]{1,0:T(8,128)(2,1)S(1)}, u32[]{:S(2)}) copy-start(bf16[1536,512]{1,0:T(8,128)(2,1)S(1)} %get-tuple-element.20.t_ref) | copy-start | bytes 4718596
  37.1 0.8 copy-start.13
  37.9 0.8 copy-start.15
  38.7 6.8 %copy-start.17 = (bf16[512,512]{1,0:T(8,128)(2,1)}, bf16[512,512]{1,0:T(8,128)(2,1)S(1)}, u32[]{:S(2)}) copy-start(bf16[512,512]{1,0:T(8,128)(2,1)S(1)} %get-tuple-element.23.v_ref) | copy-start | bytes 1572868
  38.7 6.9 %copy-start.19 = (bf16[512,512]{1,0:T(8,128)(2,1)}, bf16[512,512]{1,0:T(8,128)(2,1)S(1)}, u32[]{:S(2)}) copy-start(bf16[512,512]{1,0:T(8,128)(2,1)S(1)} %get-tuple-element.24.o_ref) | copy-start | bytes 1572868
  38.8 6.9 %collective-permute-start = (bf16[288,512]{1,0:T(8,128)(2,1)S(1)}, bf16[288,512]{1,0:T(8,128)(2,1)S(1)}, u32[]{:S(2)}, u32[]{:S(2)}) collective-permute-start(bf16[288,512]{1,0:T(8,128)(2,1)S(1)} %copy-done.24), channel_id=1, source_target_pairs={{0,1},{1,2},{2,3},{3,4},{4,5},{5,6},{6,7},{8,9},{9,10},{10,11},{11... | collective-permute-start | bytes 884744 | tf_op jit(solution)/shard_map/ppermute | solution.py:275
  40.1 5.6 %collective-permute-start.1 = (bf16[288,512]{1,0:T(8,128)(2,1)S(1)}, bf16[288,512]{1,0:T(8,128)(2,1)S(1)}, u32[]{:S(2)}, u32[]{:S(2)}) collective-permute-start(bf16[288,512]{1,0:T(8,128)(2,1)S(1)} %copy-done.22), channel_id=1, source_target_pairs={{1,0},{2,1},{3,2},{4,3},{5,4},{6,5},{7,6},{9,8},{10,9},{11,10},{12... | collective-permute-start | bytes 884744 | tf_op jit(solution)/shard_map/ppermute | solution.py:276
  50.8 6.8 %collective-permute-start.2 = (bf16[256,1536]{1,0:T(8,128)(2,1)S(1)}, bf16[256,1536]{1,0:T(8,128)(2,1)S(1)}, u32[]{:S(2)}, u32[]{:S(2)}) collective-permute-start(bf16[256,1536]{1,0:T(8,128)(2,1)S(1)} %get-tuple-element.27), channel_id=1, source_target_pairs={{0,1},{1,0},{2,3},{3,2},{4,5},{5,4},{6,7},{7,6},{8,9},{9,8},{10,11... | collective-permute-start | bytes 2359304 | tf_op jit(solution)/shard_map/ppermute | solution.py:312
  58.6 4.5 %copy-start.25 = (f32[512]{0:T(512)S(1)}, f32[512]{0:T(512)}, u32[]{:S(2)}) copy-start(f32[512]{0:T(512)} %param.12) | copy-start | bytes 6148
  58.6 19.8 %all-to-all-start.3 = ((bf16[4,256,384]{2,1,0:T(8,128)(2,1)}), bf16[4,256,384]{2,1,0:T(8,128)(2,1)}, u32[]{:S(2)}, u32[]{:S(2)}) async-start(bf16[4,256,384]{2,1,0:T(8,128)(2,1)} %shard_map.112), calls=%async_computation.3 | async-start | bytes 1572864 | tf_op jit(solution)/shard_map/all_to_all | solution.py:249
  63.2 1.4 %copy-start.9 = (bf16[1536,512]{1,0:T(8,128)(2,1)S(1)}, bf16[1536,512]{1,0:T(8,128)(2,1)}, u32[]{:S(2)}) copy-start(bf16[1536,512]{1,0:T(8,128)(2,1)} %copy-done.8) | copy-start | bytes 4718596
  64.6 1.3 %copy-start.12 = (bf16[4,288,512]{2,1,0:T(8,128)(2,1)S(1)}, bf16[4,288,512]{2,1,0:T(8,128)(2,1)}, u32[]{:S(2)}) copy-start(bf16[4,288,512]{2,1,0:T(8,128)(2,1)} %copy-done.10) | copy-start | bytes 3538948
  65.9 1.0 copy-start.14
  66.9 1.0 copy-start.16
  67.9 1.0 copy-start.18
  69.0 1.0 copy-start.20
  77.5 1.0 copy-start.3
  78.4 18.3 %all-to-all-start.1 = ((bf16[4,4,64,512]{3,2,1,0:T(8,128)(2,1)}), bf16[4,4,64,512]{3,2,1,0:T(8,128)(2,1)S(1)}, u32[]{:S(2)}, u32[]{:S(2)}) async-start(bf16[4,4,64,512]{3,2,1,0:T(8,128)(2,1)} %copy-done.3), calls=%async_computation.1 | async-start | bytes 2097152 | tf_op jit(solution)/shard_map/all_to_all | solution.py:249
  96.7 10.6 %all-to-all-start.4 = ((bf16[4,64,384]{2,1,0:T(8,128)(2,1)}), bf16[4,64,384]{2,1,0:T(8,128)(2,1)S(1)}, u32[]{:S(2)}, u32[]{:S(2)}) async-start(bf16[4,64,384]{2,1,0:T(8,128)(2,1)} %bitcast.6), calls=%async_computation.4 | async-start | bytes 393216 | tf_op jit(solution)/shard_map/all_to_all | solution.py:333

commit v3 on v1

--- a/solution.py
+++ b/solution.py
@@ -10,19 +10,18 @@
 BF = jnp.bfloat16
 F32 = jnp.float32
 VMEM = pl.BlockSpec(memory_space=pltpu.VMEM)
-SMEM = pl.BlockSpec(memory_space=pltpu.SMEM)
-
-
-def call(kernel, outs, *args, flops=0, scratch=()):
+
+
+def call(kernel, outs, *args, flops=0, scratch=(), limit=16):
     moved = sum(a.size * a.dtype.itemsize for a in args)
     moved += sum(o.size * o.dtype.itemsize for o in outs)
     return pl.pallas_call(
         kernel,
         out_shape=tuple(outs),
-        in_specs=[SMEM if a.dtype == jnp.int32 else VMEM for a in args],
+        in_specs=[VMEM] * len(args),
         out_specs=tuple(VMEM for _ in outs),
         scratch_shapes=scratch,
-        compiler_params=pltpu.CompilerParams(vmem_limit_bytes=40 * 2**20),
+        compiler_params=pltpu.CompilerParams(vmem_limit_bytes=limit * 2**20),
         cost_estimate=pl.CostEstimate(flops=flops, bytes_accessed=moved, transcendentals=0),
     )(*args)
 
@@ -52,36 +51,42 @@
         self.sides = 2 * rows * frames
 
 
-def pack_kernel(z, halo, me_ref, x_ref, *outs):
-    me = me_ref[0]
+def pack_kernel(z, halo, x_ref, *refs):
+    outs, (x, sem) = refs[: z.n], refs[z.n :]
+    copies = [pltpu.make_async_copy(x_ref.at[:, r], x.at[r], sem.at[r]) for r in range(z.r)]
+    for copy in copies:
+        copy.start()
+    me = lax.axis_index("tm")
 
     def source(q):
         k = q // z.piece
         f = q % z.piece // z.wc
         return f * z.w + (me ^ k) * z.wc + q % z.wc
 
+    def edge(r, q):
+        k = q // z.sides
+        side = q % z.sides // (z.r * z.fl)
+        row = q % (z.r * z.fl) // z.fl
+        col = (me ^ k) * z.wc - 1 + side * (z.wc + 1)
+        inside = (col >= 0) & (col < z.w) & (row == r)
+        return jnp.where(inside, q % z.fl * z.w + col, -1)
+
     matrix = chooser(z.n * z.piece, z.fl * z.w, source)
-    for r in range(z.r):
-        rows = x_ref[:, r].reshape(z.fl * z.w, z.c)
+    if halo:
+        edges = [chooser(z.n * z.sides, z.fl * z.w, functools.partial(edge, r)) for r in range(z.r)]
+        tails = jnp.zeros((z.n * z.sides, z.c), F32)
+    for r in range(z.r):
+        copies[r].wait()
+        rows = x[r].reshape(z.fl * z.w, z.c)
         cut = moved(matrix, rows)
         for k in range(z.n):
             outs[k][r * z.piece : (r + 1) * z.piece] = cut[k * z.piece : (k + 1) * z.piece]
-    if not halo:
-        return
-
-    def edge(q):
-        k = q // z.sides
-        side = q % z.sides // (z.r * z.fl)
-        r = q % (z.r * z.fl) // z.fl
-        f = q % z.fl
-        col = (me ^ k) * z.wc - 1 + side * (z.wc + 1)
-        inside = (col >= 0) & (col < z.w)
-        return jnp.where(inside, (f * z.r + r) * z.w + col, -1)
-
-    total = z.fl * z.r * z.w
-    cut = moved(chooser(z.n * z.sides, total, edge), x_ref[...].reshape(total, z.c))
-    for k in range(z.n):
-        outs[k][z.main : z.main + z.sides] = cut[k * z.sides : (k + 1) * z.sides]
+        if halo:
+            tails += jnp.dot(edges[r], rows, preferred_element_type=F32)
+    if halo:
+        tails = tails.astype(BF)
+        for k in range(z.n):
+            outs[k][z.main : z.main + z.sides] = tails[k * z.sides : (k + 1) * z.sides]
 
 
 def gather_matrix(z, me):
@@ -92,9 +97,9 @@
     return chooser(z.block, z.block, source)
 
 
-def assemble_kernel(z, me_ref, *refs):
+def assemble_kernel(z, *refs):
     parts, (out, top, bottom) = refs[: z.n], refs[z.n :]
-    me = me_ref[0]
+    me = lax.axis_index("tm")
     matrix = gather_matrix(z, me)
 
     def edge(q):
@@ -157,41 +162,79 @@
             out[r, :, k * z.c : (k + 1) * z.c] = late.astype(BF)
 
 
-def main_kernel(z, x_ref, act_ref, t_ref, gain_ref, q_ref, k_ref, v_ref, o_ref, out):
+def norm_kernel(z, x_ref, act_ref, t_ref, gain_ref, hidden_ref, normed_ref):
+    gain = gain_ref[...]
+    for r in range(z.r):
+        temporal = jnp.dot(act_ref[r], t_ref[...], preferred_element_type=F32)
+        hidden = (x_ref[r, z.f : z.f + z.block].astype(F32) + temporal).astype(BF)
+        wide = hidden.astype(F32)
+        mean = jnp.mean(wide * wide, axis=1, keepdims=True)
+        hidden_ref[r] = hidden
+        normed_ref[r] = (wide * (1.0 / jnp.sqrt(mean + 1e-06)) * gain).astype(BF)
+
+
+def attend_kernel(z, hidden_ref, normed_ref, q_ref, k_ref, v_ref, o_ref, *outs):
+    me = lax.axis_index("tm")
     a = lax.broadcasted_iota(jnp.int32, (z.block, z.block), 0)
     b = lax.broadcasted_iota(jnp.int32, (z.block, z.block), 1)
     allowed = (a // z.f == b // z.f) & (b % z.f <= a % z.f)
     scale = float(z.c) ** -0.5
-    back = chooser(z.block, z.block, lambda q: q % z.wc * z.f + q // z.wc)
-    gain = gain_ref[...]
-    for r in range(z.r):
-        temporal = jnp.dot(act_ref[r], t_ref[...], preferred_element_type=F32)
-        hidden = (x_ref[r, z.f : z.f + z.block].astype(F32) + temporal).astype(BF)
-        wide = hidden.astype(F32)
-        mean = jnp.mean(wide * wide, axis=1, keepdims=True)
-        normed = (wide / jnp.sqrt(mean + 1e-06) * gain).astype(BF)
-        query = jnp.dot(normed, q_ref[...], preferred_element_type=F32).astype(BF)
-        key = jnp.dot(normed, k_ref[...], preferred_element_type=F32).astype(BF)
-        value = jnp.dot(normed, v_ref[...], preferred_element_type=F32).astype(BF)
-        scores = lax.dot_general(
-            query, key, (((1,), (1,)), ((), ())), preferred_element_type=F32
+
+    def source(q):
+        t = ((me ^ (q // z.piece)) * z.fl) + q % z.piece // z.wc
+        return q % z.wc * z.f + t
+
+    back = chooser(z.block, z.block, source)
+    held = {}
+
+    def project(r):
+        rows = normed_ref[r]
+        held["q", r], held["k", r], held["v", r] = (
+            jnp.dot(rows, w[...], preferred_element_type=F32).astype(BF)
+            for w in (q_ref, k_ref, v_ref)
         )
-        scores = jnp.where(allowed, scores * scale, -1e30)
+
+    def score(r):
+        held["s", r] = lax.dot_general(
+            held.pop(("q", r)),
+            held.pop(("k", r)),
+            (((1,), (1,)), ((), ())),
+            preferred_element_type=F32,
+        )
+
+    def weigh(r):
+        scores = jnp.where(allowed, held.pop(("s", r)) * scale, -1e30)
         top = jnp.max(scores, axis=1, keepdims=True)
         expon = jnp.where(allowed, jnp.exp(scores - top), 0.0)
-        total = jnp.sum(expon, axis=1, keepdims=True)
-        mixed = jnp.dot(expon.astype(BF), value, preferred_element_type=F32)
-        attended = (mixed / total).astype(BF)
-        encoded = wide + jnp.dot(attended, o_ref[...], preferred_element_type=F32)
-        encoded = moved(back, encoded.astype(BF))
-        for i in range(z.n):
-            out[i, r] = encoded[i * z.piece : (i + 1) * z.piece]
-
-
-def grad_kernel(z, width, me_ref, *refs):
+        held["t", r] = 1.0 / jnp.sum(expon, axis=1, keepdims=True)
+        held["p", r] = expon.astype(BF)
+
+    def mix(r):
+        mixed = jnp.dot(held.pop(("p", r)), held.pop(("v", r)), preferred_element_type=F32)
+        held["a", r] = (mixed * held.pop(("t", r))).astype(BF)
+
+    def finish(r):
+        encoded = hidden_ref[r].astype(F32) + jnp.dot(
+            held.pop(("a", r)), o_ref[...], preferred_element_type=F32
+        )
+        held["e", r] = encoded.astype(BF)
+
+    def spread(r):
+        encoded = moved(back, held.pop(("e", r)))
+        for k in range(z.n):
+            outs[k][r] = encoded[k * z.piece : (k + 1) * z.piece]
+
+    stages = (project, score, weigh, mix, finish, spread)
+    for step in range(z.r + len(stages) - 1):
+        for late, stage in reversed(list(enumerate(stages))):
+            if 0 <= step - late < z.r:
+                stage(step - late)
+
+
+def grad_kernel(z, width, *refs):
     parts, (act_ref, keep, send, cot) = refs[: z.n], refs[z.n :]
-    matrix = gather_matrix(z, me_ref[0])
-    mine = me_ref[1] == 0
+    matrix = gather_matrix(z, lax.axis_index("tm"))
+    mine = lax.axis_index("space") % 2 == 0
     for r in range(z.r):
         rows = jnp.concatenate([p[r * z.piece : (r + 1) * z.piece] for p in parts], axis=0)
         cot[r * z.block : (r + 1) * z.block] = moved(matrix, rows)
@@ -211,8 +254,8 @@
             send[i * width : (i + 1) * width, lanes] = jnp.where(mine, high, low).astype(BF)
 
 
-def split_kernel(z, me_ref, keep_ref, got_ref, *outs):
-    me = me_ref[0]
+def split_kernel(z, keep_ref, got_ref, *outs):
+    me = lax.axis_index("tm")
     wide = z.c // z.n
     for tap in range(3):
         place = slice(tap * wide, (tap + 1) * wide)
@@ -236,29 +279,102 @@
     return lax.ppermute(value, axis, [(i, i ^ k) for i in range(count)])
 
 
+def load_kernel(count, after_ref, *refs):
+    sources, places, sem = refs[:count], refs[count : 2 * count], refs[2 * count]
+    copies = [
+        pltpu.make_async_copy(source, place, sem.at[i])
+        for i, (source, place) in enumerate(zip(sources, places))
+    ]
+    for copy in copies:
+        copy.start()
+    for copy in copies:
+        copy.wait()
+
+
+def write_kernel(z, k, piece_ref, *refs):
+    out, sem = refs[-2:]
+    first = pl.multiple_of((lax.axis_index("tm") ^ k) * z.wc, z.wc)
+    copies = [
+        pltpu.make_async_copy(
+            piece_ref.at[r], out.at[:, r, pl.ds(first, z.wc)], sem.at[r]
+        )
+        for r in range(z.r)
+    ]
+    for copy in copies:
+        copy.start()
+    for copy in copies:
+        copy.wait()
+
+
+def write(z, k, piece, *whole):
+    return pl.pallas_call(
+        functools.partial(write_kernel, z, k),
+        out_shape=shape((z.fl, z.r, z.w, z.c)),
+        in_specs=[pl.BlockSpec(memory_space=pl.ANY)] * (1 + len(whole)),
+        out_specs=pl.BlockSpec(memory_space=pl.ANY),
+        input_output_aliases={1: 0} if whole else {},
+        scratch_shapes=[pltpu.SemaphoreType.DMA((z.r,))],
+        cost_estimate=pl.CostEstimate(
+            flops=0, bytes_accessed=4 * z.main * z.c, transcendentals=0
+        ),
+    )(piece.reshape(z.r, z.fl, z.wc, z.c), *whole)
+
+
 def on_device(frames_in, spatial, temporal, gain, q_w, k_w, v_w, o_w, cotangent):
     n = lax.axis_size("tm")
     space = lax.axis_size("space")
     z = Sizes(n, *frames_in.shape)
     me = lax.axis_index("tm")
     here = lax.axis_index("space")
-    ids = jnp.stack([me, here % 2]).astype(jnp.int32)
-    part = [shape((z.main + z.sides, z.c))] * n
-    packed = call(functools.partial(pack_kernel, z, True), part, ids, frames_in)
-    got = [packed[0]] + [swap(packed[k], "tm", k) for k in range(1, n)]
+    one = 2 * z.r * z.block * z.c * z.c
+    others = sorted(range(1, n), key=lambda k: -k.bit_count())
+
+    def pack(value, halo):
+        rows = z.main + (z.sides if halo else 0)
+        return pl.pallas_call(
+            functools.partial(pack_kernel, z, halo),
+            out_shape=tuple([shape((rows, z.c))] * n),
+            in_specs=[pl.BlockSpec(memory_space=pltpu.HBM)],
+            out_specs=tuple([VMEM] * n),
+            scratch_shapes=[
+                pltpu.VMEM((z.r, z.fl, z.w, z.c), BF),
+                pltpu.SemaphoreType.DMA((z.r,)),
+            ],
+            compiler_params=pltpu.CompilerParams(vmem_limit_bytes=16 * 2**20),
+            cost_estimate=pl.CostEstimate(flops=one, bytes_accessed=2**22, transcendentals=0),
+        )(value)
+
+    def exchange(pieces):
+        pieces = list(pieces)
+        for k in others:
+            pieces[k] = swap(pieces[k], "tm", k)
+        return pieces
+
+    packed = pack(frames_in, True)
+    got = exchange(packed)
+    weights = (spatial, temporal.reshape(3 * z.c, z.c), q_w, k_w, v_w, o_w)
+    spatial, temporal, q_w, k_w, v_w, o_w = pl.pallas_call(
+        functools.partial(load_kernel, len(weights)),
+        out_shape=tuple(shape(w.shape) for w in weights),
+        in_specs=[pl.BlockSpec(memory_space=pl.ANY)] + [pl.BlockSpec(memory_space=pltpu.HBM)] * len(weights),
+        out_specs=tuple(VMEM for _ in weights),
+        scratch_shapes=[pltpu.SemaphoreType.DMA((len(weights),))],
+        compiler_params=pltpu.CompilerParams(vmem_limit_bytes=16 * 2**20),
+        cost_estimate=pl.CostEstimate(flops=0, bytes_accessed=16 * 2**20, transcendentals=0),
+    )(packed[0], *weights)
+    cot = pack(cotangent, False)
+    tied = lax.optimization_barrier((*cot, *(got[k] for k in others[1:])))
+    cot = exchange(tied[:n])
+    for k, piece in zip(others[1:], tied[n:]):
+        got[k] = piece
     line = z.block + 2 * z.f
     x, top, bottom = call(
         functools.partial(assemble_kernel, z),
         [shape((z.r, line, z.c)), shape((line, z.c)), shape((line, z.c))],
-        ids,
         *got,
     )
     up = lax.ppermute(bottom, "space", [(i, i + 1) for i in range(space - 1)])
     down = lax.ppermute(top, "space", [(i + 1, i) for i in range(space - 1)])
-    part = [shape((z.main, z.c))] * n
-    cot = call(functools.partial(pack_kernel, z, False), part, ids, cotangent)
-    cot = [cot[0]] + [swap(cot[k], "tm", k) for k in range(1, n)]
-    one = 2 * z.r * z.block * z.c * z.c
     (inner,) = call(
         functools.partial(inner_kernel, z),
         [shape((z.r, z.block, z.c), F32)],
@@ -279,39 +395,42 @@
     keep, send = call(
         functools.partial(grad_kernel, z, width),
         [shape((z.c // 2, 3 * z.c), F32), shape((z.c // 2, 3 * z.c))],
-        ids,
         *cot,
         acts,
         flops=3 * one,
         scratch=[pltpu.VMEM((z.r * z.block, z.c), BF)],
     )
     other = swap(send, "space", 1)
-    (encoded,) = call(
-        functools.partial(main_kernel, z),
-        [shape((n, z.r, z.piece, z.c))],
+    hidden, normed = call(
+        functools.partial(norm_kernel, z),
+        [shape((z.r, z.block, z.c))] * 2,
         x,
         acts,
-        temporal.reshape(3 * z.c, z.c),
+        temporal,
         gain.reshape(1, z.c),
+        flops=3 * one,
+    )
+    wide = z.c // n
+    pieces = call(
+        functools.partial(split_kernel, z),
+        [shape((z.c // 2, 3 * wide), F32)] + [shape((z.c // 2, 3 * wide))] * (n - 1),
+        keep,
+        other,
+    )
+    normed, *pieces = lax.optimization_barrier((normed, *pieces))
+    pieces = exchange(pieces)
+    encoded = call(
+        functools.partial(attend_kernel, z),
+        [shape((z.r, z.piece, z.c))] * n,
+        hidden,
+        normed,
         q_w,
         k_w,
         v_w,
         o_w,
-        flops=8 * one,
-    )
-    wide = z.c // n
-    pieces = call(
-        functools.partial(split_kernel, z),
-        [shape((z.c // 2, 3 * wide), F32)] + [shape((z.c // 2, 3 * wide))] * (n - 1),
-        ids,
-        keep,
-        other,
-    )
-    back = [lax.dynamic_index_in_dim(encoded, me ^ k, 0, False) for k in range(n)]
-    back = [back[0]] + [swap(back[k], "tm", k) for k in range(1, n)]
-    total = pieces[0]
-    for k in range(1, n):
-        total = total + swap(pieces[k], "tm", k).astype(F32)
+        flops=5 * one,
+    )
+    total = sum(piece.astype(F32) for piece in pieces)
     chips = space // 2
     total = total.reshape(chips, width, 3 * wide)
     sums = lax.dynamic_index_in_dim(total, here // 2, 0, False)
@@ -320,10 +439,16 @@
         mine = lax.dynamic_index_in_dim(total, here // 2 ^ k, 0, False)
         sums = sums + swap(mine, "space", 2 * k).astype(F32)
     kernel_grad = sums.reshape(width, 3, wide).transpose(1, 2, 0)
-    whole = jnp.zeros((z.fl, z.r, n, z.wc, z.c), BF)
-    for k in range(n):
-        rows = back[k].reshape(z.r, z.fl, 1, z.wc, z.c).transpose(1, 0, 2, 3, 4)
-        whole = lax.dynamic_update_slice_in_dim(whole, rows, me ^ k, 2)
+    back = exchange(encoded)
+    if z.wc % 16 == 0:
+        whole = write(z, 0, back[0])
+        for k in reversed(others):
+            whole = write(z, k, back[k], whole)
+    else:
+        whole = jnp.zeros((z.fl, z.r, n, z.wc, z.c), BF)
+        for k in range(n):
+            rows = back[k].reshape(z.r, z.fl, 1, z.wc, z.c).transpose(1, 0, 2, 3, 4)
+            whole = lax.dynamic_update_slice_in_dim(whole, rows, me ^ k, 2)
     return whole.reshape(frames_in.shape), kernel_grad
 
 

time: 91.3 us -> 111 us (1.22)
  Pallas kernels: 21.4 us -> 53.6 us
  waiting for transfers between devices: 27.4 us -> 17 us
  local copies, waits for them, and re-layouts: 13.8 us -> 12 us
    pallas_call x8 -> x14, Pallas kernels: 21.4 us -> 53.6 us  [the longest x4 36.3 us: write(): pl.pallas_call(functools.partial(write_kernel, z, k), out_shape=shape((z....]
    ppermute x16, waiting for transfers between devices: 27.4 us -> 16.9 us  [swap(): return lax.ppermute(value, axis, [(i, i ^ k) for i in range(count)])]
    unnamed x29 -> x35, local copies, waits for them, and re-layouts: 7.82 us -> 11.9 us
    dynamic_update_slice x4 -> x0, local copies, waits for them, and re-layouts: 3.83 us -> none  [on_device(): whole = lax.dynamic_update_slice_in_dim(whole, rows, me ^ k, 2)]
    ppermute x16, starting transfers between devices: 24.7 us -> 23.5 us  [swap(): return lax.ppermute(value, axis, [(i, i ^ k) for i in range(count)])]
  transfers between devices with their start and end apart: 18 -> 18, of which waited for: 7 -> 4; matrix products, arithmetic and copies ran while one was open for 7% -> 1% of each run, Pallas kernels for 19% -> 36%
where the time goes in v3:
time: 111 us
  Pallas kernels  53.6 us (48%)
  starting transfers between devices  26.3 us (24%)
  waiting for transfers between devices  17 us (15%)
  local copies, waits for them, and re-layouts  12 us (11%)
  between operations  1.11 us (1%)
    pallas_call x4, Pallas kernels, write(): pl.pallas_call(functools.partial(write_kernel, z, k), out_shape=shape((z....  36.3 us
    ppermute x16, starting transfers between devices, swap(): return lax.ppermute(value, axis, [(i, i ^ k) for i in range(count)])  23.5 us
    ppermute x16, waiting for transfers between devices, swap(): return lax.ppermute(value, axis, [(i, i ^ k) for i in range(count)])  16.9 us
    pallas_call x7, Pallas kernels, call(): pl.pallas_call(kernel, out_shape=tuple(outs), in_specs=[VMEM] * len(args)...  14.4 us
    unnamed x35, local copies, waits for them, and re-layouts  11.9 us
    pallas_call x2, Pallas kernels, pack(): pl.pallas_call(functools.partial(pack_kernel, z, halo), out_shape=tuple([...  2.35 us
  transfers between devices with their start and end apart: 18, of which 4 were waited for; matrix products, arithmetic and copies ran while one was open for 1% of the time, Pallas kernels for 36%

profile of v3, /device:TPU:0, one launch (start us, length us, event | category | flops | bytes accessed | tf_op | source)
XLA Modules:
  0.0 111.0 jit_solution(13704988374411583455)
XLA Ops:
  0.6 1.3 %copy-done.7 = bf16[4,4,64,512]{3,2,1,0:T(8,128)(2,1)S(1)} copy-done((bf16[4,4,64,512]{3,2,1,0:T(8,128)(2,1)S(1)}, bf16[4,4,64,512]{3,2,1,0:T(8,128)(2,1)}, u32[]{:S(2)}) %copy-start.7) | copy-done | bytes 1048600
  2.0 1.2 %shard_map.104 = (bf16[288,512]{1,0:T(8,128)(2,1)S(1)}, bf16[288,512]{1,0:T(8,128)(2,1)S(1)}, bf16[288,512]{1,0:T(8,128)(2,1)S(1)}, bf16[288,512]{1,0:T(8,128)(2,1)S(1)}) custom-call(bf16[4,4,64,512]{3,2,1,0:T(8,128)(2,1)S(1)} %copy-done.7), custom_call_target="tpu_custom_call" | custom-call | flops 536870912 | bytes 4194304 | tf_op jit(solution)/shard_map/pallas_call | solution.py:334
  3.2 3.0 %collective-permute-start = (bf16[288,512]{1,0:T(8,128)(2,1)S(1)}, bf16[288,512]{1,0:T(8,128)(2,1)S(1)}, u32[]{:S(2)}, u32[]{:S(2)}) collective-permute-start(bf16[288,512]{1,0:T(8,128)(2,1)S(1)} %get-tuple-element.47), channel_id=1, source_target_pairs={{0,8},{8,0},{16,24},{24,16},{1,9},{9,1},{17,25},{25,17},{2,10},{10... | collective-permute-start | bytes 884744 | tf_op jit(solution)/shard_map/ppermute | solution.py:279
  6.2 1.5 %collective-permute-start.1 = (bf16[288,512]{1,0:T(8,128)(2,1)S(1)}, bf16[288,512]{1,0:T(8,128)(2,1)S(1)}, u32[]{:S(2)}, u32[]{:S(2)}) collective-permute-start(bf16[288,512]{1,0:T(8,128)(2,1)S(1)} %get-tuple-element.48), channel_id=1, source_target_pairs={{0,16},{8,24},{16,0},{24,8},{1,17},{9,25},{17,1},{25,9},{2,18},{10... | collective-permute-start | bytes 884744 | tf_op jit(solution)/shard_map/ppermute | solution.py:279
  7.8 2.3 %copy-done = bf16[3,3,512,512]{3,2,1,0:T(8,128)(2,1)S(1)} copy-done((bf16[3,3,512,512]{3,2,1,0:T(8,128)(2,1)S(1)}, bf16[3,3,512,512]{3,2,1,0:T(8,128)(2,1)}, u32[]{:S(2)}) %copy-start) | copy-done | bytes 4718616
  10.1 1.0 copy-done.2
  11.2 1.0 copy-done.3
  12.2 1.0 copy-done.4
  13.3 1.0 copy-done.5
  14.3 0.6 shard_map.107
  14.9 0.6 copy-done.8
  15.5 1.1 shard_map.105
  16.6 4.4 %collective-permute-done.1.refs_2_ = bf16[288,512]{1,0:T(8,128)(2,1)S(1)} collective-permute-done((bf16[288,512]{1,0:T(8,128)(2,1)S(1)}, bf16[288,512]{1,0:T(8,128)(2,1)S(1)}, u32[]{:S(2)}, u32[]{:S(2)}) %collective-permute-start.1) | collective-permute-done | bytes 294944 | tf_op jit(solution)/shard_map/ppermute | solution.py:279
  21.0 0.5 shard_map.106
  21.5 1.3 %collective-permute-start.3 = (bf16[288,512]{1,0:T(8,128)(2,1)S(1)}, bf16[288,512]{1,0:T(8,128)(2,1)S(1)}, u32[]{:S(2)}, u32[]{:S(2)}) collective-permute-start(bf16[288,512]{1,0:T(8,128)(2,1)S(1)} %get-tuple-element.54), channel_id=1, source_target_pairs={{0,1},{1,2},{2,3},{3,4},{4,5},{5,6},{6,7},{8,9},{9,10},{10,11},{11... | collective-permute-start | bytes 884744 | tf_op jit(solution)/shard_map/ppermute | solution.py:376
  22.8 1.5 %collective-permute-start.4 = (bf16[288,512]{1,0:T(8,128)(2,1)S(1)}, bf16[288,512]{1,0:T(8,128)(2,1)S(1)}, u32[]{:S(2)}, u32[]{:S(2)}) collective-permute-start(bf16[288,512]{1,0:T(8,128)(2,1)S(1)} %get-tuple-element.55), channel_id=1, source_target_pairs={{1,0},{2,1},{3,2},{4,3},{5,4},{6,5},{7,6},{9,8},{10,9},{11,10},{12... | collective-permute-start | bytes 884744 | tf_op jit(solution)/shard_map/ppermute | solution.py:377
  24.3 1.3 %collective-permute-start.5 = (bf16[256,512]{1,0:T(8,128)(2,1)S(1)}, bf16[256,512]{1,0:T(8,128)(2,1)S(1)}, u32[]{:S(2)}, u32[]{:S(2)}) collective-permute-start(bf16[256,512]{1,0:T(8,128)(2,1)S(1)} %get-tuple-element.60), channel_id=1, source_target_pairs={{0,8},{8,0},{16,24},{24,16},{1,9},{9,1},{17,25},{25,17},{2,10},{10... | collective-permute-start | bytes 786440 | tf_op jit(solution)/shard_map/ppermute | solution.py:279
  25.6 0.8 collective-permute-start.6
  26.4 1.4 %collective-permute-start.7 = (bf16[256,512]{1,0:T(8,128)(2,1)S(1)}, bf16[256,512]{1,0:T(8,128)(2,1)S(1)}, u32[]{:S(2)}, u32[]{:S(2)}) collective-permute-start(bf16[256,512]{1,0:T(8,128)(2,1)S(1)} %get-tuple-element.62), channel_id=1, source_target_pairs={{0,24},{8,16},{16,8},{24,0},{1,25},{9,17},{17,9},{25,1},{2,26},{10... | collective-permute-start | bytes 786440 | tf_op jit(solution)/shard_map/ppermute | solution.py:279
  27.9 4.2 %shard_map.108.part_ref = f32[4,256,512]{2,1,0:T(8,128)S(1)} custom-call(bf16[4,288,512]{2,1,0:T(8,128)(2,1)S(1)} %get-tuple-element.52.x_ref, bf16[3,3,512,512]{3,2,1,0:T(8,128)(2,1)S(1)} %get-tuple-element.53.w_ref), custom_call_target="tpu_custom_call" | custom-call | flops 4026531840 | bytes 7995392 | tf_op jit(solution)/shard_map/pallas_call | solution.py:18
  32.1 1.8 %shard_map.109.act_ref.refs_4_ = bf16[4,256,1536]{2,1,0:T(8,128)(2,1)S(1)} custom-call(f32[4,256,512]{2,1,0:T(8,128)S(1)} %shard_map.108.part_ref, bf16[288,512]{1,0:T(8,128)(2,1)S(1)} %collective-permute-done.3.up_ref, bf16[288,512]{1,0:T(8,128)(2,1)S(1)} %collective-permute-done.4.down_ref, bf16[3,3,512,512]{3,2,1,0:T(8,128)(2,1)S(1)} %get-tuple-element.53.w_ref), custom_call_target="tpu_custom_call" | custom-call | flops 805306368 | bytes 10551296 | tf_op jit(solution)/shard_map/pallas_call | solution.py:18
  34.0 4.3 %collective-permute-done.7.refs_3_ = bf16[256,512]{1,0:T(8,128)(2,1)S(1)} collective-permute-done((bf16[256,512]{1,0:T(8,128)(2,1)S(1)}, bf16[256,512]{1,0:T(8,128)(2,1)S(1)}, u32[]{:S(2)}, u32[]{:S(2)}) %collective-permute-start.7) | collective-permute-done | bytes 262176 | tf_op jit(solution)/shard_map/ppermute | solution.py:279
  38.2 2.1 %shard_map.111 = (f32[256,1536]{1,0:T(8,128)S(1)}, bf16[256,1536]{1,0:T(8,128)(2,1)S(1)}) custom-call(bf16[256,512]{1,0:T(8,128)(2,1)S(1)} %get-tuple-element.59.refs_0_, bf16[256,512]{1,0:T(8,128)(2,1)S(1)} %collective-permute-done.5.refs_1_, bf16[256,512]{1,0:T(8,128)(2,1)S(1)} %collective-permute-done.6.refs_2_, ...), custom_call_target="tpu_custom_call" | custom-call | flops 1610612736 | bytes 6553600 | tf_op jit(solution)/shard_map/pallas_call | solution.py:18
  40.3 2.1 %collective-permute-start.8 = (bf16[256,1536]{1,0:T(8,128)(2,1)S(1)}, bf16[256,1536]{1,0:T(8,128)(2,1)S(1)}, u32[]{:S(2)}, u32[]{:S(2)}) collective-permute-start(bf16[256,1536]{1,0:T(8,128)(2,1)S(1)} %get-tuple-element.64), channel_id=1, source_target_pairs={{0,1},{1,0},{2,3},{3,2},{4,5},{5,4},{6,7},{7,6},{8,9},{9,8},{10,11... | collective-permute-start | bytes 2359304 | tf_op jit(solution)/shard_map/ppermute | solution.py:279
  42.4 2.0 %shard_map.110 = (bf16[4,256,512]{2,1,0:T(8,128)(2,1)S(1)}, bf16[4,256,512]{2,1,0:T(8,128)(2,1)S(1)}) custom-call(bf16[4,288,512]{2,1,0:T(8,128)(2,1)S(1)} %get-tuple-element.52.x_ref, bf16[4,256,1536]{2,1,0:T(8,128)(2,1)S(1)} %shard_map.109.act_ref.refs_4_, bf16[1536,512]{1,0:T(8,128)(2,1)S(1)} %get-tuple-element.56.t_ref, f32[1,512]{1,0:T(1,128)S(1)} %bitcast.22), custom_call_target="tpu_custom_call" | custom-call | flops 1610612736 | bytes 7997440 | tf_op jit(solution)/shard_map/pallas_call | solution.py:18
  44.4 0.3 shard_map.112
  44.7 0.9 collective-permute-start.12
  45.6 1.5 %collective-permute-start.13 = (bf16[256,384]{1,0:T(8,128)(2,1)S(1)}, bf16[256,384]{1,0:T(8,128)(2,1)S(1)}, u32[]{:S(2)}, u32[]{:S(2)}) collective-permute-start(bf16[256,384]{1,0:T(8,128)(2,1)S(1)} %get-tuple-element.80), channel_id=1, source_target_pairs={{0,16},{8,24},{16,0},{24,8},{1,17},{9,25},{17,1},{25,9},{2,18},{10... | collective-permute-start | bytes 589832 | tf_op jit(solution)/shard_map/ppermute | solution.py:279
  47.1 1.2 %collective-permute-start.14 = (bf16[256,384]{1,0:T(8,128)(2,1)S(1)}, bf16[256,384]{1,0:T(8,128)(2,1)}, u32[]{:S(2)}, u32[]{:S(2)}) collective-permute-start(bf16[256,384]{1,0:T(8,128)(2,1)S(1)} %get-tuple-element.81), channel_id=1, source_target_pairs={{0,24},{8,16},{16,8},{24,0},{1,25},{9,17},{17,9},{25,1},{2,26},{10... | collective-permute-start | bytes 589832 | tf_op jit(solution)/shard_map/ppermute | solution.py:279
  48.3 4.2 %collective-permute-done.12 = bf16[256,384]{1,0:T(8,128)(2,1)S(1)} collective-permute-done((bf16[256,384]{1,0:T(8,128)(2,1)S(1)}, bf16[256,384]{1,0:T(8,128)(2,1)S(1)}, u32[]{:S(2)}, u32[]{:S(2)}) %collective-permute-start.12) | collective-permute-done | bytes 196640 | tf_op jit(solution)/shard_map/ppermute | solution.py:279
  52.5 4.0 %collective-permute-done.13 = bf16[256,384]{1,0:T(8,128)(2,1)S(1)} collective-permute-done((bf16[256,384]{1,0:T(8,128)(2,1)S(1)}, bf16[256,384]{1,0:T(8,128)(2,1)S(1)}, u32[]{:S(2)}, u32[]{:S(2)}) %collective-permute-start.13) | collective-permute-done | bytes 196640 | tf_op jit(solution)/shard_map/ppermute | solution.py:279
  56.6 1.0 convert_add_fusion
  57.7 3.8 %collective-permute-start.15 = (bf16[64,384]{1,0:T(8,128)(2,1)S(1)}, bf16[64,384]{1,0:T(8,128)(2,1)S(1)}, u32[]{:S(2)}, u32[]{:S(2)}) collective-permute-start(bf16[64,384]{1,0:T(8,128)(2,1)S(1)} %get-tuple-element.84), channel_id=1, source_target_pairs={{0,2},{1,3},{2,0},{3,1},{4,6},{5,7},{6,4},{7,5},{8,10},{9,11},{10,... | collective-permute-start | bytes 147464 | tf_op jit(solution)/shard_map/ppermute | solution.py:279
  61.4 1.4 %collective-permute-start.16 = (bf16[64,384]{1,0:T(8,128)(2,1)S(1)}, bf16[64,384]{1,0:T(8,128)(2,1)S(1)}, u32[]{:S(2)}, u32[]{:S(2)}) collective-permute-start(bf16[64,384]{1,0:T(8,128)(2,1)S(1)} %get-tuple-element.86), channel_id=1, source_target_pairs={{0,4},{1,5},{2,6},{3,7},{4,0},{5,1},{6,2},{7,3},{8,12},{9,13},{10,... | collective-permute-start | bytes 147464 | tf_op jit(solution)/shard_map/ppermute | solution.py:279
  62.9 1.1 collective-permute-start.17
  63.9 3.5 %shard_map.113 = (bf16[4,64,512]{2,1,0:T(8,128)(2,1)S(1)}, bf16[4,64,512]{2,1,0:T(8,128)(2,1)S(1)}, bf16[4,64,512]{2,1,0:T(8,128)(2,1)S(1)}, bf16[4,64,512]{2,1,0:T(8,128)(2,1)S(1)}) custom-call(bf16[4,256,512]{2,1,0:T(8,128)(2,1)S(1)} %copy-done.11, bf16[4,256,512]{2,1,0:T(8,128)(2,1)S(1)} %copy-done.13, bf16[512,512]{1,0:T(8,128)(2,1)S(1)} %get-tuple-element.70.q_ref, ...), custom_call_target="tpu_custom_call" | custom-call | flops 2684354560 | bytes 5242880 | tf_op jit(solution)/shard_map/pallas_call | solution.py:18
  67.4 0.7 copy-done.6
  68.1 1.5 %collective-permute-start.11 = (bf16[4,64,512]{2,1,0:T(8,128)(2,1)S(1)}, bf16[4,64,512]{2,1,0:T(8,128)(2,1)S(1)}, u32[]{:S(2)}, u32[]{:S(2)}) collective-permute-start(bf16[4,64,512]{2,1,0:T(8,128)(2,1)S(1)} %get-tuple-element.76), channel_id=1, source_target_pairs={{0,16},{8,24},{16,0},{24,8},{1,17},{9,25},{17,1},{25,9},{2,18},{10... | collective-permute-start | bytes 786440 | tf_op jit(solution)/shard_map/ppermute | solution.py:279
  69.7 0.5 collective-permute-start.10
  70.2 1.4 %collective-permute-start.9 = (bf16[4,64,512]{2,1,0:T(8,128)(2,1)S(1)}, bf16[4,64,512]{2,1,0:T(8,128)(2,1)S(1)}, u32[]{:S(2)}, u32[]{:S(2)}) collective-permute-start(bf16[4,64,512]{2,1,0:T(8,128)(2,1)S(1)} %get-tuple-element.74), channel_id=1, source_target_pairs={{0,24},{8,16},{16,8},{24,0},{1,25},{9,17},{17,9},{25,1},{2,26},{10... | collective-permute-start | bytes 786440 | tf_op jit(solution)/shard_map/ppermute | solution.py:279
  71.6 9.1 %shard_map.114.refs_0_ = bf16[4,4,64,512]{3,2,1,0:T(8,128)(2,1)} custom-call(bf16[4,4,16,512]{3,2,1,0:T(8,128)(2,1)} %bitcast.21), custom_call_target="tpu_custom_call" | custom-call | bytes 524288 | tf_op jit(solution)/shard_map/pallas_call | solution.py:310
  80.8 0.6 copy.14
  81.5 0.7 copy-done.16
  82.2 9.1 %shard_map.115.refs_0_ = bf16[4,4,64,512]{3,2,1,0:T(8,128)(2,1)} custom-call(bf16[4,4,16,512]{3,2,1,0:T(8,128)(2,1)} %bitcast.28, bf16[4,4,64,512]{3,2,1,0:T(8,128)(2,1)} %shard_map.114.refs_0_), custom_call_target="tpu_custom_call", output_to_operand_aliasing={{}: (1, {})} | custom-call | bytes 524288 | tf_op jit(solution)/shard_map/pallas_call | solution.py:310
  91.3 0.7 copy-done.14
  92.0 9.1 %shard_map.116.refs_0_ = bf16[4,4,64,512]{3,2,1,0:T(8,128)(2,1)} custom-call(bf16[4,4,16,512]{3,2,1,0:T(8,128)(2,1)} %bitcast.26, bf16[4,4,64,512]{3,2,1,0:T(8,128)(2,1)} %shard_map.115.refs_0_), custom_call_target="tpu_custom_call", output_to_operand_aliasing={{}: (1, {})} | custom-call | bytes 524288 | tf_op jit(solution)/shard_map/pallas_call | solution.py:310
  101.1 0.7 copy-done.15
  101.8 9.1 %shard_map.117 = bf16[4,4,64,512]{3,2,1,0:T(8,128)(2,1)} custom-call(bf16[4,4,16,512]{3,2,1,0:T(8,128)(2,1)} %bitcast.27, bf16[4,4,64,512]{3,2,1,0:T(8,128)(2,1)} %shard_map.116.refs_0_), custom_call_target="tpu_custom_call", output_to_operand_aliasing={{}: (1, {})} | custom-call | bytes 524288 | tf_op jit(solution)/shard_map/pallas_call | solution.py:310
  (42 shorter events, 0.2 us)
Async XLA Ops:
  0.6 7.2 %copy-start.1 = (bf16[3,512,512]{2,1,0:T(8,128)(2,1)S(1)}, bf16[3,512,512]{2,1,0:T(8,128)(2,1)}, u32[]{:S(2)}) copy-start(bf16[3,512,512]{2,1,0:T(8,128)(2,1)} %param.11) | copy-start | bytes 4718596
  0.6 1.3 %copy-start.7 = (bf16[4,4,64,512]{3,2,1,0:T(8,128)(2,1)S(1)}, bf16[4,4,64,512]{3,2,1,0:T(8,128)(2,1)}, u32[]{:S(2)}) copy-start(bf16[4,4,64,512]{3,2,1,0:T(8,128)(2,1)} %x_ref.2) | copy-start | bytes 3145732
  3.2 13.4 %collective-permute-start = (bf16[288,512]{1,0:T(8,128)(2,1)S(1)}, bf16[288,512]{1,0:T(8,128)(2,1)S(1)}, u32[]{:S(2)}, u32[]{:S(2)}) collective-permute-start(bf16[288,512]{1,0:T(8,128)(2,1)S(1)} %get-tuple-element.47), channel_id=1, source_target_pairs={{0,8},{8,0},{16,24},{24,16},{1,9},{9,1},{17,25},{25,17},{2,10},{10... | collective-permute-start | bytes 884744 | tf_op jit(solution)/shard_map/ppermute | solution.py:279
  6.2 14.8 %collective-permute-start.1 = (bf16[288,512]{1,0:T(8,128)(2,1)S(1)}, bf16[288,512]{1,0:T(8,128)(2,1)S(1)}, u32[]{:S(2)}, u32[]{:S(2)}) collective-permute-start(bf16[288,512]{1,0:T(8,128)(2,1)S(1)} %get-tuple-element.48), channel_id=1, source_target_pairs={{0,16},{8,24},{16,0},{24,8},{1,17},{9,25},{17,1},{25,9},{2,18},{10... | collective-permute-start | bytes 884744 | tf_op jit(solution)/shard_map/ppermute | solution.py:279
  7.8 13.3 %collective-permute-start.2 = (bf16[288,512]{1,0:T(8,128)(2,1)S(1)}, bf16[288,512]{1,0:T(8,128)(2,1)S(1)}, u32[]{:S(2)}, u32[]{:S(2)}) collective-permute-start(bf16[288,512]{1,0:T(8,128)(2,1)S(1)} %get-tuple-element.51), channel_id=1, source_target_pairs={{0,24},{8,16},{16,8},{24,0},{1,25},{9,17},{17,9},{25,1},{2,26},{10... | collective-permute-start | bytes 884744 | tf_op jit(solution)/shard_map/ppermute | solution.py:279
  7.8 2.3 %copy-start = (bf16[3,3,512,512]{3,2,1,0:T(8,128)(2,1)S(1)}, bf16[3,3,512,512]{3,2,1,0:T(8,128)(2,1)}, u32[]{:S(2)}) copy-start(bf16[3,3,512,512]{3,2,1,0:T(8,128)(2,1)} %refs_0_.1) | copy-start | bytes 14155780
  10.1 1.0 copy-start.2
  11.2 1.0 copy-start.3
  12.2 1.0 copy-start.4
  13.3 1.0 copy-start.5
  14.3 1.2 %copy-start.8 = (bf16[4,4,64,512]{3,2,1,0:T(8,128)(2,1)S(1)}, bf16[4,4,64,512]{3,2,1,0:T(8,128)(2,1)}, u32[]{:S(2)}) copy-start(bf16[4,4,64,512]{3,2,1,0:T(8,128)(2,1)} %x_ref.3) | copy-start | bytes 3145732
  21.5 10.6 %collective-permute-start.3 = (bf16[288,512]{1,0:T(8,128)(2,1)S(1)}, bf16[288,512]{1,0:T(8,128)(2,1)S(1)}, u32[]{:S(2)}, u32[]{:S(2)}) collective-permute-start(bf16[288,512]{1,0:T(8,128)(2,1)S(1)} %get-tuple-element.54), channel_id=1, source_target_pairs={{0,1},{1,2},{2,3},{3,4},{4,5},{5,6},{6,7},{8,9},{9,10},{10,11},{11... | collective-permute-start | bytes 884744 | tf_op jit(solution)/shard_map/ppermute | solution.py:376
  22.8 9.3 %collective-permute-start.4 = (bf16[288,512]{1,0:T(8,128)(2,1)S(1)}, bf16[288,512]{1,0:T(8,128)(2,1)S(1)}, u32[]{:S(2)}, u32[]{:S(2)}) collective-permute-start(bf16[288,512]{1,0:T(8,128)(2,1)S(1)} %get-tuple-element.55), channel_id=1, source_target_pairs={{1,0},{2,1},{3,2},{4,3},{5,4},{6,5},{7,6},{9,8},{10,9},{11,10},{12... | collective-permute-start | bytes 884744 | tf_op jit(solution)/shard_map/ppermute | solution.py:377
  24.3 9.6 %collective-permute-start.5 = (bf16[256,512]{1,0:T(8,128)(2,1)S(1)}, bf16[256,512]{1,0:T(8,128)(2,1)S(1)}, u32[]{:S(2)}, u32[]{:S(2)}) collective-permute-start(bf16[256,512]{1,0:T(8,128)(2,1)S(1)} %get-tuple-element.60), channel_id=1, source_target_pairs={{0,8},{8,0},{16,24},{24,16},{1,9},{9,1},{17,25},{25,17},{2,10},{10... | collective-permute-start | bytes 786440 | tf_op jit(solution)/shard_map/ppermute | solution.py:279
  25.6 8.3 %collective-permute-start.6 = (bf16[256,512]{1,0:T(8,128)(2,1)S(1)}, bf16[256,512]{1,0:T(8,128)(2,1)S(1)}, u32[]{:S(2)}, u32[]{:S(2)}) collective-permute-start(bf16[256,512]{1,0:T(8,128)(2,1)S(1)} %get-tuple-element.61), channel_id=1, source_target_pairs={{0,16},{8,24},{16,0},{24,8},{1,17},{9,25},{17,1},{25,9},{2,18},{10... | collective-permute-start | bytes 786440 | tf_op jit(solution)/shard_map/ppermute | solution.py:279
  26.4 11.8 %collective-permute-start.7 = (bf16[256,512]{1,0:T(8,128)(2,1)S(1)}, bf16[256,512]{1,0:T(8,128)(2,1)S(1)}, u32[]{:S(2)}, u32[]{:S(2)}) collective-permute-start(bf16[256,512]{1,0:T(8,128)(2,1)S(1)} %get-tuple-element.62), channel_id=1, source_target_pairs={{0,24},{8,16},{16,8},{24,0},{1,25},{9,17},{17,9},{25,1},{2,26},{10... | collective-permute-start | bytes 786440 | tf_op jit(solution)/shard_map/ppermute | solution.py:279
  33.9 8.5 %copy-start.9 = (f32[512]{0:T(512)S(1)}, f32[512]{0:T(512)}, u32[]{:S(2)}) copy-start(f32[512]{0:T(512)} %param.12) | copy-start | bytes 6148
  40.3 4.1 %collective-permute-start.8 = (bf16[256,1536]{1,0:T(8,128)(2,1)S(1)}, bf16[256,1536]{1,0:T(8,128)(2,1)S(1)}, u32[]{:S(2)}, u32[]{:S(2)}) collective-permute-start(bf16[256,1536]{1,0:T(8,128)(2,1)S(1)} %get-tuple-element.64), channel_id=1, source_target_pairs={{0,1},{1,0},{2,3},{3,2},{4,5},{5,4},{6,7},{7,6},{8,9},{9,8},{10,11... | collective-permute-start | bytes 2359304 | tf_op jit(solution)/shard_map/ppermute | solution.py:279
  44.4 3.9 %copy-start.10 = (bf16[4,256,512]{2,1,0:T(8,128)(2,1)}, bf16[4,256,512]{2,1,0:T(8,128)(2,1)S(1)}, u32[]{:S(2)}) copy-start(bf16[4,256,512]{2,1,0:T(8,128)(2,1)S(1)} %get-tuple-element.57.hidden_ref) | copy-start | bytes 3145732
  44.4 3.9 %copy-start.12 = (bf16[4,256,512]{2,1,0:T(8,128)(2,1)}, bf16[4,256,512]{2,1,0:T(8,128)(2,1)S(1)}, u32[]{:S(2)}) copy-start(bf16[4,256,512]{2,1,0:T(8,128)(2,1)S(1)} %get-tuple-element.69.normed_ref) | copy-start | bytes 3145732
  44.7 7.8 %collective-permute-start.12 = (bf16[256,384]{1,0:T(8,128)(2,1)S(1)}, bf16[256,384]{1,0:T(8,128)(2,1)S(1)}, u32[]{:S(2)}, u32[]{:S(2)}) collective-permute-start(bf16[256,384]{1,0:T(8,128)(2,1)S(1)} %get-tuple-element.79), channel_id=1, source_target_pairs={{0,8},{8,0},{16,24},{24,16},{1,9},{9,1},{17,25},{25,17},{2,10},{10... | collective-permute-start | bytes 589832 | tf_op jit(solution)/shard_map/ppermute | solution.py:279
  45.6 11.0 %collective-permute-start.13 = (bf16[256,384]{1,0:T(8,128)(2,1)S(1)}, bf16[256,384]{1,0:T(8,128)(2,1)S(1)}, u32[]{:S(2)}, u32[]{:S(2)}) collective-permute-start(bf16[256,384]{1,0:T(8,128)(2,1)S(1)} %get-tuple-element.80), channel_id=1, source_target_pairs={{0,16},{8,24},{16,0},{24,8},{1,17},{9,25},{17,1},{25,9},{2,18},{10... | collective-permute-start | bytes 589832 | tf_op jit(solution)/shard_map/ppermute | solution.py:279
  47.1 9.4 %collective-permute-start.14 = (bf16[256,384]{1,0:T(8,128)(2,1)S(1)}, bf16[256,384]{1,0:T(8,128)(2,1)}, u32[]{:S(2)}, u32[]{:S(2)}) collective-permute-start(bf16[256,384]{1,0:T(8,128)(2,1)S(1)} %get-tuple-element.81), channel_id=1, source_target_pairs={{0,24},{8,16},{16,8},{24,0},{1,25},{9,17},{17,9},{25,1},{2,26},{10... | collective-permute-start | bytes 589832 | tf_op jit(solution)/shard_map/ppermute | solution.py:279
  48.3 15.6 %copy-start.11 = (bf16[4,256,512]{2,1,0:T(8,128)(2,1)S(1)}, bf16[4,256,512]{2,1,0:T(8,128)(2,1)}, u32[]{:S(2)}) copy-start(bf16[4,256,512]{2,1,0:T(8,128)(2,1)} %copy-done.10) | copy-start | bytes 3145732
  48.3 15.6 %copy-start.13 = (bf16[4,256,512]{2,1,0:T(8,128)(2,1)S(1)}, bf16[4,256,512]{2,1,0:T(8,128)(2,1)}, u32[]{:S(2)}) copy-start(bf16[4,256,512]{2,1,0:T(8,128)(2,1)} %copy-done.12) | copy-start | bytes 3145732
  57.7 12.5 %collective-permute-start.15 = (bf16[64,384]{1,0:T(8,128)(2,1)S(1)}, bf16[64,384]{1,0:T(8,128)(2,1)S(1)}, u32[]{:S(2)}, u32[]{:S(2)}) collective-permute-start(bf16[64,384]{1,0:T(8,128)(2,1)S(1)} %get-tuple-element.84), channel_id=1, source_target_pairs={{0,2},{1,3},{2,0},{3,1},{4,6},{5,7},{6,4},{7,5},{8,10},{9,11},{10,... | collective-permute-start | bytes 147464 | tf_op jit(solution)/shard_map/ppermute | solution.py:279
  61.4 19.3 %collective-permute-start.16 = (bf16[64,384]{1,0:T(8,128)(2,1)S(1)}, bf16[64,384]{1,0:T(8,128)(2,1)S(1)}, u32[]{:S(2)}, u32[]{:S(2)}) collective-permute-start(bf16[64,384]{1,0:T(8,128)(2,1)S(1)} %get-tuple-element.86), channel_id=1, source_target_pairs={{0,4},{1,5},{2,6},{3,7},{4,0},{5,1},{6,2},{7,3},{8,12},{9,13},{10,... | collective-permute-start | bytes 147464 | tf_op jit(solution)/shard_map/ppermute | solution.py:279
  62.9 17.9 %collective-permute-start.17 = (bf16[64,384]{1,0:T(8,128)(2,1)S(1)}, bf16[64,384]{1,0:T(8,128)(2,1)S(1)}, u32[]{:S(2)}, u32[]{:S(2)}) collective-permute-start(bf16[64,384]{1,0:T(8,128)(2,1)S(1)} %get-tuple-element.85), channel_id=1, source_target_pairs={{0,6},{1,7},{2,4},{3,5},{4,2},{5,3},{6,0},{7,1},{8,14},{9,15},{10,... | collective-permute-start | bytes 147464 | tf_op jit(solution)/shard_map/ppermute | solution.py:279
  67.4 0.7 copy-start.6
  68.1 13.3 %collective-permute-start.11 = (bf16[4,64,512]{2,1,0:T(8,128)(2,1)S(1)}, bf16[4,64,512]{2,1,0:T(8,128)(2,1)S(1)}, u32[]{:S(2)}, u32[]{:S(2)}) collective-permute-start(bf16[4,64,512]{2,1,0:T(8,128)(2,1)S(1)} %get-tuple-element.76), channel_id=1, source_target_pairs={{0,16},{8,24},{16,0},{24,8},{1,17},{9,25},{17,1},{25,9},{2,18},{10... | collective-permute-start | bytes 786440 | tf_op jit(solution)/shard_map/ppermute | solution.py:279
  69.7 21.6 %collective-permute-start.10 = (bf16[4,64,512]{2,1,0:T(8,128)(2,1)S(1)}, bf16[4,64,512]{2,1,0:T(8,128)(2,1)S(1)}, u32[]{:S(2)}, u32[]{:S(2)}) collective-permute-start(bf16[4,64,512]{2,1,0:T(8,128)(2,1)S(1)} %get-tuple-element.75), channel_id=1, source_target_pairs={{0,8},{8,0},{16,24},{24,16},{1,9},{9,1},{17,25},{25,17},{2,10},{10... | collective-permute-start | bytes 786440 | tf_op jit(solution)/shard_map/ppermute | solution.py:279
  70.2 30.9 %collective-permute-start.9 = (bf16[4,64,512]{2,1,0:T(8,128)(2,1)S(1)}, bf16[4,64,512]{2,1,0:T(8,128)(2,1)S(1)}, u32[]{:S(2)}, u32[]{:S(2)}) collective-permute-start(bf16[4,64,512]{2,1,0:T(8,128)(2,1)S(1)} %get-tuple-element.74), channel_id=1, source_target_pairs={{0,24},{8,16},{16,8},{24,0},{1,25},{9,17},{17,9},{25,1},{2,26},{10... | collective-permute-start | bytes 786440 | tf_op jit(solution)/shard_map/ppermute | solution.py:279
  81.5 0.7 copy-start.16
  91.3 0.7 copy-start.14
  101.1 0.7 copy-start.15

commit v4 on v3

--- a/solution.py
+++ b/solution.py
@@ -51,11 +51,7 @@
         self.sides = 2 * rows * frames
 
 
-def pack_kernel(z, halo, x_ref, *refs):
-    outs, (x, sem) = refs[: z.n], refs[z.n :]
-    copies = [pltpu.make_async_copy(x_ref.at[:, r], x.at[r], sem.at[r]) for r in range(z.r)]
-    for copy in copies:
-        copy.start()
+def pack_kernel(z, halo, x_ref, *outs):
     me = lax.axis_index("tm")
 
     def source(q):
@@ -76,8 +72,7 @@
         edges = [chooser(z.n * z.sides, z.fl * z.w, functools.partial(edge, r)) for r in range(z.r)]
         tails = jnp.zeros((z.n * z.sides, z.c), F32)
     for r in range(z.r):
-        copies[r].wait()
-        rows = x[r].reshape(z.fl * z.w, z.c)
+        rows = x_ref[:, r].reshape(z.fl * z.w, z.c)
         cut = moved(matrix, rows)
         for k in range(z.n):
             outs[k][r * z.piece : (r + 1) * z.piece] = cut[k * z.piece : (k + 1) * z.piece]
@@ -291,35 +286,6 @@
         copy.wait()
 
 
-def write_kernel(z, k, piece_ref, *refs):
-    out, sem = refs[-2:]
-    first = pl.multiple_of((lax.axis_index("tm") ^ k) * z.wc, z.wc)
-    copies = [
-        pltpu.make_async_copy(
-            piece_ref.at[r], out.at[:, r, pl.ds(first, z.wc)], sem.at[r]
-        )
-        for r in range(z.r)
-    ]
-    for copy in copies:
-        copy.start()
-    for copy in copies:
-        copy.wait()
-
-
-def write(z, k, piece, *whole):
-    return pl.pallas_call(
-        functools.partial(write_kernel, z, k),
-        out_shape=shape((z.fl, z.r, z.w, z.c)),
-        in_specs=[pl.BlockSpec(memory_space=pl.ANY)] * (1 + len(whole)),
-        out_specs=pl.BlockSpec(memory_space=pl.ANY),
-        input_output_aliases={1: 0} if whole else {},
-        scratch_shapes=[pltpu.SemaphoreType.DMA((z.r,))],
-        cost_estimate=pl.CostEstimate(
-            flops=0, bytes_accessed=4 * z.main * z.c, transcendentals=0
-        ),
-    )(piece.reshape(z.r, z.fl, z.wc, z.c), *whole)
-
-
 def on_device(frames_in, spatial, temporal, gain, q_w, k_w, v_w, o_w, cotangent):
     n = lax.axis_size("tm")
     space = lax.axis_size("space")
@@ -331,18 +297,8 @@
 
     def pack(value, halo):
         rows = z.main + (z.sides if halo else 0)
-        return pl.pallas_call(
-            functools.partial(pack_kernel, z, halo),
-            out_shape=tuple([shape((rows, z.c))] * n),
-            in_specs=[pl.BlockSpec(memory_space=pltpu.HBM)],
-            out_specs=tuple([VMEM] * n),
-            scratch_shapes=[
-                pltpu.VMEM((z.r, z.fl, z.w, z.c), BF),
-                pltpu.SemaphoreType.DMA((z.r,)),
-            ],
-            compiler_params=pltpu.CompilerParams(vmem_limit_bytes=16 * 2**20),
-            cost_estimate=pl.CostEstimate(flops=one, bytes_accessed=2**22, transcendentals=0),
-        )(value)
+        kernel = functools.partial(pack_kernel, z, halo)
+        return call(kernel, [shape((rows, z.c))] * n, value, flops=one)
 
     def exchange(pieces):
         pieces = list(pieces)
@@ -430,6 +386,8 @@
         o_w,
         flops=5 * one,
     )
+    back = exchange(encoded)
+    pieces = lax.optimization_barrier((*pieces, *encoded))[:n]
     total = sum(piece.astype(F32) for piece in pieces)
     chips = space // 2
     total = total.reshape(chips, width, 3 * wide)
@@ -439,16 +397,10 @@
         mine = lax.dynamic_index_in_dim(total, here // 2 ^ k, 0, False)
         sums = sums + swap(mine, "space", 2 * k).astype(F32)
     kernel_grad = sums.reshape(width, 3, wide).transpose(1, 2, 0)
-    back = exchange(encoded)
-    if z.wc % 16 == 0:
-        whole = write(z, 0, back[0])
-        for k in reversed(others):
-            whole = write(z, k, back[k], whole)
-    else:
-        whole = jnp.zeros((z.fl, z.r, n, z.wc, z.c), BF)
-        for k in range(n):
-            rows = back[k].reshape(z.r, z.fl, 1, z.wc, z.c).transpose(1, 0, 2, 3, 4)
-            whole = lax.dynamic_update_slice_in_dim(whole, rows, me ^ k, 2)
+    whole = jnp.zeros((z.fl, z.r, n, z.wc, z.c), BF)
+    for k in [0] + others[::-1]:
+        rows = back[k].reshape(z.r, z.fl, 1, z.wc, z.c).transpose(1, 0, 2, 3, 4)
+        whole = lax.dynamic_update_slice_in_dim(whole, rows, me ^ k, 2)
     return whole.reshape(frames_in.shape), kernel_grad
 
 

time: 111 us -> 77.9 us (0.70)
  Pallas kernels: 53.6 us -> 18.2 us
  local copies, waits for them, and re-layouts: 12 us -> 14.2 us
    pallas_call x6 -> x0, Pallas kernels: 38.7 us -> none  [the longest x4 36.3 us: write(): pl.pallas_call(functools.partial(write_kernel, z, k), out_shape=shape((z....]
    pallas_call x7 -> x9, Pallas kernels: 14.4 us -> 17.5 us  [call(): pl.pallas_call(kernel, out_shape=tuple(outs), in_specs=[VMEM] * len(args)...]
    unnamed x35 -> x49, local copies, waits for them, and re-layouts: 11.9 us -> 13.9 us
  transfers between devices with their start and end apart: 18 -> 18, of which waited for: 4 -> 7; matrix products, arithmetic and copies ran while one was open for 1% -> 1% of each run, Pallas kernels for 36% -> 16%
where the time goes in v4:
time: 77.9 us; the launch traced here: 77.4 us
  starting transfers between devices  26.1 us (34%)
  Pallas kernels  18.2 us (23%)
  waiting for transfers between devices  17.8 us (23%)
  local copies, waits for them, and re-layouts  14.2 us (18%)
  between operations  1.01 us (1%)
    ppermute x16, starting transfers between devices, swap(): return lax.ppermute(value, axis, [(i, i ^ k) for i in range(count)])  23.5 us
    ppermute x16, waiting for transfers between devices, swap(): return lax.ppermute(value, axis, [(i, i ^ k) for i in range(count)])  17.8 us
    pallas_call x9, Pallas kernels, call(): pl.pallas_call(kernel, out_shape=tuple(outs), in_specs=[VMEM] * len(args)...  17.5 us
    unnamed x49, local copies, waits for them, and re-layouts  13.9 us
  transfers between devices with their start and end apart: 18, of which 7 were waited for; matrix products, arithmetic and copies ran while one was open for 1% of the time, Pallas kernels for 16%

profile of v4, /device:TPU:0, one launch (start us, length us, event | category | flops | bytes accessed | tf_op | source)
XLA Modules:
  0.0 77.4 jit_solution(1076069950564292096)
XLA Ops:
  0.6 1.3 %copy-done.12 = bf16[4,4,64,512]{3,2,1,0:T(8,128)(2,1)S(1)} copy-done((bf16[4,4,64,512]{3,2,1,0:T(8,128)(2,1)S(1)}, bf16[4,4,64,512]{3,2,1,0:T(8,128)(2,1)}, u32[]{:S(2)}) %copy-start.12) | copy-done | bytes 1048600
  2.0 0.6 shard_map.104
  2.6 3.0 %collective-permute-start = (bf16[288,512]{1,0:T(8,128)(2,1)S(1)}, bf16[288,512]{1,0:T(8,128)(2,1)S(1)}, u32[]{:S(2)}, u32[]{:S(2)}) collective-permute-start(bf16[288,512]{1,0:T(8,128)(2,1)S(1)} %get-tuple-element.51), channel_id=1, source_target_pairs={{0,8},{8,0},{16,24},{24,16},{1,9},{9,1},{17,25},{25,17},{2,10},{10... | collective-permute-start | bytes 884744 | tf_op jit(solution)/shard_map/ppermute | solution.py:274
  5.6 1.5 %collective-permute-start.1 = (bf16[288,512]{1,0:T(8,128)(2,1)S(1)}, bf16[288,512]{1,0:T(8,128)(2,1)S(1)}, u32[]{:S(2)}, u32[]{:S(2)}) collective-permute-start(bf16[288,512]{1,0:T(8,128)(2,1)S(1)} %get-tuple-element.52), channel_id=1, source_target_pairs={{0,16},{8,24},{16,0},{24,8},{1,17},{9,25},{17,1},{25,9},{2,18},{10... | collective-permute-start | bytes 884744 | tf_op jit(solution)/shard_map/ppermute | solution.py:274
  7.1 2.3 %copy-done = bf16[3,3,512,512]{3,2,1,0:T(8,128)(2,1)S(1)} copy-done((bf16[3,3,512,512]{3,2,1,0:T(8,128)(2,1)S(1)}, bf16[3,3,512,512]{3,2,1,0:T(8,128)(2,1)}, u32[]{:S(2)}) %copy-start) | copy-done | bytes 4718616
  9.4 1.0 %copy-done.4 = bf16[512,512]{1,0:T(8,128)(2,1)S(1)} copy-done((bf16[512,512]{1,0:T(8,128)(2,1)S(1)}, bf16[512,512]{1,0:T(8,128)(2,1)}, u32[]{:S(2)}) %copy-start.4) | copy-done | bytes 524312
  10.5 1.0 %copy-done.5 = bf16[512,512]{1,0:T(8,128)(2,1)S(1)} copy-done((bf16[512,512]{1,0:T(8,128)(2,1)S(1)}, bf16[512,512]{1,0:T(8,128)(2,1)}, u32[]{:S(2)}) %copy-start.5) | copy-done | bytes 524312
  11.5 1.0 %copy-done.6 = bf16[512,512]{1,0:T(8,128)(2,1)S(1)} copy-done((bf16[512,512]{1,0:T(8,128)(2,1)S(1)}, bf16[512,512]{1,0:T(8,128)(2,1)}, u32[]{:S(2)}) %copy-start.6) | copy-done | bytes 524312
  12.6 1.0 %copy-done.7 = bf16[512,512]{1,0:T(8,128)(2,1)S(1)} copy-done((bf16[512,512]{1,0:T(8,128)(2,1)S(1)}, bf16[512,512]{1,0:T(8,128)(2,1)}, u32[]{:S(2)}) %copy-start.7) | copy-done | bytes 524312
  13.6 0.6 shard_map.107
  14.2 0.6 copy-done.13
  14.9 0.4 shard_map.105
  15.3 5.0 %collective-permute-done.1.refs_2_ = bf16[288,512]{1,0:T(8,128)(2,1)S(1)} collective-permute-done((bf16[288,512]{1,0:T(8,128)(2,1)S(1)}, bf16[288,512]{1,0:T(8,128)(2,1)S(1)}, u32[]{:S(2)}, u32[]{:S(2)}) %collective-permute-start.1) | collective-permute-done | bytes 294944 | tf_op jit(solution)/shard_map/ppermute | solution.py:274
  20.4 0.5 shard_map.106
  20.9 1.3 %collective-permute-start.3 = (bf16[288,512]{1,0:T(8,128)(2,1)S(1)}, bf16[288,512]{1,0:T(8,128)(2,1)S(1)}, u32[]{:S(2)}, u32[]{:S(2)}) collective-permute-start(bf16[288,512]{1,0:T(8,128)(2,1)S(1)} %get-tuple-element.58), channel_id=1, source_target_pairs={{0,1},{1,2},{2,3},{3,4},{4,5},{5,6},{6,7},{8,9},{9,10},{10,11},{11... | collective-permute-start | bytes 884744 | tf_op jit(solution)/shard_map/ppermute | solution.py:332
  22.2 1.3 %collective-permute-start.4 = (bf16[288,512]{1,0:T(8,128)(2,1)S(1)}, bf16[288,512]{1,0:T(8,128)(2,1)S(1)}, u32[]{:S(2)}, u32[]{:S(2)}) collective-permute-start(bf16[288,512]{1,0:T(8,128)(2,1)S(1)} %get-tuple-element.59), channel_id=1, source_target_pairs={{1,0},{2,1},{3,2},{4,3},{5,4},{6,5},{7,6},{9,8},{10,9},{11,10},{12... | collective-permute-start | bytes 884744 | tf_op jit(solution)/shard_map/ppermute | solution.py:333
  23.5 1.3 %collective-permute-start.5 = (bf16[256,512]{1,0:T(8,128)(2,1)S(1)}, bf16[256,512]{1,0:T(8,128)(2,1)S(1)}, u32[]{:S(2)}, u32[]{:S(2)}) collective-permute-start(bf16[256,512]{1,0:T(8,128)(2,1)S(1)} %get-tuple-element.64), channel_id=1, source_target_pairs={{0,8},{8,0},{16,24},{24,16},{1,9},{9,1},{17,25},{25,17},{2,10},{10... | collective-permute-start | bytes 786440 | tf_op jit(solution)/shard_map/ppermute | solution.py:274
  24.8 0.8 %collective-permute-start.6 = (bf16[256,512]{1,0:T(8,128)(2,1)S(1)}, bf16[256,512]{1,0:T(8,128)(2,1)S(1)}, u32[]{:S(2)}, u32[]{:S(2)}) collective-permute-start(bf16[256,512]{1,0:T(8,128)(2,1)S(1)} %get-tuple-element.65), channel_id=1, source_target_pairs={{0,16},{8,24},{16,0},{24,8},{1,17},{9,25},{17,1},{25,9},{2,18},{10... | collective-permute-start | bytes 786440 | tf_op jit(solution)/shard_map/ppermute | solution.py:274
  25.6 1.4 %collective-permute-start.7 = (bf16[256,512]{1,0:T(8,128)(2,1)S(1)}, bf16[256,512]{1,0:T(8,128)(2,1)S(1)}, u32[]{:S(2)}, u32[]{:S(2)}) collective-permute-start(bf16[256,512]{1,0:T(8,128)(2,1)S(1)} %get-tuple-element.66), channel_id=1, source_target_pairs={{0,24},{8,16},{16,8},{24,0},{1,25},{9,17},{17,9},{25,1},{2,26},{10... | collective-permute-start | bytes 786440 | tf_op jit(solution)/shard_map/ppermute | solution.py:274
  27.0 4.2 %shard_map.108.part_ref = f32[4,256,512]{2,1,0:T(8,128)S(1)} custom-call(bf16[4,288,512]{2,1,0:T(8,128)(2,1)S(1)} %get-tuple-element.56.x_ref, bf16[3,3,512,512]{3,2,1,0:T(8,128)(2,1)S(1)} %get-tuple-element.57.w_ref), custom_call_target="tpu_custom_call" | custom-call | flops 4026531840 | bytes 7995392 | tf_op jit(solution)/shard_map/pallas_call | solution.py:18
  31.3 1.8 %shard_map.109.act_ref.refs_4_ = bf16[4,256,1536]{2,1,0:T(8,128)(2,1)S(1)} custom-call(f32[4,256,512]{2,1,0:T(8,128)S(1)} %shard_map.108.part_ref, bf16[288,512]{1,0:T(8,128)(2,1)S(1)} %collective-permute-done.3.up_ref, bf16[288,512]{1,0:T(8,128)(2,1)S(1)} %collective-permute-done.4.down_ref, bf16[3,3,512,512]{3,2,1,0:T(8,128)(2,1)S(1)} %get-tuple-element.57.w_ref), custom_call_target="tpu_custom_call" | custom-call | flops 805306368 | bytes 10551296 | tf_op jit(solution)/shard_map/pallas_call | solution.py:18
  33.2 4.2 %collective-permute-done.7.refs_3_ = bf16[256,512]{1,0:T(8,128)(2,1)S(1)} collective-permute-done((bf16[256,512]{1,0:T(8,128)(2,1)S(1)}, bf16[256,512]{1,0:T(8,128)(2,1)S(1)}, u32[]{:S(2)}, u32[]{:S(2)}) %collective-permute-start.7) | collective-permute-done | bytes 262176 | tf_op jit(solution)/shard_map/ppermute | solution.py:274
  37.4 3.0 %shard_map.111 = (f32[256,1536]{1,0:T(8,128)S(1)}, bf16[256,1536]{1,0:T(8,128)(2,1)}) custom-call(bf16[256,512]{1,0:T(8,128)(2,1)S(1)} %get-tuple-element.63.refs_0_, bf16[256,512]{1,0:T(8,128)(2,1)S(1)} %collective-permute-done.5.refs_1_, bf16[256,512]{1,0:T(8,128)(2,1)S(1)} %collective-permute-done.6.refs_2_, ...), custom_call_target="tpu_custom_call" | custom-call | flops 1610612736 | bytes 6553600 | tf_op jit(solution)/shard_map/pallas_call | solution.py:18
  40.3 1.1 %copy-done.1 = f32[256,1536]{1,0:T(8,128)} copy-done((f32[256,1536]{1,0:T(8,128)}, f32[256,1536]{1,0:T(8,128)S(1)}, u32[]{:S(2)}) %copy-start.1) | copy-done | bytes 1572888
  41.5 2.0 %collective-permute-start.8 = (bf16[256,1536]{1,0:T(8,128)(2,1)}, bf16[256,1536]{1,0:T(8,128)(2,1)}, u32[]{:S(2)}, u32[]{:S(2)}) collective-permute-start(bf16[256,1536]{1,0:T(8,128)(2,1)} %get-tuple-element.68), channel_id=1, source_target_pairs={{0,1},{1,0},{2,3},{3,2},{4,5},{5,4},{6,7},{7,6},{8,9},{9,8},{10,11... | collective-permute-start | bytes 2359304 | tf_op jit(solution)/shard_map/ppermute | solution.py:274
  43.5 1.4 %copy-done.9 = bf16[1536,512]{1,0:T(8,128)(2,1)S(1)} copy-done((bf16[1536,512]{1,0:T(8,128)(2,1)S(1)}, bf16[1536,512]{1,0:T(8,128)(2,1)}, u32[]{:S(2)}) %copy-start.9) | copy-done | bytes 1572888
  44.9 1.3 %copy-done.11 = bf16[4,288,512]{2,1,0:T(8,128)(2,1)S(1)} copy-done((bf16[4,288,512]{2,1,0:T(8,128)(2,1)S(1)}, bf16[4,288,512]{2,1,0:T(8,128)(2,1)}, u32[]{:S(2)}) %copy-start.11) | copy-done | bytes 1179672
  46.2 2.0 %shard_map.110 = (bf16[4,256,512]{2,1,0:T(8,128)(2,1)S(1)}, bf16[4,256,512]{2,1,0:T(8,128)(2,1)S(1)}) custom-call(bf16[4,288,512]{2,1,0:T(8,128)(2,1)S(1)} %copy-done.11, bf16[4,256,1536]{2,1,0:T(8,128)(2,1)S(1)} %shard_map.109.act_ref.refs_4_, bf16[1536,512]{1,0:T(8,128)(2,1)S(1)} %copy-done.9, f32[1,512]{1,0:T(1,128)S(1)} %bitcast.31), custom_call_target="tpu_custom_call" | custom-call | flops 1610612736 | bytes 7997440 | tf_op jit(solution)/shard_map/pallas_call | solution.py:18
  48.2 1.6 %shard_map.112 = (f32[256,384]{1,0:T(8,128)S(1)}, bf16[256,384]{1,0:T(8,128)(2,1)S(1)}, bf16[256,384]{1,0:T(8,128)(2,1)S(1)}, bf16[256,384]{1,0:T(8,128)(2,1)S(1)}) custom-call(f32[256,1536]{1,0:T(8,128)S(1)} %copy-done.2, bf16[256,1536]{1,0:T(8,128)(2,1)} %collective-permute-done.8.got_ref), custom_call_target="tpu_custom_call" | custom-call | bytes 3342336 | tf_op jit(solution)/shard_map/pallas_call | solution.py:18
  49.8 0.9 %collective-permute-start.12 = (bf16[256,384]{1,0:T(8,128)(2,1)S(1)}, bf16[256,384]{1,0:T(8,128)(2,1)S(1)}, u32[]{:S(2)}, u32[]{:S(2)}) collective-permute-start(bf16[256,384]{1,0:T(8,128)(2,1)S(1)} %get-tuple-element.83), channel_id=1, source_target_pairs={{0,8},{8,0},{16,24},{24,16},{1,9},{9,1},{17,25},{25,17},{2,10},{10... | collective-permute-start | bytes 589832 | tf_op jit(solution)/shard_map/ppermute | solution.py:274
  50.7 1.5 %collective-permute-start.13 = (bf16[256,384]{1,0:T(8,128)(2,1)S(1)}, bf16[256,384]{1,0:T(8,128)(2,1)S(1)}, u32[]{:S(2)}, u32[]{:S(2)}) collective-permute-start(bf16[256,384]{1,0:T(8,128)(2,1)S(1)} %get-tuple-element.84), channel_id=1, source_target_pairs={{0,16},{8,24},{16,0},{24,8},{1,17},{9,25},{17,1},{25,9},{2,18},{10... | collective-permute-start | bytes 589832 | tf_op jit(solution)/shard_map/ppermute | solution.py:274
  52.2 1.2 %collective-permute-start.14 = (bf16[256,384]{1,0:T(8,128)(2,1)S(1)}, bf16[256,384]{1,0:T(8,128)(2,1)S(1)}, u32[]{:S(2)}, u32[]{:S(2)}) collective-permute-start(bf16[256,384]{1,0:T(8,128)(2,1)S(1)} %get-tuple-element.85), channel_id=1, source_target_pairs={{0,24},{8,16},{16,8},{24,0},{1,25},{9,17},{17,9},{25,1},{2,26},{10... | collective-permute-start | bytes 589832 | tf_op jit(solution)/shard_map/ppermute | solution.py:274
  53.4 3.5 %shard_map.113 = (bf16[4,64,512]{2,1,0:T(8,128)(2,1)S(1)}, bf16[4,64,512]{2,1,0:T(8,128)(2,1)S(1)}, bf16[4,64,512]{2,1,0:T(8,128)(2,1)S(1)}, bf16[4,64,512]{2,1,0:T(8,128)(2,1)S(1)}) custom-call(bf16[4,256,512]{2,1,0:T(8,128)(2,1)S(1)} %get-tuple-element.61.hidden_ref, bf16[4,256,512]{2,1,0:T(8,128)(2,1)S(1)} %get-tuple-element.73.normed_ref, ...), custom_call_target="tpu_custom_call" | custom-call | flops 2684354560 | bytes 5242880 | tf_op jit(solution)/shard_map/pallas_call | solution.py:18
  56.9 0.9 %collective-permute-start.9 = (bf16[4,64,512]{2,1,0:T(8,128)(2,1)S(1)}, bf16[4,64,512]{2,1,0:T(8,128)(2,1)S(1)}, u32[]{:S(2)}, u32[]{:S(2)}) collective-permute-start(bf16[4,64,512]{2,1,0:T(8,128)(2,1)S(1)} %get-tuple-element.79), channel_id=1, source_target_pairs={{0,16},{8,24},{16,0},{24,8},{1,17},{9,25},{17,1},{25,9},{2,18},{10... | collective-permute-start | bytes 786440 | tf_op jit(solution)/shard_map/ppermute | solution.py:274
  57.8 1.5 %collective-permute-start.10 = (bf16[4,64,512]{2,1,0:T(8,128)(2,1)S(1)}, bf16[4,64,512]{2,1,0:T(8,128)(2,1)S(1)}, u32[]{:S(2)}, u32[]{:S(2)}) collective-permute-start(bf16[4,64,512]{2,1,0:T(8,128)(2,1)S(1)} %get-tuple-element.80), channel_id=1, source_target_pairs={{0,8},{8,0},{16,24},{24,16},{1,9},{9,1},{17,25},{25,17},{2,10},{10... | collective-permute-start | bytes 786440 | tf_op jit(solution)/shard_map/ppermute | solution.py:274
  59.3 1.6 %collective-permute-done.13 = bf16[256,384]{1,0:T(8,128)(2,1)S(1)} collective-permute-done((bf16[256,384]{1,0:T(8,128)(2,1)S(1)}, bf16[256,384]{1,0:T(8,128)(2,1)S(1)}, u32[]{:S(2)}, u32[]{:S(2)}) %collective-permute-start.13) | collective-permute-done | bytes 196640 | tf_op jit(solution)/shard_map/ppermute | solution.py:274
  60.8 1.3 %collective-permute-done.14 = bf16[256,384]{1,0:T(8,128)(2,1)S(1)} collective-permute-done((bf16[256,384]{1,0:T(8,128)(2,1)S(1)}, bf16[256,384]{1,0:T(8,128)(2,1)S(1)}, u32[]{:S(2)}, u32[]{:S(2)}) %collective-permute-start.14) | collective-permute-done | bytes 196640 | tf_op jit(solution)/shard_map/ppermute | solution.py:274
  62.2 0.1 convert_add_fusion
  62.3 3.4 %collective-permute-start.15 = (bf16[64,384]{1,0:T(8,128)(2,1)S(1)}, bf16[64,384]{1,0:T(8,128)(2,1)S(1)}, u32[]{:S(2)}, u32[]{:S(2)}) collective-permute-start(bf16[64,384]{1,0:T(8,128)(2,1)S(1)} %get-tuple-element.92), channel_id=1, source_target_pairs={{0,2},{1,3},{2,0},{3,1},{4,6},{5,7},{6,4},{7,5},{8,10},{9,11},{10,... | collective-permute-start | bytes 147464 | tf_op jit(solution)/shard_map/ppermute | solution.py:274
  65.8 1.4 %collective-permute-start.16 = (bf16[64,384]{1,0:T(8,128)(2,1)S(1)}, bf16[64,384]{1,0:T(8,128)(2,1)S(1)}, u32[]{:S(2)}, u32[]{:S(2)}) collective-permute-start(bf16[64,384]{1,0:T(8,128)(2,1)S(1)} %get-tuple-element.94), channel_id=1, source_target_pairs={{0,4},{1,5},{2,6},{3,7},{4,0},{5,1},{6,2},{7,3},{8,12},{9,13},{10,... | collective-permute-start | bytes 147464 | tf_op jit(solution)/shard_map/ppermute | solution.py:274
  67.2 1.1 %collective-permute-start.17 = (bf16[64,384]{1,0:T(8,128)(2,1)S(1)}, bf16[64,384]{1,0:T(8,128)(2,1)S(1)}, u32[]{:S(2)}, u32[]{:S(2)}) collective-permute-start(bf16[64,384]{1,0:T(8,128)(2,1)S(1)} %get-tuple-element.93), channel_id=1, source_target_pairs={{0,6},{1,7},{2,4},{3,5},{4,2},{5,3},{6,0},{7,1},{8,14},{9,15},{10,... | collective-permute-start | bytes 147464 | tf_op jit(solution)/shard_map/ppermute | solution.py:274
  68.2 0.1 broadcast_in_dim.3
  68.4 1.5 %collective-permute-start.11 = (bf16[4,64,512]{2,1,0:T(8,128)(2,1)S(1)}, bf16[4,64,512]{2,1,0:T(8,128)(2,1)S(1)}, u32[]{:S(2)}, u32[]{:S(2)}) collective-permute-start(bf16[4,64,512]{2,1,0:T(8,128)(2,1)S(1)} %get-tuple-element.81), channel_id=1, source_target_pairs={{0,24},{8,16},{16,8},{24,0},{1,25},{9,17},{17,9},{25,1},{2,26},{10... | collective-permute-start | bytes 786440 | tf_op jit(solution)/shard_map/ppermute | solution.py:274
  69.9 1.9 %collective-permute-done.16 = bf16[64,384]{1,0:T(8,128)(2,1)S(1)} collective-permute-done((bf16[64,384]{1,0:T(8,128)(2,1)S(1)}, bf16[64,384]{1,0:T(8,128)(2,1)S(1)}, u32[]{:S(2)}, u32[]{:S(2)}) %collective-permute-start.16) | collective-permute-done | bytes 49184 | tf_op jit(solution)/shard_map/ppermute | solution.py:274
  71.8 1.3 %collective-permute-done.17 = bf16[64,384]{1,0:T(8,128)(2,1)S(1)} collective-permute-done((bf16[64,384]{1,0:T(8,128)(2,1)S(1)}, bf16[64,384]{1,0:T(8,128)(2,1)S(1)}, u32[]{:S(2)}, u32[]{:S(2)}) %collective-permute-start.17) | collective-permute-done | bytes 49184 | tf_op jit(solution)/shard_map/ppermute | solution.py:274
  73.1 0.6 copy.19
  73.9 2.5 %collective-permute-done.11 = bf16[4,64,512]{2,1,0:T(8,128)(2,1)S(1)} collective-permute-done((bf16[4,64,512]{2,1,0:T(8,128)(2,1)S(1)}, bf16[4,64,512]{2,1,0:T(8,128)(2,1)S(1)}, u32[]{:S(2)}, u32[]{:S(2)}) %collective-permute-start.11) | collective-permute-done | bytes 262176 | tf_op jit(solution)/shard_map/ppermute | solution.py:274
  76.4 1.0 %copy-done.23 = bf16[4,4,4,16,512]{4,3,2,1,0:T(8,128)(2,1)} copy-done((bf16[4,4,4,16,512]{4,3,2,1,0:T(8,128)(2,1)}, bf16[4,4,4,16,512]{4,3,2,1,0:T(8,128)(2,1)S(1)}, u32[]{:S(2)}) %copy-start.23) | copy-done | bytes 1048600
  (57 shorter events, 0.3 us)
Async XLA Ops:
  0.6 6.5 %copy-start.3 = (bf16[3,512,512]{2,1,0:T(8,128)(2,1)S(1)}, bf16[3,512,512]{2,1,0:T(8,128)(2,1)}, u32[]{:S(2)}) copy-start(bf16[3,512,512]{2,1,0:T(8,128)(2,1)} %param.11) | copy-start | bytes 4718596
  0.6 1.3 %copy-start.12 = (bf16[4,4,64,512]{3,2,1,0:T(8,128)(2,1)S(1)}, bf16[4,4,64,512]{3,2,1,0:T(8,128)(2,1)}, u32[]{:S(2)}) copy-start(bf16[4,4,64,512]{3,2,1,0:T(8,128)(2,1)} %x_ref.2) | copy-start | bytes 3145732
  2.6 12.7 %collective-permute-start = (bf16[288,512]{1,0:T(8,128)(2,1)S(1)}, bf16[288,512]{1,0:T(8,128)(2,1)S(1)}, u32[]{:S(2)}, u32[]{:S(2)}) collective-permute-start(bf16[288,512]{1,0:T(8,128)(2,1)S(1)} %get-tuple-element.51), channel_id=1, source_target_pairs={{0,8},{8,0},{16,24},{24,16},{1,9},{9,1},{17,25},{25,17},{2,10},{10... | collective-permute-start | bytes 884744 | tf_op jit(solution)/shard_map/ppermute | solution.py:274
  5.6 14.8 %collective-permute-start.1 = (bf16[288,512]{1,0:T(8,128)(2,1)S(1)}, bf16[288,512]{1,0:T(8,128)(2,1)S(1)}, u32[]{:S(2)}, u32[]{:S(2)}) collective-permute-start(bf16[288,512]{1,0:T(8,128)(2,1)S(1)} %get-tuple-element.52), channel_id=1, source_target_pairs={{0,16},{8,24},{16,0},{24,8},{1,17},{9,25},{17,1},{25,9},{2,18},{10... | collective-permute-start | bytes 884744 | tf_op jit(solution)/shard_map/ppermute | solution.py:274
  7.1 13.3 %collective-permute-start.2 = (bf16[288,512]{1,0:T(8,128)(2,1)S(1)}, bf16[288,512]{1,0:T(8,128)(2,1)S(1)}, u32[]{:S(2)}, u32[]{:S(2)}) collective-permute-start(bf16[288,512]{1,0:T(8,128)(2,1)S(1)} %get-tuple-element.55), channel_id=1, source_target_pairs={{0,24},{8,16},{16,8},{24,0},{1,25},{9,17},{17,9},{25,1},{2,26},{10... | collective-permute-start | bytes 884744 | tf_op jit(solution)/shard_map/ppermute | solution.py:274
  7.1 2.3 %copy-start = (bf16[3,3,512,512]{3,2,1,0:T(8,128)(2,1)S(1)}, bf16[3,3,512,512]{3,2,1,0:T(8,128)(2,1)}, u32[]{:S(2)}) copy-start(bf16[3,3,512,512]{3,2,1,0:T(8,128)(2,1)} %refs_0_.1) | copy-start | bytes 14155780
  9.4 1.0 %copy-start.4 = (bf16[512,512]{1,0:T(8,128)(2,1)S(1)}, bf16[512,512]{1,0:T(8,128)(2,1)}, u32[]{:S(2)}) copy-start(bf16[512,512]{1,0:T(8,128)(2,1)} %refs_2_.1) | copy-start | bytes 1572868
  10.5 1.0 %copy-start.5 = (bf16[512,512]{1,0:T(8,128)(2,1)S(1)}, bf16[512,512]{1,0:T(8,128)(2,1)}, u32[]{:S(2)}) copy-start(bf16[512,512]{1,0:T(8,128)(2,1)} %refs_3_.1) | copy-start | bytes 1572868
  11.5 1.0 %copy-start.6 = (bf16[512,512]{1,0:T(8,128)(2,1)S(1)}, bf16[512,512]{1,0:T(8,128)(2,1)}, u32[]{:S(2)}) copy-start(bf16[512,512]{1,0:T(8,128)(2,1)} %refs_4_.1) | copy-start | bytes 1572868
  12.6 1.0 %copy-start.7 = (bf16[512,512]{1,0:T(8,128)(2,1)S(1)}, bf16[512,512]{1,0:T(8,128)(2,1)}, u32[]{:S(2)}) copy-start(bf16[512,512]{1,0:T(8,128)(2,1)} %refs_5_.1) | copy-start | bytes 1572868
  13.6 1.2 %copy-start.13 = (bf16[4,4,64,512]{3,2,1,0:T(8,128)(2,1)S(1)}, bf16[4,4,64,512]{3,2,1,0:T(8,128)(2,1)}, u32[]{:S(2)}) copy-start(bf16[4,4,64,512]{3,2,1,0:T(8,128)(2,1)} %x_ref.3) | copy-start | bytes 3145732
  14.8 16.4 %copy-start.8 = (bf16[1536,512]{1,0:T(8,128)(2,1)}, bf16[1536,512]{1,0:T(8,128)(2,1)S(1)}, u32[]{:S(2)}) copy-start(bf16[1536,512]{1,0:T(8,128)(2,1)S(1)} %get-tuple-element.60.t_ref) | copy-start | bytes 4718596
  14.8 16.4 %copy-start.14 = (bf16[512,512]{1,0:T(8,128)(2,1)}, bf16[512,512]{1,0:T(8,128)(2,1)S(1)}, u32[]{:S(2)}) copy-start(bf16[512,512]{1,0:T(8,128)(2,1)S(1)} %get-tuple-element.74.q_ref) | copy-start | bytes 1572868
  14.8 16.4 %copy-start.16 = (bf16[512,512]{1,0:T(8,128)(2,1)}, bf16[512,512]{1,0:T(8,128)(2,1)S(1)}, u32[]{:S(2)}) copy-start(bf16[512,512]{1,0:T(8,128)(2,1)S(1)} %get-tuple-element.75.k_ref) | copy-start | bytes 1572868
  14.8 16.4 %copy-start.18 = (bf16[512,512]{1,0:T(8,128)(2,1)}, bf16[512,512]{1,0:T(8,128)(2,1)S(1)}, u32[]{:S(2)}) copy-start(bf16[512,512]{1,0:T(8,128)(2,1)S(1)} %get-tuple-element.76.v_ref) | copy-start | bytes 1572868
  14.9 16.4 %copy-start.20 = (bf16[512,512]{1,0:T(8,128)(2,1)}, bf16[512,512]{1,0:T(8,128)(2,1)S(1)}, u32[]{:S(2)}) copy-start(bf16[512,512]{1,0:T(8,128)(2,1)S(1)} %get-tuple-element.77.o_ref) | copy-start | bytes 1572868
  20.8 10.4 %copy-start.10 = (bf16[4,288,512]{2,1,0:T(8,128)(2,1)}, bf16[4,288,512]{2,1,0:T(8,128)(2,1)S(1)}, u32[]{:S(2)}) copy-start(bf16[4,288,512]{2,1,0:T(8,128)(2,1)S(1)} %get-tuple-element.56.x_ref) | copy-start | bytes 3538948
  20.9 10.4 %collective-permute-start.3 = (bf16[288,512]{1,0:T(8,128)(2,1)S(1)}, bf16[288,512]{1,0:T(8,128)(2,1)S(1)}, u32[]{:S(2)}, u32[]{:S(2)}) collective-permute-start(bf16[288,512]{1,0:T(8,128)(2,1)S(1)} %get-tuple-element.58), channel_id=1, source_target_pairs={{0,1},{1,2},{2,3},{3,4},{4,5},{5,6},{6,7},{8,9},{9,10},{10,11},{11... | collective-permute-start | bytes 884744 | tf_op jit(solution)/shard_map/ppermute | solution.py:332
  22.2 9.1 %collective-permute-start.4 = (bf16[288,512]{1,0:T(8,128)(2,1)S(1)}, bf16[288,512]{1,0:T(8,128)(2,1)S(1)}, u32[]{:S(2)}, u32[]{:S(2)}) collective-permute-start(bf16[288,512]{1,0:T(8,128)(2,1)S(1)} %get-tuple-element.59), channel_id=1, source_target_pairs={{1,0},{2,1},{3,2},{4,3},{5,4},{6,5},{7,6},{9,8},{10,9},{11,10},{12... | collective-permute-start | bytes 884744 | tf_op jit(solution)/shard_map/ppermute | solution.py:333
  23.5 9.7 %collective-permute-start.5 = (bf16[256,512]{1,0:T(8,128)(2,1)S(1)}, bf16[256,512]{1,0:T(8,128)(2,1)S(1)}, u32[]{:S(2)}, u32[]{:S(2)}) collective-permute-start(bf16[256,512]{1,0:T(8,128)(2,1)S(1)} %get-tuple-element.64), channel_id=1, source_target_pairs={{0,8},{8,0},{16,24},{24,16},{1,9},{9,1},{17,25},{25,17},{2,10},{10... | collective-permute-start | bytes 786440 | tf_op jit(solution)/shard_map/ppermute | solution.py:274
  24.8 8.4 %collective-permute-start.6 = (bf16[256,512]{1,0:T(8,128)(2,1)S(1)}, bf16[256,512]{1,0:T(8,128)(2,1)S(1)}, u32[]{:S(2)}, u32[]{:S(2)}) collective-permute-start(bf16[256,512]{1,0:T(8,128)(2,1)S(1)} %get-tuple-element.65), channel_id=1, source_target_pairs={{0,16},{8,24},{16,0},{24,8},{1,17},{9,25},{17,1},{25,9},{2,18},{10... | collective-permute-start | bytes 786440 | tf_op jit(solution)/shard_map/ppermute | solution.py:274
  25.6 11.8 %collective-permute-start.7 = (bf16[256,512]{1,0:T(8,128)(2,1)S(1)}, bf16[256,512]{1,0:T(8,128)(2,1)S(1)}, u32[]{:S(2)}, u32[]{:S(2)}) collective-permute-start(bf16[256,512]{1,0:T(8,128)(2,1)S(1)} %get-tuple-element.66), channel_id=1, source_target_pairs={{0,24},{8,16},{16,8},{24,0},{1,25},{9,17},{17,9},{25,1},{2,26},{10... | collective-permute-start | bytes 786440 | tf_op jit(solution)/shard_map/ppermute | solution.py:274
  33.1 10.4 %copy-start.22 = (f32[512]{0:T(512)S(1)}, f32[512]{0:T(512)}, u32[]{:S(2)}) copy-start(f32[512]{0:T(512)} %param.12) | copy-start | bytes 6148
  40.3 1.1 %copy-start.1 = (f32[256,1536]{1,0:T(8,128)}, f32[256,1536]{1,0:T(8,128)S(1)}, u32[]{:S(2)}) copy-start(f32[256,1536]{1,0:T(8,128)S(1)} %get-tuple-element.67.keep_ref) | copy-start | bytes 4718596
  41.5 6.8 %collective-permute-start.8 = (bf16[256,1536]{1,0:T(8,128)(2,1)}, bf16[256,1536]{1,0:T(8,128)(2,1)}, u32[]{:S(2)}, u32[]{:S(2)}) collective-permute-start(bf16[256,1536]{1,0:T(8,128)(2,1)} %get-tuple-element.68), channel_id=1, source_target_pairs={{0,1},{1,0},{2,3},{3,2},{4,5},{5,4},{6,7},{7,6},{8,9},{9,8},{10,11... | collective-permute-start | bytes 2359304 | tf_op jit(solution)/shard_map/ppermute | solution.py:274
  43.5 1.4 %copy-start.9 = (bf16[1536,512]{1,0:T(8,128)(2,1)S(1)}, bf16[1536,512]{1,0:T(8,128)(2,1)}, u32[]{:S(2)}) copy-start(bf16[1536,512]{1,0:T(8,128)(2,1)} %copy-done.8) | copy-start | bytes 4718596
  44.9 1.3 %copy-start.11 = (bf16[4,288,512]{2,1,0:T(8,128)(2,1)S(1)}, bf16[4,288,512]{2,1,0:T(8,128)(2,1)}, u32[]{:S(2)}) copy-start(bf16[4,288,512]{2,1,0:T(8,128)(2,1)} %copy-done.10) | copy-start | bytes 3538948
  46.2 2.1 %copy-start.2 = (f32[256,1536]{1,0:T(8,128)S(1)}, f32[256,1536]{1,0:T(8,128)}, u32[]{:S(2)}) copy-start(f32[256,1536]{1,0:T(8,128)} %copy-done.1) | copy-start | bytes 4718596
  48.2 5.2 %copy-start.15 = (bf16[512,512]{1,0:T(8,128)(2,1)S(1)}, bf16[512,512]{1,0:T(8,128)(2,1)}, u32[]{:S(2)}) copy-start(bf16[512,512]{1,0:T(8,128)(2,1)} %copy-done.14) | copy-start | bytes 1572868
  48.2 5.2 %copy-start.17 = (bf16[512,512]{1,0:T(8,128)(2,1)S(1)}, bf16[512,512]{1,0:T(8,128)(2,1)}, u32[]{:S(2)}) copy-start(bf16[512,512]{1,0:T(8,128)(2,1)} %copy-done.16) | copy-start | bytes 1572868
  48.2 5.2 %copy-start.19 = (bf16[512,512]{1,0:T(8,128)(2,1)S(1)}, bf16[512,512]{1,0:T(8,128)(2,1)}, u32[]{:S(2)}) copy-start(bf16[512,512]{1,0:T(8,128)(2,1)} %copy-done.18) | copy-start | bytes 1572868
  48.2 5.2 %copy-start.21 = (bf16[512,512]{1,0:T(8,128)(2,1)S(1)}, bf16[512,512]{1,0:T(8,128)(2,1)}, u32[]{:S(2)}) copy-start(bf16[512,512]{1,0:T(8,128)(2,1)} %copy-done.20) | copy-start | bytes 1572868
  49.8 9.5 %collective-permute-start.12 = (bf16[256,384]{1,0:T(8,128)(2,1)S(1)}, bf16[256,384]{1,0:T(8,128)(2,1)S(1)}, u32[]{:S(2)}, u32[]{:S(2)}) collective-permute-start(bf16[256,384]{1,0:T(8,128)(2,1)S(1)} %get-tuple-element.83), channel_id=1, source_target_pairs={{0,8},{8,0},{16,24},{24,16},{1,9},{9,1},{17,25},{25,17},{2,10},{10... | collective-permute-start | bytes 589832 | tf_op jit(solution)/shard_map/ppermute | solution.py:274
  50.7 10.2 %collective-permute-start.13 = (bf16[256,384]{1,0:T(8,128)(2,1)S(1)}, bf16[256,384]{1,0:T(8,128)(2,1)S(1)}, u32[]{:S(2)}, u32[]{:S(2)}) collective-permute-start(bf16[256,384]{1,0:T(8,128)(2,1)S(1)} %get-tuple-element.84), channel_id=1, source_target_pairs={{0,16},{8,24},{16,0},{24,8},{1,17},{9,25},{17,1},{25,9},{2,18},{10... | collective-permute-start | bytes 589832 | tf_op jit(solution)/shard_map/ppermute | solution.py:274
  52.2 10.0 %collective-permute-start.14 = (bf16[256,384]{1,0:T(8,128)(2,1)S(1)}, bf16[256,384]{1,0:T(8,128)(2,1)S(1)}, u32[]{:S(2)}, u32[]{:S(2)}) collective-permute-start(bf16[256,384]{1,0:T(8,128)(2,1)S(1)} %get-tuple-element.85), channel_id=1, source_target_pairs={{0,24},{8,16},{16,8},{24,0},{1,25},{9,17},{17,9},{25,1},{2,26},{10... | collective-permute-start | bytes 589832 | tf_op jit(solution)/shard_map/ppermute | solution.py:274
  56.9 16.9 %collective-permute-start.9 = (bf16[4,64,512]{2,1,0:T(8,128)(2,1)S(1)}, bf16[4,64,512]{2,1,0:T(8,128)(2,1)S(1)}, u32[]{:S(2)}, u32[]{:S(2)}) collective-permute-start(bf16[4,64,512]{2,1,0:T(8,128)(2,1)S(1)} %get-tuple-element.79), channel_id=1, source_target_pairs={{0,16},{8,24},{16,0},{24,8},{1,17},{9,25},{17,1},{25,9},{2,18},{10... | collective-permute-start | bytes 786440 | tf_op jit(solution)/shard_map/ppermute | solution.py:274
  57.8 16.0 %collective-permute-start.10 = (bf16[4,64,512]{2,1,0:T(8,128)(2,1)S(1)}, bf16[4,64,512]{2,1,0:T(8,128)(2,1)S(1)}, u32[]{:S(2)}, u32[]{:S(2)}) collective-permute-start(bf16[4,64,512]{2,1,0:T(8,128)(2,1)S(1)} %get-tuple-element.80), channel_id=1, source_target_pairs={{0,8},{8,0},{16,24},{24,16},{1,9},{9,1},{17,25},{25,17},{2,10},{10... | collective-permute-start | bytes 786440 | tf_op jit(solution)/shard_map/ppermute | solution.py:274
  62.3 6.1 %collective-permute-start.15 = (bf16[64,384]{1,0:T(8,128)(2,1)S(1)}, bf16[64,384]{1,0:T(8,128)(2,1)S(1)}, u32[]{:S(2)}, u32[]{:S(2)}) collective-permute-start(bf16[64,384]{1,0:T(8,128)(2,1)S(1)} %get-tuple-element.92), channel_id=1, source_target_pairs={{0,2},{1,3},{2,0},{3,1},{4,6},{5,7},{6,4},{7,5},{8,10},{9,11},{10,... | collective-permute-start | bytes 147464 | tf_op jit(solution)/shard_map/ppermute | solution.py:274
  65.8 6.0 %collective-permute-start.16 = (bf16[64,384]{1,0:T(8,128)(2,1)S(1)}, bf16[64,384]{1,0:T(8,128)(2,1)S(1)}, u32[]{:S(2)}, u32[]{:S(2)}) collective-permute-start(bf16[64,384]{1,0:T(8,128)(2,1)S(1)} %get-tuple-element.94), channel_id=1, source_target_pairs={{0,4},{1,5},{2,6},{3,7},{4,0},{5,1},{6,2},{7,3},{8,12},{9,13},{10,... | collective-permute-start | bytes 147464 | tf_op jit(solution)/shard_map/ppermute | solution.py:274
  67.2 5.9 %collective-permute-start.17 = (bf16[64,384]{1,0:T(8,128)(2,1)S(1)}, bf16[64,384]{1,0:T(8,128)(2,1)S(1)}, u32[]{:S(2)}, u32[]{:S(2)}) collective-permute-start(bf16[64,384]{1,0:T(8,128)(2,1)S(1)} %get-tuple-element.93), channel_id=1, source_target_pairs={{0,6},{1,7},{2,4},{3,5},{4,2},{5,3},{6,0},{7,1},{8,14},{9,15},{10,... | collective-permute-start | bytes 147464 | tf_op jit(solution)/shard_map/ppermute | solution.py:274
  68.4 8.0 %collective-permute-start.11 = (bf16[4,64,512]{2,1,0:T(8,128)(2,1)S(1)}, bf16[4,64,512]{2,1,0:T(8,128)(2,1)S(1)}, u32[]{:S(2)}, u32[]{:S(2)}) collective-permute-start(bf16[4,64,512]{2,1,0:T(8,128)(2,1)S(1)} %get-tuple-element.81), channel_id=1, source_target_pairs={{0,24},{8,16},{16,8},{24,0},{1,25},{9,17},{17,9},{25,1},{2,26},{10... | collective-permute-start | bytes 786440 | tf_op jit(solution)/shard_map/ppermute | solution.py:274
  76.4 1.0 %copy-start.23 = (bf16[4,4,4,16,512]{4,3,2,1,0:T(8,128)(2,1)}, bf16[4,4,4,16,512]{4,3,2,1,0:T(8,128)(2,1)S(1)}, u32[]{:S(2)}) copy-start(bf16[4,4,4,16,512]{4,3,2,1,0:T(8,128)(2,1)S(1)} %copy_dynamic-update-slice_fusion) | copy-start | bytes 3145732

commit v5 on v4

--- a/solution.py
+++ b/solution.py
@@ -51,7 +51,12 @@
         self.sides = 2 * rows * frames
 
 
-def pack_kernel(z, halo, x_ref, *outs):
+def edge_kernel(z, x_ref, after_ref, top, bottom):
+    top[...] = x_ref[:, 0].reshape(z.fl * z.w, z.c)
+    bottom[...] = x_ref[:, z.r - 1].reshape(z.fl * z.w, z.c)
+
+
+def pack_kernel(z, x_ref, *outs):
     me = lax.axis_index("tm")
 
     def source(q):
@@ -68,20 +73,87 @@
         return jnp.where(inside, q % z.fl * z.w + col, -1)
 
     matrix = chooser(z.n * z.piece, z.fl * z.w, source)
-    if halo:
-        edges = [chooser(z.n * z.sides, z.fl * z.w, functools.partial(edge, r)) for r in range(z.r)]
-        tails = jnp.zeros((z.n * z.sides, z.c), F32)
+    tails = jnp.zeros((z.n * z.sides, z.c), F32)
     for r in range(z.r):
         rows = x_ref[:, r].reshape(z.fl * z.w, z.c)
         cut = moved(matrix, rows)
         for k in range(z.n):
             outs[k][r * z.piece : (r + 1) * z.piece] = cut[k * z.piece : (k + 1) * z.piece]
-        if halo:
-            tails += jnp.dot(edges[r], rows, preferred_element_type=F32)
-    if halo:
-        tails = tails.astype(BF)
-        for k in range(z.n):
-            outs[k][z.main : z.main + z.sides] = tails[k * z.sides : (k + 1) * z.sides]
+        picked = chooser(z.n * z.sides, z.fl * z.w, functools.partial(edge, r))
+        tails += jnp.dot(picked, rows, preferred_element_type=F32)
+    tails = tails.astype(BF)
+    for k in range(z.n):
+        outs[k][z.main : z.main + z.sides] = tails[k * z.sides : (k + 1) * z.sides]
+
+
+def aside(z, rows):
+    count = z.fl * z.w
+    left = chooser(count, count, lambda q: jnp.where(q % z.w > 0, q - 1, -1))
+    right = chooser(count, count, lambda q: jnp.where(q % z.w < z.w - 1, q + 1, -1))
+    return moved(left, rows), rows, moved(right, rows)
+
+
+def own_inner_kernel(z, x_ref, w_ref, out, beside):
+    for r in range(z.r):
+        for dj, rows in enumerate(aside(z, x_ref[:, r].reshape(z.fl * z.w, z.c))):
+            beside[dj, r] = rows
+    for r in range(z.r):
+        total = jnp.zeros((z.fl * z.w, z.c), F32)
+        for di in range(3):
+            if 0 <= r + di - 1 < z.r:
+                for dj in range(3):
+                    total += jnp.dot(
+                        beside[dj, r + di - 1], w_ref[di, dj], preferred_element_type=F32
+                    )
+        out[r] = total
+
+
+def own_act_kernel(z, part_ref, up_ref, down_ref, w_ref, out, last):
+    for r in range(z.r):
+        total = part_ref[r]
+        for edge, di, ref in ((0, 0, up_ref), (z.r - 1, 2, down_ref)):
+            if r == edge:
+                for dj, rows in enumerate(aside(z, ref[...])):
+                    total += jnp.dot(rows, w_ref[di, dj], preferred_element_type=F32)
+        act = silu(total).reshape(z.fl, z.w, z.c)
+        out[:, r] = act
+        last[r] = act[z.fl - 1]
+
+
+def silu(total):
+    return (total / (1.0 + jnp.exp(-total))).astype(BF)
+
+
+def flat(value):
+    return value.reshape(-1, value.shape[-1])
+
+
+def outer(left, right):
+    return lax.dot_general(
+        flat(left), flat(right), (((0,), (0,)), ((), ())), preferred_element_type=F32
+    )
+
+
+def own_grad_kernel(z, act_ref, cot_ref, out):
+    for k in range(3):
+        out[:, k * z.c : (k + 1) * z.c] = outer(cot_ref[k:], act_ref[: z.fl - k])
+
+
+def cross_kernel(z, width, part_ref, before_ref, act_ref, cot_ref, after_ref, keep, send):
+    mine = lax.axis_index("space") % 2 == 0
+    for k in range(3):
+        lanes = slice(k * z.c, (k + 1) * z.c)
+        grad = part_ref[:, lanes]
+        if k == 1:
+            grad += outer(cot_ref[0], before_ref[...])
+        if k == 2:
+            grad += outer(cot_ref[1], before_ref[...])
+            grad += outer(after_ref[...], act_ref[z.fl - 2])
+        for i in range(z.c // (2 * width)):
+            low = grad[2 * i * width : (2 * i + 1) * width]
+            high = grad[(2 * i + 1) * width : (2 * i + 2) * width]
+            keep[i * width : (i + 1) * width, lanes] = jnp.where(mine, low, high)
+            send[i * width : (i + 1) * width, lanes] = jnp.where(mine, high, low).astype(BF)
 
 
 def gather_matrix(z, me):
@@ -137,9 +209,13 @@
         out[r] = total
 
 
-def act_kernel(z, part_ref, up_ref, down_ref, w_ref, out):
+def norm_kernel(
+    z, part_ref, up_ref, down_ref, w_ref, x_ref, t_ref, gain_ref, hidden_ref, normed_ref
+):
     frame = lax.broadcasted_iota(jnp.int32, (z.block, z.c), 0) % z.f
-    for r in range(z.r):
+    held = {}
+
+    def activate(r):
         total = part_ref[r]
         for edge, di, ref in ((0, 0, up_ref), (z.r - 1, 2, down_ref)):
             if r == edge:
@@ -149,23 +225,34 @@
                         w_ref[di, dj],
                         preferred_element_type=F32,
                     )
-        act = (total / (1.0 + jnp.exp(-total))).astype(BF)
-        out[r, :, 0 : z.c] = act
+        act = silu(total)
         wide = act.astype(F32)
-        for k in (1, 2):
-            late = jnp.where(frame >= k, pltpu.roll(wide, k, 0), 0.0)
-            out[r, :, k * z.c : (k + 1) * z.c] = late.astype(BF)
-
-
-def norm_kernel(z, x_ref, act_ref, t_ref, gain_ref, hidden_ref, normed_ref):
-    gain = gain_ref[...]
-    for r in range(z.r):
-        temporal = jnp.dot(act_ref[r], t_ref[...], preferred_element_type=F32)
+        held["a", r] = [act] + [
+            jnp.where(frame >= k, pltpu.roll(wide, k, 0), 0.0).astype(BF) for k in (1, 2)
+        ]
+
+    def hide(r):
+        temporal = sum(
+            jnp.dot(late, t_ref[k], preferred_element_type=F32)
+            for k, late in enumerate(held.pop(("a", r)))
+        )
         hidden = (x_ref[r, z.f : z.f + z.block].astype(F32) + temporal).astype(BF)
-        wide = hidden.astype(F32)
+        hidden_ref[r] = hidden
+        held["h", r] = hidden
+
+    def norm(r):
+        wide = held.pop(("h", r)).astype(F32)
         mean = jnp.mean(wide * wide, axis=1, keepdims=True)
-        hidden_ref[r] = hidden
-        normed_ref[r] = (wide * (1.0 / jnp.sqrt(mean + 1e-06)) * gain).astype(BF)
+        normed_ref[r] = (wide * (1.0 / jnp.sqrt(mean + 1e-06)) * gain_ref[...]).astype(BF)
+
+    staged(z, (activate, hide, norm))
+
+
+def staged(z, stages):
+    for step in range(z.r + len(stages) - 1):
+        for late, stage in reversed(list(enumerate(stages))):
+            if 0 <= step - late < z.r:
+                stage(step - late)
 
 
 def attend_kernel(z, hidden_ref, normed_ref, q_ref, k_ref, v_ref, o_ref, *outs):
@@ -219,34 +306,7 @@
         for k in range(z.n):
             outs[k][r] = encoded[k * z.piece : (k + 1) * z.piece]
 
-    stages = (project, score, weigh, mix, finish, spread)
-    for step in range(z.r + len(stages) - 1):
-        for late, stage in reversed(list(enumerate(stages))):
-            if 0 <= step - late < z.r:
-                stage(step - late)
-
-
-def grad_kernel(z, width, *refs):
-    parts, (act_ref, keep, send, cot) = refs[: z.n], refs[z.n :]
-    matrix = gather_matrix(z, lax.axis_index("tm"))
-    mine = lax.axis_index("space") % 2 == 0
-    for r in range(z.r):
-        rows = jnp.concatenate([p[r * z.piece : (r + 1) * z.piece] for p in parts], axis=0)
-        cot[r * z.block : (r + 1) * z.block] = moved(matrix, rows)
-    flat = cot[...]
-    for k in range(3):
-        lanes = slice(k * z.c, (k + 1) * z.c)
-        grad = lax.dot_general(
-            flat,
-            act_ref[:, :, lanes].reshape(z.r * z.block, z.c),
-            (((0,), (0,)), ((), ())),
-            preferred_element_type=F32,
-        )
-        for i in range(z.c // (2 * width)):
-            low = grad[2 * i * width : (2 * i + 1) * width]
-            high = grad[(2 * i + 1) * width : (2 * i + 2) * width]
-            keep[i * width : (i + 1) * width, lanes] = jnp.where(mine, low, high)
-            send[i * width : (i + 1) * width, lanes] = jnp.where(mine, high, low).astype(BF)
+    staged(z, (project, score, weigh, mix, finish, spread))
 
 
 def split_kernel(z, keep_ref, got_ref, *outs):
@@ -274,31 +334,68 @@
     return lax.ppermute(value, axis, [(i, i ^ k) for i in range(count)])
 
 
-def load_kernel(count, after_ref, *refs):
-    sources, places, sem = refs[:count], refs[count : 2 * count], refs[2 * count]
-    copies = [
-        pltpu.make_async_copy(source, place, sem.at[i])
-        for i, (source, place) in enumerate(zip(sources, places))
-    ]
-    for copy in copies:
-        copy.start()
+def chip_kernel(z, width, *refs):
+    parts, outs, total = refs[: z.n], refs[z.n : -1], refs[-1]
+    total[...] = sum(part[...].astype(F32) for part in parts)
+    chip = lax.axis_index("space") // 2
+    for k, out in enumerate(outs):
+        rows = pl.ds(pl.multiple_of((chip ^ k) * width, width), width)
+        out[...] = total[rows].astype(out.dtype)
+
+
+def sum_kernel(z, *refs):
+    out, wide = refs[-1], z.c // z.n
+    total = sum(part[...].astype(F32) for part in refs[:-1])
+    for k in range(3):
+        out[k] = total[:, k * wide : (k + 1) * wide]
+
+
+def join_kernel(z, *refs):
+    parts, (out, whole, sem) = refs[: z.n], refs[z.n :]
+    me = lax.axis_index("tm")
+    copies = []
+    for f in range(z.fl):
+        for k in range(z.n):
+            cols = pl.ds(pl.multiple_of((me ^ k) * z.wc, z.wc), z.wc)
+            whole[f, :, cols] = parts[k][:, f * z.wc : (f + 1) * z.wc]
+        copies.append(pltpu.make_async_copy(whole.at[f], out.at[f], sem.at[f]))
+        copies[f].start()
     for copy in copies:
         copy.wait()
+
+
+def joined(z, back):
+    if z.wc % 16 == 0:
+        return pl.pallas_call(
+            functools.partial(join_kernel, z),
+            out_shape=shape((z.fl, z.r, z.w, z.c)),
+            in_specs=[VMEM] * z.n,
+            out_specs=pl.BlockSpec(memory_space=pl.ANY),
+            scratch_shapes=[
+                pltpu.VMEM((z.fl, z.r, z.w, z.c), BF),
+                pltpu.SemaphoreType.DMA((z.fl,)),
+            ],
+            compiler_params=pltpu.CompilerParams(vmem_limit_bytes=16 * 2**20),
+            cost_estimate=pl.CostEstimate(
+                flops=0, bytes_accessed=8 * z.n * z.main * z.c, transcendentals=0
+            ),
+        )(*back)
+    whole = jnp.zeros((z.fl, z.r, z.n, z.wc, z.c), BF)
+    for k in range(z.n):
+        rows = back[k].reshape(z.r, z.fl, 1, z.wc, z.c).transpose(1, 0, 2, 3, 4)
+        whole = lax.dynamic_update_slice_in_dim(whole, rows, lax.axis_index("tm") ^ k, 2)
+    return whole.reshape(z.fl, z.r, z.w, z.c)
 
 
 def on_device(frames_in, spatial, temporal, gain, q_w, k_w, v_w, o_w, cotangent):
     n = lax.axis_size("tm")
     space = lax.axis_size("space")
     z = Sizes(n, *frames_in.shape)
-    me = lax.axis_index("tm")
-    here = lax.axis_index("space")
     one = 2 * z.r * z.block * z.c * z.c
     others = sorted(range(1, n), key=lambda k: -k.bit_count())
-
-    def pack(value, halo):
-        rows = z.main + (z.sides if halo else 0)
-        kernel = functools.partial(pack_kernel, z, halo)
-        return call(kernel, [shape((rows, z.c))] * n, value, flops=one)
+    width, wide, chips = z.c // space, z.c // n, space // 2
+    up_by_one = [(i, i + 1) for i in range(space - 1)]
+    down_by_one = [(i + 1, i) for i in range(space - 1)]
 
     def exchange(pieces):
         pieces = list(pieces)
@@ -306,31 +403,53 @@
             pieces[k] = swap(pieces[k], "tm", k)
         return pieces
 
-    packed = pack(frames_in, True)
+    edge = shape((z.fl * z.w, z.c))
+    packed = call(
+        functools.partial(pack_kernel, z),
+        [shape((z.main + z.sides, z.c))] * n,
+        frames_in,
+        flops=one // 2,
+    )
+    top, bottom = call(
+        functools.partial(edge_kernel, z), [edge, edge], frames_in, packed[0]
+    )
     got = exchange(packed)
-    weights = (spatial, temporal.reshape(3 * z.c, z.c), q_w, k_w, v_w, o_w)
-    spatial, temporal, q_w, k_w, v_w, o_w = pl.pallas_call(
-        functools.partial(load_kernel, len(weights)),
-        out_shape=tuple(shape(w.shape) for w in weights),
-        in_specs=[pl.BlockSpec(memory_space=pl.ANY)] + [pl.BlockSpec(memory_space=pltpu.HBM)] * len(weights),
-        out_specs=tuple(VMEM for _ in weights),
-        scratch_shapes=[pltpu.SemaphoreType.DMA((len(weights),))],
-        compiler_params=pltpu.CompilerParams(vmem_limit_bytes=16 * 2**20),
-        cost_estimate=pl.CostEstimate(flops=0, bytes_accessed=16 * 2**20, transcendentals=0),
-    )(packed[0], *weights)
-    cot = pack(cotangent, False)
-    tied = lax.optimization_barrier((*cot, *(got[k] for k in others[1:])))
-    cot = exchange(tied[:n])
-    for k, piece in zip(others[1:], tied[n:]):
-        got[k] = piece
+    up = lax.ppermute(bottom, "space", up_by_one)
+    down = lax.ppermute(top, "space", down_by_one)
+    (own,) = call(
+        functools.partial(own_inner_kernel, z),
+        [shape((z.r, z.fl * z.w, z.c), F32)],
+        frames_in,
+        spatial,
+        flops=8 * one,
+        scratch=[pltpu.VMEM((3, z.r, z.fl * z.w, z.c), BF)],
+    )
+    own_act, last = call(
+        functools.partial(own_act_kernel, z),
+        [shape(frames_in.shape), shape((z.r, z.w, z.c))],
+        own,
+        up,
+        down,
+        spatial,
+        flops=3 * one,
+    )
+    before = lax.ppermute(last, "tm", [(i, i + 1) for i in range(n - 1)])
+    after = lax.ppermute(cotangent[0], "tm", [(i + 1, i) for i in range(n - 1)])
+    (own_grad,) = call(
+        functools.partial(own_grad_kernel, z),
+        [shape((z.c, 3 * z.c), F32)],
+        own_act,
+        cotangent,
+        flops=9 * one // 4,
+    )
     line = z.block + 2 * z.f
     x, top, bottom = call(
         functools.partial(assemble_kernel, z),
         [shape((z.r, line, z.c)), shape((line, z.c)), shape((line, z.c))],
         *got,
     )
-    up = lax.ppermute(bottom, "space", [(i, i + 1) for i in range(space - 1)])
-    down = lax.ppermute(top, "space", [(i + 1, i) for i in range(space - 1)])
+    up = lax.ppermute(bottom, "space", up_by_one)
+    down = lax.ppermute(top, "space", down_by_one)
     (inner,) = call(
         functools.partial(inner_kernel, z),
         [shape((z.r, z.block, z.c), F32)],
@@ -338,35 +457,32 @@
         spatial,
         flops=9 * one * (3 * z.r - 2) // (3 * z.r),
     )
-    (acts,) = call(
-        functools.partial(act_kernel, z),
-        [shape((z.r, z.block, 3 * z.c))],
+    tied = lax.optimization_barrier((before, after, inner, up, down))
+    before, after, inner, up, down = tied
+    keep, send = call(
+        functools.partial(cross_kernel, z, width),
+        [shape((z.c // 2, 3 * z.c), F32), shape((z.c // 2, 3 * z.c))],
+        own_grad,
+        before,
+        own_act,
+        cotangent,
+        after,
+        flops=3 * one // 4,
+    )
+    inner, send = lax.optimization_barrier((inner, send))
+    other = swap(send, "space", 1)
+    hidden, normed = call(
+        functools.partial(norm_kernel, z),
+        [shape((z.r, z.block, z.c))] * 2,
         inner,
         up,
         down,
         spatial,
-        flops=6 * one // z.r,
-    )
-    width = z.c // space
-    keep, send = call(
-        functools.partial(grad_kernel, z, width),
-        [shape((z.c // 2, 3 * z.c), F32), shape((z.c // 2, 3 * z.c))],
-        *cot,
-        acts,
-        flops=3 * one,
-        scratch=[pltpu.VMEM((z.r * z.block, z.c), BF)],
-    )
-    other = swap(send, "space", 1)
-    hidden, normed = call(
-        functools.partial(norm_kernel, z),
-        [shape((z.r, z.block, z.c))] * 2,
         x,
-        acts,
         temporal,
         gain.reshape(1, z.c),
-        flops=3 * one,
-    )
-    wide = z.c // n
+        flops=5 * one,
+    )
     pieces = call(
         functools.partial(split_kernel, z),
         [shape((z.c // 2, 3 * wide), F32)] + [shape((z.c // 2, 3 * wide))] * (n - 1),
@@ -388,20 +504,17 @@
     )
     back = exchange(encoded)
     pieces = lax.optimization_barrier((*pieces, *encoded))[:n]
-    total = sum(piece.astype(F32) for piece in pieces)
-    chips = space // 2
-    total = total.reshape(chips, width, 3 * wide)
-    sums = lax.dynamic_index_in_dim(total, here // 2, 0, False)
-    total = total.astype(BF)
-    for k in range(1, chips):
-        mine = lax.dynamic_index_in_dim(total, here // 2 ^ k, 0, False)
-        sums = sums + swap(mine, "space", 2 * k).astype(F32)
-    kernel_grad = sums.reshape(width, 3, wide).transpose(1, 2, 0)
-    whole = jnp.zeros((z.fl, z.r, n, z.wc, z.c), BF)
-    for k in [0] + others[::-1]:
-        rows = back[k].reshape(z.r, z.fl, 1, z.wc, z.c).transpose(1, 0, 2, 3, 4)
-        whole = lax.dynamic_update_slice_in_dim(whole, rows, me ^ k, 2)
-    return whole.reshape(frames_in.shape), kernel_grad
+    totals = call(
+        functools.partial(chip_kernel, z, width),
+        [shape((width, 3 * wide), F32)] + [shape((width, 3 * wide))] * (chips - 1),
+        *pieces,
+        scratch=[pltpu.VMEM((z.c // 2, 3 * wide), F32)],
+    )
+    totals = [totals[0]] + [swap(totals[k], "space", 2 * k) for k in range(1, chips)]
+    (kernel_grad,) = call(
+        functools.partial(sum_kernel, z), [shape((3, width, wide), F32)], *totals
+    )
+    return joined(z, back), kernel_grad.transpose(0, 2, 1)
 
 
 def solution(mesh):

time: 77.9 us -> 72.9 us (0.936)
  starting transfers between devices: 26.1 us -> 36.9 us
  local copies, waits for them, and re-layouts: 14.2 us -> 3.61 us
  waiting for transfers between devices: 17.8 us -> 7.65 us
  Pallas kernels: 18.2 us -> 23.3 us
    ppermute x2 -> x6, starting transfers between devices: 2.6 us -> 14.7 us  [the longest x2 6.04 us: on_device(): up = lax.ppermute(bottom, 'space', up_by_one)]
    unnamed x49 -> x20, local copies, waits for them, and re-layouts: 13.9 us -> 3.6 us
    ppermute x16 -> x13, waiting for transfers between devices: 17.8 us -> 7.63 us  [swap(): return lax.ppermute(value, axis, [(i, i ^ k) for i in range(count)])]
    pallas_call x9 -> x13, Pallas kernels: 17.5 us -> 22.2 us  [call(): pl.pallas_call(kernel, out_shape=tuple(outs), in_specs=[VMEM] * len(args)...]
    ppermute x16 -> x13, starting transfers between devices: 23.5 us -> 22.3 us  [swap(): return lax.ppermute(value, axis, [(i, i ^ k) for i in range(count)])]
  transfers between devices with their start and end apart: 18 -> 19, of which waited for: 7 -> 4; matrix products, arithmetic and copies ran while one was open for 1% -> 0% of each run, Pallas kernels for 16% -> 28%
where the time goes in v5:
time: 72.9 us; the launch traced here: 72.6 us
  starting transfers between devices  36.9 us (51%)
  Pallas kernels  23.3 us (32%)
  waiting for transfers between devices  7.65 us (10%)
  local copies, waits for them, and re-layouts  3.61 us (5%)
  between operations  1.1 us (2%)
    ppermute x13, starting transfers between devices, swap(): return lax.ppermute(value, axis, [(i, i ^ k) for i in range(count)])  22.3 us
    pallas_call x13, Pallas kernels, call(): pl.pallas_call(kernel, out_shape=tuple(outs), in_specs=[VMEM] * len(args)...  22.2 us
    ppermute x13, waiting for transfers between devices, swap(): return lax.ppermute(value, axis, [(i, i ^ k) for i in range(count)])  7.63 us
    ppermute x2, starting transfers between devices, on_device(): up = lax.ppermute(bottom, 'space', up_by_one)  6.04 us
    ppermute x1, starting transfers between devices, on_device(): before = lax.ppermute(last, 'tm', [(i, i + 1) for i in range(n - 1)])  4.57 us
    unnamed x20, local copies, waits for them, and re-layouts  3.6 us
    ppermute x2, starting transfers between devices, on_device(): down = lax.ppermute(top, 'space', down_by_one)  2.76 us
  transfers between devices with their start and end apart: 19, of which 4 were waited for; matrix products, arithmetic and copies ran while one was open for 0% of the time, Pallas kernels for 28%

profile of v5, /device:TPU:0, one launch (start us, length us, event | category | flops | bytes accessed | tf_op | source)
XLA Modules:
  0.0 72.6 jit_solution(9122381760740188455)
XLA Ops:
  0.6 1.2 %copy-done.3 = bf16[4,4,64,512]{3,2,1,0:T(8,128)(2,1)S(1)} copy-done((bf16[4,4,64,512]{3,2,1,0:T(8,128)(2,1)S(1)}, bf16[4,4,64,512]{3,2,1,0:T(8,128)(2,1)}, u32[]{:S(2)}) %copy-start.3) | copy-done | bytes 1048600
  1.9 0.6 shard_map.105
  2.4 3.0 %collective-permute-start.4 = (bf16[288,512]{1,0:T(8,128)(2,1)S(1)}, bf16[288,512]{1,0:T(8,128)(2,1)S(1)}, u32[]{:S(2)}, u32[]{:S(2)}) collective-permute-start(bf16[288,512]{1,0:T(8,128)(2,1)S(1)} %get-tuple-element.49), channel_id=1, source_target_pairs={{0,8},{8,0},{16,24},{24,16},{1,9},{9,1},{17,25},{25,17},{2,10},{10... | collective-permute-start | bytes 884744 | tf_op jit(solution)/shard_map/ppermute | solution.py:334
  5.4 1.5 %collective-permute-start.5 = (bf16[288,512]{1,0:T(8,128)(2,1)S(1)}, bf16[288,512]{1,0:T(8,128)(2,1)S(1)}, u32[]{:S(2)}, u32[]{:S(2)}) collective-permute-start(bf16[288,512]{1,0:T(8,128)(2,1)S(1)} %get-tuple-element.50), channel_id=1, source_target_pairs={{0,16},{8,24},{16,0},{24,8},{1,17},{9,25},{17,1},{25,9},{2,18},{10... | collective-permute-start | bytes 884744 | tf_op jit(solution)/shard_map/ppermute | solution.py:334
  7.0 0.0 collective-permute-start.6
  7.0 1.3 %collective-permute-start = (bf16[256,512]{1,0:T(8,128)(2,1)S(1)}, bf16[256,512]{1,0:T(8,128)(2,1)S(1)}, u32[]{:S(2)}, u32[]{:S(2)}) collective-permute-start(bf16[256,512]{1,0:T(8,128)(2,1)S(1)} %get-tuple-element.46), channel_id=1, source_target_pairs={{0,1},{1,2},{2,3},{3,4},{4,5},{5,6},{6,7},{8,9},{9,10},{10,11},{11... | collective-permute-start | bytes 786440 | tf_op jit(solution)/shard_map/ppermute | solution.py:417
  8.3 1.3 %collective-permute-start.1 = (bf16[256,512]{1,0:T(8,128)(2,1)S(1)}, bf16[256,512]{1,0:T(8,128)(2,1)S(1)}, u32[]{:S(2)}, u32[]{:S(2)}) collective-permute-start(bf16[256,512]{1,0:T(8,128)(2,1)S(1)} %get-tuple-element.47), channel_id=1, source_target_pairs={{1,0},{2,1},{3,2},{4,3},{5,4},{6,5},{7,6},{9,8},{10,9},{11,10},{12... | collective-permute-start | bytes 786440 | tf_op jit(solution)/shard_map/ppermute | solution.py:418
  9.6 0.0 copy-start
  9.6 2.3 %copy-done = bf16[3,3,512,512]{3,2,1,0:T(8,128)(2,1)S(1)} copy-done((bf16[3,3,512,512]{3,2,1,0:T(8,128)(2,1)S(1)}, bf16[3,3,512,512]{3,2,1,0:T(8,128)(2,1)}, u32[]{:S(2)}) %copy-start) | copy-done | bytes 4718616
  12.0 4.8 %shard_map.104.part_ref = f32[4,256,512]{2,1,0:T(8,128)S(1)} custom-call(bf16[4,4,64,512]{3,2,1,0:T(8,128)(2,1)S(1)} %copy-done.3, bf16[3,3,512,512]{3,2,1,0:T(8,128)(2,1)S(1)} %copy-done), custom_call_target="tpu_custom_call" | custom-call | flops 4294967296 | bytes 7864320 | tf_op jit(solution)/shard_map/pallas_call | solution.py:18
  16.8 0.0 collective-permute-done.up_ref
  16.8 1.3 %collective-permute-start.3 = (bf16[4,64,512]{2,1,0:T(8,128)(2,1)S(1)}, bf16[4,64,512]{2,1,0:T(8,128)(2,1)S(1)}, u32[]{:S(2)}, u32[]{:S(2)}) collective-permute-start(bf16[4,64,512]{2,1,0:T(8,128)(2,1)S(1)} %slice_bitcast_fusion), channel_id=1, source_target_pairs={{8,0},{16,8},{24,16},{9,1},{17,9},{25,17},{10,2},{18,10},{26,18},{... | collective-permute-start | bytes 786440 | tf_op jit(solution)/shard_map/ppermute | solution.py:437
  18.1 1.8 %shard_map.107 = (bf16[4,4,64,512]{3,2,1,0:T(8,128)(2,1)S(1)}, bf16[4,64,512]{2,1,0:T(8,128)(2,1)S(1)}) custom-call(f32[4,256,512]{2,1,0:T(8,128)S(1)} %shard_map.104.part_ref, bf16[256,512]{1,0:T(8,128)(2,1)S(1)} %collective-permute-done.up_ref, bf16[256,512]{1,0:T(8,128)(2,1)S(1)} %collective-permute-done.1.down_ref, bf16[3,3,512,512]{3,2,1,0:T(8,128)(2,1)S(1)} %copy-done.1), custom_call_target="tpu_custom_call" | custom-call | flops 1610612736 | bytes 8650752 | tf_op jit(solution)/shard_map/pallas_call | solution.py:18
  19.9 4.6 %collective-permute-start.2 = (bf16[4,64,512]{2,1,0:T(8,128)(2,1)S(1)}, bf16[4,64,512]{2,1,0:T(8,128)(2,1)S(1)}, u32[]{:S(2)}, u32[]{:S(2)}) collective-permute-start(bf16[4,64,512]{2,1,0:T(8,128)(2,1)S(1)} %get-tuple-element.48), channel_id=1, source_target_pairs={{0,8},{8,16},{16,24},{1,9},{9,17},{17,25},{2,10},{10,18},{18,26},{... | collective-permute-start | bytes 786440 | tf_op jit(solution)/shard_map/ppermute | solution.py:436
  24.5 1.4 %shard_map.110.part_ref = f32[512,1536]{1,0:T(8,128)S(1)} custom-call(bf16[4,4,64,512]{3,2,1,0:T(8,128)(2,1)S(1)} %get-tuple-element.56.act_ref, bf16[4,4,64,512]{3,2,1,0:T(8,128)(2,1)S(1)} %copy-done.2), custom_call_target="tpu_custom_call" | custom-call | flops 1207959552 | bytes 5242880 | tf_op jit(solution)/shard_map/pallas_call | solution.py:18
  26.0 0.0 collective-permute-done.6.refs_3_
  26.0 0.5 shard_map.108
  26.5 4.7 %collective-permute-start.7 = (bf16[288,512]{1,0:T(8,128)(2,1)S(1)}, bf16[288,512]{1,0:T(8,128)(2,1)S(1)}, u32[]{:S(2)}, u32[]{:S(2)}) collective-permute-start(bf16[288,512]{1,0:T(8,128)(2,1)S(1)} %get-tuple-element.53), channel_id=1, source_target_pairs={{0,1},{1,2},{2,3},{3,4},{4,5},{5,6},{6,7},{8,9},{9,10},{10,11},{11... | collective-permute-start | bytes 884744 | tf_op jit(solution)/shard_map/ppermute | solution.py:451
  31.2 1.5 %collective-permute-start.8 = (bf16[288,512]{1,0:T(8,128)(2,1)S(1)}, bf16[288,512]{1,0:T(8,128)(2,1)S(1)}, u32[]{:S(2)}, u32[]{:S(2)}) collective-permute-start(bf16[288,512]{1,0:T(8,128)(2,1)S(1)} %get-tuple-element.54), channel_id=1, source_target_pairs={{1,0},{2,1},{3,2},{4,3},{5,4},{6,5},{7,6},{9,8},{10,9},{11,10},{12... | collective-permute-start | bytes 884744 | tf_op jit(solution)/shard_map/ppermute | solution.py:452
  32.7 4.2 %shard_map.109.part_ref = f32[4,256,512]{2,1,0:T(8,128)S(1)} custom-call(bf16[4,288,512]{2,1,0:T(8,128)(2,1)S(1)} %get-tuple-element.52.x_ref, bf16[3,3,512,512]{3,2,1,0:T(8,128)(2,1)S(1)} %copy-done.1), custom_call_target="tpu_custom_call" | custom-call | flops 4026531840 | bytes 7995392 | tf_op jit(solution)/shard_map/pallas_call | solution.py:18
  36.9 0.0 copy-start.4
  36.9 0.0 copy-start.5
  36.9 0.0 collective-permute-done.2.before_ref
  37.0 0.7 shard_map.111
  37.6 4.6 %collective-permute-start.9 = (bf16[256,1536]{1,0:T(8,128)(2,1)S(1)}, bf16[256,1536]{1,0:T(8,128)(2,1)S(1)}, u32[]{:S(2)}, u32[]{:S(2)}) collective-permute-start(bf16[256,1536]{1,0:T(8,128)(2,1)S(1)} %get-tuple-element.66), channel_id=1, source_target_pairs={{0,1},{1,0},{2,3},{3,2},{4,5},{5,4},{6,7},{7,6},{8,9},{9,8},{10,11... | collective-permute-start | bytes 2359304 | tf_op jit(solution)/shard_map/ppermute | solution.py:334
  42.3 3.5 %shard_map.112 = (bf16[4,256,512]{2,1,0:T(8,128)(2,1)S(1)}, bf16[4,256,512]{2,1,0:T(8,128)(2,1)S(1)}) custom-call(f32[4,256,512]{2,1,0:T(8,128)S(1)} %shard_map.109.part_ref, bf16[288,512]{1,0:T(8,128)(2,1)S(1)} %collective-permute-done.7.up_ref, bf16[288,512]{1,0:T(8,128)(2,1)S(1)} %collective-permute-done.8.down_ref, ...), custom_call_target="tpu_custom_call" | custom-call | flops 2684354560 | bytes 12257280 | tf_op jit(solution)/shard_map/pallas_call | solution.py:18
  45.8 0.0 copy-start.6
  45.8 0.0 copy-start.7
  45.9 0.0 copy-start.8
  45.9 0.0 copy-start.9
  45.9 0.3 shard_map.113
  46.2 2.4 %collective-permute-start.13 = (bf16[256,384]{1,0:T(8,128)(2,1)S(1)}, bf16[256,384]{1,0:T(8,128)(2,1)S(1)}, u32[]{:S(2)}, u32[]{:S(2)}) collective-permute-start(bf16[256,384]{1,0:T(8,128)(2,1)S(1)} %get-tuple-element.77), channel_id=1, source_target_pairs={{0,8},{8,0},{16,24},{24,16},{1,9},{9,1},{17,25},{25,17},{2,10},{10... | collective-permute-start | bytes 589832 | tf_op jit(solution)/shard_map/ppermute | solution.py:334
  48.7 1.5 %collective-permute-start.15 = (bf16[256,384]{1,0:T(8,128)(2,1)S(1)}, bf16[256,384]{1,0:T(8,128)(2,1)S(1)}, u32[]{:S(2)}, u32[]{:S(2)}) collective-permute-start(bf16[256,384]{1,0:T(8,128)(2,1)S(1)} %get-tuple-element.79), channel_id=1, source_target_pairs={{0,24},{8,16},{16,8},{24,0},{1,25},{9,17},{17,9},{25,1},{2,26},{10... | collective-permute-start | bytes 589832 | tf_op jit(solution)/shard_map/ppermute | solution.py:334
  50.2 3.6 %shard_map.114 = (bf16[4,64,512]{2,1,0:T(8,128)(2,1)S(1)}, bf16[4,64,512]{2,1,0:T(8,128)(2,1)S(1)}, bf16[4,64,512]{2,1,0:T(8,128)(2,1)S(1)}, bf16[4,64,512]{2,1,0:T(8,128)(2,1)S(1)}) custom-call(bf16[4,256,512]{2,1,0:T(8,128)(2,1)S(1)} %get-tuple-element.63.hidden_ref, bf16[4,256,512]{2,1,0:T(8,128)(2,1)S(1)} %get-tuple-element.71.normed_ref, ...), custom_call_target="tpu_custom_call" | custom-call | flops 2684354560 | bytes 5242880 | tf_op jit(solution)/shard_map/pallas_call | solution.py:18
  53.8 2.0 %collective-permute-start.10 = (bf16[4,64,512]{2,1,0:T(8,128)(2,1)S(1)}, bf16[4,64,512]{2,1,0:T(8,128)(2,1)S(1)}, u32[]{:S(2)}, u32[]{:S(2)}) collective-permute-start(bf16[4,64,512]{2,1,0:T(8,128)(2,1)S(1)} %get-tuple-element.73), channel_id=1, source_target_pairs={{0,8},{8,0},{16,24},{24,16},{1,9},{9,1},{17,25},{25,17},{2,10},{10... | collective-permute-start | bytes 786440 | tf_op jit(solution)/shard_map/ppermute | solution.py:334
  55.8 0.0 collective-permute-done.13.refs_1_
  55.8 1.5 %collective-permute-start.12 = (bf16[4,64,512]{2,1,0:T(8,128)(2,1)S(1)}, bf16[4,64,512]{2,1,0:T(8,128)(2,1)S(1)}, u32[]{:S(2)}, u32[]{:S(2)}) collective-permute-start(bf16[4,64,512]{2,1,0:T(8,128)(2,1)S(1)} %get-tuple-element.75), channel_id=1, source_target_pairs={{0,24},{8,16},{16,8},{24,0},{1,25},{9,17},{17,9},{25,1},{2,26},{10... | collective-permute-start | bytes 786440 | tf_op jit(solution)/shard_map/ppermute | solution.py:334
  57.4 3.0 %collective-permute-done.14.refs_2_ = bf16[256,384]{1,0:T(8,128)(2,1)S(1)} collective-permute-done((bf16[256,384]{1,0:T(8,128)(2,1)S(1)}, bf16[256,384]{1,0:T(8,128)(2,1)S(1)}, u32[]{:S(2)}, u32[]{:S(2)}) %collective-permute-start.14) | collective-permute-done | bytes 196640 | tf_op jit(solution)/shard_map/ppermute | solution.py:334
  60.4 0.1 shard_map.116
  60.6 1.6 %collective-permute-start.16 = (bf16[64,384]{1,0:T(8,128)(2,1)S(1)}, bf16[64,384]{1,0:T(8,128)(2,1)S(1)}, u32[]{:S(2)}, u32[]{:S(2)}) collective-permute-start(bf16[64,384]{1,0:T(8,128)(2,1)S(1)} %get-tuple-element.85), channel_id=1, source_target_pairs={{0,2},{1,3},{2,0},{3,1},{4,6},{5,7},{6,4},{7,5},{8,10},{9,11},{10,... | collective-permute-start | bytes 147464 | tf_op jit(solution)/shard_map/ppermute | solution.py:334
  62.2 1.5 %collective-permute-start.17 = (bf16[64,384]{1,0:T(8,128)(2,1)S(1)}, bf16[64,384]{1,0:T(8,128)(2,1)S(1)}, u32[]{:S(2)}, u32[]{:S(2)}) collective-permute-start(bf16[64,384]{1,0:T(8,128)(2,1)S(1)} %get-tuple-element.86), channel_id=1, source_target_pairs={{0,4},{1,5},{2,6},{3,7},{4,0},{5,1},{6,2},{7,3},{8,12},{9,13},{10,... | collective-permute-start | bytes 147464 | tf_op jit(solution)/shard_map/ppermute | solution.py:334
  63.7 1.1 %collective-permute-done.16.refs_1_ = bf16[64,384]{1,0:T(8,128)(2,1)S(1)} collective-permute-done((bf16[64,384]{1,0:T(8,128)(2,1)S(1)}, bf16[64,384]{1,0:T(8,128)(2,1)S(1)}, u32[]{:S(2)}, u32[]{:S(2)}) %collective-permute-start.16) | collective-permute-done | bytes 49184 | tf_op jit(solution)/shard_map/ppermute | solution.py:334
  64.7 2.5 %collective-permute-start.18 = (bf16[64,384]{1,0:T(8,128)(2,1)S(1)}, bf16[64,384]{1,0:T(8,128)(2,1)S(1)}, u32[]{:S(2)}, u32[]{:S(2)}) collective-permute-start(bf16[64,384]{1,0:T(8,128)(2,1)S(1)} %get-tuple-element.87), channel_id=1, source_target_pairs={{0,6},{1,7},{2,4},{3,5},{4,2},{5,3},{6,0},{7,1},{8,14},{9,15},{10,... | collective-permute-start | bytes 147464 | tf_op jit(solution)/shard_map/ppermute | solution.py:334
  67.2 0.5 collective-permute-done.17.refs_2_
  67.7 3.0 %collective-permute-done.18.refs_3_ = bf16[64,384]{1,0:T(8,128)(2,1)S(1)} collective-permute-done((bf16[64,384]{1,0:T(8,128)(2,1)S(1)}, bf16[64,384]{1,0:T(8,128)(2,1)S(1)}, u32[]{:S(2)}, u32[]{:S(2)}) %collective-permute-start.18) | collective-permute-done | bytes 49184 | tf_op jit(solution)/shard_map/ppermute | solution.py:334
  70.7 0.7 shard_map.117
  71.4 0.0 collective-permute-done.11.refs_2_
  71.4 1.0 %shard_map.115 = bf16[4,4,64,512]{3,2,1,0:T(8,128)(2,1)} custom-call(bf16[4,64,512]{2,1,0:T(8,128)(2,1)S(1)} %get-tuple-element.72.refs_0_, bf16[4,64,512]{2,1,0:T(8,128)(2,1)S(1)} %collective-permute-done.10.refs_1_, bf16[4,64,512]{2,1,0:T(8,128)(2,1)S(1)} %collective-permute-done.11.refs_2_, bf16[4,64,512]{2,1,0:T(8,128)(2,1)S(1)} %collective-permute-done.12.refs_3_), custom_call_target="tpu_custom_call" | custom-call | bytes 4194304 | tf_op jit(solution)/shard_map/pallas_call | solution.py:369
  (25 shorter events, 0.1 us)
Async XLA Ops:
  0.6 1.2 %copy-start.3 = (bf16[4,4,64,512]{3,2,1,0:T(8,128)(2,1)S(1)}, bf16[4,4,64,512]{3,2,1,0:T(8,128)(2,1)}, u32[]{:S(2)}) copy-start(bf16[4,4,64,512]{3,2,1,0:T(8,128)(2,1)} %x_ref.5) | copy-start | bytes 3145732
  2.4 23.5 %collective-permute-start.4 = (bf16[288,512]{1,0:T(8,128)(2,1)S(1)}, bf16[288,512]{1,0:T(8,128)(2,1)S(1)}, u32[]{:S(2)}, u32[]{:S(2)}) collective-permute-start(bf16[288,512]{1,0:T(8,128)(2,1)S(1)} %get-tuple-element.49), channel_id=1, source_target_pairs={{0,8},{8,0},{16,24},{24,16},{1,9},{9,1},{17,25},{25,17},{2,10},{10... | collective-permute-start | bytes 884744 | tf_op jit(solution)/shard_map/ppermute | solution.py:334
  5.4 20.5 %collective-permute-start.5 = (bf16[288,512]{1,0:T(8,128)(2,1)S(1)}, bf16[288,512]{1,0:T(8,128)(2,1)S(1)}, u32[]{:S(2)}, u32[]{:S(2)}) collective-permute-start(bf16[288,512]{1,0:T(8,128)(2,1)S(1)} %get-tuple-element.50), channel_id=1, source_target_pairs={{0,16},{8,24},{16,0},{24,8},{1,17},{9,25},{17,1},{25,9},{2,18},{10... | collective-permute-start | bytes 884744 | tf_op jit(solution)/shard_map/ppermute | solution.py:334
  7.0 19.0 %collective-permute-start.6 = (bf16[288,512]{1,0:T(8,128)(2,1)S(1)}, bf16[288,512]{1,0:T(8,128)(2,1)S(1)}, u32[]{:S(2)}, u32[]{:S(2)}) collective-permute-start(bf16[288,512]{1,0:T(8,128)(2,1)S(1)} %get-tuple-element.51), channel_id=1, source_target_pairs={{0,24},{8,16},{16,8},{24,0},{1,25},{9,17},{17,9},{25,1},{2,26},{10... | collective-permute-start | bytes 884744 | tf_op jit(solution)/shard_map/ppermute | solution.py:334
  7.0 9.8 %collective-permute-start = (bf16[256,512]{1,0:T(8,128)(2,1)S(1)}, bf16[256,512]{1,0:T(8,128)(2,1)S(1)}, u32[]{:S(2)}, u32[]{:S(2)}) collective-permute-start(bf16[256,512]{1,0:T(8,128)(2,1)S(1)} %get-tuple-element.46), channel_id=1, source_target_pairs={{0,1},{1,2},{2,3},{3,4},{4,5},{5,6},{6,7},{8,9},{9,10},{10,11},{11... | collective-permute-start | bytes 786440 | tf_op jit(solution)/shard_map/ppermute | solution.py:417
  8.3 9.8 %collective-permute-start.1 = (bf16[256,512]{1,0:T(8,128)(2,1)S(1)}, bf16[256,512]{1,0:T(8,128)(2,1)S(1)}, u32[]{:S(2)}, u32[]{:S(2)}) collective-permute-start(bf16[256,512]{1,0:T(8,128)(2,1)S(1)} %get-tuple-element.47), channel_id=1, source_target_pairs={{1,0},{2,1},{3,2},{4,3},{5,4},{6,5},{7,6},{9,8},{10,9},{11,10},{12... | collective-permute-start | bytes 786440 | tf_op jit(solution)/shard_map/ppermute | solution.py:418
  9.6 2.3 %copy-start = (bf16[3,3,512,512]{3,2,1,0:T(8,128)(2,1)S(1)}, bf16[3,3,512,512]{3,2,1,0:T(8,128)(2,1)}, u32[]{:S(2)}) copy-start(bf16[3,3,512,512]{3,2,1,0:T(8,128)(2,1)} %w_ref.7) | copy-start | bytes 14155780
  12.0 4.8 %copy-start.2 = (bf16[4,4,64,512]{3,2,1,0:T(8,128)(2,1)S(1)}, bf16[4,4,64,512]{3,2,1,0:T(8,128)(2,1)}, u32[]{:S(2)}) copy-start(bf16[4,4,64,512]{3,2,1,0:T(8,128)(2,1)} %cot_ref.3) | copy-start | bytes 3145732
  12.0 6.1 %copy-start.1 = (bf16[3,3,512,512]{3,2,1,0:T(8,128)(2,1)S(1)}, bf16[3,3,512,512]{3,2,1,0:T(8,128)(2,1)}, u32[]{:S(2)}) copy-start(bf16[3,3,512,512]{3,2,1,0:T(8,128)(2,1)} %w_ref.7) | copy-start | bytes 14155780
  16.8 20.2 %collective-permute-start.3 = (bf16[4,64,512]{2,1,0:T(8,128)(2,1)S(1)}, bf16[4,64,512]{2,1,0:T(8,128)(2,1)S(1)}, u32[]{:S(2)}, u32[]{:S(2)}) collective-permute-start(bf16[4,64,512]{2,1,0:T(8,128)(2,1)S(1)} %slice_bitcast_fusion), channel_id=1, source_target_pairs={{8,0},{16,8},{24,16},{9,1},{17,9},{25,17},{10,2},{18,10},{26,18},{... | collective-permute-start | bytes 786440 | tf_op jit(solution)/shard_map/ppermute | solution.py:437
  19.9 17.0 %collective-permute-start.2 = (bf16[4,64,512]{2,1,0:T(8,128)(2,1)S(1)}, bf16[4,64,512]{2,1,0:T(8,128)(2,1)S(1)}, u32[]{:S(2)}, u32[]{:S(2)}) collective-permute-start(bf16[4,64,512]{2,1,0:T(8,128)(2,1)S(1)} %get-tuple-element.48), channel_id=1, source_target_pairs={{0,8},{8,16},{16,24},{1,9},{9,17},{17,25},{2,10},{10,18},{18,26},{... | collective-permute-start | bytes 786440 | tf_op jit(solution)/shard_map/ppermute | solution.py:436
  26.5 10.5 %collective-permute-start.7 = (bf16[288,512]{1,0:T(8,128)(2,1)S(1)}, bf16[288,512]{1,0:T(8,128)(2,1)S(1)}, u32[]{:S(2)}, u32[]{:S(2)}) collective-permute-start(bf16[288,512]{1,0:T(8,128)(2,1)S(1)} %get-tuple-element.53), channel_id=1, source_target_pairs={{0,1},{1,2},{2,3},{3,4},{4,5},{5,6},{6,7},{8,9},{9,10},{10,11},{11... | collective-permute-start | bytes 884744 | tf_op jit(solution)/shard_map/ppermute | solution.py:451
  31.2 5.8 %collective-permute-start.8 = (bf16[288,512]{1,0:T(8,128)(2,1)S(1)}, bf16[288,512]{1,0:T(8,128)(2,1)S(1)}, u32[]{:S(2)}, u32[]{:S(2)}) collective-permute-start(bf16[288,512]{1,0:T(8,128)(2,1)S(1)} %get-tuple-element.54), channel_id=1, source_target_pairs={{1,0},{2,1},{3,2},{4,3},{5,4},{6,5},{7,6},{9,8},{10,9},{11,10},{12... | collective-permute-start | bytes 884744 | tf_op jit(solution)/shard_map/ppermute | solution.py:452
  36.9 5.4 %copy-start.4 = (bf16[3,512,512]{2,1,0:T(8,128)(2,1)S(1)}, bf16[3,512,512]{2,1,0:T(8,128)(2,1)}, u32[]{:S(2)}) copy-start(bf16[3,512,512]{2,1,0:T(8,128)(2,1)} %t_ref.1) | copy-start | bytes 4718596
  36.9 5.4 %copy-start.5 = (f32[512]{0:T(512)S(1)}, f32[512]{0:T(512)}, u32[]{:S(2)}) copy-start(f32[512]{0:T(512)} %param.12) | copy-start | bytes 6148
  37.6 8.2 %collective-permute-start.9 = (bf16[256,1536]{1,0:T(8,128)(2,1)S(1)}, bf16[256,1536]{1,0:T(8,128)(2,1)S(1)}, u32[]{:S(2)}, u32[]{:S(2)}) collective-permute-start(bf16[256,1536]{1,0:T(8,128)(2,1)S(1)} %get-tuple-element.66), channel_id=1, source_target_pairs={{0,1},{1,0},{2,3},{3,2},{4,5},{5,4},{6,7},{7,6},{8,9},{9,8},{10,11... | collective-permute-start | bytes 2359304 | tf_op jit(solution)/shard_map/ppermute | solution.py:334
  45.8 4.4 %copy-start.6 = (bf16[512,512]{1,0:T(8,128)(2,1)S(1)}, bf16[512,512]{1,0:T(8,128)(2,1)}, u32[]{:S(2)}) copy-start(bf16[512,512]{1,0:T(8,128)(2,1)} %q_ref.1) | copy-start | bytes 1572868
  45.8 4.4 %copy-start.7 = (bf16[512,512]{1,0:T(8,128)(2,1)S(1)}, bf16[512,512]{1,0:T(8,128)(2,1)}, u32[]{:S(2)}) copy-start(bf16[512,512]{1,0:T(8,128)(2,1)} %k_ref.1) | copy-start | bytes 1572868
  45.9 4.3 %copy-start.8 = (bf16[512,512]{1,0:T(8,128)(2,1)S(1)}, bf16[512,512]{1,0:T(8,128)(2,1)}, u32[]{:S(2)}) copy-start(bf16[512,512]{1,0:T(8,128)(2,1)} %v_ref.1) | copy-start | bytes 1572868
  45.9 4.3 %copy-start.9 = (bf16[512,512]{1,0:T(8,128)(2,1)S(1)}, bf16[512,512]{1,0:T(8,128)(2,1)}, u32[]{:S(2)}) copy-start(bf16[512,512]{1,0:T(8,128)(2,1)} %o_ref.1) | copy-start | bytes 1572868
  46.2 9.6 %collective-permute-start.13 = (bf16[256,384]{1,0:T(8,128)(2,1)S(1)}, bf16[256,384]{1,0:T(8,128)(2,1)S(1)}, u32[]{:S(2)}, u32[]{:S(2)}) collective-permute-start(bf16[256,384]{1,0:T(8,128)(2,1)S(1)} %get-tuple-element.77), channel_id=1, source_target_pairs={{0,8},{8,0},{16,24},{24,16},{1,9},{9,1},{17,25},{25,17},{2,10},{10... | collective-permute-start | bytes 589832 | tf_op jit(solution)/shard_map/ppermute | solution.py:334
  48.7 11.7 %collective-permute-start.14 = (bf16[256,384]{1,0:T(8,128)(2,1)S(1)}, bf16[256,384]{1,0:T(8,128)(2,1)S(1)}, u32[]{:S(2)}, u32[]{:S(2)}) collective-permute-start(bf16[256,384]{1,0:T(8,128)(2,1)S(1)} %get-tuple-element.78), channel_id=1, source_target_pairs={{0,16},{8,24},{16,0},{24,8},{1,17},{9,25},{17,1},{25,9},{2,18},{10... | collective-permute-start | bytes 589832 | tf_op jit(solution)/shard_map/ppermute | solution.py:334
  48.7 11.7 %collective-permute-start.15 = (bf16[256,384]{1,0:T(8,128)(2,1)S(1)}, bf16[256,384]{1,0:T(8,128)(2,1)S(1)}, u32[]{:S(2)}, u32[]{:S(2)}) collective-permute-start(bf16[256,384]{1,0:T(8,128)(2,1)S(1)} %get-tuple-element.79), channel_id=1, source_target_pairs={{0,24},{8,16},{16,8},{24,0},{1,25},{9,17},{17,9},{25,1},{2,26},{10... | collective-permute-start | bytes 589832 | tf_op jit(solution)/shard_map/ppermute | solution.py:334
  53.8 17.6 %collective-permute-start.10 = (bf16[4,64,512]{2,1,0:T(8,128)(2,1)S(1)}, bf16[4,64,512]{2,1,0:T(8,128)(2,1)S(1)}, u32[]{:S(2)}, u32[]{:S(2)}) collective-permute-start(bf16[4,64,512]{2,1,0:T(8,128)(2,1)S(1)} %get-tuple-element.73), channel_id=1, source_target_pairs={{0,8},{8,0},{16,24},{24,16},{1,9},{9,1},{17,25},{25,17},{2,10},{10... | collective-permute-start | bytes 786440 | tf_op jit(solution)/shard_map/ppermute | solution.py:334
  55.8 15.5 %collective-permute-start.11 = (bf16[4,64,512]{2,1,0:T(8,128)(2,1)S(1)}, bf16[4,64,512]{2,1,0:T(8,128)(2,1)S(1)}, u32[]{:S(2)}, u32[]{:S(2)}) collective-permute-start(bf16[4,64,512]{2,1,0:T(8,128)(2,1)S(1)} %get-tuple-element.74), channel_id=1, source_target_pairs={{0,16},{8,24},{16,0},{24,8},{1,17},{9,25},{17,1},{25,9},{2,18},{10... | collective-permute-start | bytes 786440 | tf_op jit(solution)/shard_map/ppermute | solution.py:334
  55.8 15.5 %collective-permute-start.12 = (bf16[4,64,512]{2,1,0:T(8,128)(2,1)S(1)}, bf16[4,64,512]{2,1,0:T(8,128)(2,1)S(1)}, u32[]{:S(2)}, u32[]{:S(2)}) collective-permute-start(bf16[4,64,512]{2,1,0:T(8,128)(2,1)S(1)} %get-tuple-element.75), channel_id=1, source_target_pairs={{0,24},{8,16},{16,8},{24,0},{1,25},{9,17},{17,9},{25,1},{2,26},{10... | collective-permute-start | bytes 786440 | tf_op jit(solution)/shard_map/ppermute | solution.py:334
  60.6 4.2 %collective-permute-start.16 = (bf16[64,384]{1,0:T(8,128)(2,1)S(1)}, bf16[64,384]{1,0:T(8,128)(2,1)S(1)}, u32[]{:S(2)}, u32[]{:S(2)}) collective-permute-start(bf16[64,384]{1,0:T(8,128)(2,1)S(1)} %get-tuple-element.85), channel_id=1, source_target_pairs={{0,2},{1,3},{2,0},{3,1},{4,6},{5,7},{6,4},{7,5},{8,10},{9,11},{10,... | collective-permute-start | bytes 147464 | tf_op jit(solution)/shard_map/ppermute | solution.py:334
  62.2 5.5 %collective-permute-start.17 = (bf16[64,384]{1,0:T(8,128)(2,1)S(1)}, bf16[64,384]{1,0:T(8,128)(2,1)S(1)}, u32[]{:S(2)}, u32[]{:S(2)}) collective-permute-start(bf16[64,384]{1,0:T(8,128)(2,1)S(1)} %get-tuple-element.86), channel_id=1, source_target_pairs={{0,4},{1,5},{2,6},{3,7},{4,0},{5,1},{6,2},{7,3},{8,12},{9,13},{10,... | collective-permute-start | bytes 147464 | tf_op jit(solution)/shard_map/ppermute | solution.py:334
  64.7 6.0 %collective-permute-start.18 = (bf16[64,384]{1,0:T(8,128)(2,1)S(1)}, bf16[64,384]{1,0:T(8,128)(2,1)S(1)}, u32[]{:S(2)}, u32[]{:S(2)}) collective-permute-start(bf16[64,384]{1,0:T(8,128)(2,1)S(1)} %get-tuple-element.87), channel_id=1, source_target_pairs={{0,6},{1,7},{2,4},{3,5},{4,2},{5,3},{6,0},{7,1},{8,14},{9,15},{10,... | collective-permute-start | bytes 147464 | tf_op jit(solution)/shard_map/ppermute | solution.py:334

commit v6 on v5

--- a/solution.py
+++ b/solution.py
@@ -51,9 +51,14 @@
         self.sides = 2 * rows * frames
 
 
-def edge_kernel(z, x_ref, after_ref, top, bottom):
-    top[...] = x_ref[:, 0].reshape(z.fl * z.w, z.c)
-    bottom[...] = x_ref[:, z.r - 1].reshape(z.fl * z.w, z.c)
+def even(axis):
+    return lax.axis_index(axis) % 2 == 0
+
+
+def edge_kernel(z, x_ref, after_ref, near, far):
+    top, bottom = (flat(x_ref[:, r]) for r in (0, z.r - 1))
+    near[...] = jnp.where(even("space"), bottom, top)
+    far[...] = jnp.where(even("space"), top, bottom)
 
 
 def pack_kernel(z, x_ref, *outs):
@@ -108,16 +113,21 @@
         out[r] = total
 
 
-def own_act_kernel(z, part_ref, up_ref, down_ref, w_ref, out, last):
+def own_act_kernel(z, part_ref, near_ref, far_ref, w_ref, cot_ref, out, near, far):
+    lower = even("space")
+    first = even("tm")
     for r in range(z.r):
         total = part_ref[r]
-        for edge, di, ref in ((0, 0, up_ref), (z.r - 1, 2, down_ref)):
+        for edge, di in ((0, 0), (z.r - 1, 2)):
             if r == edge:
-                for dj, rows in enumerate(aside(z, ref[...])):
+                rows = jnp.where(lower == (di == 2), near_ref[...], far_ref[...])
+                for dj, rows in enumerate(aside(z, rows)):
                     total += jnp.dot(rows, w_ref[di, dj], preferred_element_type=F32)
         act = silu(total).reshape(z.fl, z.w, z.c)
         out[:, r] = act
-        last[r] = act[z.fl - 1]
+        last = act[z.fl - 1]
+        near[r] = jnp.where(first, last, cot_ref[0, r])
+        far[r] = jnp.where(first, cot_ref[0, r], last)
 
 
 def silu(total):
@@ -139,16 +149,18 @@
         out[:, k * z.c : (k + 1) * z.c] = outer(cot_ref[k:], act_ref[: z.fl - k])
 
 
-def cross_kernel(z, width, part_ref, before_ref, act_ref, cot_ref, after_ref, keep, send):
-    mine = lax.axis_index("space") % 2 == 0
+def cross_kernel(z, width, part_ref, near_ref, far_ref, act_ref, cot_ref, keep, send):
+    mine = even("space")
+    before = jnp.where(even("tm"), far_ref[...], near_ref[...])
+    after = jnp.where(even("tm"), near_ref[...], far_ref[...])
     for k in range(3):
         lanes = slice(k * z.c, (k + 1) * z.c)
         grad = part_ref[:, lanes]
         if k == 1:
-            grad += outer(cot_ref[0], before_ref[...])
+            grad += outer(cot_ref[0], before)
         if k == 2:
-            grad += outer(cot_ref[1], before_ref[...])
-            grad += outer(after_ref[...], act_ref[z.fl - 2])
+            grad += outer(cot_ref[1], before)
+            grad += outer(after, act_ref[z.fl - 2])
         for i in range(z.c // (2 * width)):
             low = grad[2 * i * width : (2 * i + 1) * width]
             high = grad[(2 * i + 1) * width : (2 * i + 2) * width]
@@ -165,8 +177,9 @@
 
 
 def assemble_kernel(z, *refs):
-    parts, (out, top, bottom) = refs[: z.n], refs[z.n :]
+    parts, (out, near, far) = refs[: z.n], refs[z.n :]
     me = lax.axis_index("tm")
+    lower = even("space")
     matrix = gather_matrix(z, me)
 
     def edge(q):
@@ -183,15 +196,11 @@
         rows = moved(matrix, rows)
         left = tails[r * z.f : (r + 1) * z.f]
         right = tails[(z.r + r) * z.f : (z.r + r + 1) * z.f]
-        copies = [out.at[r]]
-        if r == 0:
-            copies.append(top)
-        if r == z.r - 1:
-            copies.append(bottom)
-        for ref in copies:
-            ref[0 : z.f] = left
-            ref[z.f : last] = rows
-            ref[last : last + z.f] = right
+        out[r, 0 : z.f] = left
+        out[r, z.f : last] = rows
+        out[r, last : last + z.f] = right
+    near[...] = jnp.where(lower, out[z.r - 1], out[0])
+    far[...] = jnp.where(lower, out[0], out[z.r - 1])
 
 
 def inner_kernel(z, x_ref, w_ref, out):
@@ -210,18 +219,20 @@
 
 
 def norm_kernel(
-    z, part_ref, up_ref, down_ref, w_ref, x_ref, t_ref, gain_ref, hidden_ref, normed_ref
+    z, part_ref, near_ref, far_ref, w_ref, x_ref, t_ref, gain_ref, hidden_ref, normed_ref
 ):
+    lower = even("space")
     frame = lax.broadcasted_iota(jnp.int32, (z.block, z.c), 0) % z.f
     held = {}
 
     def activate(r):
         total = part_ref[r]
-        for edge, di, ref in ((0, 0, up_ref), (z.r - 1, 2, down_ref)):
+        for edge, di in ((0, 0), (z.r - 1, 2)):
             if r == edge:
+                rows = jnp.where(lower == (di == 2), near_ref[...], far_ref[...])
                 for dj in range(3):
                     total += jnp.dot(
-                        ref[dj * z.f : dj * z.f + z.block],
+                        rows[dj * z.f : dj * z.f + z.block],
                         w_ref[di, dj],
                         preferred_element_type=F32,
                     )
@@ -332,6 +343,12 @@
 def swap(value, axis, k):
     count = lax.axis_size(axis)
     return lax.ppermute(value, axis, [(i, i ^ k) for i in range(count)])
+
+
+def swap_both(near, far, axis):
+    pairs = [(i, i + 1) for i in range(1, lax.axis_size(axis) - 1, 2)]
+    other = lax.ppermute(far, axis, pairs + [(b, a) for a, b in pairs])
+    return swap(near, axis, 1), other
 
 
 def chip_kernel(z, width, *refs):
@@ -394,8 +411,6 @@
     one = 2 * z.r * z.block * z.c * z.c
     others = sorted(range(1, n), key=lambda k: -k.bit_count())
     width, wide, chips = z.c // space, z.c // n, space // 2
-    up_by_one = [(i, i + 1) for i in range(space - 1)]
-    down_by_one = [(i + 1, i) for i in range(space - 1)]
 
     def exchange(pieces):
         pieces = list(pieces)
@@ -410,12 +425,11 @@
         frames_in,
         flops=one // 2,
     )
-    top, bottom = call(
-        functools.partial(edge_kernel, z), [edge, edge], frames_in, packed[0]
+    near, far = call(
+        functools.partial(edge_kernel, z), [edge, edge], frames_in, packed[0], flops=8 * one
     )
     got = exchange(packed)
-    up = lax.ppermute(bottom, "space", up_by_one)
-    down = lax.ppermute(top, "space", down_by_one)
+    near, far = swap_both(near, far, "space")
     (own,) = call(
         functools.partial(own_inner_kernel, z),
         [shape((z.r, z.fl * z.w, z.c), F32)],
@@ -424,17 +438,17 @@
         flops=8 * one,
         scratch=[pltpu.VMEM((3, z.r, z.fl * z.w, z.c), BF)],
     )
-    own_act, last = call(
+    own_act, near, far = call(
         functools.partial(own_act_kernel, z),
-        [shape(frames_in.shape), shape((z.r, z.w, z.c))],
+        [shape(frames_in.shape), shape((z.r, z.w, z.c)), shape((z.r, z.w, z.c))],
         own,
-        up,
-        down,
+        near,
+        far,
         spatial,
+        cotangent,
         flops=3 * one,
     )
-    before = lax.ppermute(last, "tm", [(i, i + 1) for i in range(n - 1)])
-    after = lax.ppermute(cotangent[0], "tm", [(i + 1, i) for i in range(n - 1)])
+    near, far = swap_both(near, far, "tm")
     (own_grad,) = call(
         functools.partial(own_grad_kernel, z),
         [shape((z.c, 3 * z.c), F32)],
@@ -443,13 +457,12 @@
         flops=9 * one // 4,
     )
     line = z.block + 2 * z.f
-    x, top, bottom = call(
+    x, close, apart = call(
         functools.partial(assemble_kernel, z),
         [shape((z.r, line, z.c)), shape((line, z.c)), shape((line, z.c))],
         *got,
     )
-    up = lax.ppermute(bottom, "space", up_by_one)
-    down = lax.ppermute(top, "space", down_by_one)
+    close, apart = swap_both(close, apart, "space")
     (inner,) = call(
         functools.partial(inner_kernel, z),
         [shape((z.r, z.block, z.c), F32)],
@@ -457,16 +470,16 @@
         spatial,
         flops=9 * one * (3 * z.r - 2) // (3 * z.r),
     )
-    tied = lax.optimization_barrier((before, after, inner, up, down))
-    before, after, inner, up, down = tied
+    tied = lax.optimization_barrier((near, far, inner, close, apart))
+    near, far, inner, close, apart = tied
     keep, send = call(
         functools.partial(cross_kernel, z, width),
         [shape((z.c // 2, 3 * z.c), F32), shape((z.c // 2, 3 * z.c))],
         own_grad,
-        before,
+        near,
+        far,
         own_act,
         cotangent,
-        after,
         flops=3 * one // 4,
     )
     inner, send = lax.optimization_barrier((inner, send))
@@ -475,8 +488,8 @@
         functools.partial(norm_kernel, z),
         [shape((z.r, z.block, z.c))] * 2,
         inner,
-        up,
-        down,
+        close,
+        apart,
         spatial,
         x,
         temporal,

time: 72.9 us -> 63.6 us (0.87)
  starting transfers between devices: 36.9 us -> 29.4 us
  local copies, waits for them, and re-layouts: 3.61 us -> 1.33 us
    ppermute x6 -> x3, starting transfers between devices: 14.7 us -> 2.32 us  [swap_both(): other = lax.ppermute(far, axis, pairs + [(b, a) for a, b in pairs])]
    ppermute x13 -> x16, starting transfers between devices: 22.3 us -> 27 us  [swap(): return lax.ppermute(value, axis, [(i, i ^ k) for i in range(count)])]
    unnamed x20, local copies, waits for them, and re-layouts: 3.6 us -> 1.33 us
    ppermute x13 -> x16, waiting for transfers between devices: 7.63 us -> 8.23 us  [swap(): return lax.ppermute(value, axis, [(i, i ^ k) for i in range(count)])]
  transfers between devices with their start and end apart: 19 -> 19, of which waited for: 4 -> 5; matrix products, arithmetic and copies ran while one was open for 0% -> 0% of each run, Pallas kernels for 28% -> 33%
where the time goes in v6:
time: 63.6 us; the launch traced here: 63.4 us
  starting transfers between devices  29.4 us (46%)
  Pallas kernels  23.4 us (37%)
  waiting for transfers between devices  8.24 us (13%)
  local copies, waits for them, and re-layouts  1.33 us (2%)
  between operations  1.07 us (2%)
    ppermute x16, starting transfers between devices, swap(): return lax.ppermute(value, axis, [(i, i ^ k) for i in range(count)])  27 us
    pallas_call x13, Pallas kernels, call(): pl.pallas_call(kernel, out_shape=tuple(outs), in_specs=[VMEM] * len(args)...  22.4 us
    ppermute x16, waiting for transfers between devices, swap(): return lax.ppermute(value, axis, [(i, i ^ k) for i in range(count)])  8.23 us
    ppermute x3, starting transfers between devices, swap_both(): other = lax.ppermute(far, axis, pairs + [(b, a) for a, b in pairs])  2.32 us
    unnamed x20, local copies, waits for them, and re-layouts  1.33 us
  transfers between devices with their start and end apart: 19, of which 5 were waited for; matrix products, arithmetic and copies ran while one was open for 0% of the time, Pallas kernels for 33%

profile of v6, /device:TPU:0, one launch (start us, length us, event | category | flops | bytes accessed | tf_op | source)
XLA Modules:
  0.0 63.4 jit_solution(8166661322789658722)
XLA Ops:
  0.6 1.2 %copy-done.2 = bf16[4,4,64,512]{3,2,1,0:T(8,128)(2,1)S(1)} copy-done((bf16[4,4,64,512]{3,2,1,0:T(8,128)(2,1)S(1)}, bf16[4,4,64,512]{3,2,1,0:T(8,128)(2,1)}, u32[]{:S(2)}) %copy-start.2) | copy-done | bytes 1048600
  1.9 0.6 shard_map.105
  2.4 3.0 %collective-permute-start.4 = (bf16[288,512]{1,0:T(8,128)(2,1)S(1)}, bf16[288,512]{1,0:T(8,128)(2,1)S(1)}, u32[]{:S(2)}, u32[]{:S(2)}) collective-permute-start(bf16[288,512]{1,0:T(8,128)(2,1)S(1)} %get-tuple-element.51), channel_id=1, source_target_pairs={{0,8},{8,0},{16,24},{24,16},{1,9},{9,1},{17,25},{25,17},{2,10},{10... | collective-permute-start | bytes 884744 | tf_op jit(solution)/shard_map/ppermute | solution.py:345
  5.4 1.5 %collective-permute-start.5 = (bf16[288,512]{1,0:T(8,128)(2,1)S(1)}, bf16[288,512]{1,0:T(8,128)(2,1)S(1)}, u32[]{:S(2)}, u32[]{:S(2)}) collective-permute-start(bf16[288,512]{1,0:T(8,128)(2,1)S(1)} %get-tuple-element.52), channel_id=1, source_target_pairs={{0,16},{8,24},{16,0},{24,8},{1,17},{9,25},{17,1},{25,9},{2,18},{10... | collective-permute-start | bytes 884744 | tf_op jit(solution)/shard_map/ppermute | solution.py:345
  7.0 0.0 collective-permute-start.6
  7.0 0.1 shard_map.106
  7.0 0.1 collective-permute-start
  7.1 0.0 copy-start
  7.1 0.8 %collective-permute-start.1 = (bf16[256,512]{1,0:T(8,128)(2,1)S(1)}, bf16[256,512]{1,0:T(8,128)(2,1)S(1)}, u32[]{:S(2)}, u32[]{:S(2)}) collective-permute-start(bf16[256,512]{1,0:T(8,128)(2,1)S(1)} %get-tuple-element.48), channel_id=1, source_target_pairs={{1,2},{3,4},{5,6},{2,1},{4,3},{6,5},{9,10},{11,12},{13,14},{10,9},... | collective-permute-start | bytes 786440 | tf_op jit(solution)/shard_map/ppermute | solution.py:350
  8.0 0.1 slice-done.1
  8.0 4.9 %shard_map.104.part_ref = f32[4,256,512]{2,1,0:T(8,128)S(1)} custom-call(bf16[4,4,64,512]{3,2,1,0:T(8,128)(2,1)S(1)} %copy-done.2, bf16[3,3,512,512]{3,2,1,0:T(8,128)(2,1)S(1)} %bitcast.3), custom_call_target="tpu_custom_call" | custom-call | flops 4294967296 | bytes 7864320 | tf_op jit(solution)/shard_map/pallas_call | solution.py:18
  12.9 0.0 collective-permute-done.1.far_ref
  12.9 1.9 %shard_map.107 = (bf16[4,4,64,512]{3,2,1,0:T(8,128)(2,1)S(1)}, bf16[4,64,512]{2,1,0:T(8,128)(2,1)S(1)}, bf16[4,64,512]{2,1,0:T(8,128)(2,1)S(1)}) custom-call(f32[4,256,512]{2,1,0:T(8,128)S(1)} %shard_map.104.part_ref, bf16[256,512]{1,0:T(8,128)(2,1)S(1)} %collective-permute-done.near_ref, bf16[256,512]{1,0:T(8,128)(2,1)S(1)} %collective-permute-done.1.far_ref, ...), custom_call_target="tpu_custom_call" | custom-call | flops 1610612736 | bytes 9961472 | tf_op jit(solution)/shard_map/pallas_call | solution.py:18
  14.9 2.0 %collective-permute-start.2 = (bf16[4,64,512]{2,1,0:T(8,128)(2,1)S(1)}, bf16[4,64,512]{2,1,0:T(8,128)(2,1)S(1)}, u32[]{:S(2)}, u32[]{:S(2)}) collective-permute-start(bf16[4,64,512]{2,1,0:T(8,128)(2,1)S(1)} %get-tuple-element.49), channel_id=1, source_target_pairs={{0,8},{8,0},{16,24},{24,16},{1,9},{9,1},{17,25},{25,17},{2,10},{10... | collective-permute-start | bytes 786440 | tf_op jit(solution)/shard_map/ppermute | solution.py:345
  16.9 0.7 %collective-permute-start.3 = (bf16[4,64,512]{2,1,0:T(8,128)(2,1)S(1)}, bf16[4,64,512]{2,1,0:T(8,128)(2,1)S(1)}, u32[]{:S(2)}, u32[]{:S(2)}) collective-permute-start(bf16[4,64,512]{2,1,0:T(8,128)(2,1)S(1)} %get-tuple-element.50), channel_id=1, source_target_pairs={{8,16},{16,8},{9,17},{17,9},{10,18},{18,10},{11,19},{19,11},{12,20... | collective-permute-start | bytes 786440 | tf_op jit(solution)/shard_map/ppermute | solution.py:350
  17.5 1.4 %shard_map.110.part_ref = f32[512,1536]{1,0:T(8,128)S(1)} custom-call(bf16[4,4,64,512]{3,2,1,0:T(8,128)(2,1)S(1)} %get-tuple-element.58.act_ref, bf16[4,4,64,512]{3,2,1,0:T(8,128)(2,1)S(1)} %copy-done), custom_call_target="tpu_custom_call" | custom-call | flops 1207959552 | bytes 5242880 | tf_op jit(solution)/shard_map/pallas_call | solution.py:18
  19.0 0.0 collective-permute-done.4.refs_1_
  19.0 1.2 %collective-permute-done.5.refs_2_ = bf16[288,512]{1,0:T(8,128)(2,1)S(1)} collective-permute-done((bf16[288,512]{1,0:T(8,128)(2,1)S(1)}, bf16[288,512]{1,0:T(8,128)(2,1)S(1)}, u32[]{:S(2)}, u32[]{:S(2)}) %collective-permute-start.5) | collective-permute-done | bytes 294944 | tf_op jit(solution)/shard_map/ppermute | solution.py:345
  20.2 0.0 collective-permute-done.6.refs_3_
  20.2 0.5 shard_map.108
  20.7 1.4 %collective-permute-start.7 = (bf16[288,512]{1,0:T(8,128)(2,1)S(1)}, bf16[288,512]{1,0:T(8,128)(2,1)S(1)}, u32[]{:S(2)}, u32[]{:S(2)}) collective-permute-start(bf16[288,512]{1,0:T(8,128)(2,1)S(1)} %get-tuple-element.55), channel_id=1, source_target_pairs={{0,1},{1,0},{2,3},{3,2},{4,5},{5,4},{6,7},{7,6},{8,9},{9,8},{10,11... | collective-permute-start | bytes 884744 | tf_op jit(solution)/shard_map/ppermute | solution.py:345
  22.2 0.8 %collective-permute-start.8 = (bf16[288,512]{1,0:T(8,128)(2,1)S(1)}, bf16[288,512]{1,0:T(8,128)(2,1)S(1)}, u32[]{:S(2)}, u32[]{:S(2)}) collective-permute-start(bf16[288,512]{1,0:T(8,128)(2,1)S(1)} %get-tuple-element.56), channel_id=1, source_target_pairs={{1,2},{3,4},{5,6},{2,1},{4,3},{6,5},{9,10},{11,12},{13,14},{10,9},... | collective-permute-start | bytes 884744 | tf_op jit(solution)/shard_map/ppermute | solution.py:350
  23.0 4.2 %shard_map.109.part_ref = f32[4,256,512]{2,1,0:T(8,128)S(1)} custom-call(bf16[4,288,512]{2,1,0:T(8,128)(2,1)S(1)} %get-tuple-element.54.x_ref, bf16[3,3,512,512]{3,2,1,0:T(8,128)(2,1)S(1)} %bitcast.3), custom_call_target="tpu_custom_call" | custom-call | flops 4026531840 | bytes 7995392 | tf_op jit(solution)/shard_map/pallas_call | solution.py:18
  27.2 0.0 copy-start.1
  27.2 0.0 copy-start.3
  27.3 0.7 %shard_map.111 = (f32[256,1536]{1,0:T(8,128)S(1)}, bf16[256,1536]{1,0:T(8,128)(2,1)S(1)}) custom-call(f32[512,1536]{1,0:T(8,128)S(1)} %shard_map.110.part_ref, bf16[4,64,512]{2,1,0:T(8,128)(2,1)S(1)} %collective-permute-done.2.near_ref, bf16[4,64,512]{2,1,0:T(8,128)(2,1)S(1)} %collective-permute-done.3.far_ref, ...), custom_call_target="tpu_custom_call" | custom-call | flops 402653184 | bytes 8126464 | tf_op jit(solution)/shard_map/pallas_call | solution.py:18
  28.0 3.0 %collective-permute-start.9 = (bf16[256,1536]{1,0:T(8,128)(2,1)S(1)}, bf16[256,1536]{1,0:T(8,128)(2,1)S(1)}, u32[]{:S(2)}, u32[]{:S(2)}) collective-permute-start(bf16[256,1536]{1,0:T(8,128)(2,1)S(1)} %get-tuple-element.68), channel_id=1, source_target_pairs={{0,1},{1,0},{2,3},{3,2},{4,5},{5,4},{6,7},{7,6},{8,9},{9,8},{10,11... | collective-permute-start | bytes 2359304 | tf_op jit(solution)/shard_map/ppermute | solution.py:345
  31.0 3.6 %shard_map.112 = (bf16[4,256,512]{2,1,0:T(8,128)(2,1)S(1)}, bf16[4,256,512]{2,1,0:T(8,128)(2,1)S(1)}) custom-call(f32[4,256,512]{2,1,0:T(8,128)S(1)} %shard_map.109.part_ref, bf16[288,512]{1,0:T(8,128)(2,1)S(1)} %collective-permute-done.7.near_ref, bf16[288,512]{1,0:T(8,128)(2,1)S(1)} %collective-permute-done.8.far_ref, ...), custom_call_target="tpu_custom_call" | custom-call | flops 2684354560 | bytes 12257280 | tf_op jit(solution)/shard_map/pallas_call | solution.py:18
  34.5 0.0 copy-start.4
  34.6 0.0 copy-start.5
  34.6 0.0 copy-start.6
  34.6 0.0 copy-start.7
  34.6 0.3 shard_map.113
  34.9 4.0 %collective-permute-start.13 = (bf16[256,384]{1,0:T(8,128)(2,1)S(1)}, bf16[256,384]{1,0:T(8,128)(2,1)S(1)}, u32[]{:S(2)}, u32[]{:S(2)}) collective-permute-start(bf16[256,384]{1,0:T(8,128)(2,1)S(1)} %get-tuple-element.79), channel_id=1, source_target_pairs={{0,8},{8,0},{16,24},{24,16},{1,9},{9,1},{17,25},{25,17},{2,10},{10... | collective-permute-start | bytes 589832 | tf_op jit(solution)/shard_map/ppermute | solution.py:345
  38.9 1.5 %collective-permute-start.15 = (bf16[256,384]{1,0:T(8,128)(2,1)S(1)}, bf16[256,384]{1,0:T(8,128)(2,1)S(1)}, u32[]{:S(2)}, u32[]{:S(2)}) collective-permute-start(bf16[256,384]{1,0:T(8,128)(2,1)S(1)} %get-tuple-element.81), channel_id=1, source_target_pairs={{0,24},{8,16},{16,8},{24,0},{1,25},{9,17},{17,9},{25,1},{2,26},{10... | collective-permute-start | bytes 589832 | tf_op jit(solution)/shard_map/ppermute | solution.py:345
  40.5 3.5 %shard_map.114 = (bf16[4,64,512]{2,1,0:T(8,128)(2,1)S(1)}, bf16[4,64,512]{2,1,0:T(8,128)(2,1)S(1)}, bf16[4,64,512]{2,1,0:T(8,128)(2,1)S(1)}, bf16[4,64,512]{2,1,0:T(8,128)(2,1)S(1)}) custom-call(bf16[4,256,512]{2,1,0:T(8,128)(2,1)S(1)} %get-tuple-element.65.hidden_ref, bf16[4,256,512]{2,1,0:T(8,128)(2,1)S(1)} %get-tuple-element.73.normed_ref, ...), custom_call_target="tpu_custom_call" | custom-call | flops 2684354560 | bytes 5242880 | tf_op jit(solution)/shard_map/pallas_call | solution.py:18
  44.0 2.0 %collective-permute-start.10 = (bf16[4,64,512]{2,1,0:T(8,128)(2,1)S(1)}, bf16[4,64,512]{2,1,0:T(8,128)(2,1)S(1)}, u32[]{:S(2)}, u32[]{:S(2)}) collective-permute-start(bf16[4,64,512]{2,1,0:T(8,128)(2,1)S(1)} %get-tuple-element.75), channel_id=1, source_target_pairs={{0,8},{8,0},{16,24},{24,16},{1,9},{9,1},{17,25},{25,17},{2,10},{10... | collective-permute-start | bytes 786440 | tf_op jit(solution)/shard_map/ppermute | solution.py:345
  46.0 1.5 %collective-permute-start.12 = (bf16[4,64,512]{2,1,0:T(8,128)(2,1)S(1)}, bf16[4,64,512]{2,1,0:T(8,128)(2,1)S(1)}, u32[]{:S(2)}, u32[]{:S(2)}) collective-permute-start(bf16[4,64,512]{2,1,0:T(8,128)(2,1)S(1)} %get-tuple-element.77), channel_id=1, source_target_pairs={{0,24},{8,16},{16,8},{24,0},{1,25},{9,17},{17,9},{25,1},{2,26},{10... | collective-permute-start | bytes 786440 | tf_op jit(solution)/shard_map/ppermute | solution.py:345
  47.5 3.3 %collective-permute-done.14.refs_2_ = bf16[256,384]{1,0:T(8,128)(2,1)S(1)} collective-permute-done((bf16[256,384]{1,0:T(8,128)(2,1)S(1)}, bf16[256,384]{1,0:T(8,128)(2,1)S(1)}, u32[]{:S(2)}, u32[]{:S(2)}) %collective-permute-start.14) | collective-permute-done | bytes 196640 | tf_op jit(solution)/shard_map/ppermute | solution.py:345
  50.9 0.1 shard_map.116
  51.0 2.1 %collective-permute-start.16 = (bf16[64,384]{1,0:T(8,128)(2,1)S(1)}, bf16[64,384]{1,0:T(8,128)(2,1)S(1)}, u32[]{:S(2)}, u32[]{:S(2)}) collective-permute-start(bf16[64,384]{1,0:T(8,128)(2,1)S(1)} %get-tuple-element.87), channel_id=1, source_target_pairs={{0,2},{1,3},{2,0},{3,1},{4,6},{5,7},{6,4},{7,5},{8,10},{9,11},{10,... | collective-permute-start | bytes 147464 | tf_op jit(solution)/shard_map/ppermute | solution.py:345
  53.1 1.8 %collective-permute-start.17 = (bf16[64,384]{1,0:T(8,128)(2,1)S(1)}, bf16[64,384]{1,0:T(8,128)(2,1)S(1)}, u32[]{:S(2)}, u32[]{:S(2)}) collective-permute-start(bf16[64,384]{1,0:T(8,128)(2,1)S(1)} %get-tuple-element.88), channel_id=1, source_target_pairs={{0,4},{1,5},{2,6},{3,7},{4,0},{5,1},{6,2},{7,3},{8,12},{9,13},{10,... | collective-permute-start | bytes 147464 | tf_op jit(solution)/shard_map/ppermute | solution.py:345
  55.0 0.7 %collective-permute-done.16.refs_1_ = bf16[64,384]{1,0:T(8,128)(2,1)S(1)} collective-permute-done((bf16[64,384]{1,0:T(8,128)(2,1)S(1)}, bf16[64,384]{1,0:T(8,128)(2,1)S(1)}, u32[]{:S(2)}, u32[]{:S(2)}) %collective-permute-start.16) | collective-permute-done | bytes 49184 | tf_op jit(solution)/shard_map/ppermute | solution.py:345
  55.7 2.9 %collective-permute-start.18 = (bf16[64,384]{1,0:T(8,128)(2,1)S(1)}, bf16[64,384]{1,0:T(8,128)(2,1)S(1)}, u32[]{:S(2)}, u32[]{:S(2)}) collective-permute-start(bf16[64,384]{1,0:T(8,128)(2,1)S(1)} %get-tuple-element.89), channel_id=1, source_target_pairs={{0,6},{1,7},{2,4},{3,5},{4,2},{5,3},{6,0},{7,1},{8,14},{9,15},{10,... | collective-permute-start | bytes 147464 | tf_op jit(solution)/shard_map/ppermute | solution.py:345
  58.6 0.6 collective-permute-done.17.refs_2_
  59.2 2.4 %collective-permute-done.18.refs_3_ = bf16[64,384]{1,0:T(8,128)(2,1)S(1)} collective-permute-done((bf16[64,384]{1,0:T(8,128)(2,1)S(1)}, bf16[64,384]{1,0:T(8,128)(2,1)S(1)}, u32[]{:S(2)}, u32[]{:S(2)}) %collective-permute-start.18) | collective-permute-done | bytes 49184 | tf_op jit(solution)/shard_map/ppermute | solution.py:345
  61.5 0.7 %shard_map.117 = f32[3,64,128]{2,1,0:T(8,128)} custom-call(f32[64,384]{1,0:T(8,128)S(1)} %get-tuple-element.86.refs_0_, bf16[64,384]{1,0:T(8,128)(2,1)S(1)} %collective-permute-done.16.refs_1_, bf16[64,384]{1,0:T(8,128)(2,1)S(1)} %collective-permute-done.17.refs_2_, bf16[64,384]{1,0:T(8,128)(2,1)S(1)} %collective-permute-done.18.refs_3_), custom_call_target="tpu_custom_call" | custom-call | bytes 344064 | tf_op jit(solution)/shard_map/pallas_call | solution.py:18
  62.2 1.0 %shard_map.115 = bf16[4,4,64,512]{3,2,1,0:T(8,128)(2,1)} custom-call(bf16[4,64,512]{2,1,0:T(8,128)(2,1)S(1)} %get-tuple-element.74.refs_0_, bf16[4,64,512]{2,1,0:T(8,128)(2,1)S(1)} %collective-permute-done.10.refs_1_, bf16[4,64,512]{2,1,0:T(8,128)(2,1)S(1)} %collective-permute-done.11.refs_2_, bf16[4,64,512]{2,1,0:T(8,128)(2,1)S(1)} %collective-permute-done.12.refs_3_), custom_call_target="tpu_custom_call" | custom-call | bytes 4194304 | tf_op jit(solution)/shard_map/pallas_call | solution.py:386
  (25 shorter events, 0.1 us)
Async XLA Ops:
  0.6 1.2 %copy-start.2 = (bf16[4,4,64,512]{3,2,1,0:T(8,128)(2,1)S(1)}, bf16[4,4,64,512]{3,2,1,0:T(8,128)(2,1)}, u32[]{:S(2)}) copy-start(bf16[4,4,64,512]{3,2,1,0:T(8,128)(2,1)} %x_ref.5) | copy-start | bytes 3145732
  1.9 6.1 %slice-start = ((s8[4718592]{0:T(1024)(128)(4,1)}), s8[4194304]{0:T(1024)(128)(4,1)S(1)}, s32[]{:S(2)}) async-start(s8[4718592]{0:T(1024)(128)(4,1)} %bitcast.2), calls=%async_computation | async-start | bytes 8388608
  2.4 16.5 %collective-permute-start.4 = (bf16[288,512]{1,0:T(8,128)(2,1)S(1)}, bf16[288,512]{1,0:T(8,128)(2,1)S(1)}, u32[]{:S(2)}, u32[]{:S(2)}) collective-permute-start(bf16[288,512]{1,0:T(8,128)(2,1)S(1)} %get-tuple-element.51), channel_id=1, source_target_pairs={{0,8},{8,0},{16,24},{24,16},{1,9},{9,1},{17,25},{25,17},{2,10},{10... | collective-permute-start | bytes 884744 | tf_op jit(solution)/shard_map/ppermute | solution.py:345
  5.4 14.8 %collective-permute-start.5 = (bf16[288,512]{1,0:T(8,128)(2,1)S(1)}, bf16[288,512]{1,0:T(8,128)(2,1)S(1)}, u32[]{:S(2)}, u32[]{:S(2)}) collective-permute-start(bf16[288,512]{1,0:T(8,128)(2,1)S(1)} %get-tuple-element.52), channel_id=1, source_target_pairs={{0,16},{8,24},{16,0},{24,8},{1,17},{9,25},{17,1},{25,9},{2,18},{10... | collective-permute-start | bytes 884744 | tf_op jit(solution)/shard_map/ppermute | solution.py:345
  7.0 13.3 %collective-permute-start.6 = (bf16[288,512]{1,0:T(8,128)(2,1)S(1)}, bf16[288,512]{1,0:T(8,128)(2,1)S(1)}, u32[]{:S(2)}, u32[]{:S(2)}) collective-permute-start(bf16[288,512]{1,0:T(8,128)(2,1)S(1)} %get-tuple-element.53), channel_id=1, source_target_pairs={{0,24},{8,16},{16,8},{24,0},{1,25},{9,17},{17,9},{25,1},{2,26},{10... | collective-permute-start | bytes 884744 | tf_op jit(solution)/shard_map/ppermute | solution.py:345
  7.0 1.0 %slice-start.1 = ((s8[4718592]{0:T(1024)(128)(4,1)}), s8[524288]{0:T(1024)(128)(4,1)S(1)}, s32[]{:S(2)}) async-start(s8[4718592]{0:T(1024)(128)(4,1)} %bitcast.2), calls=%async_computation.1 | async-start | bytes 1048576
  7.0 5.9 %collective-permute-start = (bf16[256,512]{1,0:T(8,128)(2,1)S(1)}, bf16[256,512]{1,0:T(8,128)(2,1)S(1)}, u32[]{:S(2)}, u32[]{:S(2)}) collective-permute-start(bf16[256,512]{1,0:T(8,128)(2,1)S(1)} %get-tuple-element.47), channel_id=1, source_target_pairs={{0,1},{1,0},{2,3},{3,2},{4,5},{5,4},{6,7},{7,6},{8,9},{9,8},{10,11... | collective-permute-start | bytes 786440 | tf_op jit(solution)/shard_map/ppermute | solution.py:345
  7.1 5.8 %copy-start = (bf16[4,4,64,512]{3,2,1,0:T(8,128)(2,1)S(1)}, bf16[4,4,64,512]{3,2,1,0:T(8,128)(2,1)}, u32[]{:S(2)}) copy-start(bf16[4,4,64,512]{3,2,1,0:T(8,128)(2,1)} %cot_ref.5) | copy-start | bytes 3145732
  7.1 5.8 %collective-permute-start.1 = (bf16[256,512]{1,0:T(8,128)(2,1)S(1)}, bf16[256,512]{1,0:T(8,128)(2,1)S(1)}, u32[]{:S(2)}, u32[]{:S(2)}) collective-permute-start(bf16[256,512]{1,0:T(8,128)(2,1)S(1)} %get-tuple-element.48), channel_id=1, source_target_pairs={{1,2},{3,4},{5,6},{2,1},{4,3},{6,5},{9,10},{11,12},{13,14},{10,9},... | collective-permute-start | bytes 786440 | tf_op jit(solution)/shard_map/ppermute | solution.py:350
  14.9 12.4 %collective-permute-start.2 = (bf16[4,64,512]{2,1,0:T(8,128)(2,1)S(1)}, bf16[4,64,512]{2,1,0:T(8,128)(2,1)S(1)}, u32[]{:S(2)}, u32[]{:S(2)}) collective-permute-start(bf16[4,64,512]{2,1,0:T(8,128)(2,1)S(1)} %get-tuple-element.49), channel_id=1, source_target_pairs={{0,8},{8,0},{16,24},{24,16},{1,9},{9,1},{17,25},{25,17},{2,10},{10... | collective-permute-start | bytes 786440 | tf_op jit(solution)/shard_map/ppermute | solution.py:345
  16.9 10.4 %collective-permute-start.3 = (bf16[4,64,512]{2,1,0:T(8,128)(2,1)S(1)}, bf16[4,64,512]{2,1,0:T(8,128)(2,1)S(1)}, u32[]{:S(2)}, u32[]{:S(2)}) collective-permute-start(bf16[4,64,512]{2,1,0:T(8,128)(2,1)S(1)} %get-tuple-element.50), channel_id=1, source_target_pairs={{8,16},{16,8},{9,17},{17,9},{10,18},{18,10},{11,19},{19,11},{12,20... | collective-permute-start | bytes 786440 | tf_op jit(solution)/shard_map/ppermute | solution.py:350
  20.7 6.6 %collective-permute-start.7 = (bf16[288,512]{1,0:T(8,128)(2,1)S(1)}, bf16[288,512]{1,0:T(8,128)(2,1)S(1)}, u32[]{:S(2)}, u32[]{:S(2)}) collective-permute-start(bf16[288,512]{1,0:T(8,128)(2,1)S(1)} %get-tuple-element.55), channel_id=1, source_target_pairs={{0,1},{1,0},{2,3},{3,2},{4,5},{5,4},{6,7},{7,6},{8,9},{9,8},{10,11... | collective-permute-start | bytes 884744 | tf_op jit(solution)/shard_map/ppermute | solution.py:345
  22.2 5.1 %collective-permute-start.8 = (bf16[288,512]{1,0:T(8,128)(2,1)S(1)}, bf16[288,512]{1,0:T(8,128)(2,1)S(1)}, u32[]{:S(2)}, u32[]{:S(2)}) collective-permute-start(bf16[288,512]{1,0:T(8,128)(2,1)S(1)} %get-tuple-element.56), channel_id=1, source_target_pairs={{1,2},{3,4},{5,6},{2,1},{4,3},{6,5},{9,10},{11,12},{13,14},{10,9},... | collective-permute-start | bytes 884744 | tf_op jit(solution)/shard_map/ppermute | solution.py:350
  27.2 3.7 %copy-start.1 = (bf16[3,512,512]{2,1,0:T(8,128)(2,1)S(1)}, bf16[3,512,512]{2,1,0:T(8,128)(2,1)}, u32[]{:S(2)}) copy-start(bf16[3,512,512]{2,1,0:T(8,128)(2,1)} %t_ref.1) | copy-start | bytes 4718596
  27.2 3.7 %copy-start.3 = (f32[512]{0:T(512)S(1)}, f32[512]{0:T(512)}, u32[]{:S(2)}) copy-start(f32[512]{0:T(512)} %param.12) | copy-start | bytes 6148
  28.0 6.6 %collective-permute-start.9 = (bf16[256,1536]{1,0:T(8,128)(2,1)S(1)}, bf16[256,1536]{1,0:T(8,128)(2,1)S(1)}, u32[]{:S(2)}, u32[]{:S(2)}) collective-permute-start(bf16[256,1536]{1,0:T(8,128)(2,1)S(1)} %get-tuple-element.68), channel_id=1, source_target_pairs={{0,1},{1,0},{2,3},{3,2},{4,5},{5,4},{6,7},{7,6},{8,9},{9,8},{10,11... | collective-permute-start | bytes 2359304 | tf_op jit(solution)/shard_map/ppermute | solution.py:345
  34.5 5.9 %copy-start.4 = (bf16[512,512]{1,0:T(8,128)(2,1)S(1)}, bf16[512,512]{1,0:T(8,128)(2,1)}, u32[]{:S(2)}) copy-start(bf16[512,512]{1,0:T(8,128)(2,1)} %q_ref.1) | copy-start | bytes 1572868
  34.6 5.9 %copy-start.5 = (bf16[512,512]{1,0:T(8,128)(2,1)S(1)}, bf16[512,512]{1,0:T(8,128)(2,1)}, u32[]{:S(2)}) copy-start(bf16[512,512]{1,0:T(8,128)(2,1)} %k_ref.1) | copy-start | bytes 1572868
  34.6 5.9 %copy-start.6 = (bf16[512,512]{1,0:T(8,128)(2,1)S(1)}, bf16[512,512]{1,0:T(8,128)(2,1)}, u32[]{:S(2)}) copy-start(bf16[512,512]{1,0:T(8,128)(2,1)} %v_ref.1) | copy-start | bytes 1572868
  34.6 5.9 %copy-start.7 = (bf16[512,512]{1,0:T(8,128)(2,1)S(1)}, bf16[512,512]{1,0:T(8,128)(2,1)}, u32[]{:S(2)}) copy-start(bf16[512,512]{1,0:T(8,128)(2,1)} %o_ref.1) | copy-start | bytes 1572868
  34.9 11.1 %collective-permute-start.13 = (bf16[256,384]{1,0:T(8,128)(2,1)S(1)}, bf16[256,384]{1,0:T(8,128)(2,1)S(1)}, u32[]{:S(2)}, u32[]{:S(2)}) collective-permute-start(bf16[256,384]{1,0:T(8,128)(2,1)S(1)} %get-tuple-element.79), channel_id=1, source_target_pairs={{0,8},{8,0},{16,24},{24,16},{1,9},{9,1},{17,25},{25,17},{2,10},{10... | collective-permute-start | bytes 589832 | tf_op jit(solution)/shard_map/ppermute | solution.py:345
  38.9 11.9 %collective-permute-start.14 = (bf16[256,384]{1,0:T(8,128)(2,1)S(1)}, bf16[256,384]{1,0:T(8,128)(2,1)S(1)}, u32[]{:S(2)}, u32[]{:S(2)}) collective-permute-start(bf16[256,384]{1,0:T(8,128)(2,1)S(1)} %get-tuple-element.80), channel_id=1, source_target_pairs={{0,16},{8,24},{16,0},{24,8},{1,17},{9,25},{17,1},{25,9},{2,18},{10... | collective-permute-start | bytes 589832 | tf_op jit(solution)/shard_map/ppermute | solution.py:345
  38.9 11.9 %collective-permute-start.15 = (bf16[256,384]{1,0:T(8,128)(2,1)S(1)}, bf16[256,384]{1,0:T(8,128)(2,1)S(1)}, u32[]{:S(2)}, u32[]{:S(2)}) collective-permute-start(bf16[256,384]{1,0:T(8,128)(2,1)S(1)} %get-tuple-element.81), channel_id=1, source_target_pairs={{0,24},{8,16},{16,8},{24,0},{1,25},{9,17},{17,9},{25,1},{2,26},{10... | collective-permute-start | bytes 589832 | tf_op jit(solution)/shard_map/ppermute | solution.py:345
  44.0 18.2 %collective-permute-start.10 = (bf16[4,64,512]{2,1,0:T(8,128)(2,1)S(1)}, bf16[4,64,512]{2,1,0:T(8,128)(2,1)S(1)}, u32[]{:S(2)}, u32[]{:S(2)}) collective-permute-start(bf16[4,64,512]{2,1,0:T(8,128)(2,1)S(1)} %get-tuple-element.75), channel_id=1, source_target_pairs={{0,8},{8,0},{16,24},{24,16},{1,9},{9,1},{17,25},{25,17},{2,10},{10... | collective-permute-start | bytes 786440 | tf_op jit(solution)/shard_map/ppermute | solution.py:345
  46.0 16.2 %collective-permute-start.11 = (bf16[4,64,512]{2,1,0:T(8,128)(2,1)S(1)}, bf16[4,64,512]{2,1,0:T(8,128)(2,1)S(1)}, u32[]{:S(2)}, u32[]{:S(2)}) collective-permute-start(bf16[4,64,512]{2,1,0:T(8,128)(2,1)S(1)} %get-tuple-element.76), channel_id=1, source_target_pairs={{0,16},{8,24},{16,0},{24,8},{1,17},{9,25},{17,1},{25,9},{2,18},{10... | collective-permute-start | bytes 786440 | tf_op jit(solution)/shard_map/ppermute | solution.py:345
  46.0 16.2 %collective-permute-start.12 = (bf16[4,64,512]{2,1,0:T(8,128)(2,1)S(1)}, bf16[4,64,512]{2,1,0:T(8,128)(2,1)S(1)}, u32[]{:S(2)}, u32[]{:S(2)}) collective-permute-start(bf16[4,64,512]{2,1,0:T(8,128)(2,1)S(1)} %get-tuple-element.77), channel_id=1, source_target_pairs={{0,24},{8,16},{16,8},{24,0},{1,25},{9,17},{17,9},{25,1},{2,26},{10... | collective-permute-start | bytes 786440 | tf_op jit(solution)/shard_map/ppermute | solution.py:345
  51.0 4.6 %collective-permute-start.16 = (bf16[64,384]{1,0:T(8,128)(2,1)S(1)}, bf16[64,384]{1,0:T(8,128)(2,1)S(1)}, u32[]{:S(2)}, u32[]{:S(2)}) collective-permute-start(bf16[64,384]{1,0:T(8,128)(2,1)S(1)} %get-tuple-element.87), channel_id=1, source_target_pairs={{0,2},{1,3},{2,0},{3,1},{4,6},{5,7},{6,4},{7,5},{8,10},{9,11},{10,... | collective-permute-start | bytes 147464 | tf_op jit(solution)/shard_map/ppermute | solution.py:345
  53.1 6.0 %collective-permute-start.17 = (bf16[64,384]{1,0:T(8,128)(2,1)S(1)}, bf16[64,384]{1,0:T(8,128)(2,1)S(1)}, u32[]{:S(2)}, u32[]{:S(2)}) collective-permute-start(bf16[64,384]{1,0:T(8,128)(2,1)S(1)} %get-tuple-element.88), channel_id=1, source_target_pairs={{0,4},{1,5},{2,6},{3,7},{4,0},{5,1},{6,2},{7,3},{8,12},{9,13},{10,... | collective-permute-start | bytes 147464 | tf_op jit(solution)/shard_map/ppermute | solution.py:345
  55.7 5.9 %collective-permute-start.18 = (bf16[64,384]{1,0:T(8,128)(2,1)S(1)}, bf16[64,384]{1,0:T(8,128)(2,1)S(1)}, u32[]{:S(2)}, u32[]{:S(2)}) collective-permute-start(bf16[64,384]{1,0:T(8,128)(2,1)S(1)} %get-tuple-element.89), channel_id=1, source_target_pairs={{0,6},{1,7},{2,4},{3,5},{4,2},{5,3},{6,0},{7,1},{8,14},{9,15},{10,... | collective-permute-start | bytes 147464 | tf_op jit(solution)/shard_map/ppermute | solution.py:345

commit v7 on v6

--- a/solution.py
+++ b/solution.py
@@ -203,40 +203,55 @@
     far[...] = jnp.where(lower, out[0], out[z.r - 1])
 
 
-def inner_kernel(z, x_ref, w_ref, out):
-    for r in range(z.r):
-        total = jnp.zeros((z.block, z.c), F32)
-        for di in range(3):
-            if not 0 <= r + di - 1 < z.r:
-                continue
-            for dj in range(3):
-                total += jnp.dot(
-                    x_ref[r + di - 1, dj * z.f : dj * z.f + z.block],
-                    w_ref[di, dj],
-                    preferred_element_type=F32,
-                )
-        out[r] = total
-
-
-def norm_kernel(
-    z, part_ref, near_ref, far_ref, w_ref, x_ref, t_ref, gain_ref, hidden_ref, normed_ref
+def conv_row(z, w_ref, three):
+    total = jnp.zeros((z.block, z.c), F32)
+    for di, rows in enumerate(three):
+        for dj in range(3):
+            total += jnp.dot(
+                rows[dj * z.f : dj * z.f + z.block], w_ref[di, dj], preferred_element_type=F32
+            )
+    return silu(total)
+
+
+def middle_kernel(z, x_ref, w_ref, out):
+    for r in range(1, z.r - 1):
+        out[r - 1] = conv_row(z, w_ref, [x_ref.at[r + di] for di in (-1, 0, 1)])
+
+
+def border_kernel(z, x_ref, near_ref, far_ref, w_ref, out, edges):
+    lower = even("space")
+    edges[0] = jnp.where(lower, far_ref[...], near_ref[...])
+    edges[1] = jnp.where(lower, near_ref[...], far_ref[...])
+    out[0] = conv_row(z, w_ref, [edges.at[0], x_ref.at[0], x_ref.at[1]])
+    out[1] = conv_row(z, w_ref, [x_ref.at[z.r - 2], x_ref.at[z.r - 1], edges.at[1]])
+
+
+def staged(z, stages):
+    for step in range(z.r + len(stages) - 1):
+        for late, stage in reversed(list(enumerate(stages))):
+            if 0 <= step - late < z.r:
+                stage(step - late)
+
+
+def main_kernel(
+    z, middle_ref, border_ref, x_ref, t_ref, gain_ref, q_ref, k_ref, v_ref, o_ref, *outs
 ):
-    lower = even("space")
+    me = lax.axis_index("tm")
+    a = lax.broadcasted_iota(jnp.int32, (z.block, z.block), 0)
+    b = lax.broadcasted_iota(jnp.int32, (z.block, z.block), 1)
+    allowed = (a // z.f == b // z.f) & (b % z.f <= a % z.f)
+    scale = float(z.c) ** -0.5
+
+    def source(q):
+        t = ((me ^ (q // z.piece)) * z.fl) + q % z.piece // z.wc
+        return q % z.wc * z.f + t
+
+    back = chooser(z.block, z.block, source)
     frame = lax.broadcasted_iota(jnp.int32, (z.block, z.c), 0) % z.f
     held = {}
 
     def activate(r):
-        total = part_ref[r]
-        for edge, di in ((0, 0), (z.r - 1, 2)):
-            if r == edge:
-                rows = jnp.where(lower == (di == 2), near_ref[...], far_ref[...])
-                for dj in range(3):
-                    total += jnp.dot(
-                        rows[dj * z.f : dj * z.f + z.block],
-                        w_ref[di, dj],
-                        preferred_element_type=F32,
-                    )
-        act = silu(total)
+        act = border_ref[r // (z.r - 1)] if r in (0, z.r - 1) else middle_ref[r - 1]
         wide = act.astype(F32)
         held["a", r] = [act] + [
             jnp.where(frame >= k, pltpu.roll(wide, k, 0), 0.0).astype(BF) for k in (1, 2)
@@ -248,40 +263,15 @@
             for k, late in enumerate(held.pop(("a", r)))
         )
         hidden = (x_ref[r, z.f : z.f + z.block].astype(F32) + temporal).astype(BF)
-        hidden_ref[r] = hidden
         held["h", r] = hidden
 
     def norm(r):
-        wide = held.pop(("h", r)).astype(F32)
+        wide = held["h", r].astype(F32)
         mean = jnp.mean(wide * wide, axis=1, keepdims=True)
-        normed_ref[r] = (wide * (1.0 / jnp.sqrt(mean + 1e-06)) * gain_ref[...]).astype(BF)
-
-    staged(z, (activate, hide, norm))
-
-
-def staged(z, stages):
-    for step in range(z.r + len(stages) - 1):
-        for late, stage in reversed(list(enumerate(stages))):
-            if 0 <= step - late < z.r:
-                stage(step - late)
-
-
-def attend_kernel(z, hidden_ref, normed_ref, q_ref, k_ref, v_ref, o_ref, *outs):
-    me = lax.axis_index("tm")
-    a = lax.broadcasted_iota(jnp.int32, (z.block, z.block), 0)
-    b = lax.broadcasted_iota(jnp.int32, (z.block, z.block), 1)
-    allowed = (a // z.f == b // z.f) & (b % z.f <= a % z.f)
-    scale = float(z.c) ** -0.5
-
-    def source(q):
-        t = ((me ^ (q // z.piece)) * z.fl) + q % z.piece // z.wc
-        return q % z.wc * z.f + t
-
-    back = chooser(z.block, z.block, source)
-    held = {}
+        held["n", r] = (wide * (1.0 / jnp.sqrt(mean + 1e-06)) * gain_ref[...]).astype(BF)
 
     def project(r):
-        rows = normed_ref[r]
+        rows = held.pop(("n", r))
         held["q", r], held["k", r], held["v", r] = (
             jnp.dot(rows, w[...], preferred_element_type=F32).astype(BF)
             for w in (q_ref, k_ref, v_ref)
@@ -307,7 +297,7 @@
         held["a", r] = (mixed * held.pop(("t", r))).astype(BF)
 
     def finish(r):
-        encoded = hidden_ref[r].astype(F32) + jnp.dot(
+        encoded = held.pop(("h", r)).astype(F32) + jnp.dot(
             held.pop(("a", r)), o_ref[...], preferred_element_type=F32
         )
         held["e", r] = encoded.astype(BF)
@@ -317,7 +307,7 @@
         for k in range(z.n):
             outs[k][r] = encoded[k * z.piece : (k + 1) * z.piece]
 
-    staged(z, (project, score, weigh, mix, finish, spread))
+    staged(z, (activate, hide, norm, project, score, weigh, mix, finish, spread))
 
 
 def split_kernel(z, keep_ref, got_ref, *outs):
@@ -463,15 +453,15 @@
         *got,
     )
     close, apart = swap_both(close, apart, "space")
-    (inner,) = call(
-        functools.partial(inner_kernel, z),
-        [shape((z.r, z.block, z.c), F32)],
+    (middle,) = call(
+        functools.partial(middle_kernel, z),
+        [shape((z.r - 2, z.block, z.c))],
         x,
         spatial,
-        flops=9 * one * (3 * z.r - 2) // (3 * z.r),
-    )
-    tied = lax.optimization_barrier((near, far, inner, close, apart))
-    near, far, inner, close, apart = tied
+        flops=9 * one * (z.r - 2) // z.r,
+    )
+    tied = lax.optimization_barrier((near, far, middle, close, apart))
+    near, far, middle, close, apart = tied
     keep, send = call(
         functools.partial(cross_kernel, z, width),
         [shape((z.c // 2, 3 * z.c), F32), shape((z.c // 2, 3 * z.c))],
@@ -482,38 +472,40 @@
         cotangent,
         flops=3 * one // 4,
     )
-    inner, send = lax.optimization_barrier((inner, send))
     other = swap(send, "space", 1)
-    hidden, normed = call(
-        functools.partial(norm_kernel, z),
-        [shape((z.r, z.block, z.c))] * 2,
-        inner,
+    x, _ = lax.optimization_barrier((x, send))
+    (border,) = call(
+        functools.partial(border_kernel, z),
+        [shape((2, z.block, z.c))],
+        x,
         close,
         apart,
         spatial,
-        x,
-        temporal,
-        gain.reshape(1, z.c),
-        flops=5 * one,
-    )
+        flops=18 * one // z.r,
+        scratch=[pltpu.VMEM((2, line, z.c), BF)],
+    )
+    other, border = lax.optimization_barrier((other, border))
     pieces = call(
         functools.partial(split_kernel, z),
         [shape((z.c // 2, 3 * wide), F32)] + [shape((z.c // 2, 3 * wide))] * (n - 1),
         keep,
         other,
     )
-    normed, *pieces = lax.optimization_barrier((normed, *pieces))
+    border, *pieces = lax.optimization_barrier((border, *pieces))
     pieces = exchange(pieces)
     encoded = call(
-        functools.partial(attend_kernel, z),
+        functools.partial(main_kernel, z),
         [shape((z.r, z.piece, z.c))] * n,
-        hidden,
-        normed,
+        middle,
+        border,
+        x,
+        temporal,
+        gain.reshape(1, z.c),
         q_w,
         k_w,
         v_w,
         o_w,
-        flops=5 * one,
+        flops=9 * one,
     )
     back = exchange(encoded)
     pieces = lax.optimization_barrier((*pieces, *encoded))[:n]

time: 63.6 us -> 61.7 us (0.970)
  Pallas kernels: 23.4 us -> 22.6 us
  starting transfers between devices: 29.4 us -> 28.6 us
    ppermute x16, starting transfers between devices: 27 us -> 26.2 us  [swap(): return lax.ppermute(value, axis, [(i, i ^ k) for i in range(count)])]
    pallas_call x13, Pallas kernels: 22.4 us -> 21.6 us  [call(): pl.pallas_call(kernel, out_shape=tuple(outs), in_specs=[VMEM] * len(args)...]
where the time goes in v7:
time: 61.7 us; the launch traced here: 61.5 us
  starting transfers between devices  28.6 us (46%)
  Pallas kernels  22.6 us (37%)
  waiting for transfers between devices  8 us (13%)
  local copies, waits for them, and re-layouts  1.32 us (2%)
  between operations  1.07 us (2%)
    ppermute x16, starting transfers between devices, swap(): return lax.ppermute(value, axis, [(i, i ^ k) for i in range(count)])  26.2 us
    pallas_call x13, Pallas kernels, call(): pl.pallas_call(kernel, out_shape=tuple(outs), in_specs=[VMEM] * len(args)...  21.6 us
    ppermute x16, waiting for transfers between devices, swap(): return lax.ppermute(value, axis, [(i, i ^ k) for i in range(count)])  8 us
    ppermute x3, starting transfers between devices, swap_both(): other = lax.ppermute(far, axis, pairs + [(b, a) for a, b in pairs])  2.33 us
    unnamed x20, local copies, waits for them, and re-layouts  1.32 us
  transfers between devices with their start and end apart: 19, of which 5 were waited for; matrix products, arithmetic and copies ran while one was open for 0% of the time, Pallas kernels for 33%

profile of v7, /device:TPU:0, one launch (start us, length us, event | category | flops | bytes accessed | tf_op | source)
XLA Modules:
  0.0 61.5 jit_solution(11245786593468709950)
XLA Ops:
  0.6 1.2 %copy-done.1 = bf16[4,4,64,512]{3,2,1,0:T(8,128)(2,1)S(1)} copy-done((bf16[4,4,64,512]{3,2,1,0:T(8,128)(2,1)S(1)}, bf16[4,4,64,512]{3,2,1,0:T(8,128)(2,1)}, u32[]{:S(2)}) %copy-start.1) | copy-done | bytes 1048600
  1.9 0.6 shard_map.105
  2.4 3.0 %collective-permute-start.4 = (bf16[288,512]{1,0:T(8,128)(2,1)S(1)}, bf16[288,512]{1,0:T(8,128)(2,1)S(1)}, u32[]{:S(2)}, u32[]{:S(2)}) collective-permute-start(bf16[288,512]{1,0:T(8,128)(2,1)S(1)} %get-tuple-element.50), channel_id=1, source_target_pairs={{0,8},{8,0},{16,24},{24,16},{1,9},{9,1},{17,25},{25,17},{2,10},{10... | collective-permute-start | bytes 884744 | tf_op jit(solution)/shard_map/ppermute | solution.py:335
  5.4 1.5 %collective-permute-start.5 = (bf16[288,512]{1,0:T(8,128)(2,1)S(1)}, bf16[288,512]{1,0:T(8,128)(2,1)S(1)}, u32[]{:S(2)}, u32[]{:S(2)}) collective-permute-start(bf16[288,512]{1,0:T(8,128)(2,1)S(1)} %get-tuple-element.51), channel_id=1, source_target_pairs={{0,16},{8,24},{16,0},{24,8},{1,17},{9,25},{17,1},{25,9},{2,18},{10... | collective-permute-start | bytes 884744 | tf_op jit(solution)/shard_map/ppermute | solution.py:335
  7.0 0.0 collective-permute-start.6
  7.0 0.1 shard_map.106
  7.0 0.1 collective-permute-start
  7.1 0.0 copy-start
  7.1 0.8 %collective-permute-start.1 = (bf16[256,512]{1,0:T(8,128)(2,1)S(1)}, bf16[256,512]{1,0:T(8,128)(2,1)S(1)}, u32[]{:S(2)}, u32[]{:S(2)}) collective-permute-start(bf16[256,512]{1,0:T(8,128)(2,1)S(1)} %get-tuple-element.47), channel_id=1, source_target_pairs={{1,2},{3,4},{5,6},{2,1},{4,3},{6,5},{9,10},{11,12},{13,14},{10,9},... | collective-permute-start | bytes 786440 | tf_op jit(solution)/shard_map/ppermute | solution.py:340
  8.0 0.1 slice-done.1
  8.0 4.8 %shard_map.104.part_ref = f32[4,256,512]{2,1,0:T(8,128)S(1)} custom-call(bf16[4,4,64,512]{3,2,1,0:T(8,128)(2,1)S(1)} %copy-done.1, bf16[3,3,512,512]{3,2,1,0:T(8,128)(2,1)S(1)} %bitcast.3), custom_call_target="tpu_custom_call" | custom-call | flops 4294967296 | bytes 7864320 | tf_op jit(solution)/shard_map/pallas_call | solution.py:18
  12.8 0.0 collective-permute-done.near_ref
  12.8 1.9 %shard_map.107 = (bf16[4,4,64,512]{3,2,1,0:T(8,128)(2,1)S(1)}, bf16[4,64,512]{2,1,0:T(8,128)(2,1)S(1)}, bf16[4,64,512]{2,1,0:T(8,128)(2,1)S(1)}) custom-call(f32[4,256,512]{2,1,0:T(8,128)S(1)} %shard_map.104.part_ref, bf16[256,512]{1,0:T(8,128)(2,1)S(1)} %collective-permute-done.near_ref, bf16[256,512]{1,0:T(8,128)(2,1)S(1)} %collective-permute-done.1.far_ref, ...), custom_call_target="tpu_custom_call" | custom-call | flops 1610612736 | bytes 9961472 | tf_op jit(solution)/shard_map/pallas_call | solution.py:18
  14.7 2.0 %collective-permute-start.2 = (bf16[4,64,512]{2,1,0:T(8,128)(2,1)S(1)}, bf16[4,64,512]{2,1,0:T(8,128)(2,1)S(1)}, u32[]{:S(2)}, u32[]{:S(2)}) collective-permute-start(bf16[4,64,512]{2,1,0:T(8,128)(2,1)S(1)} %get-tuple-element.48), channel_id=1, source_target_pairs={{0,8},{8,0},{16,24},{24,16},{1,9},{9,1},{17,25},{25,17},{2,10},{10... | collective-permute-start | bytes 786440 | tf_op jit(solution)/shard_map/ppermute | solution.py:335
  16.7 0.7 %collective-permute-start.3 = (bf16[4,64,512]{2,1,0:T(8,128)(2,1)S(1)}, bf16[4,64,512]{2,1,0:T(8,128)(2,1)S(1)}, u32[]{:S(2)}, u32[]{:S(2)}) collective-permute-start(bf16[4,64,512]{2,1,0:T(8,128)(2,1)S(1)} %get-tuple-element.49), channel_id=1, source_target_pairs={{8,16},{16,8},{9,17},{17,9},{10,18},{18,10},{11,19},{19,11},{12,20... | collective-permute-start | bytes 786440 | tf_op jit(solution)/shard_map/ppermute | solution.py:340
  17.4 0.0 collective-permute-done.4.refs_1_
  17.4 2.8 %collective-permute-done.5.refs_2_ = bf16[288,512]{1,0:T(8,128)(2,1)S(1)} collective-permute-done((bf16[288,512]{1,0:T(8,128)(2,1)S(1)}, bf16[288,512]{1,0:T(8,128)(2,1)S(1)}, u32[]{:S(2)}, u32[]{:S(2)}) %collective-permute-start.5) | collective-permute-done | bytes 294944 | tf_op jit(solution)/shard_map/ppermute | solution.py:335
  20.2 0.0 collective-permute-done.6.refs_3_
  20.2 0.5 shard_map.108
  20.7 0.1 collective-permute-start.7
  20.8 0.9 %collective-permute-start.8 = (bf16[288,512]{1,0:T(8,128)(2,1)S(1)}, bf16[288,512]{1,0:T(8,128)(2,1)S(1)}, u32[]{:S(2)}, u32[]{:S(2)}) collective-permute-start(bf16[288,512]{1,0:T(8,128)(2,1)S(1)} %get-tuple-element.55), channel_id=1, source_target_pairs={{1,2},{3,4},{5,6},{2,1},{4,3},{6,5},{9,10},{11,12},{13,14},{10,9},... | collective-permute-start | bytes 884744 | tf_op jit(solution)/shard_map/ppermute | solution.py:340
  21.7 1.4 %shard_map.110.part_ref = f32[512,1536]{1,0:T(8,128)S(1)} custom-call(bf16[4,4,64,512]{3,2,1,0:T(8,128)(2,1)S(1)} %get-tuple-element.57.act_ref, bf16[4,4,64,512]{3,2,1,0:T(8,128)(2,1)S(1)} %copy-done), custom_call_target="tpu_custom_call" | custom-call | flops 1207959552 | bytes 5242880 | tf_op jit(solution)/shard_map/pallas_call | solution.py:18
  23.1 2.7 %shard_map.109.middle_ref = bf16[2,256,512]{2,1,0:T(8,128)(2,1)S(1)} custom-call(bf16[4,288,512]{2,1,0:T(8,128)(2,1)S(1)} %get-tuple-element.61.x_ref, bf16[3,3,512,512]{3,2,1,0:T(8,128)(2,1)S(1)} %bitcast.3), custom_call_target="tpu_custom_call" | custom-call | flops 2415919104 | bytes 6422528 | tf_op jit(solution)/shard_map/pallas_call | solution.py:18
  25.8 0.0 collective-permute-done.3.far_ref
  25.8 0.0 collective-permute-done.7.near_ref
  25.8 0.7 %shard_map.111 = (f32[256,1536]{1,0:T(8,128)S(1)}, bf16[256,1536]{1,0:T(8,128)(2,1)S(1)}) custom-call(f32[512,1536]{1,0:T(8,128)S(1)} %shard_map.110.part_ref, bf16[4,64,512]{2,1,0:T(8,128)(2,1)S(1)} %collective-permute-done.2.near_ref, bf16[4,64,512]{2,1,0:T(8,128)(2,1)S(1)} %collective-permute-done.3.far_ref, ...), custom_call_target="tpu_custom_call" | custom-call | flops 402653184 | bytes 8126464 | tf_op jit(solution)/shard_map/pallas_call | solution.py:18
  26.5 3.6 %collective-permute-start.9 = (bf16[256,1536]{1,0:T(8,128)(2,1)S(1)}, bf16[256,1536]{1,0:T(8,128)(2,1)S(1)}, u32[]{:S(2)}, u32[]{:S(2)}) collective-permute-start(bf16[256,1536]{1,0:T(8,128)(2,1)S(1)} %get-tuple-element.60), channel_id=1, source_target_pairs={{0,1},{1,0},{2,3},{3,2},{4,5},{5,4},{6,7},{7,6},{8,9},{9,8},{10,11... | collective-permute-start | bytes 2359304 | tf_op jit(solution)/shard_map/ppermute | solution.py:335
  30.0 2.7 %shard_map.112.border_ref = bf16[2,256,512]{2,1,0:T(8,128)(2,1)S(1)} custom-call(bf16[4,288,512]{2,1,0:T(8,128)(2,1)S(1)} %get-tuple-element.61.x_ref, bf16[288,512]{1,0:T(8,128)(2,1)S(1)} %collective-permute-done.7.near_ref, bf16[288,512]{1,0:T(8,128)(2,1)S(1)} %collective-permute-done.8.far_ref, bf16[3,3,512,512]{3,2,1,0:T(8,128)(2,1)S(1)} %bitcast.3), custom_call_target="tpu_custom_call" | custom-call | flops 2415919104 | bytes 7012352 | tf_op jit(solution)/shard_map/pallas_call | solution.py:18
  32.7 0.0 copy-start.2
  32.7 0.0 copy-start.3
  32.8 0.0 copy-start.7
  32.8 0.3 shard_map.113
  33.1 3.3 %collective-permute-start.13 = (bf16[256,384]{1,0:T(8,128)(2,1)S(1)}, bf16[256,384]{1,0:T(8,128)(2,1)S(1)}, u32[]{:S(2)}, u32[]{:S(2)}) collective-permute-start(bf16[256,384]{1,0:T(8,128)(2,1)S(1)} %get-tuple-element.77), channel_id=1, source_target_pairs={{0,8},{8,0},{16,24},{24,16},{1,9},{9,1},{17,25},{25,17},{2,10},{10... | collective-permute-start | bytes 589832 | tf_op jit(solution)/shard_map/ppermute | solution.py:335
  36.4 0.0 collective-permute-start.14
  36.4 1.5 %collective-permute-start.15 = (bf16[256,384]{1,0:T(8,128)(2,1)S(1)}, bf16[256,384]{1,0:T(8,128)(2,1)S(1)}, u32[]{:S(2)}, u32[]{:S(2)}) collective-permute-start(bf16[256,384]{1,0:T(8,128)(2,1)S(1)} %get-tuple-element.79), channel_id=1, source_target_pairs={{0,24},{8,16},{16,8},{24,0},{1,25},{9,17},{17,9},{25,1},{2,26},{10... | collective-permute-start | bytes 589832 | tf_op jit(solution)/shard_map/ppermute | solution.py:335
  38.0 5.3 %shard_map.114 = (bf16[4,64,512]{2,1,0:T(8,128)(2,1)S(1)}, bf16[4,64,512]{2,1,0:T(8,128)(2,1)S(1)}, bf16[4,64,512]{2,1,0:T(8,128)(2,1)S(1)}, bf16[4,64,512]{2,1,0:T(8,128)(2,1)S(1)}) custom-call(bf16[2,256,512]{2,1,0:T(8,128)(2,1)S(1)} %shard_map.109.middle_ref, bf16[2,256,512]{2,1,0:T(8,128)(2,1)S(1)} %shard_map.112.border_ref, ...), custom_call_target="tpu_custom_call" | custom-call | flops 4831838208 | bytes 6948864 | tf_op jit(solution)/shard_map/pallas_call | solution.py:18
  43.3 2.0 %collective-permute-start.10 = (bf16[4,64,512]{2,1,0:T(8,128)(2,1)S(1)}, bf16[4,64,512]{2,1,0:T(8,128)(2,1)S(1)}, u32[]{:S(2)}, u32[]{:S(2)}) collective-permute-start(bf16[4,64,512]{2,1,0:T(8,128)(2,1)S(1)} %get-tuple-element.73), channel_id=1, source_target_pairs={{0,8},{8,0},{16,24},{24,16},{1,9},{9,1},{17,25},{25,17},{2,10},{10... | collective-permute-start | bytes 786440 | tf_op jit(solution)/shard_map/ppermute | solution.py:335
  45.3 1.5 %collective-permute-start.12 = (bf16[4,64,512]{2,1,0:T(8,128)(2,1)S(1)}, bf16[4,64,512]{2,1,0:T(8,128)(2,1)S(1)}, u32[]{:S(2)}, u32[]{:S(2)}) collective-permute-start(bf16[4,64,512]{2,1,0:T(8,128)(2,1)S(1)} %get-tuple-element.75), channel_id=1, source_target_pairs={{0,24},{8,16},{16,8},{24,0},{1,25},{9,17},{17,9},{25,1},{2,26},{10... | collective-permute-start | bytes 786440 | tf_op jit(solution)/shard_map/ppermute | solution.py:335
  46.9 0.7 %collective-permute-done.14.refs_2_ = bf16[256,384]{1,0:T(8,128)(2,1)S(1)} collective-permute-done((bf16[256,384]{1,0:T(8,128)(2,1)S(1)}, bf16[256,384]{1,0:T(8,128)(2,1)S(1)}, u32[]{:S(2)}, u32[]{:S(2)}) %collective-permute-start.14) | collective-permute-done | bytes 196640 | tf_op jit(solution)/shard_map/ppermute | solution.py:335
  47.5 0.1 shard_map.116
  47.7 3.9 %collective-permute-start.16 = (bf16[64,384]{1,0:T(8,128)(2,1)S(1)}, bf16[64,384]{1,0:T(8,128)(2,1)S(1)}, u32[]{:S(2)}, u32[]{:S(2)}) collective-permute-start(bf16[64,384]{1,0:T(8,128)(2,1)S(1)} %get-tuple-element.85), channel_id=1, source_target_pairs={{0,2},{1,3},{2,0},{3,1},{4,6},{5,7},{6,4},{7,5},{8,10},{9,11},{10,... | collective-permute-start | bytes 147464 | tf_op jit(solution)/shard_map/ppermute | solution.py:335
  51.6 1.1 %collective-permute-start.17 = (bf16[64,384]{1,0:T(8,128)(2,1)S(1)}, bf16[64,384]{1,0:T(8,128)(2,1)S(1)}, u32[]{:S(2)}, u32[]{:S(2)}) collective-permute-start(bf16[64,384]{1,0:T(8,128)(2,1)S(1)} %get-tuple-element.86), channel_id=1, source_target_pairs={{0,4},{1,5},{2,6},{3,7},{4,0},{5,1},{6,2},{7,3},{8,12},{9,13},{10,... | collective-permute-start | bytes 147464 | tf_op jit(solution)/shard_map/ppermute | solution.py:335
  52.7 1.0 %collective-permute-done.16.refs_1_ = bf16[64,384]{1,0:T(8,128)(2,1)S(1)} collective-permute-done((bf16[64,384]{1,0:T(8,128)(2,1)S(1)}, bf16[64,384]{1,0:T(8,128)(2,1)S(1)}, u32[]{:S(2)}, u32[]{:S(2)}) %collective-permute-start.16) | collective-permute-done | bytes 49184 | tf_op jit(solution)/shard_map/ppermute | solution.py:335
  53.7 2.5 %collective-permute-start.18 = (bf16[64,384]{1,0:T(8,128)(2,1)S(1)}, bf16[64,384]{1,0:T(8,128)(2,1)S(1)}, u32[]{:S(2)}, u32[]{:S(2)}) collective-permute-start(bf16[64,384]{1,0:T(8,128)(2,1)S(1)} %get-tuple-element.87), channel_id=1, source_target_pairs={{0,6},{1,7},{2,4},{3,5},{4,2},{5,3},{6,0},{7,1},{8,14},{9,15},{10,... | collective-permute-start | bytes 147464 | tf_op jit(solution)/shard_map/ppermute | solution.py:335
  56.2 1.9 %collective-permute-done.17.refs_2_ = bf16[64,384]{1,0:T(8,128)(2,1)S(1)} collective-permute-done((bf16[64,384]{1,0:T(8,128)(2,1)S(1)}, bf16[64,384]{1,0:T(8,128)(2,1)S(1)}, u32[]{:S(2)}, u32[]{:S(2)}) %collective-permute-start.17) | collective-permute-done | bytes 49184 | tf_op jit(solution)/shard_map/ppermute | solution.py:335
  58.0 1.6 %collective-permute-done.18.refs_3_ = bf16[64,384]{1,0:T(8,128)(2,1)S(1)} collective-permute-done((bf16[64,384]{1,0:T(8,128)(2,1)S(1)}, bf16[64,384]{1,0:T(8,128)(2,1)S(1)}, u32[]{:S(2)}, u32[]{:S(2)}) %collective-permute-start.18) | collective-permute-done | bytes 49184 | tf_op jit(solution)/shard_map/ppermute | solution.py:335
  59.7 0.7 %shard_map.117 = f32[3,64,128]{2,1,0:T(8,128)} custom-call(f32[64,384]{1,0:T(8,128)S(1)} %get-tuple-element.84.refs_0_, bf16[64,384]{1,0:T(8,128)(2,1)S(1)} %collective-permute-done.16.refs_1_, bf16[64,384]{1,0:T(8,128)(2,1)S(1)} %collective-permute-done.17.refs_2_, bf16[64,384]{1,0:T(8,128)(2,1)S(1)} %collective-permute-done.18.refs_3_), custom_call_target="tpu_custom_call" | custom-call | bytes 344064 | tf_op jit(solution)/shard_map/pallas_call | solution.py:18
  60.4 1.0 %shard_map.115 = bf16[4,4,64,512]{3,2,1,0:T(8,128)(2,1)} custom-call(bf16[4,64,512]{2,1,0:T(8,128)(2,1)S(1)} %get-tuple-element.72.refs_0_, bf16[4,64,512]{2,1,0:T(8,128)(2,1)S(1)} %collective-permute-done.10.refs_1_, bf16[4,64,512]{2,1,0:T(8,128)(2,1)S(1)} %collective-permute-done.11.refs_2_, bf16[4,64,512]{2,1,0:T(8,128)(2,1)S(1)} %collective-permute-done.12.refs_3_), custom_call_target="tpu_custom_call" | custom-call | bytes 4194304 | tf_op jit(solution)/shard_map/pallas_call | solution.py:376
  (25 shorter events, 0.1 us)
Async XLA Ops:
  0.6 1.2 %copy-start.1 = (bf16[4,4,64,512]{3,2,1,0:T(8,128)(2,1)S(1)}, bf16[4,4,64,512]{3,2,1,0:T(8,128)(2,1)}, u32[]{:S(2)}) copy-start(bf16[4,4,64,512]{3,2,1,0:T(8,128)(2,1)} %x_ref.5) | copy-start | bytes 3145732
  1.9 6.1 %slice-start = ((s8[4718592]{0:T(1024)(128)(4,1)}), s8[4194304]{0:T(1024)(128)(4,1)S(1)}, s32[]{:S(2)}) async-start(s8[4718592]{0:T(1024)(128)(4,1)} %bitcast.2), calls=%async_computation | async-start | bytes 8388608
  2.4 15.0 %collective-permute-start.4 = (bf16[288,512]{1,0:T(8,128)(2,1)S(1)}, bf16[288,512]{1,0:T(8,128)(2,1)S(1)}, u32[]{:S(2)}, u32[]{:S(2)}) collective-permute-start(bf16[288,512]{1,0:T(8,128)(2,1)S(1)} %get-tuple-element.50), channel_id=1, source_target_pairs={{0,8},{8,0},{16,24},{24,16},{1,9},{9,1},{17,25},{25,17},{2,10},{10... | collective-permute-start | bytes 884744 | tf_op jit(solution)/shard_map/ppermute | solution.py:335
  5.4 14.8 %collective-permute-start.5 = (bf16[288,512]{1,0:T(8,128)(2,1)S(1)}, bf16[288,512]{1,0:T(8,128)(2,1)S(1)}, u32[]{:S(2)}, u32[]{:S(2)}) collective-permute-start(bf16[288,512]{1,0:T(8,128)(2,1)S(1)} %get-tuple-element.51), channel_id=1, source_target_pairs={{0,16},{8,24},{16,0},{24,8},{1,17},{9,25},{17,1},{25,9},{2,18},{10... | collective-permute-start | bytes 884744 | tf_op jit(solution)/shard_map/ppermute | solution.py:335
  7.0 13.3 %collective-permute-start.6 = (bf16[288,512]{1,0:T(8,128)(2,1)S(1)}, bf16[288,512]{1,0:T(8,128)(2,1)S(1)}, u32[]{:S(2)}, u32[]{:S(2)}) collective-permute-start(bf16[288,512]{1,0:T(8,128)(2,1)S(1)} %get-tuple-element.52), channel_id=1, source_target_pairs={{0,24},{8,16},{16,8},{24,0},{1,25},{9,17},{17,9},{25,1},{2,26},{10... | collective-permute-start | bytes 884744 | tf_op jit(solution)/shard_map/ppermute | solution.py:335
  7.0 1.0 %slice-start.1 = ((s8[4718592]{0:T(1024)(128)(4,1)}), s8[524288]{0:T(1024)(128)(4,1)S(1)}, s32[]{:S(2)}) async-start(s8[4718592]{0:T(1024)(128)(4,1)} %bitcast.2), calls=%async_computation.1 | async-start | bytes 1048576
  7.0 5.7 %collective-permute-start = (bf16[256,512]{1,0:T(8,128)(2,1)S(1)}, bf16[256,512]{1,0:T(8,128)(2,1)S(1)}, u32[]{:S(2)}, u32[]{:S(2)}) collective-permute-start(bf16[256,512]{1,0:T(8,128)(2,1)S(1)} %get-tuple-element.46), channel_id=1, source_target_pairs={{0,1},{1,0},{2,3},{3,2},{4,5},{5,4},{6,7},{7,6},{8,9},{9,8},{10,11... | collective-permute-start | bytes 786440 | tf_op jit(solution)/shard_map/ppermute | solution.py:335
  7.1 5.7 %copy-start = (bf16[4,4,64,512]{3,2,1,0:T(8,128)(2,1)S(1)}, bf16[4,4,64,512]{3,2,1,0:T(8,128)(2,1)}, u32[]{:S(2)}) copy-start(bf16[4,4,64,512]{3,2,1,0:T(8,128)(2,1)} %cot_ref.5) | copy-start | bytes 3145732
  7.1 5.7 %collective-permute-start.1 = (bf16[256,512]{1,0:T(8,128)(2,1)S(1)}, bf16[256,512]{1,0:T(8,128)(2,1)S(1)}, u32[]{:S(2)}, u32[]{:S(2)}) collective-permute-start(bf16[256,512]{1,0:T(8,128)(2,1)S(1)} %get-tuple-element.47), channel_id=1, source_target_pairs={{1,2},{3,4},{5,6},{2,1},{4,3},{6,5},{9,10},{11,12},{13,14},{10,9},... | collective-permute-start | bytes 786440 | tf_op jit(solution)/shard_map/ppermute | solution.py:340
  14.7 11.1 %collective-permute-start.2 = (bf16[4,64,512]{2,1,0:T(8,128)(2,1)S(1)}, bf16[4,64,512]{2,1,0:T(8,128)(2,1)S(1)}, u32[]{:S(2)}, u32[]{:S(2)}) collective-permute-start(bf16[4,64,512]{2,1,0:T(8,128)(2,1)S(1)} %get-tuple-element.48), channel_id=1, source_target_pairs={{0,8},{8,0},{16,24},{24,16},{1,9},{9,1},{17,25},{25,17},{2,10},{10... | collective-permute-start | bytes 786440 | tf_op jit(solution)/shard_map/ppermute | solution.py:335
  16.7 9.1 %collective-permute-start.3 = (bf16[4,64,512]{2,1,0:T(8,128)(2,1)S(1)}, bf16[4,64,512]{2,1,0:T(8,128)(2,1)S(1)}, u32[]{:S(2)}, u32[]{:S(2)}) collective-permute-start(bf16[4,64,512]{2,1,0:T(8,128)(2,1)S(1)} %get-tuple-element.49), channel_id=1, source_target_pairs={{8,16},{16,8},{9,17},{17,9},{10,18},{18,10},{11,19},{19,11},{12,20... | collective-permute-start | bytes 786440 | tf_op jit(solution)/shard_map/ppermute | solution.py:340
  20.7 5.1 %collective-permute-start.7 = (bf16[288,512]{1,0:T(8,128)(2,1)S(1)}, bf16[288,512]{1,0:T(8,128)(2,1)S(1)}, u32[]{:S(2)}, u32[]{:S(2)}) collective-permute-start(bf16[288,512]{1,0:T(8,128)(2,1)S(1)} %get-tuple-element.54), channel_id=1, source_target_pairs={{0,1},{1,0},{2,3},{3,2},{4,5},{5,4},{6,7},{7,6},{8,9},{9,8},{10,11... | collective-permute-start | bytes 884744 | tf_op jit(solution)/shard_map/ppermute | solution.py:335
  20.8 5.0 %collective-permute-start.8 = (bf16[288,512]{1,0:T(8,128)(2,1)S(1)}, bf16[288,512]{1,0:T(8,128)(2,1)S(1)}, u32[]{:S(2)}, u32[]{:S(2)}) collective-permute-start(bf16[288,512]{1,0:T(8,128)(2,1)S(1)} %get-tuple-element.55), channel_id=1, source_target_pairs={{1,2},{3,4},{5,6},{2,1},{4,3},{6,5},{9,10},{11,12},{13,14},{10,9},... | collective-permute-start | bytes 884744 | tf_op jit(solution)/shard_map/ppermute | solution.py:340
  26.5 6.3 %collective-permute-start.9 = (bf16[256,1536]{1,0:T(8,128)(2,1)S(1)}, bf16[256,1536]{1,0:T(8,128)(2,1)S(1)}, u32[]{:S(2)}, u32[]{:S(2)}) collective-permute-start(bf16[256,1536]{1,0:T(8,128)(2,1)S(1)} %get-tuple-element.60), channel_id=1, source_target_pairs={{0,1},{1,0},{2,3},{3,2},{4,5},{5,4},{6,7},{7,6},{8,9},{9,8},{10,11... | collective-permute-start | bytes 2359304 | tf_op jit(solution)/shard_map/ppermute | solution.py:335
  30.0 7.9 %copy-start.4 = (bf16[512,512]{1,0:T(8,128)(2,1)S(1)}, bf16[512,512]{1,0:T(8,128)(2,1)}, u32[]{:S(2)}) copy-start(bf16[512,512]{1,0:T(8,128)(2,1)} %k_ref.1) | copy-start | bytes 1572868
  30.0 7.9 %copy-start.5 = (bf16[512,512]{1,0:T(8,128)(2,1)S(1)}, bf16[512,512]{1,0:T(8,128)(2,1)}, u32[]{:S(2)}) copy-start(bf16[512,512]{1,0:T(8,128)(2,1)} %v_ref.1) | copy-start | bytes 1572868
  30.0 7.9 %copy-start.6 = (bf16[512,512]{1,0:T(8,128)(2,1)S(1)}, bf16[512,512]{1,0:T(8,128)(2,1)}, u32[]{:S(2)}) copy-start(bf16[512,512]{1,0:T(8,128)(2,1)} %o_ref.1) | copy-start | bytes 1572868
  32.7 5.3 %copy-start.2 = (bf16[3,512,512]{2,1,0:T(8,128)(2,1)S(1)}, bf16[3,512,512]{2,1,0:T(8,128)(2,1)}, u32[]{:S(2)}) copy-start(bf16[3,512,512]{2,1,0:T(8,128)(2,1)} %t_ref.1) | copy-start | bytes 4718596
  32.7 5.3 %copy-start.3 = (bf16[512,512]{1,0:T(8,128)(2,1)S(1)}, bf16[512,512]{1,0:T(8,128)(2,1)}, u32[]{:S(2)}) copy-start(bf16[512,512]{1,0:T(8,128)(2,1)} %q_ref.1) | copy-start | bytes 1572868
  32.8 5.2 %copy-start.7 = (f32[512]{0:T(512)S(1)}, f32[512]{0:T(512)}, u32[]{:S(2)}) copy-start(f32[512]{0:T(512)} %param.12) | copy-start | bytes 6148
  33.1 12.2 %collective-permute-start.13 = (bf16[256,384]{1,0:T(8,128)(2,1)S(1)}, bf16[256,384]{1,0:T(8,128)(2,1)S(1)}, u32[]{:S(2)}, u32[]{:S(2)}) collective-permute-start(bf16[256,384]{1,0:T(8,128)(2,1)S(1)} %get-tuple-element.77), channel_id=1, source_target_pairs={{0,8},{8,0},{16,24},{24,16},{1,9},{9,1},{17,25},{25,17},{2,10},{10... | collective-permute-start | bytes 589832 | tf_op jit(solution)/shard_map/ppermute | solution.py:335
  36.4 11.1 %collective-permute-start.14 = (bf16[256,384]{1,0:T(8,128)(2,1)S(1)}, bf16[256,384]{1,0:T(8,128)(2,1)S(1)}, u32[]{:S(2)}, u32[]{:S(2)}) collective-permute-start(bf16[256,384]{1,0:T(8,128)(2,1)S(1)} %get-tuple-element.78), channel_id=1, source_target_pairs={{0,16},{8,24},{16,0},{24,8},{1,17},{9,25},{17,1},{25,9},{2,18},{10... | collective-permute-start | bytes 589832 | tf_op jit(solution)/shard_map/ppermute | solution.py:335
  36.4 11.1 %collective-permute-start.15 = (bf16[256,384]{1,0:T(8,128)(2,1)S(1)}, bf16[256,384]{1,0:T(8,128)(2,1)S(1)}, u32[]{:S(2)}, u32[]{:S(2)}) collective-permute-start(bf16[256,384]{1,0:T(8,128)(2,1)S(1)} %get-tuple-element.79), channel_id=1, source_target_pairs={{0,24},{8,16},{16,8},{24,0},{1,25},{9,17},{17,9},{25,1},{2,26},{10... | collective-permute-start | bytes 589832 | tf_op jit(solution)/shard_map/ppermute | solution.py:335
  43.3 17.0 %collective-permute-start.10 = (bf16[4,64,512]{2,1,0:T(8,128)(2,1)S(1)}, bf16[4,64,512]{2,1,0:T(8,128)(2,1)S(1)}, u32[]{:S(2)}, u32[]{:S(2)}) collective-permute-start(bf16[4,64,512]{2,1,0:T(8,128)(2,1)S(1)} %get-tuple-element.73), channel_id=1, source_target_pairs={{0,8},{8,0},{16,24},{24,16},{1,9},{9,1},{17,25},{25,17},{2,10},{10... | collective-permute-start | bytes 786440 | tf_op jit(solution)/shard_map/ppermute | solution.py:335
  45.3 15.0 %collective-permute-start.11 = (bf16[4,64,512]{2,1,0:T(8,128)(2,1)S(1)}, bf16[4,64,512]{2,1,0:T(8,128)(2,1)S(1)}, u32[]{:S(2)}, u32[]{:S(2)}) collective-permute-start(bf16[4,64,512]{2,1,0:T(8,128)(2,1)S(1)} %get-tuple-element.74), channel_id=1, source_target_pairs={{0,16},{8,24},{16,0},{24,8},{1,17},{9,25},{17,1},{25,9},{2,18},{10... | collective-permute-start | bytes 786440 | tf_op jit(solution)/shard_map/ppermute | solution.py:335
  45.3 15.0 %collective-permute-start.12 = (bf16[4,64,512]{2,1,0:T(8,128)(2,1)S(1)}, bf16[4,64,512]{2,1,0:T(8,128)(2,1)S(1)}, u32[]{:S(2)}, u32[]{:S(2)}) collective-permute-start(bf16[4,64,512]{2,1,0:T(8,128)(2,1)S(1)} %get-tuple-element.75), channel_id=1, source_target_pairs={{0,24},{8,16},{16,8},{24,0},{1,25},{9,17},{17,9},{25,1},{2,26},{10... | collective-permute-start | bytes 786440 | tf_op jit(solution)/shard_map/ppermute | solution.py:335
  47.7 6.0 %collective-permute-start.16 = (bf16[64,384]{1,0:T(8,128)(2,1)S(1)}, bf16[64,384]{1,0:T(8,128)(2,1)S(1)}, u32[]{:S(2)}, u32[]{:S(2)}) collective-permute-start(bf16[64,384]{1,0:T(8,128)(2,1)S(1)} %get-tuple-element.85), channel_id=1, source_target_pairs={{0,2},{1,3},{2,0},{3,1},{4,6},{5,7},{6,4},{7,5},{8,10},{9,11},{10,... | collective-permute-start | bytes 147464 | tf_op jit(solution)/shard_map/ppermute | solution.py:335
  51.6 6.4 %collective-permute-start.17 = (bf16[64,384]{1,0:T(8,128)(2,1)S(1)}, bf16[64,384]{1,0:T(8,128)(2,1)S(1)}, u32[]{:S(2)}, u32[]{:S(2)}) collective-permute-start(bf16[64,384]{1,0:T(8,128)(2,1)S(1)} %get-tuple-element.86), channel_id=1, source_target_pairs={{0,4},{1,5},{2,6},{3,7},{4,0},{5,1},{6,2},{7,3},{8,12},{9,13},{10,... | collective-permute-start | bytes 147464 | tf_op jit(solution)/shard_map/ppermute | solution.py:335
  53.7 6.0 %collective-permute-start.18 = (bf16[64,384]{1,0:T(8,128)(2,1)S(1)}, bf16[64,384]{1,0:T(8,128)(2,1)S(1)}, u32[]{:S(2)}, u32[]{:S(2)}) collective-permute-start(bf16[64,384]{1,0:T(8,128)(2,1)S(1)} %get-tuple-element.87), channel_id=1, source_target_pairs={{0,6},{1,7},{2,4},{3,5},{4,2},{5,3},{6,0},{7,1},{8,14},{9,15},{10,... | collective-permute-start | bytes 147464 | tf_op jit(solution)/shard_map/ppermute | solution.py:335

commit v8 on v7

--- a/solution.py
+++ b/solution.py
@@ -447,6 +447,7 @@
         flops=9 * one // 4,
     )
     line = z.block + 2 * z.f
+    own_grad, *got = lax.optimization_barrier((own_grad, *got))
     x, close, apart = call(
         functools.partial(assemble_kernel, z),
         [shape((z.r, line, z.c)), shape((line, z.c)), shape((line, z.c))],
@@ -460,8 +461,7 @@
         spatial,
         flops=9 * one * (z.r - 2) // z.r,
     )
-    tied = lax.optimization_barrier((near, far, middle, close, apart))
-    near, far, middle, close, apart = tied
+    near, far, middle = lax.optimization_barrier((near, far, middle))
     keep, send = call(
         functools.partial(cross_kernel, z, width),
         [shape((z.c // 2, 3 * z.c), F32), shape((z.c // 2, 3 * z.c))],
@@ -473,7 +473,14 @@
         flops=3 * one // 4,
     )
     other = swap(send, "space", 1)
-    x, _ = lax.optimization_barrier((x, send))
+    pieces = call(
+        functools.partial(split_kernel, z),
+        [shape((z.c // 2, 3 * wide), F32)] + [shape((z.c // 2, 3 * wide))] * (n - 1),
+        keep,
+        other,
+    )
+    x, *pieces = lax.optimization_barrier((x, *pieces))
+    pieces = exchange(pieces)
     (border,) = call(
         functools.partial(border_kernel, z),
         [shape((2, z.block, z.c))],
@@ -484,15 +491,6 @@
         flops=18 * one // z.r,
         scratch=[pltpu.VMEM((2, line, z.c), BF)],
     )
-    other, border = lax.optimization_barrier((other, border))
-    pieces = call(
-        functools.partial(split_kernel, z),
-        [shape((z.c // 2, 3 * wide), F32)] + [shape((z.c // 2, 3 * wide))] * (n - 1),
-        keep,
-        other,
-    )
-    border, *pieces = lax.optimization_barrier((border, *pieces))
-    pieces = exchange(pieces)
     encoded = call(
         functools.partial(main_kernel, z),
         [shape((z.r, z.piece, z.c))] * n,

time: 61.7 us -> 65.7 us (1.065)
  starting transfers between devices: 28.6 us -> 33.2 us
  waiting for transfers between devices: 8 us -> 6.84 us
    ppermute x16, starting transfers between devices: 26.2 us -> 30.8 us  [swap(): return lax.ppermute(value, axis, [(i, i ^ k) for i in range(count)])]
    ppermute x16, waiting for transfers between devices: 8 us -> 6.83 us  [swap(): return lax.ppermute(value, axis, [(i, i ^ k) for i in range(count)])]
  transfers between devices with their start and end apart: 19 -> 19, of which waited for: 5 -> 5; matrix products, arithmetic and copies ran while one was open for 0% -> 0% of each run, Pallas kernels for 33% -> 31%
where the time goes in v8:
time: 65.7 us; the launch traced here: 65.1 us
  starting transfers between devices  33.2 us (51%)
  Pallas kernels  22.6 us (34%)
  waiting for transfers between devices  6.84 us (10%)
  local copies, waits for them, and re-layouts  1.33 us (2%)
  between operations  1.08 us (2%)
    ppermute x16, starting transfers between devices, swap(): return lax.ppermute(value, axis, [(i, i ^ k) for i in range(count)])  30.8 us
    pallas_call x13, Pallas kernels, call(): pl.pallas_call(kernel, out_shape=tuple(outs), in_specs=[VMEM] * len(args)...  21.6 us
    ppermute x16, waiting for transfers between devices, swap(): return lax.ppermute(value, axis, [(i, i ^ k) for i in range(count)])  6.83 us
    ppermute x3, starting transfers between devices, swap_both(): other = lax.ppermute(far, axis, pairs + [(b, a) for a, b in pairs])  2.32 us
    unnamed x20, local copies, waits for them, and re-layouts  1.33 us
  transfers between devices with their start and end apart: 19, of which 5 were waited for; matrix products, arithmetic and copies ran while one was open for 0% of the time, Pallas kernels for 31%

profile of v8, /device:TPU:0, one launch (start us, length us, event | category | flops | bytes accessed | tf_op | source)
XLA Modules:
  0.0 65.1 jit_solution(12612788452113333503)
XLA Ops:
  0.6 1.2 %copy-done.1 = bf16[4,4,64,512]{3,2,1,0:T(8,128)(2,1)S(1)} copy-done((bf16[4,4,64,512]{3,2,1,0:T(8,128)(2,1)S(1)}, bf16[4,4,64,512]{3,2,1,0:T(8,128)(2,1)}, u32[]{:S(2)}) %copy-start.1) | copy-done | bytes 1048600
  1.9 0.6 shard_map.105
  2.4 3.0 %collective-permute-start.4 = (bf16[288,512]{1,0:T(8,128)(2,1)S(1)}, bf16[288,512]{1,0:T(8,128)(2,1)S(1)}, u32[]{:S(2)}, u32[]{:S(2)}) collective-permute-start(bf16[288,512]{1,0:T(8,128)(2,1)S(1)} %get-tuple-element.51), channel_id=1, source_target_pairs={{0,8},{8,0},{16,24},{24,16},{1,9},{9,1},{17,25},{25,17},{2,10},{10... | collective-permute-start | bytes 884744 | tf_op jit(solution)/shard_map/ppermute | solution.py:335
  5.4 1.5 %collective-permute-start.5 = (bf16[288,512]{1,0:T(8,128)(2,1)S(1)}, bf16[288,512]{1,0:T(8,128)(2,1)S(1)}, u32[]{:S(2)}, u32[]{:S(2)}) collective-permute-start(bf16[288,512]{1,0:T(8,128)(2,1)S(1)} %get-tuple-element.52), channel_id=1, source_target_pairs={{0,16},{8,24},{16,0},{24,8},{1,17},{9,25},{17,1},{25,9},{2,18},{10... | collective-permute-start | bytes 884744 | tf_op jit(solution)/shard_map/ppermute | solution.py:335
  7.0 0.0 collective-permute-start.6
  7.0 0.1 shard_map.106
  7.0 0.1 collective-permute-start
  7.1 0.0 copy-start
  7.1 0.8 %collective-permute-start.1 = (bf16[256,512]{1,0:T(8,128)(2,1)S(1)}, bf16[256,512]{1,0:T(8,128)(2,1)S(1)}, u32[]{:S(2)}, u32[]{:S(2)}) collective-permute-start(bf16[256,512]{1,0:T(8,128)(2,1)S(1)} %get-tuple-element.47), channel_id=1, source_target_pairs={{1,2},{3,4},{5,6},{2,1},{4,3},{6,5},{9,10},{11,12},{13,14},{10,9},... | collective-permute-start | bytes 786440 | tf_op jit(solution)/shard_map/ppermute | solution.py:340
  8.0 0.1 slice-done.1
  8.0 4.8 %shard_map.104.part_ref = f32[4,256,512]{2,1,0:T(8,128)S(1)} custom-call(bf16[4,4,64,512]{3,2,1,0:T(8,128)(2,1)S(1)} %copy-done.1, bf16[3,3,512,512]{3,2,1,0:T(8,128)(2,1)S(1)} %bitcast.3), custom_call_target="tpu_custom_call" | custom-call | flops 4294967296 | bytes 7864320 | tf_op jit(solution)/shard_map/pallas_call | solution.py:18
  12.8 0.0 collective-permute-done.near_ref
  12.8 1.9 %shard_map.107 = (bf16[4,4,64,512]{3,2,1,0:T(8,128)(2,1)S(1)}, bf16[4,64,512]{2,1,0:T(8,128)(2,1)S(1)}, bf16[4,64,512]{2,1,0:T(8,128)(2,1)S(1)}) custom-call(f32[4,256,512]{2,1,0:T(8,128)S(1)} %shard_map.104.part_ref, bf16[256,512]{1,0:T(8,128)(2,1)S(1)} %collective-permute-done.near_ref, bf16[256,512]{1,0:T(8,128)(2,1)S(1)} %collective-permute-done.1.far_ref, ...), custom_call_target="tpu_custom_call" | custom-call | flops 1610612736 | bytes 9961472 | tf_op jit(solution)/shard_map/pallas_call | solution.py:18
  14.7 2.0 %collective-permute-start.2 = (bf16[4,64,512]{2,1,0:T(8,128)(2,1)S(1)}, bf16[4,64,512]{2,1,0:T(8,128)(2,1)S(1)}, u32[]{:S(2)}, u32[]{:S(2)}) collective-permute-start(bf16[4,64,512]{2,1,0:T(8,128)(2,1)S(1)} %get-tuple-element.48), channel_id=1, source_target_pairs={{0,8},{8,0},{16,24},{24,16},{1,9},{9,1},{17,25},{25,17},{2,10},{10... | collective-permute-start | bytes 786440 | tf_op jit(solution)/shard_map/ppermute | solution.py:335
  16.7 0.7 %collective-permute-start.3 = (bf16[4,64,512]{2,1,0:T(8,128)(2,1)S(1)}, bf16[4,64,512]{2,1,0:T(8,128)(2,1)S(1)}, u32[]{:S(2)}, u32[]{:S(2)}) collective-permute-start(bf16[4,64,512]{2,1,0:T(8,128)(2,1)S(1)} %get-tuple-element.49), channel_id=1, source_target_pairs={{8,16},{16,8},{9,17},{17,9},{10,18},{18,10},{11,19},{19,11},{12,20... | collective-permute-start | bytes 786440 | tf_op jit(solution)/shard_map/ppermute | solution.py:340
  17.4 1.4 %shard_map.108.part_ref = f32[512,1536]{1,0:T(8,128)S(1)} custom-call(bf16[4,4,64,512]{3,2,1,0:T(8,128)(2,1)S(1)} %get-tuple-element.50.act_ref, bf16[4,4,64,512]{3,2,1,0:T(8,128)(2,1)S(1)} %copy-done), custom_call_target="tpu_custom_call" | custom-call | flops 1207959552 | bytes 5242880 | tf_op jit(solution)/shard_map/pallas_call | solution.py:18
  18.8 0.0 collective-permute-done.4.refs_1_
  18.8 1.4 %collective-permute-done.5.refs_2_ = bf16[288,512]{1,0:T(8,128)(2,1)S(1)} collective-permute-done((bf16[288,512]{1,0:T(8,128)(2,1)S(1)}, bf16[288,512]{1,0:T(8,128)(2,1)S(1)}, u32[]{:S(2)}, u32[]{:S(2)}) %collective-permute-start.5) | collective-permute-done | bytes 294944 | tf_op jit(solution)/shard_map/ppermute | solution.py:335
  20.2 0.0 collective-permute-done.6.refs_3_
  20.2 0.5 shard_map.109
  20.7 2.7 %shard_map.110.middle_ref = bf16[2,256,512]{2,1,0:T(8,128)(2,1)S(1)} custom-call(bf16[4,288,512]{2,1,0:T(8,128)(2,1)S(1)} %get-tuple-element.69.x_ref, bf16[3,3,512,512]{3,2,1,0:T(8,128)(2,1)S(1)} %bitcast.3), custom_call_target="tpu_custom_call" | custom-call | flops 2415919104 | bytes 6422528 | tf_op jit(solution)/shard_map/pallas_call | solution.py:18
  23.4 0.6 shard_map.111
  24.1 2.1 %collective-permute-start.7 = (bf16[256,1536]{1,0:T(8,128)(2,1)S(1)}, bf16[256,1536]{1,0:T(8,128)(2,1)S(1)}, u32[]{:S(2)}, u32[]{:S(2)}) collective-permute-start(bf16[256,1536]{1,0:T(8,128)(2,1)S(1)} %get-tuple-element.64), channel_id=1, source_target_pairs={{0,1},{1,0},{2,3},{3,2},{4,5},{5,4},{6,7},{7,6},{8,9},{9,8},{10,11... | collective-permute-start | bytes 2359304 | tf_op jit(solution)/shard_map/ppermute | solution.py:335
  26.2 0.1 collective-permute-start.8
  26.3 0.8 %collective-permute-start.9 = (bf16[288,512]{1,0:T(8,128)(2,1)S(1)}, bf16[288,512]{1,0:T(8,128)(2,1)S(1)}, u32[]{:S(2)}, u32[]{:S(2)}) collective-permute-start(bf16[288,512]{1,0:T(8,128)(2,1)S(1)} %get-tuple-element.71), channel_id=1, source_target_pairs={{1,2},{3,4},{5,6},{2,1},{4,3},{6,5},{9,10},{11,12},{13,14},{10,9},... | collective-permute-start | bytes 884744 | tf_op jit(solution)/shard_map/ppermute | solution.py:340
  27.2 1.0 %collective-permute-done.7.got_ref = bf16[256,1536]{1,0:T(8,128)(2,1)S(1)} collective-permute-done((bf16[256,1536]{1,0:T(8,128)(2,1)S(1)}, bf16[256,1536]{1,0:T(8,128)(2,1)S(1)}, u32[]{:S(2)}, u32[]{:S(2)}) %collective-permute-start.7) | collective-permute-done | bytes 786464 | tf_op jit(solution)/shard_map/ppermute | solution.py:335
  28.1 0.3 shard_map.112
  28.4 0.0 copy-start.2
  28.5 0.0 copy-start.3
  28.5 0.0 copy-start.4
  28.5 0.0 copy-start.5
  28.5 0.0 copy-start.6
  28.5 0.0 copy-start.7
  28.5 7.1 %collective-permute-start.13 = (bf16[256,384]{1,0:T(8,128)(2,1)S(1)}, bf16[256,384]{1,0:T(8,128)(2,1)S(1)}, u32[]{:S(2)}, u32[]{:S(2)}) collective-permute-start(bf16[256,384]{1,0:T(8,128)(2,1)S(1)} %get-tuple-element.77), channel_id=1, source_target_pairs={{0,8},{8,0},{16,24},{24,16},{1,9},{9,1},{17,25},{25,17},{2,10},{10... | collective-permute-start | bytes 589832 | tf_op jit(solution)/shard_map/ppermute | solution.py:335
  35.6 1.5 %collective-permute-start.15 = (bf16[256,384]{1,0:T(8,128)(2,1)S(1)}, bf16[256,384]{1,0:T(8,128)(2,1)S(1)}, u32[]{:S(2)}, u32[]{:S(2)}) collective-permute-start(bf16[256,384]{1,0:T(8,128)(2,1)S(1)} %get-tuple-element.79), channel_id=1, source_target_pairs={{0,24},{8,16},{16,8},{24,0},{1,25},{9,17},{17,9},{25,1},{2,26},{10... | collective-permute-start | bytes 589832 | tf_op jit(solution)/shard_map/ppermute | solution.py:335
  37.1 2.7 %shard_map.113.border_ref = bf16[2,256,512]{2,1,0:T(8,128)(2,1)S(1)} custom-call(bf16[4,288,512]{2,1,0:T(8,128)(2,1)S(1)} %get-tuple-element.69.x_ref, bf16[288,512]{1,0:T(8,128)(2,1)S(1)} %collective-permute-done.8.near_ref, bf16[288,512]{1,0:T(8,128)(2,1)S(1)} %collective-permute-done.9.far_ref, bf16[3,3,512,512]{3,2,1,0:T(8,128)(2,1)S(1)} %bitcast.3), custom_call_target="tpu_custom_call" | custom-call | flops 2415919104 | bytes 7012352 | tf_op jit(solution)/shard_map/pallas_call | solution.py:18
  39.9 5.4 %shard_map.114 = (bf16[4,64,512]{2,1,0:T(8,128)(2,1)S(1)}, bf16[4,64,512]{2,1,0:T(8,128)(2,1)S(1)}, bf16[4,64,512]{2,1,0:T(8,128)(2,1)S(1)}, bf16[4,64,512]{2,1,0:T(8,128)(2,1)S(1)}) custom-call(bf16[2,256,512]{2,1,0:T(8,128)(2,1)S(1)} %shard_map.110.middle_ref, bf16[2,256,512]{2,1,0:T(8,128)(2,1)S(1)} %shard_map.113.border_ref, ...), custom_call_target="tpu_custom_call" | custom-call | flops 4831838208 | bytes 6948864 | tf_op jit(solution)/shard_map/pallas_call | solution.py:18
  45.3 2.0 %collective-permute-start.10 = (bf16[4,64,512]{2,1,0:T(8,128)(2,1)S(1)}, bf16[4,64,512]{2,1,0:T(8,128)(2,1)S(1)}, u32[]{:S(2)}, u32[]{:S(2)}) collective-permute-start(bf16[4,64,512]{2,1,0:T(8,128)(2,1)S(1)} %get-tuple-element.73), channel_id=1, source_target_pairs={{0,8},{8,0},{16,24},{24,16},{1,9},{9,1},{17,25},{25,17},{2,10},{10... | collective-permute-start | bytes 786440 | tf_op jit(solution)/shard_map/ppermute | solution.py:335
  47.3 1.5 %collective-permute-start.12 = (bf16[4,64,512]{2,1,0:T(8,128)(2,1)S(1)}, bf16[4,64,512]{2,1,0:T(8,128)(2,1)S(1)}, u32[]{:S(2)}, u32[]{:S(2)}) collective-permute-start(bf16[4,64,512]{2,1,0:T(8,128)(2,1)S(1)} %get-tuple-element.75), channel_id=1, source_target_pairs={{0,24},{8,16},{16,8},{24,0},{1,25},{9,17},{17,9},{25,1},{2,26},{10... | collective-permute-start | bytes 786440 | tf_op jit(solution)/shard_map/ppermute | solution.py:335
  48.8 0.1 shard_map.116
  49.0 6.2 %collective-permute-start.16 = (bf16[64,384]{1,0:T(8,128)(2,1)S(1)}, bf16[64,384]{1,0:T(8,128)(2,1)S(1)}, u32[]{:S(2)}, u32[]{:S(2)}) collective-permute-start(bf16[64,384]{1,0:T(8,128)(2,1)S(1)} %get-tuple-element.85), channel_id=1, source_target_pairs={{0,2},{1,3},{2,0},{3,1},{4,6},{5,7},{6,4},{7,5},{8,10},{9,11},{10,... | collective-permute-start | bytes 147464 | tf_op jit(solution)/shard_map/ppermute | solution.py:335
  55.2 1.1 %collective-permute-start.17 = (bf16[64,384]{1,0:T(8,128)(2,1)S(1)}, bf16[64,384]{1,0:T(8,128)(2,1)S(1)}, u32[]{:S(2)}, u32[]{:S(2)}) collective-permute-start(bf16[64,384]{1,0:T(8,128)(2,1)S(1)} %get-tuple-element.86), channel_id=1, source_target_pairs={{0,4},{1,5},{2,6},{3,7},{4,0},{5,1},{6,2},{7,3},{8,12},{9,13},{10,... | collective-permute-start | bytes 147464 | tf_op jit(solution)/shard_map/ppermute | solution.py:335
  56.3 1.0 %collective-permute-done.16.refs_1_ = bf16[64,384]{1,0:T(8,128)(2,1)S(1)} collective-permute-done((bf16[64,384]{1,0:T(8,128)(2,1)S(1)}, bf16[64,384]{1,0:T(8,128)(2,1)S(1)}, u32[]{:S(2)}, u32[]{:S(2)}) %collective-permute-start.16) | collective-permute-done | bytes 49184 | tf_op jit(solution)/shard_map/ppermute | solution.py:335
  57.3 2.5 %collective-permute-start.18 = (bf16[64,384]{1,0:T(8,128)(2,1)S(1)}, bf16[64,384]{1,0:T(8,128)(2,1)S(1)}, u32[]{:S(2)}, u32[]{:S(2)}) collective-permute-start(bf16[64,384]{1,0:T(8,128)(2,1)S(1)} %get-tuple-element.87), channel_id=1, source_target_pairs={{0,6},{1,7},{2,4},{3,5},{4,2},{5,3},{6,0},{7,1},{8,14},{9,15},{10,... | collective-permute-start | bytes 147464 | tf_op jit(solution)/shard_map/ppermute | solution.py:335
  59.8 1.8 %collective-permute-done.17.refs_2_ = bf16[64,384]{1,0:T(8,128)(2,1)S(1)} collective-permute-done((bf16[64,384]{1,0:T(8,128)(2,1)S(1)}, bf16[64,384]{1,0:T(8,128)(2,1)S(1)}, u32[]{:S(2)}, u32[]{:S(2)}) %collective-permute-start.17) | collective-permute-done | bytes 49184 | tf_op jit(solution)/shard_map/ppermute | solution.py:335
  61.6 1.6 %collective-permute-done.18.refs_3_ = bf16[64,384]{1,0:T(8,128)(2,1)S(1)} collective-permute-done((bf16[64,384]{1,0:T(8,128)(2,1)S(1)}, bf16[64,384]{1,0:T(8,128)(2,1)S(1)}, u32[]{:S(2)}, u32[]{:S(2)}) %collective-permute-start.18) | collective-permute-done | bytes 49184 | tf_op jit(solution)/shard_map/ppermute | solution.py:335
  63.2 0.7 %shard_map.117 = f32[3,64,128]{2,1,0:T(8,128)} custom-call(f32[64,384]{1,0:T(8,128)S(1)} %get-tuple-element.84.refs_0_, bf16[64,384]{1,0:T(8,128)(2,1)S(1)} %collective-permute-done.16.refs_1_, bf16[64,384]{1,0:T(8,128)(2,1)S(1)} %collective-permute-done.17.refs_2_, bf16[64,384]{1,0:T(8,128)(2,1)S(1)} %collective-permute-done.18.refs_3_), custom_call_target="tpu_custom_call" | custom-call | bytes 344064 | tf_op jit(solution)/shard_map/pallas_call | solution.py:18
  63.9 1.0 %shard_map.115 = bf16[4,4,64,512]{3,2,1,0:T(8,128)(2,1)} custom-call(bf16[4,64,512]{2,1,0:T(8,128)(2,1)S(1)} %get-tuple-element.72.refs_0_, bf16[4,64,512]{2,1,0:T(8,128)(2,1)S(1)} %collective-permute-done.10.refs_1_, bf16[4,64,512]{2,1,0:T(8,128)(2,1)S(1)} %collective-permute-done.11.refs_2_, bf16[4,64,512]{2,1,0:T(8,128)(2,1)S(1)} %collective-permute-done.12.refs_3_), custom_call_target="tpu_custom_call" | custom-call | bytes 4194304 | tf_op jit(solution)/shard_map/pallas_call | solution.py:376
  (25 shorter events, 0.1 us)
Async XLA Ops:
  0.6 1.2 %copy-start.1 = (bf16[4,4,64,512]{3,2,1,0:T(8,128)(2,1)S(1)}, bf16[4,4,64,512]{3,2,1,0:T(8,128)(2,1)}, u32[]{:S(2)}) copy-start(bf16[4,4,64,512]{3,2,1,0:T(8,128)(2,1)} %x_ref.5) | copy-start | bytes 3145732
  1.9 6.1 %slice-start = ((s8[4718592]{0:T(1024)(128)(4,1)}), s8[4194304]{0:T(1024)(128)(4,1)S(1)}, s32[]{:S(2)}) async-start(s8[4718592]{0:T(1024)(128)(4,1)} %bitcast.2), calls=%async_computation | async-start | bytes 8388608
  2.4 16.4 %collective-permute-start.4 = (bf16[288,512]{1,0:T(8,128)(2,1)S(1)}, bf16[288,512]{1,0:T(8,128)(2,1)S(1)}, u32[]{:S(2)}, u32[]{:S(2)}) collective-permute-start(bf16[288,512]{1,0:T(8,128)(2,1)S(1)} %get-tuple-element.51), channel_id=1, source_target_pairs={{0,8},{8,0},{16,24},{24,16},{1,9},{9,1},{17,25},{25,17},{2,10},{10... | collective-permute-start | bytes 884744 | tf_op jit(solution)/shard_map/ppermute | solution.py:335
  5.4 14.8 %collective-permute-start.5 = (bf16[288,512]{1,0:T(8,128)(2,1)S(1)}, bf16[288,512]{1,0:T(8,128)(2,1)S(1)}, u32[]{:S(2)}, u32[]{:S(2)}) collective-permute-start(bf16[288,512]{1,0:T(8,128)(2,1)S(1)} %get-tuple-element.52), channel_id=1, source_target_pairs={{0,16},{8,24},{16,0},{24,8},{1,17},{9,25},{17,1},{25,9},{2,18},{10... | collective-permute-start | bytes 884744 | tf_op jit(solution)/shard_map/ppermute | solution.py:335
  7.0 13.3 %collective-permute-start.6 = (bf16[288,512]{1,0:T(8,128)(2,1)S(1)}, bf16[288,512]{1,0:T(8,128)(2,1)S(1)}, u32[]{:S(2)}, u32[]{:S(2)}) collective-permute-start(bf16[288,512]{1,0:T(8,128)(2,1)S(1)} %get-tuple-element.53), channel_id=1, source_target_pairs={{0,24},{8,16},{16,8},{24,0},{1,25},{9,17},{17,9},{25,1},{2,26},{10... | collective-permute-start | bytes 884744 | tf_op jit(solution)/shard_map/ppermute | solution.py:335
  7.0 1.0 %slice-start.1 = ((s8[4718592]{0:T(1024)(128)(4,1)}), s8[524288]{0:T(1024)(128)(4,1)S(1)}, s32[]{:S(2)}) async-start(s8[4718592]{0:T(1024)(128)(4,1)} %bitcast.2), calls=%async_computation.1 | async-start | bytes 1048576
  7.0 5.7 %collective-permute-start = (bf16[256,512]{1,0:T(8,128)(2,1)S(1)}, bf16[256,512]{1,0:T(8,128)(2,1)S(1)}, u32[]{:S(2)}, u32[]{:S(2)}) collective-permute-start(bf16[256,512]{1,0:T(8,128)(2,1)S(1)} %get-tuple-element.46), channel_id=1, source_target_pairs={{0,1},{1,0},{2,3},{3,2},{4,5},{5,4},{6,7},{7,6},{8,9},{9,8},{10,11... | collective-permute-start | bytes 786440 | tf_op jit(solution)/shard_map/ppermute | solution.py:335
  7.1 5.7 %copy-start = (bf16[4,4,64,512]{3,2,1,0:T(8,128)(2,1)S(1)}, bf16[4,4,64,512]{3,2,1,0:T(8,128)(2,1)}, u32[]{:S(2)}) copy-start(bf16[4,4,64,512]{3,2,1,0:T(8,128)(2,1)} %cot_ref.5) | copy-start | bytes 3145732
  7.1 5.7 %collective-permute-start.1 = (bf16[256,512]{1,0:T(8,128)(2,1)S(1)}, bf16[256,512]{1,0:T(8,128)(2,1)S(1)}, u32[]{:S(2)}, u32[]{:S(2)}) collective-permute-start(bf16[256,512]{1,0:T(8,128)(2,1)S(1)} %get-tuple-element.47), channel_id=1, source_target_pairs={{1,2},{3,4},{5,6},{2,1},{4,3},{6,5},{9,10},{11,12},{13,14},{10,9},... | collective-permute-start | bytes 786440 | tf_op jit(solution)/shard_map/ppermute | solution.py:340
  14.7 8.7 %collective-permute-start.2 = (bf16[4,64,512]{2,1,0:T(8,128)(2,1)S(1)}, bf16[4,64,512]{2,1,0:T(8,128)(2,1)S(1)}, u32[]{:S(2)}, u32[]{:S(2)}) collective-permute-start(bf16[4,64,512]{2,1,0:T(8,128)(2,1)S(1)} %get-tuple-element.48), channel_id=1, source_target_pairs={{0,8},{8,0},{16,24},{24,16},{1,9},{9,1},{17,25},{25,17},{2,10},{10... | collective-permute-start | bytes 786440 | tf_op jit(solution)/shard_map/ppermute | solution.py:335
  16.7 6.7 %collective-permute-start.3 = (bf16[4,64,512]{2,1,0:T(8,128)(2,1)S(1)}, bf16[4,64,512]{2,1,0:T(8,128)(2,1)S(1)}, u32[]{:S(2)}, u32[]{:S(2)}) collective-permute-start(bf16[4,64,512]{2,1,0:T(8,128)(2,1)S(1)} %get-tuple-element.49), channel_id=1, source_target_pairs={{8,16},{16,8},{9,17},{17,9},{10,18},{18,10},{11,19},{19,11},{12,20... | collective-permute-start | bytes 786440 | tf_op jit(solution)/shard_map/ppermute | solution.py:340
  24.1 4.1 %collective-permute-start.7 = (bf16[256,1536]{1,0:T(8,128)(2,1)S(1)}, bf16[256,1536]{1,0:T(8,128)(2,1)S(1)}, u32[]{:S(2)}, u32[]{:S(2)}) collective-permute-start(bf16[256,1536]{1,0:T(8,128)(2,1)S(1)} %get-tuple-element.64), channel_id=1, source_target_pairs={{0,1},{1,0},{2,3},{3,2},{4,5},{5,4},{6,7},{7,6},{8,9},{9,8},{10,11... | collective-permute-start | bytes 2359304 | tf_op jit(solution)/shard_map/ppermute | solution.py:335
  26.2 10.9 %collective-permute-start.8 = (bf16[288,512]{1,0:T(8,128)(2,1)S(1)}, bf16[288,512]{1,0:T(8,128)(2,1)S(1)}, u32[]{:S(2)}, u32[]{:S(2)}) collective-permute-start(bf16[288,512]{1,0:T(8,128)(2,1)S(1)} %get-tuple-element.70), channel_id=1, source_target_pairs={{0,1},{1,0},{2,3},{3,2},{4,5},{5,4},{6,7},{7,6},{8,9},{9,8},{10,11... | collective-permute-start | bytes 884744 | tf_op jit(solution)/shard_map/ppermute | solution.py:335
  26.3 10.8 %collective-permute-start.9 = (bf16[288,512]{1,0:T(8,128)(2,1)S(1)}, bf16[288,512]{1,0:T(8,128)(2,1)S(1)}, u32[]{:S(2)}, u32[]{:S(2)}) collective-permute-start(bf16[288,512]{1,0:T(8,128)(2,1)S(1)} %get-tuple-element.71), channel_id=1, source_target_pairs={{1,2},{3,4},{5,6},{2,1},{4,3},{6,5},{9,10},{11,12},{13,14},{10,9},... | collective-permute-start | bytes 884744 | tf_op jit(solution)/shard_map/ppermute | solution.py:340
  28.4 11.4 %copy-start.2 = (bf16[3,512,512]{2,1,0:T(8,128)(2,1)S(1)}, bf16[3,512,512]{2,1,0:T(8,128)(2,1)}, u32[]{:S(2)}) copy-start(bf16[3,512,512]{2,1,0:T(8,128)(2,1)} %t_ref.1) | copy-start | bytes 4718596
  28.5 11.4 %copy-start.3 = (bf16[512,512]{1,0:T(8,128)(2,1)S(1)}, bf16[512,512]{1,0:T(8,128)(2,1)}, u32[]{:S(2)}) copy-start(bf16[512,512]{1,0:T(8,128)(2,1)} %q_ref.1) | copy-start | bytes 1572868
  28.5 11.4 %copy-start.4 = (bf16[512,512]{1,0:T(8,128)(2,1)S(1)}, bf16[512,512]{1,0:T(8,128)(2,1)}, u32[]{:S(2)}) copy-start(bf16[512,512]{1,0:T(8,128)(2,1)} %k_ref.1) | copy-start | bytes 1572868
  28.5 11.4 %copy-start.5 = (bf16[512,512]{1,0:T(8,128)(2,1)S(1)}, bf16[512,512]{1,0:T(8,128)(2,1)}, u32[]{:S(2)}) copy-start(bf16[512,512]{1,0:T(8,128)(2,1)} %v_ref.1) | copy-start | bytes 1572868
  28.5 11.4 %copy-start.6 = (bf16[512,512]{1,0:T(8,128)(2,1)S(1)}, bf16[512,512]{1,0:T(8,128)(2,1)}, u32[]{:S(2)}) copy-start(bf16[512,512]{1,0:T(8,128)(2,1)} %o_ref.1) | copy-start | bytes 1572868
  28.5 11.4 %copy-start.7 = (f32[512]{0:T(512)S(1)}, f32[512]{0:T(512)}, u32[]{:S(2)}) copy-start(f32[512]{0:T(512)} %param.12) | copy-start | bytes 6148
  28.5 18.8 %collective-permute-start.13 = (bf16[256,384]{1,0:T(8,128)(2,1)S(1)}, bf16[256,384]{1,0:T(8,128)(2,1)S(1)}, u32[]{:S(2)}, u32[]{:S(2)}) collective-permute-start(bf16[256,384]{1,0:T(8,128)(2,1)S(1)} %get-tuple-element.77), channel_id=1, source_target_pairs={{0,8},{8,0},{16,24},{24,16},{1,9},{9,1},{17,25},{25,17},{2,10},{10... | collective-permute-start | bytes 589832 | tf_op jit(solution)/shard_map/ppermute | solution.py:335
  35.6 13.2 %collective-permute-start.14 = (bf16[256,384]{1,0:T(8,128)(2,1)S(1)}, bf16[256,384]{1,0:T(8,128)(2,1)S(1)}, u32[]{:S(2)}, u32[]{:S(2)}) collective-permute-start(bf16[256,384]{1,0:T(8,128)(2,1)S(1)} %get-tuple-element.78), channel_id=1, source_target_pairs={{0,16},{8,24},{16,0},{24,8},{1,17},{9,25},{17,1},{25,9},{2,18},{10... | collective-permute-start | bytes 589832 | tf_op jit(solution)/shard_map/ppermute | solution.py:335
  35.6 13.2 %collective-permute-start.15 = (bf16[256,384]{1,0:T(8,128)(2,1)S(1)}, bf16[256,384]{1,0:T(8,128)(2,1)S(1)}, u32[]{:S(2)}, u32[]{:S(2)}) collective-permute-start(bf16[256,384]{1,0:T(8,128)(2,1)S(1)} %get-tuple-element.79), channel_id=1, source_target_pairs={{0,24},{8,16},{16,8},{24,0},{1,25},{9,17},{17,9},{25,1},{2,26},{10... | collective-permute-start | bytes 589832 | tf_op jit(solution)/shard_map/ppermute | solution.py:335
  45.3 18.6 %collective-permute-start.10 = (bf16[4,64,512]{2,1,0:T(8,128)(2,1)S(1)}, bf16[4,64,512]{2,1,0:T(8,128)(2,1)S(1)}, u32[]{:S(2)}, u32[]{:S(2)}) collective-permute-start(bf16[4,64,512]{2,1,0:T(8,128)(2,1)S(1)} %get-tuple-element.73), channel_id=1, source_target_pairs={{0,8},{8,0},{16,24},{24,16},{1,9},{9,1},{17,25},{25,17},{2,10},{10... | collective-permute-start | bytes 786440 | tf_op jit(solution)/shard_map/ppermute | solution.py:335
  47.3 16.6 %collective-permute-start.11 = (bf16[4,64,512]{2,1,0:T(8,128)(2,1)S(1)}, bf16[4,64,512]{2,1,0:T(8,128)(2,1)S(1)}, u32[]{:S(2)}, u32[]{:S(2)}) collective-permute-start(bf16[4,64,512]{2,1,0:T(8,128)(2,1)S(1)} %get-tuple-element.74), channel_id=1, source_target_pairs={{0,16},{8,24},{16,0},{24,8},{1,17},{9,25},{17,1},{25,9},{2,18},{10... | collective-permute-start | bytes 786440 | tf_op jit(solution)/shard_map/ppermute | solution.py:335
  47.3 16.6 %collective-permute-start.12 = (bf16[4,64,512]{2,1,0:T(8,128)(2,1)S(1)}, bf16[4,64,512]{2,1,0:T(8,128)(2,1)S(1)}, u32[]{:S(2)}, u32[]{:S(2)}) collective-permute-start(bf16[4,64,512]{2,1,0:T(8,128)(2,1)S(1)} %get-tuple-element.75), channel_id=1, source_target_pairs={{0,24},{8,16},{16,8},{24,0},{1,25},{9,17},{17,9},{25,1},{2,26},{10... | collective-permute-start | bytes 786440 | tf_op jit(solution)/shard_map/ppermute | solution.py:335
  49.0 8.3 %collective-permute-start.16 = (bf16[64,384]{1,0:T(8,128)(2,1)S(1)}, bf16[64,384]{1,0:T(8,128)(2,1)S(1)}, u32[]{:S(2)}, u32[]{:S(2)}) collective-permute-start(bf16[64,384]{1,0:T(8,128)(2,1)S(1)} %get-tuple-element.85), channel_id=1, source_target_pairs={{0,2},{1,3},{2,0},{3,1},{4,6},{5,7},{6,4},{7,5},{8,10},{9,11},{10,... | collective-permute-start | bytes 147464 | tf_op jit(solution)/shard_map/ppermute | solution.py:335
  55.2 6.4 %collective-permute-start.17 = (bf16[64,384]{1,0:T(8,128)(2,1)S(1)}, bf16[64,384]{1,0:T(8,128)(2,1)S(1)}, u32[]{:S(2)}, u32[]{:S(2)}) collective-permute-start(bf16[64,384]{1,0:T(8,128)(2,1)S(1)} %get-tuple-element.86), channel_id=1, source_target_pairs={{0,4},{1,5},{2,6},{3,7},{4,0},{5,1},{6,2},{7,3},{8,12},{9,13},{10,... | collective-permute-start | bytes 147464 | tf_op jit(solution)/shard_map/ppermute | solution.py:335
  57.3 5.9 %collective-permute-start.18 = (bf16[64,384]{1,0:T(8,128)(2,1)S(1)}, bf16[64,384]{1,0:T(8,128)(2,1)S(1)}, u32[]{:S(2)}, u32[]{:S(2)}) collective-permute-start(bf16[64,384]{1,0:T(8,128)(2,1)S(1)} %get-tuple-element.87), channel_id=1, source_target_pairs={{0,6},{1,7},{2,4},{3,5},{4,2},{5,3},{6,0},{7,1},{8,14},{9,15},{10,... | collective-permute-start | bytes 147464 | tf_op jit(solution)/shard_map/ppermute | solution.py:335

commit v9 on v7

--- a/solution.py
+++ b/solution.py
@@ -113,7 +113,7 @@
         out[r] = total
 
 
-def own_act_kernel(z, part_ref, near_ref, far_ref, w_ref, cot_ref, out, near, far):
+def own_act_kernel(z, part_ref, near_ref, far_ref, w_ref, cot_ref, out, far, near):
     lower = even("space")
     first = even("tm")
     for r in range(z.r):
@@ -149,7 +149,7 @@
         out[:, k * z.c : (k + 1) * z.c] = outer(cot_ref[k:], act_ref[: z.fl - k])
 
 
-def cross_kernel(z, width, part_ref, near_ref, far_ref, act_ref, cot_ref, keep, send):
+def cross_kernel(z, width, part_ref, far_ref, near_ref, act_ref, cot_ref, keep, send):
     mine = even("space")
     before = jnp.where(even("tm"), far_ref[...], near_ref[...])
     after = jnp.where(even("tm"), near_ref[...], far_ref[...])
@@ -337,17 +337,20 @@
 
 def swap_both(near, far, axis):
     pairs = [(i, i + 1) for i in range(1, lax.axis_size(axis) - 1, 2)]
-    other = lax.ppermute(far, axis, pairs + [(b, a) for a, b in pairs])
-    return swap(near, axis, 1), other
-
-
-def chip_kernel(z, width, *refs):
-    parts, outs, total = refs[: z.n], refs[z.n : -1], refs[-1]
-    total[...] = sum(part[...].astype(F32) for part in parts)
-    chip = lax.axis_index("space") // 2
-    for k, out in enumerate(outs):
-        rows = pl.ds(pl.multiple_of((chip ^ k) * width, width), width)
-        out[...] = total[rows].astype(out.dtype)
+    far = lax.ppermute(far, axis, pairs + [(b, a) for a, b in pairs])
+    return swap(near, axis, 1), far
+
+
+def halve_kernel(z, width, bit, *refs):
+    parts, (keep, send) = refs[:-2], refs[-2:]
+    total = sum(part[...].astype(F32) for part in parts)
+    lower = lax.axis_index("space") // (2 << bit) % 2 == 0
+    for i in range(keep.shape[0] // width):
+        low = total[2 * i * width : (2 * i + 1) * width]
+        high = total[(2 * i + 1) * width : (2 * i + 2) * width]
+        rows = slice(i * width, (i + 1) * width)
+        keep[rows] = jnp.where(lower, low, high)
+        send[rows] = jnp.where(lower, high, low).astype(BF)
 
 
 def sum_kernel(z, *refs):
@@ -400,7 +403,7 @@
     z = Sizes(n, *frames_in.shape)
     one = 2 * z.r * z.block * z.c * z.c
     others = sorted(range(1, n), key=lambda k: -k.bit_count())
-    width, wide, chips = z.c // space, z.c // n, space // 2
+    width, wide = z.c // space, z.c // n
 
     def exchange(pieces):
         pieces = list(pieces)
@@ -428,7 +431,7 @@
         flops=8 * one,
         scratch=[pltpu.VMEM((3, z.r, z.fl * z.w, z.c), BF)],
     )
-    own_act, near, far = call(
+    own_act, far, near = call(
         functools.partial(own_act_kernel, z),
         [shape(frames_in.shape), shape((z.r, z.w, z.c)), shape((z.r, z.w, z.c))],
         own,
@@ -460,14 +463,14 @@
         spatial,
         flops=9 * one * (z.r - 2) // z.r,
     )
-    tied = lax.optimization_barrier((near, far, middle, close, apart))
-    near, far, middle, close, apart = tied
+    tied = lax.optimization_barrier((far, near, middle, close, apart))
+    far, near, middle, close, apart = tied
     keep, send = call(
         functools.partial(cross_kernel, z, width),
         [shape((z.c // 2, 3 * z.c), F32), shape((z.c // 2, 3 * z.c))],
         own_grad,
+        far,
         near,
-        far,
         own_act,
         cotangent,
         flops=3 * one // 4,
@@ -509,15 +512,16 @@
     )
     back = exchange(encoded)
     pieces = lax.optimization_barrier((*pieces, *encoded))[:n]
-    totals = call(
-        functools.partial(chip_kernel, z, width),
-        [shape((width, 3 * wide), F32)] + [shape((width, 3 * wide))] * (chips - 1),
-        *pieces,
-        scratch=[pltpu.VMEM((z.c // 2, 3 * wide), F32)],
-    )
-    totals = [totals[0]] + [swap(totals[k], "space", 2 * k) for k in range(1, chips)]
+    bit = 0
+    while 2 << bit < space:
+        half = (pieces[0].shape[0] // 2, 3 * wide)
+        keep, send = call(
+            functools.partial(halve_kernel, z, width, bit), [shape(half, F32), shape(half)], *pieces
+        )
+        pieces = (keep, swap(send, "space", 2 << bit))
+        bit += 1
     (kernel_grad,) = call(
-        functools.partial(sum_kernel, z), [shape((3, width, wide), F32)], *totals
+        functools.partial(sum_kernel, z), [shape((3, width, wide), F32)], *pieces
     )
     return joined(z, back), kernel_grad.transpose(0, 2, 1)
 

time: 61.7 us -> 62.1 us (level); the launches traced: 61.5 us -> 61.2 us
  waiting for transfers between devices: 8 us -> 6.55 us
  starting transfers between devices: 28.6 us -> 29.9 us
    ppermute x16 -> x15, waiting for transfers between devices: 8 us -> 6.54 us  [swap(): return lax.ppermute(value, axis, [(i, i ^ k) for i in range(count)])]
    ppermute x16 -> x15, starting transfers between devices: 26.2 us -> 27.6 us  [swap(): return lax.ppermute(value, axis, [(i, i ^ k) for i in range(count)])]
    pallas_call x13 -> x14, Pallas kernels: 21.6 us -> 21.5 us  [call(): pl.pallas_call(kernel, out_shape=tuple(outs), in_specs=[VMEM] * len(args)...]
  transfers between devices with their start and end apart: 19 -> 18, of which waited for: 5 -> 5; matrix products, arithmetic and copies ran while one was open for 0% -> 0% of each run, Pallas kernels for 33% -> 33%
where the time goes in v9:
time: 62.1 us; the launch traced here: 61.2 us
  starting transfers between devices  29.9 us (48%)
  Pallas kernels  22.6 us (36%)
  waiting for transfers between devices  6.55 us (11%)
  local copies, waits for them, and re-layouts  1.32 us (2%)
  between operations  0.88 us (1%)
    ppermute x15, starting transfers between devices, swap(): return lax.ppermute(value, axis, [(i, i ^ k) for i in range(count)])  27.6 us
    pallas_call x14, Pallas kernels, call(): pl.pallas_call(kernel, out_shape=tuple(outs), in_specs=[VMEM] * len(args)...  21.5 us
    ppermute x15, waiting for transfers between devices, swap(): return lax.ppermute(value, axis, [(i, i ^ k) for i in range(count)])  6.54 us
    ppermute x3, starting transfers between devices, swap_both(): far = lax.ppermute(far, axis, pairs + [(b, a) for a, b in pairs])  2.33 us
    unnamed x20, local copies, waits for them, and re-layouts  1.32 us
  transfers between devices with their start and end apart: 18, of which 5 were waited for; matrix products, arithmetic and copies ran while one was open for 0% of the time, Pallas kernels for 33%

profile of v9, /device:TPU:0, one launch (start us, length us, event | category | flops | bytes accessed | tf_op | source)
XLA Modules:
  0.0 61.2 jit_solution(7968716549846449521)
XLA Ops:
  0.6 1.2 %copy-done.1 = bf16[4,4,64,512]{3,2,1,0:T(8,128)(2,1)S(1)} copy-done((bf16[4,4,64,512]{3,2,1,0:T(8,128)(2,1)S(1)}, bf16[4,4,64,512]{3,2,1,0:T(8,128)(2,1)}, u32[]{:S(2)}) %copy-start.1) | copy-done | bytes 1048600
  1.9 0.6 shard_map.105
  2.4 3.0 %collective-permute-start.4 = (bf16[288,512]{1,0:T(8,128)(2,1)S(1)}, bf16[288,512]{1,0:T(8,128)(2,1)S(1)}, u32[]{:S(2)}, u32[]{:S(2)}) collective-permute-start(bf16[288,512]{1,0:T(8,128)(2,1)S(1)} %get-tuple-element.50), channel_id=1, source_target_pairs={{0,8},{8,0},{16,24},{24,16},{1,9},{9,1},{17,25},{25,17},{2,10},{10... | collective-permute-start | bytes 884744 | tf_op jit(solution)/shard_map/ppermute | solution.py:335
  5.4 1.5 %collective-permute-start.5 = (bf16[288,512]{1,0:T(8,128)(2,1)S(1)}, bf16[288,512]{1,0:T(8,128)(2,1)S(1)}, u32[]{:S(2)}, u32[]{:S(2)}) collective-permute-start(bf16[288,512]{1,0:T(8,128)(2,1)S(1)} %get-tuple-element.51), channel_id=1, source_target_pairs={{0,16},{8,24},{16,0},{24,8},{1,17},{9,25},{17,1},{25,9},{2,18},{10... | collective-permute-start | bytes 884744 | tf_op jit(solution)/shard_map/ppermute | solution.py:335
  7.0 0.0 collective-permute-start.6
  7.0 0.1 shard_map.106
  7.0 0.1 collective-permute-start
  7.1 0.0 copy-start
  7.1 0.8 %collective-permute-start.1 = (bf16[256,512]{1,0:T(8,128)(2,1)S(1)}, bf16[256,512]{1,0:T(8,128)(2,1)S(1)}, u32[]{:S(2)}, u32[]{:S(2)}) collective-permute-start(bf16[256,512]{1,0:T(8,128)(2,1)S(1)} %get-tuple-element.47), channel_id=1, source_target_pairs={{1,2},{3,4},{5,6},{2,1},{4,3},{6,5},{9,10},{11,12},{13,14},{10,9},... | collective-permute-start | bytes 786440 | tf_op jit(solution)/shard_map/ppermute | solution.py:340
  8.0 0.1 slice-done.1
  8.0 4.8 %shard_map.104.part_ref = f32[4,256,512]{2,1,0:T(8,128)S(1)} custom-call(bf16[4,4,64,512]{3,2,1,0:T(8,128)(2,1)S(1)} %copy-done.1, bf16[3,3,512,512]{3,2,1,0:T(8,128)(2,1)S(1)} %bitcast.3), custom_call_target="tpu_custom_call" | custom-call | flops 4294967296 | bytes 7864320 | tf_op jit(solution)/shard_map/pallas_call | solution.py:18
  12.8 1.9 %shard_map.107 = (bf16[4,4,64,512]{3,2,1,0:T(8,128)(2,1)S(1)}, bf16[4,64,512]{2,1,0:T(8,128)(2,1)S(1)}, bf16[4,64,512]{2,1,0:T(8,128)(2,1)S(1)}) custom-call(f32[4,256,512]{2,1,0:T(8,128)S(1)} %shard_map.104.part_ref, bf16[256,512]{1,0:T(8,128)(2,1)S(1)} %collective-permute-done.near_ref, bf16[256,512]{1,0:T(8,128)(2,1)S(1)} %collective-permute-done.1.far_ref, ...), custom_call_target="tpu_custom_call" | custom-call | flops 1610612736 | bytes 9961472 | tf_op jit(solution)/shard_map/pallas_call | solution.py:18
  14.7 0.7 %collective-permute-start.2 = (bf16[4,64,512]{2,1,0:T(8,128)(2,1)S(1)}, bf16[4,64,512]{2,1,0:T(8,128)(2,1)S(1)}, u32[]{:S(2)}, u32[]{:S(2)}) collective-permute-start(bf16[4,64,512]{2,1,0:T(8,128)(2,1)S(1)} %get-tuple-element.48), channel_id=1, source_target_pairs={{8,16},{16,8},{9,17},{17,9},{10,18},{18,10},{11,19},{19,11},{12,20... | collective-permute-start | bytes 786440 | tf_op jit(solution)/shard_map/ppermute | solution.py:340
  15.4 4.7 %collective-permute-start.3 = (bf16[4,64,512]{2,1,0:T(8,128)(2,1)S(1)}, bf16[4,64,512]{2,1,0:T(8,128)(2,1)S(1)}, u32[]{:S(2)}, u32[]{:S(2)}) collective-permute-start(bf16[4,64,512]{2,1,0:T(8,128)(2,1)S(1)} %get-tuple-element.49), channel_id=1, source_target_pairs={{0,8},{8,0},{16,24},{24,16},{1,9},{9,1},{17,25},{25,17},{2,10},{10... | collective-permute-start | bytes 786440 | tf_op jit(solution)/shard_map/ppermute | solution.py:335
  20.1 0.1 collective-permute-done.5.refs_2_
  20.2 0.0 collective-permute-done.6.refs_3_
  20.2 0.5 shard_map.108
  20.7 2.3 %collective-permute-start.7 = (bf16[288,512]{1,0:T(8,128)(2,1)S(1)}, bf16[288,512]{1,0:T(8,128)(2,1)S(1)}, u32[]{:S(2)}, u32[]{:S(2)}) collective-permute-start(bf16[288,512]{1,0:T(8,128)(2,1)S(1)} %get-tuple-element.54), channel_id=1, source_target_pairs={{0,1},{1,0},{2,3},{3,2},{4,5},{5,4},{6,7},{7,6},{8,9},{9,8},{10,11... | collective-permute-start | bytes 884744 | tf_op jit(solution)/shard_map/ppermute | solution.py:335
  23.0 0.8 %collective-permute-start.8 = (bf16[288,512]{1,0:T(8,128)(2,1)S(1)}, bf16[288,512]{1,0:T(8,128)(2,1)S(1)}, u32[]{:S(2)}, u32[]{:S(2)}) collective-permute-start(bf16[288,512]{1,0:T(8,128)(2,1)S(1)} %get-tuple-element.55), channel_id=1, source_target_pairs={{1,2},{3,4},{5,6},{2,1},{4,3},{6,5},{9,10},{11,12},{13,14},{10,9},... | collective-permute-start | bytes 884744 | tf_op jit(solution)/shard_map/ppermute | solution.py:340
  23.9 1.4 %shard_map.110.part_ref = f32[512,1536]{1,0:T(8,128)S(1)} custom-call(bf16[4,4,64,512]{3,2,1,0:T(8,128)(2,1)S(1)} %get-tuple-element.57.act_ref, bf16[4,4,64,512]{3,2,1,0:T(8,128)(2,1)S(1)} %copy-done), custom_call_target="tpu_custom_call" | custom-call | flops 1207959552 | bytes 5242880 | tf_op jit(solution)/shard_map/pallas_call | solution.py:18
  25.3 2.7 %shard_map.109.middle_ref = bf16[2,256,512]{2,1,0:T(8,128)(2,1)S(1)} custom-call(bf16[4,288,512]{2,1,0:T(8,128)(2,1)S(1)} %get-tuple-element.61.x_ref, bf16[3,3,512,512]{3,2,1,0:T(8,128)(2,1)S(1)} %bitcast.3), custom_call_target="tpu_custom_call" | custom-call | flops 2415919104 | bytes 6422528 | tf_op jit(solution)/shard_map/pallas_call | solution.py:18
  28.0 2.8 %collective-permute-done.3.near_ref = bf16[4,64,512]{2,1,0:T(8,128)(2,1)S(1)} collective-permute-done((bf16[4,64,512]{2,1,0:T(8,128)(2,1)S(1)}, bf16[4,64,512]{2,1,0:T(8,128)(2,1)S(1)}, u32[]{:S(2)}, u32[]{:S(2)}) %collective-permute-start.3) | collective-permute-done | bytes 262176 | tf_op jit(solution)/shard_map/ppermute | solution.py:335
  30.8 0.0 collective-permute-done.7.near_ref
  30.8 0.0 collective-permute-done.8.far_ref
  30.8 0.6 %shard_map.111 = (f32[256,1536]{1,0:T(8,128)S(1)}, bf16[256,1536]{1,0:T(8,128)(2,1)S(1)}) custom-call(f32[512,1536]{1,0:T(8,128)S(1)} %shard_map.110.part_ref, bf16[4,64,512]{2,1,0:T(8,128)(2,1)S(1)} %collective-permute-done.2.far_ref, bf16[4,64,512]{2,1,0:T(8,128)(2,1)S(1)} %collective-permute-done.3.near_ref, ...), custom_call_target="tpu_custom_call" | custom-call | flops 402653184 | bytes 8126464 | tf_op jit(solution)/shard_map/pallas_call | solution.py:18
  31.4 1.9 %collective-permute-start.9 = (bf16[256,1536]{1,0:T(8,128)(2,1)S(1)}, bf16[256,1536]{1,0:T(8,128)(2,1)S(1)}, u32[]{:S(2)}, u32[]{:S(2)}) collective-permute-start(bf16[256,1536]{1,0:T(8,128)(2,1)S(1)} %get-tuple-element.60), channel_id=1, source_target_pairs={{0,1},{1,0},{2,3},{3,2},{4,5},{5,4},{6,7},{7,6},{8,9},{9,8},{10,11... | collective-permute-start | bytes 2359304 | tf_op jit(solution)/shard_map/ppermute | solution.py:335
  33.4 2.7 %shard_map.112.border_ref = bf16[2,256,512]{2,1,0:T(8,128)(2,1)S(1)} custom-call(bf16[4,288,512]{2,1,0:T(8,128)(2,1)S(1)} %get-tuple-element.61.x_ref, bf16[288,512]{1,0:T(8,128)(2,1)S(1)} %collective-permute-done.7.near_ref, bf16[288,512]{1,0:T(8,128)(2,1)S(1)} %collective-permute-done.8.far_ref, bf16[3,3,512,512]{3,2,1,0:T(8,128)(2,1)S(1)} %bitcast.3), custom_call_target="tpu_custom_call" | custom-call | flops 2415919104 | bytes 7012352 | tf_op jit(solution)/shard_map/pallas_call | solution.py:18
  36.0 0.0 copy-start.2
  36.0 0.0 copy-start.3
  36.1 0.0 copy-start.7
  36.1 0.3 shard_map.113
  36.4 0.1 collective-permute-start.13
  36.5 2.0 %collective-permute-start.14 = (bf16[256,384]{1,0:T(8,128)(2,1)S(1)}, bf16[256,384]{1,0:T(8,128)(2,1)S(1)}, u32[]{:S(2)}, u32[]{:S(2)}) collective-permute-start(bf16[256,384]{1,0:T(8,128)(2,1)S(1)} %get-tuple-element.78), channel_id=1, source_target_pairs={{0,16},{8,24},{16,0},{24,8},{1,17},{9,25},{17,1},{25,9},{2,18},{10... | collective-permute-start | bytes 589832 | tf_op jit(solution)/shard_map/ppermute | solution.py:335
  38.5 1.5 %collective-permute-start.15 = (bf16[256,384]{1,0:T(8,128)(2,1)S(1)}, bf16[256,384]{1,0:T(8,128)(2,1)S(1)}, u32[]{:S(2)}, u32[]{:S(2)}) collective-permute-start(bf16[256,384]{1,0:T(8,128)(2,1)S(1)} %get-tuple-element.79), channel_id=1, source_target_pairs={{0,24},{8,16},{16,8},{24,0},{1,25},{9,17},{17,9},{25,1},{2,26},{10... | collective-permute-start | bytes 589832 | tf_op jit(solution)/shard_map/ppermute | solution.py:335
  40.0 5.3 %shard_map.114 = (bf16[4,64,512]{2,1,0:T(8,128)(2,1)S(1)}, bf16[4,64,512]{2,1,0:T(8,128)(2,1)S(1)}, bf16[4,64,512]{2,1,0:T(8,128)(2,1)S(1)}, bf16[4,64,512]{2,1,0:T(8,128)(2,1)S(1)}) custom-call(bf16[2,256,512]{2,1,0:T(8,128)(2,1)S(1)} %shard_map.109.middle_ref, bf16[2,256,512]{2,1,0:T(8,128)(2,1)S(1)} %shard_map.112.border_ref, ...), custom_call_target="tpu_custom_call" | custom-call | flops 4831838208 | bytes 6948864 | tf_op jit(solution)/shard_map/pallas_call | solution.py:18
  45.3 0.1 collective-permute-start.10
  45.4 1.9 %collective-permute-start.11 = (bf16[4,64,512]{2,1,0:T(8,128)(2,1)S(1)}, bf16[4,64,512]{2,1,0:T(8,128)(2,1)S(1)}, u32[]{:S(2)}, u32[]{:S(2)}) collective-permute-start(bf16[4,64,512]{2,1,0:T(8,128)(2,1)S(1)} %get-tuple-element.74), channel_id=1, source_target_pairs={{0,16},{8,24},{16,0},{24,8},{1,17},{9,25},{17,1},{25,9},{2,18},{10... | collective-permute-start | bytes 786440 | tf_op jit(solution)/shard_map/ppermute | solution.py:335
  47.4 0.0 collective-permute-done.13.refs_1_
  47.4 1.5 %collective-permute-start.12 = (bf16[4,64,512]{2,1,0:T(8,128)(2,1)S(1)}, bf16[4,64,512]{2,1,0:T(8,128)(2,1)S(1)}, u32[]{:S(2)}, u32[]{:S(2)}) collective-permute-start(bf16[4,64,512]{2,1,0:T(8,128)(2,1)S(1)} %get-tuple-element.75), channel_id=1, source_target_pairs={{0,24},{8,16},{16,8},{24,0},{1,25},{9,17},{17,9},{25,1},{2,26},{10... | collective-permute-start | bytes 786440 | tf_op jit(solution)/shard_map/ppermute | solution.py:335
  48.9 0.0 collective-permute-done.14.refs_2_
  48.9 0.1 shard_map.116
  49.0 3.8 %collective-permute-start.16 = (bf16[128,384]{1,0:T(8,128)(2,1)S(1)}, bf16[128,384]{1,0:T(8,128)(2,1)S(1)}, u32[]{:S(2)}, u32[]{:S(2)}) collective-permute-start(bf16[128,384]{1,0:T(8,128)(2,1)S(1)} %get-tuple-element.85), channel_id=1, source_target_pairs={{0,2},{1,3},{2,0},{3,1},{4,6},{5,7},{6,4},{7,5},{8,10},{9,11},{10,... | collective-permute-start | bytes 294920 | tf_op jit(solution)/shard_map/ppermute | solution.py:335
  52.8 2.6 %collective-permute-done.16.refs_1_ = bf16[128,384]{1,0:T(8,128)(2,1)S(1)} collective-permute-done((bf16[128,384]{1,0:T(8,128)(2,1)S(1)}, bf16[128,384]{1,0:T(8,128)(2,1)S(1)}, u32[]{:S(2)}, u32[]{:S(2)}) %collective-permute-start.16) | collective-permute-done | bytes 98336 | tf_op jit(solution)/shard_map/ppermute | solution.py:335
  55.4 3.1 %collective-permute-start.17 = (bf16[64,384]{1,0:T(8,128)(2,1)S(1)}, bf16[64,384]{1,0:T(8,128)(2,1)S(1)}, u32[]{:S(2)}, u32[]{:S(2)}) collective-permute-start(bf16[64,384]{1,0:T(8,128)(2,1)S(1)} %get-tuple-element.87), channel_id=1, source_target_pairs={{0,4},{1,5},{2,6},{3,7},{4,0},{5,1},{6,2},{7,3},{8,12},{9,13},{10,... | collective-permute-start | bytes 147464 | tf_op jit(solution)/shard_map/ppermute | solution.py:335
  58.5 0.3 collective-permute-done.11.refs_2_
  58.9 1.0 %shard_map.115 = bf16[4,4,64,512]{3,2,1,0:T(8,128)(2,1)} custom-call(bf16[4,64,512]{2,1,0:T(8,128)(2,1)S(1)} %get-tuple-element.72.refs_0_, bf16[4,64,512]{2,1,0:T(8,128)(2,1)S(1)} %collective-permute-done.10.refs_1_, bf16[4,64,512]{2,1,0:T(8,128)(2,1)S(1)} %collective-permute-done.11.refs_2_, bf16[4,64,512]{2,1,0:T(8,128)(2,1)S(1)} %collective-permute-done.12.refs_3_), custom_call_target="tpu_custom_call" | custom-call | bytes 4194304 | tf_op jit(solution)/shard_map/pallas_call | solution.py:379
  59.9 0.7 %collective-permute-done.17.refs_1_ = bf16[64,384]{1,0:T(8,128)(2,1)S(1)} collective-permute-done((bf16[64,384]{1,0:T(8,128)(2,1)S(1)}, bf16[64,384]{1,0:T(8,128)(2,1)S(1)}, u32[]{:S(2)}, u32[]{:S(2)}) %collective-permute-start.17) | collective-permute-done | bytes 49184 | tf_op jit(solution)/shard_map/ppermute | solution.py:335
  60.6 0.7 %shard_map.118 = f32[3,64,128]{2,1,0:T(8,128)} custom-call(f32[64,384]{1,0:T(8,128)S(1)} %get-tuple-element.86.refs_0_, bf16[64,384]{1,0:T(8,128)(2,1)S(1)} %collective-permute-done.17.refs_1_), custom_call_target="tpu_custom_call" | custom-call | bytes 245760 | tf_op jit(solution)/shard_map/pallas_call | solution.py:18
  (24 shorter events, 0.1 us)
Async XLA Ops:
  0.6 1.2 %copy-start.1 = (bf16[4,4,64,512]{3,2,1,0:T(8,128)(2,1)S(1)}, bf16[4,4,64,512]{3,2,1,0:T(8,128)(2,1)}, u32[]{:S(2)}) copy-start(bf16[4,4,64,512]{3,2,1,0:T(8,128)(2,1)} %x_ref.5) | copy-start | bytes 3145732
  1.9 6.1 %slice-start = ((s8[4718592]{0:T(1024)(128)(4,1)}), s8[4194304]{0:T(1024)(128)(4,1)S(1)}, s32[]{:S(2)}) async-start(s8[4718592]{0:T(1024)(128)(4,1)} %bitcast.2), calls=%async_computation | async-start | bytes 8388608
  2.4 17.7 %collective-permute-start.4 = (bf16[288,512]{1,0:T(8,128)(2,1)S(1)}, bf16[288,512]{1,0:T(8,128)(2,1)S(1)}, u32[]{:S(2)}, u32[]{:S(2)}) collective-permute-start(bf16[288,512]{1,0:T(8,128)(2,1)S(1)} %get-tuple-element.50), channel_id=1, source_target_pairs={{0,8},{8,0},{16,24},{24,16},{1,9},{9,1},{17,25},{25,17},{2,10},{10... | collective-permute-start | bytes 884744 | tf_op jit(solution)/shard_map/ppermute | solution.py:335
  5.4 14.8 %collective-permute-start.5 = (bf16[288,512]{1,0:T(8,128)(2,1)S(1)}, bf16[288,512]{1,0:T(8,128)(2,1)S(1)}, u32[]{:S(2)}, u32[]{:S(2)}) collective-permute-start(bf16[288,512]{1,0:T(8,128)(2,1)S(1)} %get-tuple-element.51), channel_id=1, source_target_pairs={{0,16},{8,24},{16,0},{24,8},{1,17},{9,25},{17,1},{25,9},{2,18},{10... | collective-permute-start | bytes 884744 | tf_op jit(solution)/shard_map/ppermute | solution.py:335
  7.0 13.3 %collective-permute-start.6 = (bf16[288,512]{1,0:T(8,128)(2,1)S(1)}, bf16[288,512]{1,0:T(8,128)(2,1)S(1)}, u32[]{:S(2)}, u32[]{:S(2)}) collective-permute-start(bf16[288,512]{1,0:T(8,128)(2,1)S(1)} %get-tuple-element.52), channel_id=1, source_target_pairs={{0,24},{8,16},{16,8},{24,0},{1,25},{9,17},{17,9},{25,1},{2,26},{10... | collective-permute-start | bytes 884744 | tf_op jit(solution)/shard_map/ppermute | solution.py:335
  7.0 1.0 %slice-start.1 = ((s8[4718592]{0:T(1024)(128)(4,1)}), s8[524288]{0:T(1024)(128)(4,1)S(1)}, s32[]{:S(2)}) async-start(s8[4718592]{0:T(1024)(128)(4,1)} %bitcast.2), calls=%async_computation.1 | async-start | bytes 1048576
  7.0 5.7 %collective-permute-start = (bf16[256,512]{1,0:T(8,128)(2,1)S(1)}, bf16[256,512]{1,0:T(8,128)(2,1)S(1)}, u32[]{:S(2)}, u32[]{:S(2)}) collective-permute-start(bf16[256,512]{1,0:T(8,128)(2,1)S(1)} %get-tuple-element.46), channel_id=1, source_target_pairs={{0,1},{1,0},{2,3},{3,2},{4,5},{5,4},{6,7},{7,6},{8,9},{9,8},{10,11... | collective-permute-start | bytes 786440 | tf_op jit(solution)/shard_map/ppermute | solution.py:335
  7.1 5.7 %copy-start = (bf16[4,4,64,512]{3,2,1,0:T(8,128)(2,1)S(1)}, bf16[4,4,64,512]{3,2,1,0:T(8,128)(2,1)}, u32[]{:S(2)}) copy-start(bf16[4,4,64,512]{3,2,1,0:T(8,128)(2,1)} %cot_ref.5) | copy-start | bytes 3145732
  7.1 5.7 %collective-permute-start.1 = (bf16[256,512]{1,0:T(8,128)(2,1)S(1)}, bf16[256,512]{1,0:T(8,128)(2,1)S(1)}, u32[]{:S(2)}, u32[]{:S(2)}) collective-permute-start(bf16[256,512]{1,0:T(8,128)(2,1)S(1)} %get-tuple-element.47), channel_id=1, source_target_pairs={{1,2},{3,4},{5,6},{2,1},{4,3},{6,5},{9,10},{11,12},{13,14},{10,9},... | collective-permute-start | bytes 786440 | tf_op jit(solution)/shard_map/ppermute | solution.py:340
  14.7 13.3 %collective-permute-start.2 = (bf16[4,64,512]{2,1,0:T(8,128)(2,1)S(1)}, bf16[4,64,512]{2,1,0:T(8,128)(2,1)S(1)}, u32[]{:S(2)}, u32[]{:S(2)}) collective-permute-start(bf16[4,64,512]{2,1,0:T(8,128)(2,1)S(1)} %get-tuple-element.48), channel_id=1, source_target_pairs={{8,16},{16,8},{9,17},{17,9},{10,18},{18,10},{11,19},{19,11},{12,20... | collective-permute-start | bytes 786440 | tf_op jit(solution)/shard_map/ppermute | solution.py:340
  15.4 15.4 %collective-permute-start.3 = (bf16[4,64,512]{2,1,0:T(8,128)(2,1)S(1)}, bf16[4,64,512]{2,1,0:T(8,128)(2,1)S(1)}, u32[]{:S(2)}, u32[]{:S(2)}) collective-permute-start(bf16[4,64,512]{2,1,0:T(8,128)(2,1)S(1)} %get-tuple-element.49), channel_id=1, source_target_pairs={{0,8},{8,0},{16,24},{24,16},{1,9},{9,1},{17,25},{25,17},{2,10},{10... | collective-permute-start | bytes 786440 | tf_op jit(solution)/shard_map/ppermute | solution.py:335
  20.7 10.1 %collective-permute-start.7 = (bf16[288,512]{1,0:T(8,128)(2,1)S(1)}, bf16[288,512]{1,0:T(8,128)(2,1)S(1)}, u32[]{:S(2)}, u32[]{:S(2)}) collective-permute-start(bf16[288,512]{1,0:T(8,128)(2,1)S(1)} %get-tuple-element.54), channel_id=1, source_target_pairs={{0,1},{1,0},{2,3},{3,2},{4,5},{5,4},{6,7},{7,6},{8,9},{9,8},{10,11... | collective-permute-start | bytes 884744 | tf_op jit(solution)/shard_map/ppermute | solution.py:335
  23.0 7.7 %collective-permute-start.8 = (bf16[288,512]{1,0:T(8,128)(2,1)S(1)}, bf16[288,512]{1,0:T(8,128)(2,1)S(1)}, u32[]{:S(2)}, u32[]{:S(2)}) collective-permute-start(bf16[288,512]{1,0:T(8,128)(2,1)S(1)} %get-tuple-element.55), channel_id=1, source_target_pairs={{1,2},{3,4},{5,6},{2,1},{4,3},{6,5},{9,10},{11,12},{13,14},{10,9},... | collective-permute-start | bytes 884744 | tf_op jit(solution)/shard_map/ppermute | solution.py:340
  31.4 4.6 %collective-permute-start.9 = (bf16[256,1536]{1,0:T(8,128)(2,1)S(1)}, bf16[256,1536]{1,0:T(8,128)(2,1)S(1)}, u32[]{:S(2)}, u32[]{:S(2)}) collective-permute-start(bf16[256,1536]{1,0:T(8,128)(2,1)S(1)} %get-tuple-element.60), channel_id=1, source_target_pairs={{0,1},{1,0},{2,3},{3,2},{4,5},{5,4},{6,7},{7,6},{8,9},{9,8},{10,11... | collective-permute-start | bytes 2359304 | tf_op jit(solution)/shard_map/ppermute | solution.py:335
  33.3 6.6 %copy-start.4 = (bf16[512,512]{1,0:T(8,128)(2,1)S(1)}, bf16[512,512]{1,0:T(8,128)(2,1)}, u32[]{:S(2)}) copy-start(bf16[512,512]{1,0:T(8,128)(2,1)} %k_ref.1) | copy-start | bytes 1572868
  33.3 6.6 %copy-start.5 = (bf16[512,512]{1,0:T(8,128)(2,1)S(1)}, bf16[512,512]{1,0:T(8,128)(2,1)}, u32[]{:S(2)}) copy-start(bf16[512,512]{1,0:T(8,128)(2,1)} %v_ref.1) | copy-start | bytes 1572868
  33.3 6.6 %copy-start.6 = (bf16[512,512]{1,0:T(8,128)(2,1)S(1)}, bf16[512,512]{1,0:T(8,128)(2,1)}, u32[]{:S(2)}) copy-start(bf16[512,512]{1,0:T(8,128)(2,1)} %o_ref.1) | copy-start | bytes 1572868
  36.0 3.9 %copy-start.2 = (bf16[3,512,512]{2,1,0:T(8,128)(2,1)S(1)}, bf16[3,512,512]{2,1,0:T(8,128)(2,1)}, u32[]{:S(2)}) copy-start(bf16[3,512,512]{2,1,0:T(8,128)(2,1)} %t_ref.1) | copy-start | bytes 4718596
  36.0 3.9 %copy-start.3 = (bf16[512,512]{1,0:T(8,128)(2,1)S(1)}, bf16[512,512]{1,0:T(8,128)(2,1)}, u32[]{:S(2)}) copy-start(bf16[512,512]{1,0:T(8,128)(2,1)} %q_ref.1) | copy-start | bytes 1572868
  36.1 3.9 %copy-start.7 = (f32[512]{0:T(512)S(1)}, f32[512]{0:T(512)}, u32[]{:S(2)}) copy-start(f32[512]{0:T(512)} %param.12) | copy-start | bytes 6148
  36.4 11.0 %collective-permute-start.13 = (bf16[256,384]{1,0:T(8,128)(2,1)S(1)}, bf16[256,384]{1,0:T(8,128)(2,1)S(1)}, u32[]{:S(2)}, u32[]{:S(2)}) collective-permute-start(bf16[256,384]{1,0:T(8,128)(2,1)S(1)} %get-tuple-element.77), channel_id=1, source_target_pairs={{0,8},{8,0},{16,24},{24,16},{1,9},{9,1},{17,25},{25,17},{2,10},{10... | collective-permute-start | bytes 589832 | tf_op jit(solution)/shard_map/ppermute | solution.py:335
  36.5 12.4 %collective-permute-start.14 = (bf16[256,384]{1,0:T(8,128)(2,1)S(1)}, bf16[256,384]{1,0:T(8,128)(2,1)S(1)}, u32[]{:S(2)}, u32[]{:S(2)}) collective-permute-start(bf16[256,384]{1,0:T(8,128)(2,1)S(1)} %get-tuple-element.78), channel_id=1, source_target_pairs={{0,16},{8,24},{16,0},{24,8},{1,17},{9,25},{17,1},{25,9},{2,18},{10... | collective-permute-start | bytes 589832 | tf_op jit(solution)/shard_map/ppermute | solution.py:335
  38.5 10.4 %collective-permute-start.15 = (bf16[256,384]{1,0:T(8,128)(2,1)S(1)}, bf16[256,384]{1,0:T(8,128)(2,1)S(1)}, u32[]{:S(2)}, u32[]{:S(2)}) collective-permute-start(bf16[256,384]{1,0:T(8,128)(2,1)S(1)} %get-tuple-element.79), channel_id=1, source_target_pairs={{0,24},{8,16},{16,8},{24,0},{1,25},{9,17},{17,9},{25,1},{2,26},{10... | collective-permute-start | bytes 589832 | tf_op jit(solution)/shard_map/ppermute | solution.py:335
  45.3 13.2 %collective-permute-start.10 = (bf16[4,64,512]{2,1,0:T(8,128)(2,1)S(1)}, bf16[4,64,512]{2,1,0:T(8,128)(2,1)S(1)}, u32[]{:S(2)}, u32[]{:S(2)}) collective-permute-start(bf16[4,64,512]{2,1,0:T(8,128)(2,1)S(1)} %get-tuple-element.73), channel_id=1, source_target_pairs={{0,8},{8,0},{16,24},{24,16},{1,9},{9,1},{17,25},{25,17},{2,10},{10... | collective-permute-start | bytes 786440 | tf_op jit(solution)/shard_map/ppermute | solution.py:335
  45.4 13.4 %collective-permute-start.11 = (bf16[4,64,512]{2,1,0:T(8,128)(2,1)S(1)}, bf16[4,64,512]{2,1,0:T(8,128)(2,1)S(1)}, u32[]{:S(2)}, u32[]{:S(2)}) collective-permute-start(bf16[4,64,512]{2,1,0:T(8,128)(2,1)S(1)} %get-tuple-element.74), channel_id=1, source_target_pairs={{0,16},{8,24},{16,0},{24,8},{1,17},{9,25},{17,1},{25,9},{2,18},{10... | collective-permute-start | bytes 786440 | tf_op jit(solution)/shard_map/ppermute | solution.py:335
  47.4 11.5 %collective-permute-start.12 = (bf16[4,64,512]{2,1,0:T(8,128)(2,1)S(1)}, bf16[4,64,512]{2,1,0:T(8,128)(2,1)S(1)}, u32[]{:S(2)}, u32[]{:S(2)}) collective-permute-start(bf16[4,64,512]{2,1,0:T(8,128)(2,1)S(1)} %get-tuple-element.75), channel_id=1, source_target_pairs={{0,24},{8,16},{16,8},{24,0},{1,25},{9,17},{17,9},{25,1},{2,26},{10... | collective-permute-start | bytes 786440 | tf_op jit(solution)/shard_map/ppermute | solution.py:335
  49.0 6.4 %collective-permute-start.16 = (bf16[128,384]{1,0:T(8,128)(2,1)S(1)}, bf16[128,384]{1,0:T(8,128)(2,1)S(1)}, u32[]{:S(2)}, u32[]{:S(2)}) collective-permute-start(bf16[128,384]{1,0:T(8,128)(2,1)S(1)} %get-tuple-element.85), channel_id=1, source_target_pairs={{0,2},{1,3},{2,0},{3,1},{4,6},{5,7},{6,4},{7,5},{8,10},{9,11},{10,... | collective-permute-start | bytes 294920 | tf_op jit(solution)/shard_map/ppermute | solution.py:335
  55.4 5.2 %collective-permute-start.17 = (bf16[64,384]{1,0:T(8,128)(2,1)S(1)}, bf16[64,384]{1,0:T(8,128)(2,1)S(1)}, u32[]{:S(2)}, u32[]{:S(2)}) collective-permute-start(bf16[64,384]{1,0:T(8,128)(2,1)S(1)} %get-tuple-element.87), channel_id=1, source_target_pairs={{0,4},{1,5},{2,6},{3,7},{4,0},{5,1},{6,2},{7,3},{8,12},{9,13},{10,... | collective-permute-start | bytes 147464 | tf_op jit(solution)/shard_map/ppermute | solution.py:335

commit v10 on v9

--- a/solution.py
+++ b/solution.py
@@ -103,17 +103,12 @@
         for dj, rows in enumerate(aside(z, x_ref[:, r].reshape(z.fl * z.w, z.c))):
             beside[dj, r] = rows
     for r in range(z.r):
-        total = jnp.zeros((z.fl * z.w, z.c), F32)
-        for di in range(3):
-            if 0 <= r + di - 1 < z.r:
-                for dj in range(3):
-                    total += jnp.dot(
-                        beside[dj, r + di - 1], w_ref[di, dj], preferred_element_type=F32
-                    )
-        out[r] = total
-
-
-def own_act_kernel(z, part_ref, near_ref, far_ref, w_ref, cot_ref, out, far, near):
+        low, high = max(0, 1 - r), min(3, z.r + 1 - r)
+        pieces = [beside[dj, r + di - 1] for di in range(low, high) for dj in range(3)]
+        out[r] = taps(pieces, w_ref[low:high])
+
+
+def own_act_kernel(z, part_ref, near_ref, far_ref, w_ref, cot_ref, out, near, far):
     lower = even("space")
     first = even("tm")
     for r in range(z.r):
@@ -121,8 +116,7 @@
         for edge, di in ((0, 0), (z.r - 1, 2)):
             if r == edge:
                 rows = jnp.where(lower == (di == 2), near_ref[...], far_ref[...])
-                for dj, rows in enumerate(aside(z, rows)):
-                    total += jnp.dot(rows, w_ref[di, dj], preferred_element_type=F32)
+                total += taps(aside(z, rows), w_ref[di])
         act = silu(total).reshape(z.fl, z.w, z.c)
         out[:, r] = act
         last = act[z.fl - 1]
@@ -149,7 +143,7 @@
         out[:, k * z.c : (k + 1) * z.c] = outer(cot_ref[k:], act_ref[: z.fl - k])
 
 
-def cross_kernel(z, width, part_ref, far_ref, near_ref, act_ref, cot_ref, keep, send):
+def cross_kernel(z, width, part_ref, near_ref, far_ref, act_ref, cot_ref, keep, send):
     mine = even("space")
     before = jnp.where(even("tm"), far_ref[...], near_ref[...])
     after = jnp.where(even("tm"), near_ref[...], far_ref[...])
@@ -203,14 +197,13 @@
     far[...] = jnp.where(lower, out[0], out[z.r - 1])
 
 
+def taps(pieces, weights):
+    rows = jnp.concatenate(pieces, axis=1)
+    return jnp.dot(rows, flat(weights), preferred_element_type=F32)
+
+
 def conv_row(z, w_ref, three):
-    total = jnp.zeros((z.block, z.c), F32)
-    for di, rows in enumerate(three):
-        for dj in range(3):
-            total += jnp.dot(
-                rows[dj * z.f : dj * z.f + z.block], w_ref[di, dj], preferred_element_type=F32
-            )
-    return silu(total)
+    return silu(taps([rows[dj * z.f : dj * z.f + z.block] for rows in three for dj in range(3)], w_ref[...]))
 
 
 def middle_kernel(z, x_ref, w_ref, out):
@@ -258,10 +251,7 @@
         ]
 
     def hide(r):
-        temporal = sum(
-            jnp.dot(late, t_ref[k], preferred_element_type=F32)
-            for k, late in enumerate(held.pop(("a", r)))
-        )
+        temporal = taps(held.pop(("a", r)), t_ref[...])
         hidden = (x_ref[r, z.f : z.f + z.block].astype(F32) + temporal).astype(BF)
         held["h", r] = hidden
 
@@ -431,7 +421,7 @@
         flops=8 * one,
         scratch=[pltpu.VMEM((3, z.r, z.fl * z.w, z.c), BF)],
     )
-    own_act, far, near = call(
+    own_act, near, far = call(
         functools.partial(own_act_kernel, z),
         [shape(frames_in.shape), shape((z.r, z.w, z.c)), shape((z.r, z.w, z.c))],
         own,
@@ -463,14 +453,14 @@
         spatial,
         flops=9 * one * (z.r - 2) // z.r,
     )
-    tied = lax.optimization_barrier((far, near, middle, close, apart))
-    far, near, middle, close, apart = tied
+    tied = lax.optimization_barrier((near, far, middle, close, apart))
+    near, far, middle, close, apart = tied
     keep, send = call(
         functools.partial(cross_kernel, z, width),
         [shape((z.c // 2, 3 * z.c), F32), shape((z.c // 2, 3 * z.c))],
         own_grad,
+        near,
         far,
-        near,
         own_act,
         cotangent,
         flops=3 * one // 4,

time: 62.1 us -> 61.2 us (0.986)
  starting transfers between devices: 29.9 us -> 28.1 us
  waiting for transfers between devices: 6.55 us -> 7.28 us
    ppermute x15, starting transfers between devices: 27.6 us -> 25.7 us  [swap(): return lax.ppermute(value, axis, [(i, i ^ k) for i in range(count)])]
    ppermute x15, waiting for transfers between devices: 6.54 us -> 7.27 us  [swap(): return lax.ppermute(value, axis, [(i, i ^ k) for i in range(count)])]
  transfers between devices with their start and end apart: 18 -> 18, of which waited for: 5 -> 4; matrix products, arithmetic and copies ran while one was open for 0% -> 0% of each run, Pallas kernels for 33% -> 34%
where the time goes in v10:
time: 61.2 us; the launch traced here: 60.2 us
  starting transfers between devices  28.1 us (46%)
  Pallas kernels  22.6 us (37%)
  waiting for transfers between devices  7.28 us (12%)
  local copies, waits for them, and re-layouts  1.32 us (2%)
  between operations  0.92 us (2%)
    ppermute x15, starting transfers between devices, swap(): return lax.ppermute(value, axis, [(i, i ^ k) for i in range(count)])  25.7 us
    pallas_call x14, Pallas kernels, call(): pl.pallas_call(kernel, out_shape=tuple(outs), in_specs=[VMEM] * len(args)...  21.5 us
    ppermute x15, waiting for transfers between devices, swap(): return lax.ppermute(value, axis, [(i, i ^ k) for i in range(count)])  7.27 us
    ppermute x3, starting transfers between devices, swap_both(): far = lax.ppermute(far, axis, pairs + [(b, a) for a, b in pairs])  2.33 us
    unnamed x20, local copies, waits for them, and re-layouts  1.32 us
  transfers between devices with their start and end apart: 18, of which 4 were waited for; matrix products, arithmetic and copies ran while one was open for 0% of the time, Pallas kernels for 34%

profile of v10, /device:TPU:0, one launch (start us, length us, event | category | flops | bytes accessed | tf_op | source)
XLA Modules:
  0.0 60.2 jit_solution(15445038396831700086)
XLA Ops:
  0.6 1.2 %copy-done.1 = bf16[4,4,64,512]{3,2,1,0:T(8,128)(2,1)S(1)} copy-done((bf16[4,4,64,512]{3,2,1,0:T(8,128)(2,1)S(1)}, bf16[4,4,64,512]{3,2,1,0:T(8,128)(2,1)}, u32[]{:S(2)}) %copy-start.1) | copy-done | bytes 1048600
  1.9 0.6 shard_map.105
  2.4 3.0 %collective-permute-start.4 = (bf16[288,512]{1,0:T(8,128)(2,1)S(1)}, bf16[288,512]{1,0:T(8,128)(2,1)S(1)}, u32[]{:S(2)}, u32[]{:S(2)}) collective-permute-start(bf16[288,512]{1,0:T(8,128)(2,1)S(1)} %get-tuple-element.50), channel_id=1, source_target_pairs={{0,8},{8,0},{16,24},{24,16},{1,9},{9,1},{17,25},{25,17},{2,10},{10... | collective-permute-start | bytes 884744 | tf_op jit(solution)/shard_map/ppermute | solution.py:325
  5.4 1.5 %collective-permute-start.5 = (bf16[288,512]{1,0:T(8,128)(2,1)S(1)}, bf16[288,512]{1,0:T(8,128)(2,1)S(1)}, u32[]{:S(2)}, u32[]{:S(2)}) collective-permute-start(bf16[288,512]{1,0:T(8,128)(2,1)S(1)} %get-tuple-element.51), channel_id=1, source_target_pairs={{0,16},{8,24},{16,0},{24,8},{1,17},{9,25},{17,1},{25,9},{2,18},{10... | collective-permute-start | bytes 884744 | tf_op jit(solution)/shard_map/ppermute | solution.py:325
  7.0 0.0 collective-permute-start.6
  7.0 0.1 shard_map.106
  7.0 0.1 collective-permute-start
  7.1 0.0 copy-start
  7.1 0.8 %collective-permute-start.1 = (bf16[256,512]{1,0:T(8,128)(2,1)S(1)}, bf16[256,512]{1,0:T(8,128)(2,1)S(1)}, u32[]{:S(2)}, u32[]{:S(2)}) collective-permute-start(bf16[256,512]{1,0:T(8,128)(2,1)S(1)} %get-tuple-element.47), channel_id=1, source_target_pairs={{1,2},{3,4},{5,6},{2,1},{4,3},{6,5},{9,10},{11,12},{13,14},{10,9},... | collective-permute-start | bytes 786440 | tf_op jit(solution)/shard_map/ppermute | solution.py:330
  8.0 0.1 slice-done.1
  8.0 4.8 %shard_map.104.part_ref = f32[4,256,512]{2,1,0:T(8,128)S(1)} custom-call(bf16[4,4,64,512]{3,2,1,0:T(8,128)(2,1)S(1)} %copy-done.1, bf16[3,3,512,512]{3,2,1,0:T(8,128)(2,1)S(1)} %bitcast.3), custom_call_target="tpu_custom_call" | custom-call | flops 4294967296 | bytes 7864320 | tf_op jit(solution)/shard_map/pallas_call | solution.py:18
  12.8 0.0 collective-permute-done.near_ref
  12.8 0.0 collective-permute-done.1.far_ref
  12.8 1.9 %shard_map.107 = (bf16[4,4,64,512]{3,2,1,0:T(8,128)(2,1)S(1)}, bf16[4,64,512]{2,1,0:T(8,128)(2,1)S(1)}, bf16[4,64,512]{2,1,0:T(8,128)(2,1)S(1)}) custom-call(f32[4,256,512]{2,1,0:T(8,128)S(1)} %shard_map.104.part_ref, bf16[256,512]{1,0:T(8,128)(2,1)S(1)} %collective-permute-done.near_ref, bf16[256,512]{1,0:T(8,128)(2,1)S(1)} %collective-permute-done.1.far_ref, ...), custom_call_target="tpu_custom_call" | custom-call | flops 1610612736 | bytes 9961472 | tf_op jit(solution)/shard_map/pallas_call | solution.py:18
  14.7 2.0 %collective-permute-start.2 = (bf16[4,64,512]{2,1,0:T(8,128)(2,1)S(1)}, bf16[4,64,512]{2,1,0:T(8,128)(2,1)S(1)}, u32[]{:S(2)}, u32[]{:S(2)}) collective-permute-start(bf16[4,64,512]{2,1,0:T(8,128)(2,1)S(1)} %get-tuple-element.48), channel_id=1, source_target_pairs={{0,8},{8,0},{16,24},{24,16},{1,9},{9,1},{17,25},{25,17},{2,10},{10... | collective-permute-start | bytes 786440 | tf_op jit(solution)/shard_map/ppermute | solution.py:325
  16.7 0.7 %collective-permute-start.3 = (bf16[4,64,512]{2,1,0:T(8,128)(2,1)S(1)}, bf16[4,64,512]{2,1,0:T(8,128)(2,1)S(1)}, u32[]{:S(2)}, u32[]{:S(2)}) collective-permute-start(bf16[4,64,512]{2,1,0:T(8,128)(2,1)S(1)} %get-tuple-element.49), channel_id=1, source_target_pairs={{8,16},{16,8},{9,17},{17,9},{10,18},{18,10},{11,19},{19,11},{12,20... | collective-permute-start | bytes 786440 | tf_op jit(solution)/shard_map/ppermute | solution.py:330
  17.4 0.0 collective-permute-done.4.refs_1_
  17.4 2.8 %collective-permute-done.5.refs_2_ = bf16[288,512]{1,0:T(8,128)(2,1)S(1)} collective-permute-done((bf16[288,512]{1,0:T(8,128)(2,1)S(1)}, bf16[288,512]{1,0:T(8,128)(2,1)S(1)}, u32[]{:S(2)}, u32[]{:S(2)}) %collective-permute-start.5) | collective-permute-done | bytes 294944 | tf_op jit(solution)/shard_map/ppermute | solution.py:325
  20.2 0.5 shard_map.108
  20.7 0.1 collective-permute-start.7
  20.8 0.9 %collective-permute-start.8 = (bf16[288,512]{1,0:T(8,128)(2,1)S(1)}, bf16[288,512]{1,0:T(8,128)(2,1)S(1)}, u32[]{:S(2)}, u32[]{:S(2)}) collective-permute-start(bf16[288,512]{1,0:T(8,128)(2,1)S(1)} %get-tuple-element.55), channel_id=1, source_target_pairs={{1,2},{3,4},{5,6},{2,1},{4,3},{6,5},{9,10},{11,12},{13,14},{10,9},... | collective-permute-start | bytes 884744 | tf_op jit(solution)/shard_map/ppermute | solution.py:330
  21.7 1.4 %shard_map.110.part_ref = f32[512,1536]{1,0:T(8,128)S(1)} custom-call(bf16[4,4,64,512]{3,2,1,0:T(8,128)(2,1)S(1)} %get-tuple-element.57.act_ref, bf16[4,4,64,512]{3,2,1,0:T(8,128)(2,1)S(1)} %copy-done), custom_call_target="tpu_custom_call" | custom-call | flops 1207959552 | bytes 5242880 | tf_op jit(solution)/shard_map/pallas_call | solution.py:18
  23.1 2.7 %shard_map.109.middle_ref = bf16[2,256,512]{2,1,0:T(8,128)(2,1)S(1)} custom-call(bf16[4,288,512]{2,1,0:T(8,128)(2,1)S(1)} %get-tuple-element.61.x_ref, bf16[3,3,512,512]{3,2,1,0:T(8,128)(2,1)S(1)} %bitcast.3), custom_call_target="tpu_custom_call" | custom-call | flops 2415919104 | bytes 6422528 | tf_op jit(solution)/shard_map/pallas_call | solution.py:18
  25.8 0.0 collective-permute-done.7.near_ref
  25.8 0.7 %shard_map.111 = (f32[256,1536]{1,0:T(8,128)S(1)}, bf16[256,1536]{1,0:T(8,128)(2,1)S(1)}) custom-call(f32[512,1536]{1,0:T(8,128)S(1)} %shard_map.110.part_ref, bf16[4,64,512]{2,1,0:T(8,128)(2,1)S(1)} %collective-permute-done.2.near_ref, bf16[4,64,512]{2,1,0:T(8,128)(2,1)S(1)} %collective-permute-done.3.far_ref, ...), custom_call_target="tpu_custom_call" | custom-call | flops 402653184 | bytes 8126464 | tf_op jit(solution)/shard_map/pallas_call | solution.py:18
  26.5 3.6 %collective-permute-start.9 = (bf16[256,1536]{1,0:T(8,128)(2,1)S(1)}, bf16[256,1536]{1,0:T(8,128)(2,1)S(1)}, u32[]{:S(2)}, u32[]{:S(2)}) collective-permute-start(bf16[256,1536]{1,0:T(8,128)(2,1)S(1)} %get-tuple-element.60), channel_id=1, source_target_pairs={{0,1},{1,0},{2,3},{3,2},{4,5},{5,4},{6,7},{7,6},{8,9},{9,8},{10,11... | collective-permute-start | bytes 2359304 | tf_op jit(solution)/shard_map/ppermute | solution.py:325
  30.0 2.7 %shard_map.112.border_ref = bf16[2,256,512]{2,1,0:T(8,128)(2,1)S(1)} custom-call(bf16[4,288,512]{2,1,0:T(8,128)(2,1)S(1)} %get-tuple-element.61.x_ref, bf16[288,512]{1,0:T(8,128)(2,1)S(1)} %collective-permute-done.7.near_ref, bf16[288,512]{1,0:T(8,128)(2,1)S(1)} %collective-permute-done.8.far_ref, bf16[3,3,512,512]{3,2,1,0:T(8,128)(2,1)S(1)} %bitcast.3), custom_call_target="tpu_custom_call" | custom-call | flops 2415919104 | bytes 7012352 | tf_op jit(solution)/shard_map/pallas_call | solution.py:18
  32.7 0.0 copy-start.2
  32.7 0.0 copy-start.3
  32.8 0.0 copy-start.7
  32.8 0.0 collective-permute-done.9.got_ref
  32.8 0.3 shard_map.113
  33.1 3.3 %collective-permute-start.13 = (bf16[256,384]{1,0:T(8,128)(2,1)S(1)}, bf16[256,384]{1,0:T(8,128)(2,1)S(1)}, u32[]{:S(2)}, u32[]{:S(2)}) collective-permute-start(bf16[256,384]{1,0:T(8,128)(2,1)S(1)} %get-tuple-element.77), channel_id=1, source_target_pairs={{0,8},{8,0},{16,24},{24,16},{1,9},{9,1},{17,25},{25,17},{2,10},{10... | collective-permute-start | bytes 589832 | tf_op jit(solution)/shard_map/ppermute | solution.py:325
  36.4 0.0 collective-permute-start.14
  36.4 1.5 %collective-permute-start.15 = (bf16[256,384]{1,0:T(8,128)(2,1)S(1)}, bf16[256,384]{1,0:T(8,128)(2,1)S(1)}, u32[]{:S(2)}, u32[]{:S(2)}) collective-permute-start(bf16[256,384]{1,0:T(8,128)(2,1)S(1)} %get-tuple-element.79), channel_id=1, source_target_pairs={{0,24},{8,16},{16,8},{24,0},{1,25},{9,17},{17,9},{25,1},{2,26},{10... | collective-permute-start | bytes 589832 | tf_op jit(solution)/shard_map/ppermute | solution.py:325
  38.0 5.3 %shard_map.114 = (bf16[4,64,512]{2,1,0:T(8,128)(2,1)S(1)}, bf16[4,64,512]{2,1,0:T(8,128)(2,1)S(1)}, bf16[4,64,512]{2,1,0:T(8,128)(2,1)S(1)}, bf16[4,64,512]{2,1,0:T(8,128)(2,1)S(1)}) custom-call(bf16[2,256,512]{2,1,0:T(8,128)(2,1)S(1)} %shard_map.109.middle_ref, bf16[2,256,512]{2,1,0:T(8,128)(2,1)S(1)} %shard_map.112.border_ref, ...), custom_call_target="tpu_custom_call" | custom-call | flops 4831838208 | bytes 6948864 | tf_op jit(solution)/shard_map/pallas_call | solution.py:18
  43.3 2.0 %collective-permute-start.10 = (bf16[4,64,512]{2,1,0:T(8,128)(2,1)S(1)}, bf16[4,64,512]{2,1,0:T(8,128)(2,1)S(1)}, u32[]{:S(2)}, u32[]{:S(2)}) collective-permute-start(bf16[4,64,512]{2,1,0:T(8,128)(2,1)S(1)} %get-tuple-element.73), channel_id=1, source_target_pairs={{0,8},{8,0},{16,24},{24,16},{1,9},{9,1},{17,25},{25,17},{2,10},{10... | collective-permute-start | bytes 786440 | tf_op jit(solution)/shard_map/ppermute | solution.py:325
  45.3 0.0 collective-permute-start.11
  45.3 1.5 %collective-permute-start.12 = (bf16[4,64,512]{2,1,0:T(8,128)(2,1)S(1)}, bf16[4,64,512]{2,1,0:T(8,128)(2,1)S(1)}, u32[]{:S(2)}, u32[]{:S(2)}) collective-permute-start(bf16[4,64,512]{2,1,0:T(8,128)(2,1)S(1)} %get-tuple-element.75), channel_id=1, source_target_pairs={{0,24},{8,16},{16,8},{24,0},{1,25},{9,17},{17,9},{25,1},{2,26},{10... | collective-permute-start | bytes 786440 | tf_op jit(solution)/shard_map/ppermute | solution.py:325
  46.9 0.7 %collective-permute-done.14.refs_2_ = bf16[256,384]{1,0:T(8,128)(2,1)S(1)} collective-permute-done((bf16[256,384]{1,0:T(8,128)(2,1)S(1)}, bf16[256,384]{1,0:T(8,128)(2,1)S(1)}, u32[]{:S(2)}, u32[]{:S(2)}) %collective-permute-start.14) | collective-permute-done | bytes 196640 | tf_op jit(solution)/shard_map/ppermute | solution.py:325
  47.5 0.1 shard_map.116
  47.6 3.9 %collective-permute-start.16 = (bf16[128,384]{1,0:T(8,128)(2,1)S(1)}, bf16[128,384]{1,0:T(8,128)(2,1)S(1)}, u32[]{:S(2)}, u32[]{:S(2)}) collective-permute-start(bf16[128,384]{1,0:T(8,128)(2,1)S(1)} %get-tuple-element.85), channel_id=1, source_target_pairs={{0,2},{1,3},{2,0},{3,1},{4,6},{5,7},{6,4},{7,5},{8,10},{9,11},{10,... | collective-permute-start | bytes 294920 | tf_op jit(solution)/shard_map/ppermute | solution.py:325
  51.6 2.6 %collective-permute-done.16.refs_1_ = bf16[128,384]{1,0:T(8,128)(2,1)S(1)} collective-permute-done((bf16[128,384]{1,0:T(8,128)(2,1)S(1)}, bf16[128,384]{1,0:T(8,128)(2,1)S(1)}, u32[]{:S(2)}, u32[]{:S(2)}) %collective-permute-start.16) | collective-permute-done | bytes 98336 | tf_op jit(solution)/shard_map/ppermute | solution.py:325
  54.2 3.1 %collective-permute-start.17 = (bf16[64,384]{1,0:T(8,128)(2,1)S(1)}, bf16[64,384]{1,0:T(8,128)(2,1)S(1)}, u32[]{:S(2)}, u32[]{:S(2)}) collective-permute-start(bf16[64,384]{1,0:T(8,128)(2,1)S(1)} %get-tuple-element.87), channel_id=1, source_target_pairs={{0,4},{1,5},{2,6},{3,7},{4,0},{5,1},{6,2},{7,3},{8,12},{9,13},{10,... | collective-permute-start | bytes 147464 | tf_op jit(solution)/shard_map/ppermute | solution.py:325
  57.3 1.1 %collective-permute-done.11.refs_2_ = bf16[4,64,512]{2,1,0:T(8,128)(2,1)S(1)} collective-permute-done((bf16[4,64,512]{2,1,0:T(8,128)(2,1)S(1)}, bf16[4,64,512]{2,1,0:T(8,128)(2,1)S(1)}, u32[]{:S(2)}, u32[]{:S(2)}) %collective-permute-start.11) | collective-permute-done | bytes 262176 | tf_op jit(solution)/shard_map/ppermute | solution.py:325
  58.5 0.0 collective-permute-done.12.refs_3_
  58.5 1.0 %shard_map.115 = bf16[4,4,64,512]{3,2,1,0:T(8,128)(2,1)} custom-call(bf16[4,64,512]{2,1,0:T(8,128)(2,1)S(1)} %get-tuple-element.72.refs_0_, bf16[4,64,512]{2,1,0:T(8,128)(2,1)S(1)} %collective-permute-done.10.refs_1_, bf16[4,64,512]{2,1,0:T(8,128)(2,1)S(1)} %collective-permute-done.11.refs_2_, bf16[4,64,512]{2,1,0:T(8,128)(2,1)S(1)} %collective-permute-done.12.refs_3_), custom_call_target="tpu_custom_call" | custom-call | bytes 4194304 | tf_op jit(solution)/shard_map/pallas_call | solution.py:369
  59.5 0.7 %shard_map.118 = f32[3,64,128]{2,1,0:T(8,128)} custom-call(f32[64,384]{1,0:T(8,128)S(1)} %get-tuple-element.86.refs_0_, bf16[64,384]{1,0:T(8,128)(2,1)S(1)} %collective-permute-done.17.refs_1_), custom_call_target="tpu_custom_call" | custom-call | bytes 245760 | tf_op jit(solution)/shard_map/pallas_call | solution.py:18
  (24 shorter events, 0.1 us)
Async XLA Ops:
  0.6 1.2 %copy-start.1 = (bf16[4,4,64,512]{3,2,1,0:T(8,128)(2,1)S(1)}, bf16[4,4,64,512]{3,2,1,0:T(8,128)(2,1)}, u32[]{:S(2)}) copy-start(bf16[4,4,64,512]{3,2,1,0:T(8,128)(2,1)} %x_ref.5) | copy-start | bytes 3145732
  1.9 6.1 %slice-start = ((s8[4718592]{0:T(1024)(128)(4,1)}), s8[4194304]{0:T(1024)(128)(4,1)S(1)}, s32[]{:S(2)}) async-start(s8[4718592]{0:T(1024)(128)(4,1)} %bitcast.2), calls=%async_computation | async-start | bytes 8388608
  2.4 15.0 %collective-permute-start.4 = (bf16[288,512]{1,0:T(8,128)(2,1)S(1)}, bf16[288,512]{1,0:T(8,128)(2,1)S(1)}, u32[]{:S(2)}, u32[]{:S(2)}) collective-permute-start(bf16[288,512]{1,0:T(8,128)(2,1)S(1)} %get-tuple-element.50), channel_id=1, source_target_pairs={{0,8},{8,0},{16,24},{24,16},{1,9},{9,1},{17,25},{25,17},{2,10},{10... | collective-permute-start | bytes 884744 | tf_op jit(solution)/shard_map/ppermute | solution.py:325
  5.4 14.8 %collective-permute-start.5 = (bf16[288,512]{1,0:T(8,128)(2,1)S(1)}, bf16[288,512]{1,0:T(8,128)(2,1)S(1)}, u32[]{:S(2)}, u32[]{:S(2)}) collective-permute-start(bf16[288,512]{1,0:T(8,128)(2,1)S(1)} %get-tuple-element.51), channel_id=1, source_target_pairs={{0,16},{8,24},{16,0},{24,8},{1,17},{9,25},{17,1},{25,9},{2,18},{10... | collective-permute-start | bytes 884744 | tf_op jit(solution)/shard_map/ppermute | solution.py:325
  7.0 13.3 %collective-permute-start.6 = (bf16[288,512]{1,0:T(8,128)(2,1)S(1)}, bf16[288,512]{1,0:T(8,128)(2,1)S(1)}, u32[]{:S(2)}, u32[]{:S(2)}) collective-permute-start(bf16[288,512]{1,0:T(8,128)(2,1)S(1)} %get-tuple-element.52), channel_id=1, source_target_pairs={{0,24},{8,16},{16,8},{24,0},{1,25},{9,17},{17,9},{25,1},{2,26},{10... | collective-permute-start | bytes 884744 | tf_op jit(solution)/shard_map/ppermute | solution.py:325
  7.0 1.0 %slice-start.1 = ((s8[4718592]{0:T(1024)(128)(4,1)}), s8[524288]{0:T(1024)(128)(4,1)S(1)}, s32[]{:S(2)}) async-start(s8[4718592]{0:T(1024)(128)(4,1)} %bitcast.2), calls=%async_computation.1 | async-start | bytes 1048576
  7.0 5.7 %collective-permute-start = (bf16[256,512]{1,0:T(8,128)(2,1)S(1)}, bf16[256,512]{1,0:T(8,128)(2,1)S(1)}, u32[]{:S(2)}, u32[]{:S(2)}) collective-permute-start(bf16[256,512]{1,0:T(8,128)(2,1)S(1)} %get-tuple-element.46), channel_id=1, source_target_pairs={{0,1},{1,0},{2,3},{3,2},{4,5},{5,4},{6,7},{7,6},{8,9},{9,8},{10,11... | collective-permute-start | bytes 786440 | tf_op jit(solution)/shard_map/ppermute | solution.py:325
  7.1 5.7 %copy-start = (bf16[4,4,64,512]{3,2,1,0:T(8,128)(2,1)S(1)}, bf16[4,4,64,512]{3,2,1,0:T(8,128)(2,1)}, u32[]{:S(2)}) copy-start(bf16[4,4,64,512]{3,2,1,0:T(8,128)(2,1)} %cot_ref.5) | copy-start | bytes 3145732
  7.1 5.7 %collective-permute-start.1 = (bf16[256,512]{1,0:T(8,128)(2,1)S(1)}, bf16[256,512]{1,0:T(8,128)(2,1)S(1)}, u32[]{:S(2)}, u32[]{:S(2)}) collective-permute-start(bf16[256,512]{1,0:T(8,128)(2,1)S(1)} %get-tuple-element.47), channel_id=1, source_target_pairs={{1,2},{3,4},{5,6},{2,1},{4,3},{6,5},{9,10},{11,12},{13,14},{10,9},... | collective-permute-start | bytes 786440 | tf_op jit(solution)/shard_map/ppermute | solution.py:330
  14.7 11.1 %collective-permute-start.2 = (bf16[4,64,512]{2,1,0:T(8,128)(2,1)S(1)}, bf16[4,64,512]{2,1,0:T(8,128)(2,1)S(1)}, u32[]{:S(2)}, u32[]{:S(2)}) collective-permute-start(bf16[4,64,512]{2,1,0:T(8,128)(2,1)S(1)} %get-tuple-element.48), channel_id=1, source_target_pairs={{0,8},{8,0},{16,24},{24,16},{1,9},{9,1},{17,25},{25,17},{2,10},{10... | collective-permute-start | bytes 786440 | tf_op jit(solution)/shard_map/ppermute | solution.py:325
  16.7 9.1 %collective-permute-start.3 = (bf16[4,64,512]{2,1,0:T(8,128)(2,1)S(1)}, bf16[4,64,512]{2,1,0:T(8,128)(2,1)S(1)}, u32[]{:S(2)}, u32[]{:S(2)}) collective-permute-start(bf16[4,64,512]{2,1,0:T(8,128)(2,1)S(1)} %get-tuple-element.49), channel_id=1, source_target_pairs={{8,16},{16,8},{9,17},{17,9},{10,18},{18,10},{11,19},{19,11},{12,20... | collective-permute-start | bytes 786440 | tf_op jit(solution)/shard_map/ppermute | solution.py:330
  20.7 5.1 %collective-permute-start.7 = (bf16[288,512]{1,0:T(8,128)(2,1)S(1)}, bf16[288,512]{1,0:T(8,128)(2,1)S(1)}, u32[]{:S(2)}, u32[]{:S(2)}) collective-permute-start(bf16[288,512]{1,0:T(8,128)(2,1)S(1)} %get-tuple-element.54), channel_id=1, source_target_pairs={{0,1},{1,0},{2,3},{3,2},{4,5},{5,4},{6,7},{7,6},{8,9},{9,8},{10,11... | collective-permute-start | bytes 884744 | tf_op jit(solution)/shard_map/ppermute | solution.py:325
  20.8 5.0 %collective-permute-start.8 = (bf16[288,512]{1,0:T(8,128)(2,1)S(1)}, bf16[288,512]{1,0:T(8,128)(2,1)S(1)}, u32[]{:S(2)}, u32[]{:S(2)}) collective-permute-start(bf16[288,512]{1,0:T(8,128)(2,1)S(1)} %get-tuple-element.55), channel_id=1, source_target_pairs={{1,2},{3,4},{5,6},{2,1},{4,3},{6,5},{9,10},{11,12},{13,14},{10,9},... | collective-permute-start | bytes 884744 | tf_op jit(solution)/shard_map/ppermute | solution.py:330
  26.5 6.3 %collective-permute-start.9 = (bf16[256,1536]{1,0:T(8,128)(2,1)S(1)}, bf16[256,1536]{1,0:T(8,128)(2,1)S(1)}, u32[]{:S(2)}, u32[]{:S(2)}) collective-permute-start(bf16[256,1536]{1,0:T(8,128)(2,1)S(1)} %get-tuple-element.60), channel_id=1, source_target_pairs={{0,1},{1,0},{2,3},{3,2},{4,5},{5,4},{6,7},{7,6},{8,9},{9,8},{10,11... | collective-permute-start | bytes 2359304 | tf_op jit(solution)/shard_map/ppermute | solution.py:325
  30.0 7.9 %copy-start.4 = (bf16[512,512]{1,0:T(8,128)(2,1)S(1)}, bf16[512,512]{1,0:T(8,128)(2,1)}, u32[]{:S(2)}) copy-start(bf16[512,512]{1,0:T(8,128)(2,1)} %k_ref.1) | copy-start | bytes 1572868
  30.0 7.9 %copy-start.5 = (bf16[512,512]{1,0:T(8,128)(2,1)S(1)}, bf16[512,512]{1,0:T(8,128)(2,1)}, u32[]{:S(2)}) copy-start(bf16[512,512]{1,0:T(8,128)(2,1)} %v_ref.1) | copy-start | bytes 1572868
  30.0 7.9 %copy-start.6 = (bf16[512,512]{1,0:T(8,128)(2,1)S(1)}, bf16[512,512]{1,0:T(8,128)(2,1)}, u32[]{:S(2)}) copy-start(bf16[512,512]{1,0:T(8,128)(2,1)} %o_ref.1) | copy-start | bytes 1572868
  32.7 5.3 %copy-start.2 = (bf16[3,512,512]{2,1,0:T(8,128)(2,1)S(1)}, bf16[3,512,512]{2,1,0:T(8,128)(2,1)}, u32[]{:S(2)}) copy-start(bf16[3,512,512]{2,1,0:T(8,128)(2,1)} %t_ref.1) | copy-start | bytes 4718596
  32.7 5.3 %copy-start.3 = (bf16[512,512]{1,0:T(8,128)(2,1)S(1)}, bf16[512,512]{1,0:T(8,128)(2,1)}, u32[]{:S(2)}) copy-start(bf16[512,512]{1,0:T(8,128)(2,1)} %q_ref.1) | copy-start | bytes 1572868
  32.8 5.2 %copy-start.7 = (f32[512]{0:T(512)S(1)}, f32[512]{0:T(512)}, u32[]{:S(2)}) copy-start(f32[512]{0:T(512)} %param.12) | copy-start | bytes 6148
  33.1 12.2 %collective-permute-start.13 = (bf16[256,384]{1,0:T(8,128)(2,1)S(1)}, bf16[256,384]{1,0:T(8,128)(2,1)S(1)}, u32[]{:S(2)}, u32[]{:S(2)}) collective-permute-start(bf16[256,384]{1,0:T(8,128)(2,1)S(1)} %get-tuple-element.77), channel_id=1, source_target_pairs={{0,8},{8,0},{16,24},{24,16},{1,9},{9,1},{17,25},{25,17},{2,10},{10... | collective-permute-start | bytes 589832 | tf_op jit(solution)/shard_map/ppermute | solution.py:325
  36.4 11.1 %collective-permute-start.14 = (bf16[256,384]{1,0:T(8,128)(2,1)S(1)}, bf16[256,384]{1,0:T(8,128)(2,1)S(1)}, u32[]{:S(2)}, u32[]{:S(2)}) collective-permute-start(bf16[256,384]{1,0:T(8,128)(2,1)S(1)} %get-tuple-element.78), channel_id=1, source_target_pairs={{0,16},{8,24},{16,0},{24,8},{1,17},{9,25},{17,1},{25,9},{2,18},{10... | collective-permute-start | bytes 589832 | tf_op jit(solution)/shard_map/ppermute | solution.py:325
  36.4 11.1 %collective-permute-start.15 = (bf16[256,384]{1,0:T(8,128)(2,1)S(1)}, bf16[256,384]{1,0:T(8,128)(2,1)S(1)}, u32[]{:S(2)}, u32[]{:S(2)}) collective-permute-start(bf16[256,384]{1,0:T(8,128)(2,1)S(1)} %get-tuple-element.79), channel_id=1, source_target_pairs={{0,24},{8,16},{16,8},{24,0},{1,25},{9,17},{17,9},{25,1},{2,26},{10... | collective-permute-start | bytes 589832 | tf_op jit(solution)/shard_map/ppermute | solution.py:325
  43.3 14.0 %collective-permute-start.10 = (bf16[4,64,512]{2,1,0:T(8,128)(2,1)S(1)}, bf16[4,64,512]{2,1,0:T(8,128)(2,1)S(1)}, u32[]{:S(2)}, u32[]{:S(2)}) collective-permute-start(bf16[4,64,512]{2,1,0:T(8,128)(2,1)S(1)} %get-tuple-element.73), channel_id=1, source_target_pairs={{0,8},{8,0},{16,24},{24,16},{1,9},{9,1},{17,25},{25,17},{2,10},{10... | collective-permute-start | bytes 786440 | tf_op jit(solution)/shard_map/ppermute | solution.py:325
  45.3 13.1 %collective-permute-start.11 = (bf16[4,64,512]{2,1,0:T(8,128)(2,1)S(1)}, bf16[4,64,512]{2,1,0:T(8,128)(2,1)S(1)}, u32[]{:S(2)}, u32[]{:S(2)}) collective-permute-start(bf16[4,64,512]{2,1,0:T(8,128)(2,1)S(1)} %get-tuple-element.74), channel_id=1, source_target_pairs={{0,16},{8,24},{16,0},{24,8},{1,17},{9,25},{17,1},{25,9},{2,18},{10... | collective-permute-start | bytes 786440 | tf_op jit(solution)/shard_map/ppermute | solution.py:325
  45.3 13.1 %collective-permute-start.12 = (bf16[4,64,512]{2,1,0:T(8,128)(2,1)S(1)}, bf16[4,64,512]{2,1,0:T(8,128)(2,1)S(1)}, u32[]{:S(2)}, u32[]{:S(2)}) collective-permute-start(bf16[4,64,512]{2,1,0:T(8,128)(2,1)S(1)} %get-tuple-element.75), channel_id=1, source_target_pairs={{0,24},{8,16},{16,8},{24,0},{1,25},{9,17},{17,9},{25,1},{2,26},{10... | collective-permute-start | bytes 786440 | tf_op jit(solution)/shard_map/ppermute | solution.py:325
  47.6 6.5 %collective-permute-start.16 = (bf16[128,384]{1,0:T(8,128)(2,1)S(1)}, bf16[128,384]{1,0:T(8,128)(2,1)S(1)}, u32[]{:S(2)}, u32[]{:S(2)}) collective-permute-start(bf16[128,384]{1,0:T(8,128)(2,1)S(1)} %get-tuple-element.85), channel_id=1, source_target_pairs={{0,2},{1,3},{2,0},{3,1},{4,6},{5,7},{6,4},{7,5},{8,10},{9,11},{10,... | collective-permute-start | bytes 294920 | tf_op jit(solution)/shard_map/ppermute | solution.py:325
  54.2 5.3 %collective-permute-start.17 = (bf16[64,384]{1,0:T(8,128)(2,1)S(1)}, bf16[64,384]{1,0:T(8,128)(2,1)S(1)}, u32[]{:S(2)}, u32[]{:S(2)}) collective-permute-start(bf16[64,384]{1,0:T(8,128)(2,1)S(1)} %get-tuple-element.87), channel_id=1, source_target_pairs={{0,4},{1,5},{2,6},{3,7},{4,0},{5,1},{6,2},{7,3},{8,12},{9,13},{10,... | collective-permute-start | bytes 147464 | tf_op jit(solution)/shard_map/ppermute | solution.py:325

commit v11 on v10

--- a/solution.py
+++ b/solution.py
@@ -108,20 +108,15 @@
         out[r] = taps(pieces, w_ref[low:high])
 
 
-def own_act_kernel(z, part_ref, near_ref, far_ref, w_ref, cot_ref, out, near, far):
+def own_act_kernel(z, part_ref, near_ref, far_ref, w_ref, out):
     lower = even("space")
-    first = even("tm")
     for r in range(z.r):
         total = part_ref[r]
         for edge, di in ((0, 0), (z.r - 1, 2)):
             if r == edge:
                 rows = jnp.where(lower == (di == 2), near_ref[...], far_ref[...])
                 total += taps(aside(z, rows), w_ref[di])
-        act = silu(total).reshape(z.fl, z.w, z.c)
-        out[:, r] = act
-        last = act[z.fl - 1]
-        near[r] = jnp.where(first, last, cot_ref[0, r])
-        far[r] = jnp.where(first, cot_ref[0, r], last)
+        out[:, r] = silu(total).reshape(z.fl, z.w, z.c)
 
 
 def silu(total):
@@ -143,18 +138,55 @@
         out[:, k * z.c : (k + 1) * z.c] = outer(cot_ref[k:], act_ref[: z.fl - k])
 
 
-def cross_kernel(z, width, part_ref, near_ref, far_ref, act_ref, cot_ref, keep, send):
+def head_kernel(z, cot_ref, after_ref, keep, send):
+    me = lax.axis_index("tm")
+
+    def source(q):
+        k = q // (2 * z.wc)
+        return q % (2 * z.wc) // z.wc * z.w + (me ^ k) * z.wc + q % z.wc
+
+    matrix = chooser(2 * z.w, 2 * z.w, source)
+    for r in range(z.r):
+        cut = moved(matrix, flat(cot_ref[0:2, r]))
+        for k in range(z.n):
+            out = (keep, send)[k % 2]
+            out[k // 2, r] = cut[2 * z.wc * k : 2 * z.wc * (k + 1)]
+
+
+def relay_kernel(picks, *refs):
+    for i, (array, place) in enumerate(picks):
+        refs[-1][i] = refs[array][place]
+
+
+def cross_kernel(z, width, picks, part_ref, middle_ref, border_ref, *refs):
+    heads, (keep, send, cot, late) = refs[:-4], refs[-4:]
+    me = lax.axis_index("tm")
+    count = 2 * z.n * z.wc
+
+    def head(q):
+        s = q % (2 * z.n) // 2
+        return ((me ^ s) * 2 + q % 2) * z.wc + q // (2 * z.n)
+
+    def earlier(k, q):
+        s = q % (2 * z.n) // 2
+        return jnp.where((s > 0) & (q % 2 < k), q // (2 * z.n) * z.f + s * z.fl + q % 2 - k, -1)
+
+    first = chooser(count, count, head)
+    backs = [chooser(count, z.block, functools.partial(earlier, k)) for k in (1, 2)]
+    for r in range(z.r):
+        rows = slice(r * count, (r + 1) * count)
+        pieces = [heads[array][place, r] for array, place in picks]
+        cot[rows] = moved(first, jnp.concatenate(pieces, axis=0))
+        act = border_ref[r // (z.r - 1)] if r in (0, z.r - 1) else middle_ref[r - 1]
+        for k in (1, 2):
+            late[rows, (k - 1) * z.c : k * z.c] = moved(backs[k - 1], act)
+    added = outer(cot[...], late[...])
     mine = even("space")
-    before = jnp.where(even("tm"), far_ref[...], near_ref[...])
-    after = jnp.where(even("tm"), near_ref[...], far_ref[...])
     for k in range(3):
         lanes = slice(k * z.c, (k + 1) * z.c)
         grad = part_ref[:, lanes]
-        if k == 1:
-            grad += outer(cot_ref[0], before)
-        if k == 2:
-            grad += outer(cot_ref[1], before)
-            grad += outer(after, act_ref[z.fl - 2])
+        if k:
+            grad += added[:, (k - 1) * z.c : k * z.c]
         for i in range(z.c // (2 * width)):
             low = grad[2 * i * width : (2 * i + 1) * width]
             high = grad[(2 * i + 1) * width : (2 * i + 2) * width]
@@ -226,20 +258,9 @@
                 stage(step - late)
 
 
-def main_kernel(
-    z, middle_ref, border_ref, x_ref, t_ref, gain_ref, q_ref, k_ref, v_ref, o_ref, *outs
+def norm_kernel(
+    z, middle_ref, border_ref, x_ref, t_ref, gain_ref, hidden_ref, normed_ref
 ):
-    me = lax.axis_index("tm")
-    a = lax.broadcasted_iota(jnp.int32, (z.block, z.block), 0)
-    b = lax.broadcasted_iota(jnp.int32, (z.block, z.block), 1)
-    allowed = (a // z.f == b // z.f) & (b % z.f <= a % z.f)
-    scale = float(z.c) ** -0.5
-
-    def source(q):
-        t = ((me ^ (q // z.piece)) * z.fl) + q % z.piece // z.wc
-        return q % z.wc * z.f + t
-
-    back = chooser(z.block, z.block, source)
     frame = lax.broadcasted_iota(jnp.int32, (z.block, z.c), 0) % z.f
     held = {}
 
@@ -253,15 +274,33 @@
     def hide(r):
         temporal = taps(held.pop(("a", r)), t_ref[...])
         hidden = (x_ref[r, z.f : z.f + z.block].astype(F32) + temporal).astype(BF)
+        hidden_ref[r] = hidden
         held["h", r] = hidden
 
     def norm(r):
-        wide = held["h", r].astype(F32)
+        wide = held.pop(("h", r)).astype(F32)
         mean = jnp.mean(wide * wide, axis=1, keepdims=True)
-        held["n", r] = (wide * (1.0 / jnp.sqrt(mean + 1e-06)) * gain_ref[...]).astype(BF)
+        normed_ref[r] = (wide * (1.0 / jnp.sqrt(mean + 1e-06)) * gain_ref[...]).astype(BF)
+
+    staged(z, (activate, hide, norm))
+
+
+def attend_kernel(z, hidden_ref, normed_ref, q_ref, k_ref, v_ref, o_ref, *outs):
+    me = lax.axis_index("tm")
+    a = lax.broadcasted_iota(jnp.int32, (z.block, z.block), 0)
+    b = lax.broadcasted_iota(jnp.int32, (z.block, z.block), 1)
+    allowed = (a // z.f == b // z.f) & (b % z.f <= a % z.f)
+    scale = float(z.c) ** -0.5
+
+    def source(q):
+        t = ((me ^ (q // z.piece)) * z.fl) + q % z.piece // z.wc
+        return q % z.wc * z.f + t
+
+    back = chooser(z.block, z.block, source)
+    held = {}
 
     def project(r):
-        rows = held.pop(("n", r))
+        rows = normed_ref[r]
         held["q", r], held["k", r], held["v", r] = (
             jnp.dot(rows, w[...], preferred_element_type=F32).astype(BF)
             for w in (q_ref, k_ref, v_ref)
@@ -287,7 +326,7 @@
         held["a", r] = (mixed * held.pop(("t", r))).astype(BF)
 
     def finish(r):
-        encoded = held.pop(("h", r)).astype(F32) + jnp.dot(
+        encoded = hidden_ref[r].astype(F32) + jnp.dot(
             held.pop(("a", r)), o_ref[...], preferred_element_type=F32
         )
         held["e", r] = encoded.astype(BF)
@@ -297,7 +336,7 @@
         for k in range(z.n):
             outs[k][r] = encoded[k * z.piece : (k + 1) * z.piece]
 
-    staged(z, (activate, hide, norm, project, score, weigh, mix, finish, spread))
+    staged(z, (project, score, weigh, mix, finish, spread))
 
 
 def split_kernel(z, keep_ref, got_ref, *outs):
@@ -421,17 +460,36 @@
         flops=8 * one,
         scratch=[pltpu.VMEM((3, z.r, z.fl * z.w, z.c), BF)],
     )
-    own_act, near, far = call(
+    (own_act,) = call(
         functools.partial(own_act_kernel, z),
-        [shape(frames_in.shape), shape((z.r, z.w, z.c)), shape((z.r, z.w, z.c))],
+        [shape(frames_in.shape)],
         own,
         near,
         far,
         spatial,
+        flops=3 * one,
+    )
+    kept, sent = call(
+        functools.partial(head_kernel, z),
+        [shape((n // 2, z.r, 2 * z.wc, z.c))] * 2,
         cotangent,
-        flops=3 * one,
-    )
-    near, far = swap_both(near, far, "tm")
+        own_act,
+    )
+    arrays = [kept, swap(sent, "tm", 1)]
+    heads = [(0, i, 2 * i, 0) for i in range(n // 2)] + [(1, i, 2 * i, 1) for i in range(n // 2)]
+    bit = 2
+    while bit < n:
+        picks = [head for head in heads if head[2] & bit]
+        (relayed,) = call(
+            functools.partial(relay_kernel, [head[:2] for head in picks]),
+            [shape((len(picks),) + kept.shape[1:])],
+            *arrays,
+        )
+        moves = [(len(arrays), i, k ^ bit, s ^ bit) for i, (_, _, k, s) in enumerate(picks)]
+        heads = [head for head in heads if not head[2] & bit] + moves
+        arrays.append(swap(relayed, "tm", bit))
+        bit *= 2
+    heads = [head[:2] for head in sorted(heads, key=lambda head: head[3])]
     (own_grad,) = call(
         functools.partial(own_grad_kernel, z),
         [shape((z.c, 3 * z.c), F32)],
@@ -440,6 +498,7 @@
         flops=9 * one // 4,
     )
     line = z.block + 2 * z.f
+    own_grad, *got = lax.optimization_barrier((own_grad, *got))
     x, close, apart = call(
         functools.partial(assemble_kernel, z),
         [shape((z.r, line, z.c)), shape((line, z.c)), shape((line, z.c))],
@@ -453,20 +512,6 @@
         spatial,
         flops=9 * one * (z.r - 2) // z.r,
     )
-    tied = lax.optimization_barrier((near, far, middle, close, apart))
-    near, far, middle, close, apart = tied
-    keep, send = call(
-        functools.partial(cross_kernel, z, width),
-        [shape((z.c // 2, 3 * z.c), F32), shape((z.c // 2, 3 * z.c))],
-        own_grad,
-        near,
-        far,
-        own_act,
-        cotangent,
-        flops=3 * one // 4,
-    )
-    other = swap(send, "space", 1)
-    x, _ = lax.optimization_barrier((x, send))
     (border,) = call(
         functools.partial(border_kernel, z),
         [shape((2, z.block, z.c))],
@@ -477,28 +522,47 @@
         flops=18 * one // z.r,
         scratch=[pltpu.VMEM((2, line, z.c), BF)],
     )
-    other, border = lax.optimization_barrier((other, border))
+    count = 2 * n * z.wc * z.r
+    keep, send = call(
+        functools.partial(cross_kernel, z, width, heads),
+        [shape((z.c // 2, 3 * z.c), F32), shape((z.c // 2, 3 * z.c))],
+        own_grad,
+        middle,
+        border,
+        *arrays,
+        flops=2 * one,
+        scratch=[pltpu.VMEM((count, z.c), BF), pltpu.VMEM((count, 2 * z.c), BF)],
+    )
+    other = swap(send, "space", 1)
+    border, _ = lax.optimization_barrier((border, send))
+    hidden, normed = call(
+        functools.partial(norm_kernel, z),
+        [shape((z.r, z.block, z.c))] * 2,
+        middle,
+        border,
+        x,
+        temporal,
+        gain.reshape(1, z.c),
+        flops=3 * one,
+    )
     pieces = call(
         functools.partial(split_kernel, z),
         [shape((z.c // 2, 3 * wide), F32)] + [shape((z.c // 2, 3 * wide))] * (n - 1),
         keep,
         other,
     )
-    border, *pieces = lax.optimization_barrier((border, *pieces))
+    normed, *pieces = lax.optimization_barrier((normed, *pieces))
     pieces = exchange(pieces)
     encoded = call(
-        functools.partial(main_kernel, z),
+        functools.partial(attend_kernel, z),
         [shape((z.r, z.piece, z.c))] * n,
-        middle,
-        border,
-        x,
-        temporal,
-        gain.reshape(1, z.c),
+        hidden,
+        normed,
         q_w,
         k_w,
         v_w,
         o_w,
-        flops=9 * one,
+        flops=5 * one,
     )
     back = exchange(encoded)
     pieces = lax.optimization_barrier((*pieces, *encoded))[:n]
@@ -513,6 +577,7 @@
     (kernel_grad,) = call(
         functools.partial(sum_kernel, z), [shape((3, width, wide), F32)], *pieces
     )
+    kernel_grad, *back = lax.optimization_barrier((kernel_grad, *back))
     return joined(z, back), kernel_grad.transpose(0, 2, 1)
 
 

time: 61.2 us -> 63.3 us (1.034); the launches traced: 60.2 us -> 63.1 us
  waiting for transfers between devices: 7.28 us -> 8.95 us
  Pallas kernels: 22.6 us -> 23.9 us
    ppermute x15 -> x16, waiting for transfers between devices: 7.27 us -> 8.94 us  [swap(): return lax.ppermute(value, axis, [(i, i ^ k) for i in range(count)])]
    pallas_call x14 -> x17, Pallas kernels: 21.5 us -> 22.9 us  [call(): pl.pallas_call(kernel, out_shape=tuple(outs), in_specs=[VMEM] * len(args)...]
    ppermute x3 -> x2, starting transfers between devices: 2.33 us -> 1.66 us  [swap_both(): far = lax.ppermute(far, axis, pairs + [(b, a) for a, b in pairs])]
    ppermute x15 -> x16, starting transfers between devices: 25.7 us -> 26.2 us  [swap(): return lax.ppermute(value, axis, [(i, i ^ k) for i in range(count)])]
  transfers between devices with their start and end apart: 18 -> 18, of which waited for: 4 -> 4; matrix products, arithmetic and copies ran while one was open for 0% -> 0% of each run, Pallas kernels for 34% -> 33%
where the time goes in v11:
time: 63.3 us; the launch traced here: 63.1 us
  starting transfers between devices  27.8 us (44%)
  Pallas kernels  23.9 us (38%)
  waiting for transfers between devices  8.95 us (14%)
  local copies, waits for them, and re-layouts  1.34 us (2%)
  between operations  1.08 us (2%)
    ppermute x16, starting transfers between devices, swap(): return lax.ppermute(value, axis, [(i, i ^ k) for i in range(count)])  26.2 us
    pallas_call x17, Pallas kernels, call(): pl.pallas_call(kernel, out_shape=tuple(outs), in_specs=[VMEM] * len(args)...  22.9 us
    ppermute x16, waiting for transfers between devices, swap(): return lax.ppermute(value, axis, [(i, i ^ k) for i in range(count)])  8.94 us
    ppermute x2, starting transfers between devices, swap_both(): far = lax.ppermute(far, axis, pairs + [(b, a) for a, b in pairs])  1.66 us
    unnamed x20, local copies, waits for them, and re-layouts  1.34 us
  transfers between devices with their start and end apart: 18, of which 4 were waited for; matrix products, arithmetic and copies ran while one was open for 0% of the time, Pallas kernels for 33%

profile of v11, /device:TPU:0, one launch (start us, length us, event | category | flops | bytes accessed | tf_op | source)
XLA Modules:
  0.0 63.1 jit_solution(17241931450191028081)
XLA Ops:
  0.6 1.2 %copy-done.1 = bf16[4,4,64,512]{3,2,1,0:T(8,128)(2,1)S(1)} copy-done((bf16[4,4,64,512]{3,2,1,0:T(8,128)(2,1)S(1)}, bf16[4,4,64,512]{3,2,1,0:T(8,128)(2,1)}, u32[]{:S(2)}) %copy-start.1) | copy-done | bytes 1048600
  1.9 0.6 shard_map.105
  2.4 3.0 %collective-permute-start.2 = (bf16[288,512]{1,0:T(8,128)(2,1)S(1)}, bf16[288,512]{1,0:T(8,128)(2,1)S(1)}, u32[]{:S(2)}, u32[]{:S(2)}) collective-permute-start(bf16[288,512]{1,0:T(8,128)(2,1)S(1)} %get-tuple-element.52), channel_id=1, source_target_pairs={{0,8},{8,0},{16,24},{24,16},{1,9},{9,1},{17,25},{25,17},{2,10},{10... | collective-permute-start | bytes 884744 | tf_op jit(solution)/shard_map/ppermute | solution.py:364
  5.4 1.5 %collective-permute-start.3 = (bf16[288,512]{1,0:T(8,128)(2,1)S(1)}, bf16[288,512]{1,0:T(8,128)(2,1)S(1)}, u32[]{:S(2)}, u32[]{:S(2)}) collective-permute-start(bf16[288,512]{1,0:T(8,128)(2,1)S(1)} %get-tuple-element.53), channel_id=1, source_target_pairs={{0,16},{8,24},{16,0},{24,8},{1,17},{9,25},{17,1},{25,9},{2,18},{10... | collective-permute-start | bytes 884744 | tf_op jit(solution)/shard_map/ppermute | solution.py:364
  7.0 0.0 collective-permute-start.4
  7.0 0.1 shard_map.106
  7.0 0.1 collective-permute-start
  7.1 0.8 %collective-permute-start.1 = (bf16[256,512]{1,0:T(8,128)(2,1)S(1)}, bf16[256,512]{1,0:T(8,128)(2,1)S(1)}, u32[]{:S(2)}, u32[]{:S(2)}) collective-permute-start(bf16[256,512]{1,0:T(8,128)(2,1)S(1)} %get-tuple-element.51), channel_id=1, source_target_pairs={{1,2},{3,4},{5,6},{2,1},{4,3},{6,5},{9,10},{11,12},{13,14},{10,9},... | collective-permute-start | bytes 786440 | tf_op jit(solution)/shard_map/ppermute | solution.py:369
  8.0 0.1 slice-done.1
  8.0 4.8 %shard_map.104.part_ref = f32[4,256,512]{2,1,0:T(8,128)S(1)} custom-call(bf16[4,4,64,512]{3,2,1,0:T(8,128)(2,1)S(1)} %copy-done.1, bf16[3,3,512,512]{3,2,1,0:T(8,128)(2,1)S(1)} %bitcast.3), custom_call_target="tpu_custom_call" | custom-call | flops 4294967296 | bytes 7864320 | tf_op jit(solution)/shard_map/pallas_call | solution.py:18
  12.8 0.0 copy-start
  12.8 0.0 collective-permute-done.near_ref
  12.8 1.8 %shard_map.107.act_ref.after_ref = bf16[4,4,64,512]{3,2,1,0:T(8,128)(2,1)S(1)} custom-call(f32[4,256,512]{2,1,0:T(8,128)S(1)} %shard_map.104.part_ref, bf16[256,512]{1,0:T(8,128)(2,1)S(1)} %collective-permute-done.near_ref, bf16[256,512]{1,0:T(8,128)(2,1)S(1)} %collective-permute-done.1.far_ref, bf16[3,3,512,512]{3,2,1,0:T(8,128)(2,1)S(1)} %bitcast.3), custom_call_target="tpu_custom_call" | custom-call | flops 1610612736 | bytes 8388608 | tf_op jit(solution)/shard_map/pallas_call | solution.py:18
  14.6 0.3 shard_map.112
  14.9 2.0 %collective-permute-start.7 = (bf16[2,4,32,512]{3,2,1,0:T(8,128)(2,1)S(1)}, bf16[2,4,32,512]{3,2,1,0:T(8,128)(2,1)S(1)}, u32[]{:S(2)}, u32[]{:S(2)}) collective-permute-start(bf16[2,4,32,512]{3,2,1,0:T(8,128)(2,1)S(1)} %get-tuple-element.64), channel_id=1, source_target_pairs={{0,8},{8,0},{16,24},{24,16},{1,9},{9,1},{17,25},{25,17},{2,10},{10... | collective-permute-start | bytes 786440 | tf_op jit(solution)/shard_map/ppermute | solution.py:364
  16.9 1.4 %shard_map.108.part_ref = f32[512,1536]{1,0:T(8,128)S(1)} custom-call(bf16[4,4,64,512]{3,2,1,0:T(8,128)(2,1)S(1)} %shard_map.107.act_ref.after_ref, bf16[4,4,64,512]{3,2,1,0:T(8,128)(2,1)S(1)} %copy-done), custom_call_target="tpu_custom_call" | custom-call | flops 1207959552 | bytes 5242880 | tf_op jit(solution)/shard_map/pallas_call | solution.py:18
  18.4 1.9 %collective-permute-done.3.refs_2_ = bf16[288,512]{1,0:T(8,128)(2,1)S(1)} collective-permute-done((bf16[288,512]{1,0:T(8,128)(2,1)S(1)}, bf16[288,512]{1,0:T(8,128)(2,1)S(1)}, u32[]{:S(2)}, u32[]{:S(2)}) %collective-permute-start.3) | collective-permute-done | bytes 294944 | tf_op jit(solution)/shard_map/ppermute | solution.py:364
  20.2 0.5 shard_map.109
  20.7 0.8 %collective-permute-start.5 = (bf16[288,512]{1,0:T(8,128)(2,1)S(1)}, bf16[288,512]{1,0:T(8,128)(2,1)S(1)}, u32[]{:S(2)}, u32[]{:S(2)}) collective-permute-start(bf16[288,512]{1,0:T(8,128)(2,1)S(1)} %get-tuple-element.60), channel_id=1, source_target_pairs={{0,1},{1,0},{2,3},{3,2},{4,5},{5,4},{6,7},{7,6},{8,9},{9,8},{10,11... | collective-permute-start | bytes 884744 | tf_op jit(solution)/shard_map/ppermute | solution.py:364
  21.5 0.8 %collective-permute-start.6 = (bf16[288,512]{1,0:T(8,128)(2,1)S(1)}, bf16[288,512]{1,0:T(8,128)(2,1)S(1)}, u32[]{:S(2)}, u32[]{:S(2)}) collective-permute-start(bf16[288,512]{1,0:T(8,128)(2,1)S(1)} %get-tuple-element.61), channel_id=1, source_target_pairs={{1,2},{3,4},{5,6},{2,1},{4,3},{6,5},{9,10},{11,12},{13,14},{10,9},... | collective-permute-start | bytes 884744 | tf_op jit(solution)/shard_map/ppermute | solution.py:369
  22.4 1.9 %collective-permute-start.8 = (bf16[2,4,32,512]{3,2,1,0:T(8,128)(2,1)S(1)}, bf16[2,4,32,512]{3,2,1,0:T(8,128)(2,1)S(1)}, u32[]{:S(2)}, u32[]{:S(2)}) collective-permute-start(bf16[2,4,32,512]{3,2,1,0:T(8,128)(2,1)S(1)} %shard_map.113), channel_id=1, source_target_pairs={{0,16},{8,24},{16,0},{24,8},{1,17},{9,25},{17,1},{25,9},{2,18},{10... | collective-permute-start | bytes 786440 | tf_op jit(solution)/shard_map/ppermute | solution.py:364
  24.4 2.7 %shard_map.110.middle_ref = bf16[2,256,512]{2,1,0:T(8,128)(2,1)S(1)} custom-call(bf16[4,288,512]{2,1,0:T(8,128)(2,1)S(1)} %get-tuple-element.59.x_ref, bf16[3,3,512,512]{3,2,1,0:T(8,128)(2,1)S(1)} %bitcast.3), custom_call_target="tpu_custom_call" | custom-call | flops 2415919104 | bytes 6422528 | tf_op jit(solution)/shard_map/pallas_call | solution.py:18
  27.1 2.7 %shard_map.111.border_ref = bf16[2,256,512]{2,1,0:T(8,128)(2,1)S(1)} custom-call(bf16[4,288,512]{2,1,0:T(8,128)(2,1)S(1)} %get-tuple-element.59.x_ref, bf16[288,512]{1,0:T(8,128)(2,1)S(1)} %collective-permute-done.5.near_ref, bf16[288,512]{1,0:T(8,128)(2,1)S(1)} %collective-permute-done.6.far_ref, bf16[3,3,512,512]{3,2,1,0:T(8,128)(2,1)S(1)} %bitcast.3), custom_call_target="tpu_custom_call" | custom-call | flops 2415919104 | bytes 7012352 | tf_op jit(solution)/shard_map/pallas_call | solution.py:18
  29.8 0.0 copy-start.2
  29.8 0.0 copy-start.7
  29.8 1.2 %shard_map.114 = (f32[256,1536]{1,0:T(8,128)S(1)}, bf16[256,1536]{1,0:T(8,128)(2,1)S(1)}) custom-call(f32[512,1536]{1,0:T(8,128)S(1)} %shard_map.108.part_ref, bf16[2,256,512]{2,1,0:T(8,128)(2,1)S(1)} %shard_map.110.middle_ref, bf16[2,256,512]{2,1,0:T(8,128)(2,1)S(1)} %shard_map.111.border_ref, bf16[2,4,32,512]{3,2,1,0:T(8,128)(2,1)S(1)} %get-tuple-element.63.refs_0_, ...), custom_call_target="tpu_custom_call" | custom-call | flops 1073741824 | bytes 7340032 | tf_op jit(solution)/shard_map/pallas_call | solution.py:18
  31.0 2.8 %collective-permute-start.9 = (bf16[256,1536]{1,0:T(8,128)(2,1)S(1)}, bf16[256,1536]{1,0:T(8,128)(2,1)S(1)}, u32[]{:S(2)}, u32[]{:S(2)}) collective-permute-start(bf16[256,1536]{1,0:T(8,128)(2,1)S(1)} %get-tuple-element.65), channel_id=1, source_target_pairs={{0,1},{1,0},{2,3},{3,2},{4,5},{5,4},{6,7},{7,6},{8,9},{9,8},{10,11... | collective-permute-start | bytes 2359304 | tf_op jit(solution)/shard_map/ppermute | solution.py:364
  33.8 2.3 %shard_map.115 = (bf16[4,256,512]{2,1,0:T(8,128)(2,1)S(1)}, bf16[4,256,512]{2,1,0:T(8,128)(2,1)S(1)}) custom-call(bf16[2,256,512]{2,1,0:T(8,128)(2,1)S(1)} %shard_map.110.middle_ref, bf16[2,256,512]{2,1,0:T(8,128)(2,1)S(1)} %shard_map.111.border_ref, bf16[4,288,512]{2,1,0:T(8,128)(2,1)S(1)} %get-tuple-element.59.x_ref, bf16[3,512,512]{2,1,0:T(8,128)(2,1)S(1)} %copy-done.2, ...), custom_call_target="tpu_custom_call" | custom-call | flops 1610612736 | bytes 5900288 | tf_op jit(solution)/shard_map/pallas_call | solution.py:18
  36.1 0.0 copy-start.3
  36.1 0.0 copy-start.4
  36.1 0.0 copy-start.5
  36.1 0.0 copy-start.6
  36.1 0.3 shard_map.116
  36.5 1.1 %collective-permute-start.10 = (bf16[256,384]{1,0:T(8,128)(2,1)S(1)}, bf16[256,384]{1,0:T(8,128)(2,1)S(1)}, u32[]{:S(2)}, u32[]{:S(2)}) collective-permute-start(bf16[256,384]{1,0:T(8,128)(2,1)S(1)} %get-tuple-element.74), channel_id=1, source_target_pairs={{0,8},{8,0},{16,24},{24,16},{1,9},{9,1},{17,25},{25,17},{2,10},{10... | collective-permute-start | bytes 589832 | tf_op jit(solution)/shard_map/ppermute | solution.py:364
  37.6 1.2 %collective-permute-start.11 = (bf16[256,384]{1,0:T(8,128)(2,1)S(1)}, bf16[256,384]{1,0:T(8,128)(2,1)S(1)}, u32[]{:S(2)}, u32[]{:S(2)}) collective-permute-start(bf16[256,384]{1,0:T(8,128)(2,1)S(1)} %get-tuple-element.75), channel_id=1, source_target_pairs={{0,16},{8,24},{16,0},{24,8},{1,17},{9,25},{17,1},{25,9},{2,18},{10... | collective-permute-start | bytes 589832 | tf_op jit(solution)/shard_map/ppermute | solution.py:364
  38.8 1.2 %collective-permute-start.12 = (bf16[256,384]{1,0:T(8,128)(2,1)S(1)}, bf16[256,384]{1,0:T(8,128)(2,1)S(1)}, u32[]{:S(2)}, u32[]{:S(2)}) collective-permute-start(bf16[256,384]{1,0:T(8,128)(2,1)S(1)} %get-tuple-element.76), channel_id=1, source_target_pairs={{0,24},{8,16},{16,8},{24,0},{1,25},{9,17},{17,9},{25,1},{2,26},{10... | collective-permute-start | bytes 589832 | tf_op jit(solution)/shard_map/ppermute | solution.py:364
  40.0 3.6 %shard_map.117 = (bf16[4,64,512]{2,1,0:T(8,128)(2,1)S(1)}, bf16[4,64,512]{2,1,0:T(8,128)(2,1)S(1)}, bf16[4,64,512]{2,1,0:T(8,128)(2,1)S(1)}, bf16[4,64,512]{2,1,0:T(8,128)(2,1)S(1)}) custom-call(bf16[4,256,512]{2,1,0:T(8,128)(2,1)S(1)} %get-tuple-element.77.hidden_ref, bf16[4,256,512]{2,1,0:T(8,128)(2,1)S(1)} %get-tuple-element.78.normed_ref, ...), custom_call_target="tpu_custom_call" | custom-call | flops 2684354560 | bytes 5242880 | tf_op jit(solution)/shard_map/pallas_call | solution.py:18
  43.6 1.1 %collective-permute-start.15 = (bf16[4,64,512]{2,1,0:T(8,128)(2,1)S(1)}, bf16[4,64,512]{2,1,0:T(8,128)(2,1)S(1)}, u32[]{:S(2)}, u32[]{:S(2)}) collective-permute-start(bf16[4,64,512]{2,1,0:T(8,128)(2,1)S(1)} %get-tuple-element.80), channel_id=1, source_target_pairs={{0,8},{8,0},{16,24},{24,16},{1,9},{9,1},{17,25},{25,17},{2,10},{10... | collective-permute-start | bytes 786440 | tf_op jit(solution)/shard_map/ppermute | solution.py:364
  44.7 1.2 %collective-permute-start.16 = (bf16[4,64,512]{2,1,0:T(8,128)(2,1)S(1)}, bf16[4,64,512]{2,1,0:T(8,128)(2,1)S(1)}, u32[]{:S(2)}, u32[]{:S(2)}) collective-permute-start(bf16[4,64,512]{2,1,0:T(8,128)(2,1)S(1)} %get-tuple-element.81), channel_id=1, source_target_pairs={{0,16},{8,24},{16,0},{24,8},{1,17},{9,25},{17,1},{25,9},{2,18},{10... | collective-permute-start | bytes 786440 | tf_op jit(solution)/shard_map/ppermute | solution.py:364
  45.9 1.2 %collective-permute-start.17 = (bf16[4,64,512]{2,1,0:T(8,128)(2,1)S(1)}, bf16[4,64,512]{2,1,0:T(8,128)(2,1)S(1)}, u32[]{:S(2)}, u32[]{:S(2)}) collective-permute-start(bf16[4,64,512]{2,1,0:T(8,128)(2,1)S(1)} %get-tuple-element.82), channel_id=1, source_target_pairs={{0,24},{8,16},{16,8},{24,0},{1,25},{9,17},{17,9},{25,1},{2,26},{10... | collective-permute-start | bytes 786440 | tf_op jit(solution)/shard_map/ppermute | solution.py:364
  47.2 2.4 %collective-permute-done.12.refs_3_ = bf16[256,384]{1,0:T(8,128)(2,1)S(1)} collective-permute-done((bf16[256,384]{1,0:T(8,128)(2,1)S(1)}, bf16[256,384]{1,0:T(8,128)(2,1)S(1)}, u32[]{:S(2)}, u32[]{:S(2)}) %collective-permute-start.12) | collective-permute-done | bytes 196640 | tf_op jit(solution)/shard_map/ppermute | solution.py:364
  49.6 0.1 shard_map.118
  49.7 3.8 %collective-permute-start.13 = (bf16[128,384]{1,0:T(8,128)(2,1)S(1)}, bf16[128,384]{1,0:T(8,128)(2,1)S(1)}, u32[]{:S(2)}, u32[]{:S(2)}) collective-permute-start(bf16[128,384]{1,0:T(8,128)(2,1)S(1)} %get-tuple-element.88), channel_id=1, source_target_pairs={{0,2},{1,3},{2,0},{3,1},{4,6},{5,7},{6,4},{7,5},{8,10},{9,11},{10,... | collective-permute-start | bytes 294920 | tf_op jit(solution)/shard_map/ppermute | solution.py:364
  53.4 2.6 %collective-permute-done.13.refs_1_ = bf16[128,384]{1,0:T(8,128)(2,1)S(1)} collective-permute-done((bf16[128,384]{1,0:T(8,128)(2,1)S(1)}, bf16[128,384]{1,0:T(8,128)(2,1)S(1)}, u32[]{:S(2)}, u32[]{:S(2)}) %collective-permute-start.13) | collective-permute-done | bytes 98336 | tf_op jit(solution)/shard_map/ppermute | solution.py:364
  56.1 3.1 %collective-permute-start.14 = (bf16[64,384]{1,0:T(8,128)(2,1)S(1)}, bf16[64,384]{1,0:T(8,128)(2,1)S(1)}, u32[]{:S(2)}, u32[]{:S(2)}) collective-permute-start(bf16[64,384]{1,0:T(8,128)(2,1)S(1)} %get-tuple-element.90), channel_id=1, source_target_pairs={{0,4},{1,5},{2,6},{3,7},{4,0},{5,1},{6,2},{7,3},{8,12},{9,13},{10,... | collective-permute-start | bytes 147464 | tf_op jit(solution)/shard_map/ppermute | solution.py:364
  59.2 2.1 %collective-permute-done.14.refs_1_ = bf16[64,384]{1,0:T(8,128)(2,1)S(1)} collective-permute-done((bf16[64,384]{1,0:T(8,128)(2,1)S(1)}, bf16[64,384]{1,0:T(8,128)(2,1)S(1)}, u32[]{:S(2)}, u32[]{:S(2)}) %collective-permute-start.14) | collective-permute-done | bytes 49184 | tf_op jit(solution)/shard_map/ppermute | solution.py:364
  61.3 0.7 %shard_map.120 = f32[3,64,128]{2,1,0:T(8,128)} custom-call(f32[64,384]{1,0:T(8,128)S(1)} %get-tuple-element.89.refs_0_, bf16[64,384]{1,0:T(8,128)(2,1)S(1)} %collective-permute-done.14.refs_1_), custom_call_target="tpu_custom_call" | custom-call | bytes 245760 | tf_op jit(solution)/shard_map/pallas_call | solution.py:18
  61.9 1.0 %shard_map.121 = bf16[4,4,64,512]{3,2,1,0:T(8,128)(2,1)} custom-call(bf16[4,64,512]{2,1,0:T(8,128)(2,1)S(1)} %get-tuple-element.91.refs_0_, bf16[4,64,512]{2,1,0:T(8,128)(2,1)S(1)} %collective-permute-done.15.refs_1_, bf16[4,64,512]{2,1,0:T(8,128)(2,1)S(1)} %collective-permute-done.16.refs_2_, bf16[4,64,512]{2,1,0:T(8,128)(2,1)S(1)} %collective-permute-done.17.refs_3_), custom_call_target="tpu_custom_call" | custom-call | bytes 4194304 | tf_op jit(solution)/shard_map/pallas_call | solution.py:408
  (27 shorter events, 0.1 us)
Async XLA Ops:
  0.6 1.2 %copy-start.1 = (bf16[4,4,64,512]{3,2,1,0:T(8,128)(2,1)S(1)}, bf16[4,4,64,512]{3,2,1,0:T(8,128)(2,1)}, u32[]{:S(2)}) copy-start(bf16[4,4,64,512]{3,2,1,0:T(8,128)(2,1)} %x_ref.5) | copy-start | bytes 3145732
  1.9 6.1 %slice-start = ((s8[4718592]{0:T(1024)(128)(4,1)}), s8[4194304]{0:T(1024)(128)(4,1)S(1)}, s32[]{:S(2)}) async-start(s8[4718592]{0:T(1024)(128)(4,1)} %bitcast.2), calls=%async_computation | async-start | bytes 8388608
  2.4 15.9 %collective-permute-start.2 = (bf16[288,512]{1,0:T(8,128)(2,1)S(1)}, bf16[288,512]{1,0:T(8,128)(2,1)S(1)}, u32[]{:S(2)}, u32[]{:S(2)}) collective-permute-start(bf16[288,512]{1,0:T(8,128)(2,1)S(1)} %get-tuple-element.52), channel_id=1, source_target_pairs={{0,8},{8,0},{16,24},{24,16},{1,9},{9,1},{17,25},{25,17},{2,10},{10... | collective-permute-start | bytes 884744 | tf_op jit(solution)/shard_map/ppermute | solution.py:364
  5.4 14.8 %collective-permute-start.3 = (bf16[288,512]{1,0:T(8,128)(2,1)S(1)}, bf16[288,512]{1,0:T(8,128)(2,1)S(1)}, u32[]{:S(2)}, u32[]{:S(2)}) collective-permute-start(bf16[288,512]{1,0:T(8,128)(2,1)S(1)} %get-tuple-element.53), channel_id=1, source_target_pairs={{0,16},{8,24},{16,0},{24,8},{1,17},{9,25},{17,1},{25,9},{2,18},{10... | collective-permute-start | bytes 884744 | tf_op jit(solution)/shard_map/ppermute | solution.py:364
  7.0 13.3 %collective-permute-start.4 = (bf16[288,512]{1,0:T(8,128)(2,1)S(1)}, bf16[288,512]{1,0:T(8,128)(2,1)S(1)}, u32[]{:S(2)}, u32[]{:S(2)}) collective-permute-start(bf16[288,512]{1,0:T(8,128)(2,1)S(1)} %get-tuple-element.54), channel_id=1, source_target_pairs={{0,24},{8,16},{16,8},{24,0},{1,25},{9,17},{17,9},{25,1},{2,26},{10... | collective-permute-start | bytes 884744 | tf_op jit(solution)/shard_map/ppermute | solution.py:364
  7.0 1.0 %slice-start.1 = ((s8[4718592]{0:T(1024)(128)(4,1)}), s8[524288]{0:T(1024)(128)(4,1)S(1)}, s32[]{:S(2)}) async-start(s8[4718592]{0:T(1024)(128)(4,1)} %bitcast.2), calls=%async_computation.1 | async-start | bytes 1048576
  7.0 5.8 %collective-permute-start = (bf16[256,512]{1,0:T(8,128)(2,1)S(1)}, bf16[256,512]{1,0:T(8,128)(2,1)S(1)}, u32[]{:S(2)}, u32[]{:S(2)}) collective-permute-start(bf16[256,512]{1,0:T(8,128)(2,1)S(1)} %get-tuple-element.50), channel_id=1, source_target_pairs={{0,1},{1,0},{2,3},{3,2},{4,5},{5,4},{6,7},{7,6},{8,9},{9,8},{10,11... | collective-permute-start | bytes 786440 | tf_op jit(solution)/shard_map/ppermute | solution.py:364
  7.1 5.7 %collective-permute-start.1 = (bf16[256,512]{1,0:T(8,128)(2,1)S(1)}, bf16[256,512]{1,0:T(8,128)(2,1)S(1)}, u32[]{:S(2)}, u32[]{:S(2)}) collective-permute-start(bf16[256,512]{1,0:T(8,128)(2,1)S(1)} %get-tuple-element.51), channel_id=1, source_target_pairs={{1,2},{3,4},{5,6},{2,1},{4,3},{6,5},{9,10},{11,12},{13,14},{10,9},... | collective-permute-start | bytes 786440 | tf_op jit(solution)/shard_map/ppermute | solution.py:369
  12.8 1.8 %copy-start = (bf16[4,4,64,512]{3,2,1,0:T(8,128)(2,1)S(1)}, bf16[4,4,64,512]{3,2,1,0:T(8,128)(2,1)}, u32[]{:S(2)}) copy-start(bf16[4,4,64,512]{3,2,1,0:T(8,128)(2,1)} %cot_ref.3) | copy-start | bytes 3145732
  14.9 7.5 %collective-permute-start.7 = (bf16[2,4,32,512]{3,2,1,0:T(8,128)(2,1)S(1)}, bf16[2,4,32,512]{3,2,1,0:T(8,128)(2,1)S(1)}, u32[]{:S(2)}, u32[]{:S(2)}) collective-permute-start(bf16[2,4,32,512]{3,2,1,0:T(8,128)(2,1)S(1)} %get-tuple-element.64), channel_id=1, source_target_pairs={{0,8},{8,0},{16,24},{24,16},{1,9},{9,1},{17,25},{25,17},{2,10},{10... | collective-permute-start | bytes 786440 | tf_op jit(solution)/shard_map/ppermute | solution.py:364
  20.7 6.3 %collective-permute-start.5 = (bf16[288,512]{1,0:T(8,128)(2,1)S(1)}, bf16[288,512]{1,0:T(8,128)(2,1)S(1)}, u32[]{:S(2)}, u32[]{:S(2)}) collective-permute-start(bf16[288,512]{1,0:T(8,128)(2,1)S(1)} %get-tuple-element.60), channel_id=1, source_target_pairs={{0,1},{1,0},{2,3},{3,2},{4,5},{5,4},{6,7},{7,6},{8,9},{9,8},{10,11... | collective-permute-start | bytes 884744 | tf_op jit(solution)/shard_map/ppermute | solution.py:364
  21.5 5.5 %collective-permute-start.6 = (bf16[288,512]{1,0:T(8,128)(2,1)S(1)}, bf16[288,512]{1,0:T(8,128)(2,1)S(1)}, u32[]{:S(2)}, u32[]{:S(2)}) collective-permute-start(bf16[288,512]{1,0:T(8,128)(2,1)S(1)} %get-tuple-element.61), channel_id=1, source_target_pairs={{1,2},{3,4},{5,6},{2,1},{4,3},{6,5},{9,10},{11,12},{13,14},{10,9},... | collective-permute-start | bytes 884744 | tf_op jit(solution)/shard_map/ppermute | solution.py:369
  22.4 7.3 %collective-permute-start.8 = (bf16[2,4,32,512]{3,2,1,0:T(8,128)(2,1)S(1)}, bf16[2,4,32,512]{3,2,1,0:T(8,128)(2,1)S(1)}, u32[]{:S(2)}, u32[]{:S(2)}) collective-permute-start(bf16[2,4,32,512]{3,2,1,0:T(8,128)(2,1)S(1)} %shard_map.113), channel_id=1, source_target_pairs={{0,16},{8,24},{16,0},{24,8},{1,17},{9,25},{17,1},{25,9},{2,18},{10... | collective-permute-start | bytes 786440 | tf_op jit(solution)/shard_map/ppermute | solution.py:364
  29.8 4.0 %copy-start.2 = (bf16[3,512,512]{2,1,0:T(8,128)(2,1)S(1)}, bf16[3,512,512]{2,1,0:T(8,128)(2,1)}, u32[]{:S(2)}) copy-start(bf16[3,512,512]{2,1,0:T(8,128)(2,1)} %t_ref.1) | copy-start | bytes 4718596
  29.8 4.0 %copy-start.7 = (f32[512]{0:T(512)S(1)}, f32[512]{0:T(512)}, u32[]{:S(2)}) copy-start(f32[512]{0:T(512)} %param.12) | copy-start | bytes 6148
  31.0 5.1 %collective-permute-start.9 = (bf16[256,1536]{1,0:T(8,128)(2,1)S(1)}, bf16[256,1536]{1,0:T(8,128)(2,1)S(1)}, u32[]{:S(2)}, u32[]{:S(2)}) collective-permute-start(bf16[256,1536]{1,0:T(8,128)(2,1)S(1)} %get-tuple-element.65), channel_id=1, source_target_pairs={{0,1},{1,0},{2,3},{3,2},{4,5},{5,4},{6,7},{7,6},{8,9},{9,8},{10,11... | collective-permute-start | bytes 2359304 | tf_op jit(solution)/shard_map/ppermute | solution.py:364
  36.1 3.9 %copy-start.3 = (bf16[512,512]{1,0:T(8,128)(2,1)S(1)}, bf16[512,512]{1,0:T(8,128)(2,1)}, u32[]{:S(2)}) copy-start(bf16[512,512]{1,0:T(8,128)(2,1)} %q_ref.1) | copy-start | bytes 1572868
  36.1 3.9 %copy-start.4 = (bf16[512,512]{1,0:T(8,128)(2,1)S(1)}, bf16[512,512]{1,0:T(8,128)(2,1)}, u32[]{:S(2)}) copy-start(bf16[512,512]{1,0:T(8,128)(2,1)} %k_ref.1) | copy-start | bytes 1572868
  36.1 3.9 %copy-start.5 = (bf16[512,512]{1,0:T(8,128)(2,1)S(1)}, bf16[512,512]{1,0:T(8,128)(2,1)}, u32[]{:S(2)}) copy-start(bf16[512,512]{1,0:T(8,128)(2,1)} %v_ref.1) | copy-start | bytes 1572868
  36.1 3.9 %copy-start.6 = (bf16[512,512]{1,0:T(8,128)(2,1)S(1)}, bf16[512,512]{1,0:T(8,128)(2,1)}, u32[]{:S(2)}) copy-start(bf16[512,512]{1,0:T(8,128)(2,1)} %o_ref.1) | copy-start | bytes 1572868
  36.5 9.5 %collective-permute-start.10 = (bf16[256,384]{1,0:T(8,128)(2,1)S(1)}, bf16[256,384]{1,0:T(8,128)(2,1)S(1)}, u32[]{:S(2)}, u32[]{:S(2)}) collective-permute-start(bf16[256,384]{1,0:T(8,128)(2,1)S(1)} %get-tuple-element.74), channel_id=1, source_target_pairs={{0,8},{8,0},{16,24},{24,16},{1,9},{9,1},{17,25},{25,17},{2,10},{10... | collective-permute-start | bytes 589832 | tf_op jit(solution)/shard_map/ppermute | solution.py:364
  37.6 9.6 %collective-permute-start.11 = (bf16[256,384]{1,0:T(8,128)(2,1)S(1)}, bf16[256,384]{1,0:T(8,128)(2,1)S(1)}, u32[]{:S(2)}, u32[]{:S(2)}) collective-permute-start(bf16[256,384]{1,0:T(8,128)(2,1)S(1)} %get-tuple-element.75), channel_id=1, source_target_pairs={{0,16},{8,24},{16,0},{24,8},{1,17},{9,25},{17,1},{25,9},{2,18},{10... | collective-permute-start | bytes 589832 | tf_op jit(solution)/shard_map/ppermute | solution.py:364
  38.8 10.8 %collective-permute-start.12 = (bf16[256,384]{1,0:T(8,128)(2,1)S(1)}, bf16[256,384]{1,0:T(8,128)(2,1)S(1)}, u32[]{:S(2)}, u32[]{:S(2)}) collective-permute-start(bf16[256,384]{1,0:T(8,128)(2,1)S(1)} %get-tuple-element.76), channel_id=1, source_target_pairs={{0,24},{8,16},{16,8},{24,0},{1,25},{9,17},{17,9},{25,1},{2,26},{10... | collective-permute-start | bytes 589832 | tf_op jit(solution)/shard_map/ppermute | solution.py:364
  43.6 18.3 %collective-permute-start.15 = (bf16[4,64,512]{2,1,0:T(8,128)(2,1)S(1)}, bf16[4,64,512]{2,1,0:T(8,128)(2,1)S(1)}, u32[]{:S(2)}, u32[]{:S(2)}) collective-permute-start(bf16[4,64,512]{2,1,0:T(8,128)(2,1)S(1)} %get-tuple-element.80), channel_id=1, source_target_pairs={{0,8},{8,0},{16,24},{24,16},{1,9},{9,1},{17,25},{25,17},{2,10},{10... | collective-permute-start | bytes 786440 | tf_op jit(solution)/shard_map/ppermute | solution.py:364
  44.7 17.2 %collective-permute-start.16 = (bf16[4,64,512]{2,1,0:T(8,128)(2,1)S(1)}, bf16[4,64,512]{2,1,0:T(8,128)(2,1)S(1)}, u32[]{:S(2)}, u32[]{:S(2)}) collective-permute-start(bf16[4,64,512]{2,1,0:T(8,128)(2,1)S(1)} %get-tuple-element.81), channel_id=1, source_target_pairs={{0,16},{8,24},{16,0},{24,8},{1,17},{9,25},{17,1},{25,9},{2,18},{10... | collective-permute-start | bytes 786440 | tf_op jit(solution)/shard_map/ppermute | solution.py:364
  45.9 16.0 %collective-permute-start.17 = (bf16[4,64,512]{2,1,0:T(8,128)(2,1)S(1)}, bf16[4,64,512]{2,1,0:T(8,128)(2,1)S(1)}, u32[]{:S(2)}, u32[]{:S(2)}) collective-permute-start(bf16[4,64,512]{2,1,0:T(8,128)(2,1)S(1)} %get-tuple-element.82), channel_id=1, source_target_pairs={{0,24},{8,16},{16,8},{24,0},{1,25},{9,17},{17,9},{25,1},{2,26},{10... | collective-permute-start | bytes 786440 | tf_op jit(solution)/shard_map/ppermute | solution.py:364
  49.7 6.4 %collective-permute-start.13 = (bf16[128,384]{1,0:T(8,128)(2,1)S(1)}, bf16[128,384]{1,0:T(8,128)(2,1)S(1)}, u32[]{:S(2)}, u32[]{:S(2)}) collective-permute-start(bf16[128,384]{1,0:T(8,128)(2,1)S(1)} %get-tuple-element.88), channel_id=1, source_target_pairs={{0,2},{1,3},{2,0},{3,1},{4,6},{5,7},{6,4},{7,5},{8,10},{9,11},{10,... | collective-permute-start | bytes 294920 | tf_op jit(solution)/shard_map/ppermute | solution.py:364
  56.1 5.2 %collective-permute-start.14 = (bf16[64,384]{1,0:T(8,128)(2,1)S(1)}, bf16[64,384]{1,0:T(8,128)(2,1)S(1)}, u32[]{:S(2)}, u32[]{:S(2)}) collective-permute-start(bf16[64,384]{1,0:T(8,128)(2,1)S(1)} %get-tuple-element.90), channel_id=1, source_target_pairs={{0,4},{1,5},{2,6},{3,7},{4,0},{5,1},{6,2},{7,3},{8,12},{9,13},{10,... | collective-permute-start | bytes 147464 | tf_op jit(solution)/shard_map/ppermute | solution.py:364

commit v12 on v10

--- a/solution.py
+++ b/solution.py
@@ -219,15 +219,15 @@
     out[1] = conv_row(z, w_ref, [x_ref.at[z.r - 2], x_ref.at[z.r - 1], edges.at[1]])
 
 
-def staged(z, stages):
-    for step in range(z.r + len(stages) - 1):
+def staged(count, stages):
+    for step in range(count + len(stages) - 1):
         for late, stage in reversed(list(enumerate(stages))):
-            if 0 <= step - late < z.r:
+            if 0 <= step - late < count:
                 stage(step - late)
 
 
 def main_kernel(
-    z, middle_ref, border_ref, x_ref, t_ref, gain_ref, q_ref, k_ref, v_ref, o_ref, *outs
+    z, places, act_ref, x_ref, t_ref, gain_ref, q_ref, k_ref, v_ref, o_ref, *outs
 ):
     me = lax.axis_index("tm")
     a = lax.broadcasted_iota(jnp.int32, (z.block, z.block), 0)
@@ -244,7 +244,7 @@
     held = {}
 
     def activate(r):
-        act = border_ref[r // (z.r - 1)] if r in (0, z.r - 1) else middle_ref[r - 1]
+        act = act_ref[r]
         wide = act.astype(F32)
         held["a", r] = [act] + [
             jnp.where(frame >= k, pltpu.roll(wide, k, 0), 0.0).astype(BF) for k in (1, 2)
@@ -252,7 +252,7 @@
 
     def hide(r):
         temporal = taps(held.pop(("a", r)), t_ref[...])
-        hidden = (x_ref[r, z.f : z.f + z.block].astype(F32) + temporal).astype(BF)
+        hidden = (x_ref[places[r], z.f : z.f + z.block].astype(F32) + temporal).astype(BF)
         held["h", r] = hidden
 
     def norm(r):
@@ -297,7 +297,7 @@
         for k in range(z.n):
             outs[k][r] = encoded[k * z.piece : (k + 1) * z.piece]
 
-    staged(z, (activate, hide, norm, project, score, weigh, mix, finish, spread))
+    staged(len(places), (activate, hide, norm, project, score, weigh, mix, finish, spread))
 
 
 def split_kernel(z, keep_ref, got_ref, *outs):
@@ -351,25 +351,28 @@
 
 
 def join_kernel(z, *refs):
-    parts, (out, whole, sem) = refs[: z.n], refs[z.n :]
+    inside, border, (out, whole, sem) = refs[: z.n], refs[z.n : 2 * z.n], refs[2 * z.n :]
     me = lax.axis_index("tm")
     copies = []
     for f in range(z.fl):
         for k in range(z.n):
             cols = pl.ds(pl.multiple_of((me ^ k) * z.wc, z.wc), z.wc)
-            whole[f, :, cols] = parts[k][:, f * z.wc : (f + 1) * z.wc]
+            rows = slice(f * z.wc, (f + 1) * z.wc)
+            whole[f, 0, cols] = border[k][0, rows]
+            whole[f, 1 : z.r - 1, cols] = inside[k][:, rows]
+            whole[f, z.r - 1, cols] = border[k][1, rows]
         copies.append(pltpu.make_async_copy(whole.at[f], out.at[f], sem.at[f]))
         copies[f].start()
     for copy in copies:
         copy.wait()
 
 
-def joined(z, back):
+def joined(z, inside, border):
     if z.wc % 16 == 0:
         return pl.pallas_call(
             functools.partial(join_kernel, z),
             out_shape=shape((z.fl, z.r, z.w, z.c)),
-            in_specs=[VMEM] * z.n,
+            in_specs=[VMEM] * (2 * z.n),
             out_specs=pl.BlockSpec(memory_space=pl.ANY),
             scratch_shapes=[
                 pltpu.VMEM((z.fl, z.r, z.w, z.c), BF),
@@ -377,12 +380,13 @@
             ],
             compiler_params=pltpu.CompilerParams(vmem_limit_bytes=16 * 2**20),
             cost_estimate=pl.CostEstimate(
-                flops=0, bytes_accessed=8 * z.n * z.main * z.c, transcendentals=0
+                flops=2**34, bytes_accessed=8 * z.n * z.main * z.c, transcendentals=0
             ),
-        )(*back)
+        )(*inside, *border)
     whole = jnp.zeros((z.fl, z.r, z.n, z.wc, z.c), BF)
     for k in range(z.n):
-        rows = back[k].reshape(z.r, z.fl, 1, z.wc, z.c).transpose(1, 0, 2, 3, 4)
+        back = jnp.concatenate([border[k][:1], inside[k], border[k][1:]], axis=0)
+        rows = back.reshape(z.r, z.fl, 1, z.wc, z.c).transpose(1, 0, 2, 3, 4)
         whole = lax.dynamic_update_slice_in_dim(whole, rows, lax.axis_index("tm") ^ k, 2)
     return whole.reshape(z.fl, z.r, z.w, z.c)
 
@@ -453,8 +457,26 @@
         spatial,
         flops=9 * one * (z.r - 2) // z.r,
     )
-    tied = lax.optimization_barrier((near, far, middle, close, apart))
-    near, far, middle, close, apart = tied
+
+    def attend(act, x, places):
+        return call(
+            functools.partial(main_kernel, z, places),
+            [shape((len(places), z.piece, z.c))] * n,
+            act,
+            x,
+            temporal.reshape(3 * z.c, z.c),
+            gain.reshape(1, z.c),
+            q_w,
+            k_w,
+            v_w,
+            o_w,
+            flops=9 * one * len(places) // z.r,
+        )
+
+    encoded = attend(middle, x, list(range(1, z.r - 1)))
+    inside = exchange(encoded)
+    tied = lax.optimization_barrier((near, far, encoded[0], close, apart))
+    near, far, _, close, apart = tied
     keep, send = call(
         functools.partial(cross_kernel, z, width),
         [shape((z.c // 2, 3 * z.c), F32), shape((z.c // 2, 3 * z.c))],
@@ -484,22 +506,10 @@
         keep,
         other,
     )
-    border, *pieces = lax.optimization_barrier((border, *pieces))
+    tied = lax.optimization_barrier((border, *pieces, *inside))
+    border, inside = tied[0], tied[1 + n :]
     pieces = exchange(pieces)
-    encoded = call(
-        functools.partial(main_kernel, z),
-        [shape((z.r, z.piece, z.c))] * n,
-        middle,
-        border,
-        x,
-        temporal,
-        gain.reshape(1, z.c),
-        q_w,
-        k_w,
-        v_w,
-        o_w,
-        flops=9 * one,
-    )
+    encoded = attend(border, x, [0, z.r - 1])
     back = exchange(encoded)
     pieces = lax.optimization_barrier((*pieces, *encoded))[:n]
     bit = 0
@@ -513,7 +523,7 @@
     (kernel_grad,) = call(
         functools.partial(sum_kernel, z), [shape((3, width, wide), F32)], *pieces
     )
-    return joined(z, back), kernel_grad.transpose(0, 2, 1)
+    return joined(z, inside, back), kernel_grad.transpose(0, 2, 1)
 
 
 def solution(mesh):

time: 61.2 us -> 65.8 us (1.075); the launches traced: 60.2 us -> 65.6 us
  waiting for transfers between devices: 7.28 us -> 10.6 us
  starting transfers between devices: 28.1 us -> 29.9 us
    ppermute x15 -> x18, waiting for transfers between devices: 7.27 us -> 10.6 us  [swap(): return lax.ppermute(value, axis, [(i, i ^ k) for i in range(count)])]
    ppermute x15 -> x18, starting transfers between devices: 25.7 us -> 27.6 us  [swap(): return lax.ppermute(value, axis, [(i, i ^ k) for i in range(count)])]
    pallas_call x14 -> x15, Pallas kernels: 21.5 us -> 21.8 us  [call(): pl.pallas_call(kernel, out_shape=tuple(outs), in_specs=[VMEM] * len(args)...]
  transfers between devices with their start and end apart: 18 -> 21, of which waited for: 4 -> 4; matrix products, arithmetic and copies ran while one was open for 0% -> 0% of each run, Pallas kernels for 34% -> 32%
where the time goes in v12:
time: 65.8 us; the launch traced here: 65.6 us
  starting transfers between devices  29.9 us (45%)
  Pallas kernels  22.8 us (35%)
  waiting for transfers between devices  10.6 us (16%)
  local copies, waits for them, and re-layouts  1.33 us (2%)
  between operations  0.97 us (1%)
    ppermute x18, starting transfers between devices, swap(): return lax.ppermute(value, axis, [(i, i ^ k) for i in range(count)])  27.6 us
    pallas_call x15, Pallas kernels, call(): pl.pallas_call(kernel, out_shape=tuple(outs), in_specs=[VMEM] * len(args)...  21.8 us
    ppermute x18, waiting for transfers between devices, swap(): return lax.ppermute(value, axis, [(i, i ^ k) for i in range(count)])  10.6 us
    ppermute x3, starting transfers between devices, swap_both(): far = lax.ppermute(far, axis, pairs + [(b, a) for a, b in pairs])  2.32 us
    unnamed x20, local copies, waits for them, and re-layouts  1.33 us
  transfers between devices with their start and end apart: 21, of which 4 were waited for; matrix products, arithmetic and copies ran while one was open for 0% of the time, Pallas kernels for 32%

profile of v12, /device:TPU:0, one launch (start us, length us, event | category | flops | bytes accessed | tf_op | source)
XLA Modules:
  0.0 65.6 jit_solution(8351000639580031515)
XLA Ops:
  0.6 1.2 %copy-done.1 = bf16[4,4,64,512]{3,2,1,0:T(8,128)(2,1)S(1)} copy-done((bf16[4,4,64,512]{3,2,1,0:T(8,128)(2,1)S(1)}, bf16[4,4,64,512]{3,2,1,0:T(8,128)(2,1)}, u32[]{:S(2)}) %copy-start.1) | copy-done | bytes 1048600
  1.9 0.6 shard_map.105
  2.4 3.0 %collective-permute-start.4 = (bf16[288,512]{1,0:T(8,128)(2,1)S(1)}, bf16[288,512]{1,0:T(8,128)(2,1)S(1)}, u32[]{:S(2)}, u32[]{:S(2)}) collective-permute-start(bf16[288,512]{1,0:T(8,128)(2,1)S(1)} %get-tuple-element.54), channel_id=1, source_target_pairs={{0,8},{8,0},{16,24},{24,16},{1,9},{9,1},{17,25},{25,17},{2,10},{10... | collective-permute-start | bytes 884744 | tf_op jit(solution)/shard_map/ppermute | solution.py:325
  5.4 1.5 %collective-permute-start.5 = (bf16[288,512]{1,0:T(8,128)(2,1)S(1)}, bf16[288,512]{1,0:T(8,128)(2,1)S(1)}, u32[]{:S(2)}, u32[]{:S(2)}) collective-permute-start(bf16[288,512]{1,0:T(8,128)(2,1)S(1)} %get-tuple-element.55), channel_id=1, source_target_pairs={{0,16},{8,24},{16,0},{24,8},{1,17},{9,25},{17,1},{25,9},{2,18},{10... | collective-permute-start | bytes 884744 | tf_op jit(solution)/shard_map/ppermute | solution.py:325
  7.0 0.0 collective-permute-start.6
  7.0 0.1 shard_map.106
  7.0 0.1 collective-permute-start
  7.1 0.0 copy-start
  7.1 0.8 %collective-permute-start.1 = (bf16[256,512]{1,0:T(8,128)(2,1)S(1)}, bf16[256,512]{1,0:T(8,128)(2,1)S(1)}, u32[]{:S(2)}, u32[]{:S(2)}) collective-permute-start(bf16[256,512]{1,0:T(8,128)(2,1)S(1)} %get-tuple-element.50), channel_id=1, source_target_pairs={{1,2},{3,4},{5,6},{2,1},{4,3},{6,5},{9,10},{11,12},{13,14},{10,9},... | collective-permute-start | bytes 786440 | tf_op jit(solution)/shard_map/ppermute | solution.py:330
  8.0 0.1 slice-done.1
  8.0 4.8 %shard_map.104.part_ref = f32[4,256,512]{2,1,0:T(8,128)S(1)} custom-call(bf16[4,4,64,512]{3,2,1,0:T(8,128)(2,1)S(1)} %copy-done.1, bf16[3,3,512,512]{3,2,1,0:T(8,128)(2,1)S(1)} %bitcast.4), custom_call_target="tpu_custom_call" | custom-call | flops 4294967296 | bytes 7864320 | tf_op jit(solution)/shard_map/pallas_call | solution.py:18
  12.8 0.0 collective-permute-done.1.far_ref
  12.8 1.9 %shard_map.107 = (bf16[4,4,64,512]{3,2,1,0:T(8,128)(2,1)S(1)}, bf16[4,64,512]{2,1,0:T(8,128)(2,1)S(1)}, bf16[4,64,512]{2,1,0:T(8,128)(2,1)S(1)}) custom-call(f32[4,256,512]{2,1,0:T(8,128)S(1)} %shard_map.104.part_ref, bf16[256,512]{1,0:T(8,128)(2,1)S(1)} %collective-permute-done.near_ref, bf16[256,512]{1,0:T(8,128)(2,1)S(1)} %collective-permute-done.1.far_ref, ...), custom_call_target="tpu_custom_call" | custom-call | flops 1610612736 | bytes 9961472 | tf_op jit(solution)/shard_map/pallas_call | solution.py:18
  14.7 2.0 %collective-permute-start.2 = (bf16[4,64,512]{2,1,0:T(8,128)(2,1)S(1)}, bf16[4,64,512]{2,1,0:T(8,128)(2,1)S(1)}, u32[]{:S(2)}, u32[]{:S(2)}) collective-permute-start(bf16[4,64,512]{2,1,0:T(8,128)(2,1)S(1)} %get-tuple-element.52), channel_id=1, source_target_pairs={{0,8},{8,0},{16,24},{24,16},{1,9},{9,1},{17,25},{25,17},{2,10},{10... | collective-permute-start | bytes 786440 | tf_op jit(solution)/shard_map/ppermute | solution.py:325
  16.7 0.7 %collective-permute-start.3 = (bf16[4,64,512]{2,1,0:T(8,128)(2,1)S(1)}, bf16[4,64,512]{2,1,0:T(8,128)(2,1)S(1)}, u32[]{:S(2)}, u32[]{:S(2)}) collective-permute-start(bf16[4,64,512]{2,1,0:T(8,128)(2,1)S(1)} %get-tuple-element.53), channel_id=1, source_target_pairs={{8,16},{16,8},{9,17},{17,9},{10,18},{18,10},{11,19},{19,11},{12,20... | collective-permute-start | bytes 786440 | tf_op jit(solution)/shard_map/ppermute | solution.py:330
  17.4 1.4 %shard_map.108.part_ref = f32[512,1536]{1,0:T(8,128)S(1)} custom-call(bf16[4,4,64,512]{3,2,1,0:T(8,128)(2,1)S(1)} %get-tuple-element.51.act_ref, bf16[4,4,64,512]{3,2,1,0:T(8,128)(2,1)S(1)} %copy-done), custom_call_target="tpu_custom_call" | custom-call | flops 1207959552 | bytes 5242880 | tf_op jit(solution)/shard_map/pallas_call | solution.py:18
  18.8 0.0 collective-permute-done.4.refs_1_
  18.8 1.4 %collective-permute-done.5.refs_2_ = bf16[288,512]{1,0:T(8,128)(2,1)S(1)} collective-permute-done((bf16[288,512]{1,0:T(8,128)(2,1)S(1)}, bf16[288,512]{1,0:T(8,128)(2,1)S(1)}, u32[]{:S(2)}, u32[]{:S(2)}) %collective-permute-start.5) | collective-permute-done | bytes 294944 | tf_op jit(solution)/shard_map/ppermute | solution.py:325
  20.2 0.5 shard_map.109
  20.7 1.3 %collective-permute-start.7 = (bf16[288,512]{1,0:T(8,128)(2,1)S(1)}, bf16[288,512]{1,0:T(8,128)(2,1)S(1)}, u32[]{:S(2)}, u32[]{:S(2)}) collective-permute-start(bf16[288,512]{1,0:T(8,128)(2,1)S(1)} %get-tuple-element.59), channel_id=1, source_target_pairs={{0,1},{1,0},{2,3},{3,2},{4,5},{5,4},{6,7},{7,6},{8,9},{9,8},{10,11... | collective-permute-start | bytes 884744 | tf_op jit(solution)/shard_map/ppermute | solution.py:325
  22.0 0.8 %collective-permute-start.8 = (bf16[288,512]{1,0:T(8,128)(2,1)S(1)}, bf16[288,512]{1,0:T(8,128)(2,1)S(1)}, u32[]{:S(2)}, u32[]{:S(2)}) collective-permute-start(bf16[288,512]{1,0:T(8,128)(2,1)S(1)} %get-tuple-element.60), channel_id=1, source_target_pairs={{1,2},{3,4},{5,6},{2,1},{4,3},{6,5},{9,10},{11,12},{13,14},{10,9},... | collective-permute-start | bytes 884744 | tf_op jit(solution)/shard_map/ppermute | solution.py:330
  22.9 0.0 copy-start.2
  22.9 0.0 copy-start.3
  22.9 0.0 copy-start.4
  22.9 0.0 copy-start.5
  22.9 0.0 copy-start.6
  22.9 0.0 copy-start.7
  22.9 2.7 %shard_map.110.act_ref = bf16[2,256,512]{2,1,0:T(8,128)(2,1)S(1)} custom-call(bf16[4,288,512]{2,1,0:T(8,128)(2,1)S(1)} %get-tuple-element.64.x_ref, bf16[3,3,512,512]{3,2,1,0:T(8,128)(2,1)S(1)} %bitcast.4), custom_call_target="tpu_custom_call" | custom-call | flops 2415919104 | bytes 6422528 | tf_op jit(solution)/shard_map/pallas_call | solution.py:18
  25.7 2.8 %shard_map.111 = (bf16[2,64,512]{2,1,0:T(8,128)(2,1)S(1)}, bf16[2,64,512]{2,1,0:T(8,128)(2,1)S(1)}, bf16[2,64,512]{2,1,0:T(8,128)(2,1)S(1)}, bf16[2,64,512]{2,1,0:T(8,128)(2,1)S(1)}) custom-call(bf16[2,256,512]{2,1,0:T(8,128)(2,1)S(1)} %shard_map.110.act_ref, bf16[4,288,512]{2,1,0:T(8,128)(2,1)S(1)} %get-tuple-element.64.x_ref, ...), custom_call_target="tpu_custom_call" | custom-call | flops 2415919104 | bytes 5900288 | tf_op jit(solution)/shard_map/pallas_call | solution.py:18
  28.5 0.6 shard_map.112
  29.2 3.0 %collective-permute-start.9 = (bf16[256,1536]{1,0:T(8,128)(2,1)S(1)}, bf16[256,1536]{1,0:T(8,128)(2,1)S(1)}, u32[]{:S(2)}, u32[]{:S(2)}) collective-permute-start(bf16[256,1536]{1,0:T(8,128)(2,1)S(1)} %get-tuple-element.63), channel_id=1, source_target_pairs={{0,1},{1,0},{2,3},{3,2},{4,5},{5,4},{6,7},{7,6},{8,9},{9,8},{10,11... | collective-permute-start | bytes 2359304 | tf_op jit(solution)/shard_map/ppermute | solution.py:325
  32.2 3.9 %collective-permute-start.10 = (bf16[2,64,512]{2,1,0:T(8,128)(2,1)S(1)}, bf16[2,64,512]{2,1,0:T(8,128)(2,1)S(1)}, u32[]{:S(2)}, u32[]{:S(2)}) collective-permute-start(bf16[2,64,512]{2,1,0:T(8,128)(2,1)S(1)} %get-tuple-element.74), channel_id=1, source_target_pairs={{0,8},{8,0},{16,24},{24,16},{1,9},{9,1},{17,25},{25,17},{2,10},{10... | collective-permute-start | bytes 393224 | tf_op jit(solution)/shard_map/ppermute | solution.py:325
  36.1 1.5 %collective-permute-start.12 = (bf16[2,64,512]{2,1,0:T(8,128)(2,1)S(1)}, bf16[2,64,512]{2,1,0:T(8,128)(2,1)S(1)}, u32[]{:S(2)}, u32[]{:S(2)}) collective-permute-start(bf16[2,64,512]{2,1,0:T(8,128)(2,1)S(1)} %get-tuple-element.76), channel_id=1, source_target_pairs={{0,24},{8,16},{16,8},{24,0},{1,25},{9,17},{17,9},{25,1},{2,26},{10... | collective-permute-start | bytes 393224 | tf_op jit(solution)/shard_map/ppermute | solution.py:325
  37.6 2.7 %shard_map.113.act_ref = bf16[2,256,512]{2,1,0:T(8,128)(2,1)S(1)} custom-call(bf16[4,288,512]{2,1,0:T(8,128)(2,1)S(1)} %get-tuple-element.64.x_ref, bf16[288,512]{1,0:T(8,128)(2,1)S(1)} %collective-permute-done.7.near_ref, bf16[288,512]{1,0:T(8,128)(2,1)S(1)} %collective-permute-done.8.far_ref, bf16[3,3,512,512]{3,2,1,0:T(8,128)(2,1)S(1)} %bitcast.4), custom_call_target="tpu_custom_call" | custom-call | flops 2415919104 | bytes 7012352 | tf_op jit(solution)/shard_map/pallas_call | solution.py:18
  40.3 0.3 shard_map.114
  40.6 2.1 %collective-permute-start.16 = (bf16[256,384]{1,0:T(8,128)(2,1)S(1)}, bf16[256,384]{1,0:T(8,128)(2,1)S(1)}, u32[]{:S(2)}, u32[]{:S(2)}) collective-permute-start(bf16[256,384]{1,0:T(8,128)(2,1)S(1)} %get-tuple-element.71), channel_id=1, source_target_pairs={{0,8},{8,0},{16,24},{24,16},{1,9},{9,1},{17,25},{25,17},{2,10},{10... | collective-permute-start | bytes 589832 | tf_op jit(solution)/shard_map/ppermute | solution.py:325
  42.7 1.5 %collective-permute-start.18 = (bf16[256,384]{1,0:T(8,128)(2,1)S(1)}, bf16[256,384]{1,0:T(8,128)(2,1)S(1)}, u32[]{:S(2)}, u32[]{:S(2)}) collective-permute-start(bf16[256,384]{1,0:T(8,128)(2,1)S(1)} %get-tuple-element.73), channel_id=1, source_target_pairs={{0,24},{8,16},{16,8},{24,0},{1,25},{9,17},{17,9},{25,1},{2,26},{10... | collective-permute-start | bytes 589832 | tf_op jit(solution)/shard_map/ppermute | solution.py:325
  44.2 2.8 %shard_map.115 = (bf16[2,64,512]{2,1,0:T(8,128)(2,1)S(1)}, bf16[2,64,512]{2,1,0:T(8,128)(2,1)S(1)}, bf16[2,64,512]{2,1,0:T(8,128)(2,1)S(1)}, bf16[2,64,512]{2,1,0:T(8,128)(2,1)S(1)}) custom-call(bf16[2,256,512]{2,1,0:T(8,128)(2,1)S(1)} %shard_map.113.act_ref, bf16[4,288,512]{2,1,0:T(8,128)(2,1)S(1)} %get-tuple-element.64.x_ref, ...), custom_call_target="tpu_custom_call" | custom-call | flops 2415919104 | bytes 5900288 | tf_op jit(solution)/shard_map/pallas_call | solution.py:18
  47.0 2.0 %collective-permute-start.13 = (bf16[2,64,512]{2,1,0:T(8,128)(2,1)S(1)}, bf16[2,64,512]{2,1,0:T(8,128)(2,1)S(1)}, u32[]{:S(2)}, u32[]{:S(2)}) collective-permute-start(bf16[2,64,512]{2,1,0:T(8,128)(2,1)S(1)} %get-tuple-element.83), channel_id=1, source_target_pairs={{0,8},{8,0},{16,24},{24,16},{1,9},{9,1},{17,25},{25,17},{2,10},{10... | collective-permute-start | bytes 393224 | tf_op jit(solution)/shard_map/ppermute | solution.py:325
  49.0 1.5 %collective-permute-start.15 = (bf16[2,64,512]{2,1,0:T(8,128)(2,1)S(1)}, bf16[2,64,512]{2,1,0:T(8,128)(2,1)S(1)}, u32[]{:S(2)}, u32[]{:S(2)}) collective-permute-start(bf16[2,64,512]{2,1,0:T(8,128)(2,1)S(1)} %get-tuple-element.85), channel_id=1, source_target_pairs={{0,24},{8,16},{16,8},{24,0},{1,25},{9,17},{17,9},{25,1},{2,26},{10... | collective-permute-start | bytes 393224 | tf_op jit(solution)/shard_map/ppermute | solution.py:325
  50.6 4.5 %collective-permute-done.17.refs_2_ = bf16[256,384]{1,0:T(8,128)(2,1)S(1)} collective-permute-done((bf16[256,384]{1,0:T(8,128)(2,1)S(1)}, bf16[256,384]{1,0:T(8,128)(2,1)S(1)}, u32[]{:S(2)}, u32[]{:S(2)}) %collective-permute-start.17) | collective-permute-done | bytes 196640 | tf_op jit(solution)/shard_map/ppermute | solution.py:325
  55.1 0.1 shard_map.117
  55.2 1.6 %collective-permute-start.19 = (bf16[128,384]{1,0:T(8,128)(2,1)S(1)}, bf16[128,384]{1,0:T(8,128)(2,1)S(1)}, u32[]{:S(2)}, u32[]{:S(2)}) collective-permute-start(bf16[128,384]{1,0:T(8,128)(2,1)S(1)} %get-tuple-element.91), channel_id=1, source_target_pairs={{0,2},{1,3},{2,0},{3,1},{4,6},{5,7},{6,4},{7,5},{8,10},{9,11},{10,... | collective-permute-start | bytes 294920 | tf_op jit(solution)/shard_map/ppermute | solution.py:325
  56.9 3.0 %collective-permute-done.19.refs_1_ = bf16[128,384]{1,0:T(8,128)(2,1)S(1)} collective-permute-done((bf16[128,384]{1,0:T(8,128)(2,1)S(1)}, bf16[128,384]{1,0:T(8,128)(2,1)S(1)}, u32[]{:S(2)}, u32[]{:S(2)}) %collective-permute-start.19) | collective-permute-done | bytes 98336 | tf_op jit(solution)/shard_map/ppermute | solution.py:325
  59.9 2.5 %collective-permute-start.20 = (bf16[64,384]{1,0:T(8,128)(2,1)S(1)}, bf16[64,384]{1,0:T(8,128)(2,1)S(1)}, u32[]{:S(2)}, u32[]{:S(2)}) collective-permute-start(bf16[64,384]{1,0:T(8,128)(2,1)S(1)} %get-tuple-element.93), channel_id=1, source_target_pairs={{0,4},{1,5},{2,6},{3,7},{4,0},{5,1},{6,2},{7,3},{8,12},{9,13},{10,... | collective-permute-start | bytes 147464 | tf_op jit(solution)/shard_map/ppermute | solution.py:325
  62.4 1.0 %shard_map.116 = bf16[4,4,64,512]{3,2,1,0:T(8,128)(2,1)} custom-call(bf16[2,64,512]{2,1,0:T(8,128)(2,1)S(1)} %get-tuple-element.77.refs_0_, bf16[2,64,512]{2,1,0:T(8,128)(2,1)S(1)} %collective-permute-done.10.refs_1_, bf16[2,64,512]{2,1,0:T(8,128)(2,1)S(1)} %collective-permute-done.11.refs_2_, bf16[2,64,512]{2,1,0:T(8,128)(2,1)S(1)} %collective-permute-done.12.refs_3_, ...), custom_call_target="tpu_custom_call" | custom-call | flops 17179869184 | bytes 4194304 | tf_op jit(solution)/shard_map/pallas_call | solution.py:372
  63.4 1.5 %collective-permute-done.20.refs_1_ = bf16[64,384]{1,0:T(8,128)(2,1)S(1)} collective-permute-done((bf16[64,384]{1,0:T(8,128)(2,1)S(1)}, bf16[64,384]{1,0:T(8,128)(2,1)S(1)}, u32[]{:S(2)}, u32[]{:S(2)}) %collective-permute-start.20) | collective-permute-done | bytes 49184 | tf_op jit(solution)/shard_map/ppermute | solution.py:325
  65.0 0.7 shard_map.119
  (31 shorter events, 0.1 us)
Async XLA Ops:
  0.6 1.2 %copy-start.1 = (bf16[4,4,64,512]{3,2,1,0:T(8,128)(2,1)S(1)}, bf16[4,4,64,512]{3,2,1,0:T(8,128)(2,1)}, u32[]{:S(2)}) copy-start(bf16[4,4,64,512]{3,2,1,0:T(8,128)(2,1)} %x_ref.5) | copy-start | bytes 3145732
  1.9 6.1 %slice-start = ((s8[4718592]{0:T(1024)(128)(4,1)}), s8[4194304]{0:T(1024)(128)(4,1)S(1)}, s32[]{:S(2)}) async-start(s8[4718592]{0:T(1024)(128)(4,1)} %bitcast.3), calls=%async_computation | async-start | bytes 8388608
  2.4 16.4 %collective-permute-start.4 = (bf16[288,512]{1,0:T(8,128)(2,1)S(1)}, bf16[288,512]{1,0:T(8,128)(2,1)S(1)}, u32[]{:S(2)}, u32[]{:S(2)}) collective-permute-start(bf16[288,512]{1,0:T(8,128)(2,1)S(1)} %get-tuple-element.54), channel_id=1, source_target_pairs={{0,8},{8,0},{16,24},{24,16},{1,9},{9,1},{17,25},{25,17},{2,10},{10... | collective-permute-start | bytes 884744 | tf_op jit(solution)/shard_map/ppermute | solution.py:325
  5.4 14.8 %collective-permute-start.5 = (bf16[288,512]{1,0:T(8,128)(2,1)S(1)}, bf16[288,512]{1,0:T(8,128)(2,1)S(1)}, u32[]{:S(2)}, u32[]{:S(2)}) collective-permute-start(bf16[288,512]{1,0:T(8,128)(2,1)S(1)} %get-tuple-element.55), channel_id=1, source_target_pairs={{0,16},{8,24},{16,0},{24,8},{1,17},{9,25},{17,1},{25,9},{2,18},{10... | collective-permute-start | bytes 884744 | tf_op jit(solution)/shard_map/ppermute | solution.py:325
  7.0 13.3 %collective-permute-start.6 = (bf16[288,512]{1,0:T(8,128)(2,1)S(1)}, bf16[288,512]{1,0:T(8,128)(2,1)S(1)}, u32[]{:S(2)}, u32[]{:S(2)}) collective-permute-start(bf16[288,512]{1,0:T(8,128)(2,1)S(1)} %get-tuple-element.56), channel_id=1, source_target_pairs={{0,24},{8,16},{16,8},{24,0},{1,25},{9,17},{17,9},{25,1},{2,26},{10... | collective-permute-start | bytes 884744 | tf_op jit(solution)/shard_map/ppermute | solution.py:325
  7.0 1.0 %slice-start.1 = ((s8[4718592]{0:T(1024)(128)(4,1)}), s8[524288]{0:T(1024)(128)(4,1)S(1)}, s32[]{:S(2)}) async-start(s8[4718592]{0:T(1024)(128)(4,1)} %bitcast.3), calls=%async_computation.1 | async-start | bytes 1048576
  7.0 5.7 %collective-permute-start = (bf16[256,512]{1,0:T(8,128)(2,1)S(1)}, bf16[256,512]{1,0:T(8,128)(2,1)S(1)}, u32[]{:S(2)}, u32[]{:S(2)}) collective-permute-start(bf16[256,512]{1,0:T(8,128)(2,1)S(1)} %get-tuple-element.49), channel_id=1, source_target_pairs={{0,1},{1,0},{2,3},{3,2},{4,5},{5,4},{6,7},{7,6},{8,9},{9,8},{10,11... | collective-permute-start | bytes 786440 | tf_op jit(solution)/shard_map/ppermute | solution.py:325
  7.1 5.7 %copy-start = (bf16[4,4,64,512]{3,2,1,0:T(8,128)(2,1)S(1)}, bf16[4,4,64,512]{3,2,1,0:T(8,128)(2,1)}, u32[]{:S(2)}) copy-start(bf16[4,4,64,512]{3,2,1,0:T(8,128)(2,1)} %cot_ref.5) | copy-start | bytes 3145732
  7.1 5.7 %collective-permute-start.1 = (bf16[256,512]{1,0:T(8,128)(2,1)S(1)}, bf16[256,512]{1,0:T(8,128)(2,1)S(1)}, u32[]{:S(2)}, u32[]{:S(2)}) collective-permute-start(bf16[256,512]{1,0:T(8,128)(2,1)S(1)} %get-tuple-element.50), channel_id=1, source_target_pairs={{1,2},{3,4},{5,6},{2,1},{4,3},{6,5},{9,10},{11,12},{13,14},{10,9},... | collective-permute-start | bytes 786440 | tf_op jit(solution)/shard_map/ppermute | solution.py:330
  14.7 13.8 %collective-permute-start.2 = (bf16[4,64,512]{2,1,0:T(8,128)(2,1)S(1)}, bf16[4,64,512]{2,1,0:T(8,128)(2,1)S(1)}, u32[]{:S(2)}, u32[]{:S(2)}) collective-permute-start(bf16[4,64,512]{2,1,0:T(8,128)(2,1)S(1)} %get-tuple-element.52), channel_id=1, source_target_pairs={{0,8},{8,0},{16,24},{24,16},{1,9},{9,1},{17,25},{25,17},{2,10},{10... | collective-permute-start | bytes 786440 | tf_op jit(solution)/shard_map/ppermute | solution.py:325
  16.7 11.8 %collective-permute-start.3 = (bf16[4,64,512]{2,1,0:T(8,128)(2,1)S(1)}, bf16[4,64,512]{2,1,0:T(8,128)(2,1)S(1)}, u32[]{:S(2)}, u32[]{:S(2)}) collective-permute-start(bf16[4,64,512]{2,1,0:T(8,128)(2,1)S(1)} %get-tuple-element.53), channel_id=1, source_target_pairs={{8,16},{16,8},{9,17},{17,9},{10,18},{18,10},{11,19},{19,11},{12,20... | collective-permute-start | bytes 786440 | tf_op jit(solution)/shard_map/ppermute | solution.py:330
  20.7 7.8 %collective-permute-start.7 = (bf16[288,512]{1,0:T(8,128)(2,1)S(1)}, bf16[288,512]{1,0:T(8,128)(2,1)S(1)}, u32[]{:S(2)}, u32[]{:S(2)}) collective-permute-start(bf16[288,512]{1,0:T(8,128)(2,1)S(1)} %get-tuple-element.59), channel_id=1, source_target_pairs={{0,1},{1,0},{2,3},{3,2},{4,5},{5,4},{6,7},{7,6},{8,9},{9,8},{10,11... | collective-permute-start | bytes 884744 | tf_op jit(solution)/shard_map/ppermute | solution.py:325
  22.0 6.5 %collective-permute-start.8 = (bf16[288,512]{1,0:T(8,128)(2,1)S(1)}, bf16[288,512]{1,0:T(8,128)(2,1)S(1)}, u32[]{:S(2)}, u32[]{:S(2)}) collective-permute-start(bf16[288,512]{1,0:T(8,128)(2,1)S(1)} %get-tuple-element.60), channel_id=1, source_target_pairs={{1,2},{3,4},{5,6},{2,1},{4,3},{6,5},{9,10},{11,12},{13,14},{10,9},... | collective-permute-start | bytes 884744 | tf_op jit(solution)/shard_map/ppermute | solution.py:330
  22.9 2.8 %copy-start.2 = (bf16[3,512,512]{2,1,0:T(8,128)(2,1)S(1)}, bf16[3,512,512]{2,1,0:T(8,128)(2,1)}, u32[]{:S(2)}) copy-start(bf16[3,512,512]{2,1,0:T(8,128)(2,1)} %param.11) | copy-start | bytes 4718596
  22.9 2.8 %copy-start.3 = (bf16[512,512]{1,0:T(8,128)(2,1)S(1)}, bf16[512,512]{1,0:T(8,128)(2,1)}, u32[]{:S(2)}) copy-start(bf16[512,512]{1,0:T(8,128)(2,1)} %q_ref.3) | copy-start | bytes 1572868
  22.9 2.8 %copy-start.4 = (bf16[512,512]{1,0:T(8,128)(2,1)S(1)}, bf16[512,512]{1,0:T(8,128)(2,1)}, u32[]{:S(2)}) copy-start(bf16[512,512]{1,0:T(8,128)(2,1)} %k_ref.3) | copy-start | bytes 1572868
  22.9 2.8 %copy-start.5 = (bf16[512,512]{1,0:T(8,128)(2,1)S(1)}, bf16[512,512]{1,0:T(8,128)(2,1)}, u32[]{:S(2)}) copy-start(bf16[512,512]{1,0:T(8,128)(2,1)} %v_ref.3) | copy-start | bytes 1572868
  22.9 2.7 %copy-start.6 = (bf16[512,512]{1,0:T(8,128)(2,1)S(1)}, bf16[512,512]{1,0:T(8,128)(2,1)}, u32[]{:S(2)}) copy-start(bf16[512,512]{1,0:T(8,128)(2,1)} %o_ref.3) | copy-start | bytes 1572868
  22.9 2.7 %copy-start.7 = (f32[512]{0:T(512)S(1)}, f32[512]{0:T(512)}, u32[]{:S(2)}) copy-start(f32[512]{0:T(512)} %param.12) | copy-start | bytes 6148
  29.2 11.1 %collective-permute-start.9 = (bf16[256,1536]{1,0:T(8,128)(2,1)S(1)}, bf16[256,1536]{1,0:T(8,128)(2,1)S(1)}, u32[]{:S(2)}, u32[]{:S(2)}) collective-permute-start(bf16[256,1536]{1,0:T(8,128)(2,1)S(1)} %get-tuple-element.63), channel_id=1, source_target_pairs={{0,1},{1,0},{2,3},{3,2},{4,5},{5,4},{6,7},{7,6},{8,9},{9,8},{10,11... | collective-permute-start | bytes 2359304 | tf_op jit(solution)/shard_map/ppermute | solution.py:325
  32.2 10.5 %collective-permute-start.10 = (bf16[2,64,512]{2,1,0:T(8,128)(2,1)S(1)}, bf16[2,64,512]{2,1,0:T(8,128)(2,1)S(1)}, u32[]{:S(2)}, u32[]{:S(2)}) collective-permute-start(bf16[2,64,512]{2,1,0:T(8,128)(2,1)S(1)} %get-tuple-element.74), channel_id=1, source_target_pairs={{0,8},{8,0},{16,24},{24,16},{1,9},{9,1},{17,25},{25,17},{2,10},{10... | collective-permute-start | bytes 393224 | tf_op jit(solution)/shard_map/ppermute | solution.py:325
  36.1 8.1 %collective-permute-start.11 = (bf16[2,64,512]{2,1,0:T(8,128)(2,1)S(1)}, bf16[2,64,512]{2,1,0:T(8,128)(2,1)S(1)}, u32[]{:S(2)}, u32[]{:S(2)}) collective-permute-start(bf16[2,64,512]{2,1,0:T(8,128)(2,1)S(1)} %get-tuple-element.75), channel_id=1, source_target_pairs={{0,16},{8,24},{16,0},{24,8},{1,17},{9,25},{17,1},{25,9},{2,18},{10... | collective-permute-start | bytes 393224 | tf_op jit(solution)/shard_map/ppermute | solution.py:325
  36.1 8.1 %collective-permute-start.12 = (bf16[2,64,512]{2,1,0:T(8,128)(2,1)S(1)}, bf16[2,64,512]{2,1,0:T(8,128)(2,1)S(1)}, u32[]{:S(2)}, u32[]{:S(2)}) collective-permute-start(bf16[2,64,512]{2,1,0:T(8,128)(2,1)S(1)} %get-tuple-element.76), channel_id=1, source_target_pairs={{0,24},{8,16},{16,8},{24,0},{1,25},{9,17},{17,9},{25,1},{2,26},{10... | collective-permute-start | bytes 393224 | tf_op jit(solution)/shard_map/ppermute | solution.py:325
  40.6 8.4 %collective-permute-start.16 = (bf16[256,384]{1,0:T(8,128)(2,1)S(1)}, bf16[256,384]{1,0:T(8,128)(2,1)S(1)}, u32[]{:S(2)}, u32[]{:S(2)}) collective-permute-start(bf16[256,384]{1,0:T(8,128)(2,1)S(1)} %get-tuple-element.71), channel_id=1, source_target_pairs={{0,8},{8,0},{16,24},{24,16},{1,9},{9,1},{17,25},{25,17},{2,10},{10... | collective-permute-start | bytes 589832 | tf_op jit(solution)/shard_map/ppermute | solution.py:325
  42.7 12.4 %collective-permute-start.17 = (bf16[256,384]{1,0:T(8,128)(2,1)S(1)}, bf16[256,384]{1,0:T(8,128)(2,1)S(1)}, u32[]{:S(2)}, u32[]{:S(2)}) collective-permute-start(bf16[256,384]{1,0:T(8,128)(2,1)S(1)} %get-tuple-element.72), channel_id=1, source_target_pairs={{0,16},{8,24},{16,0},{24,8},{1,17},{9,25},{17,1},{25,9},{2,18},{10... | collective-permute-start | bytes 589832 | tf_op jit(solution)/shard_map/ppermute | solution.py:325
  42.7 12.4 %collective-permute-start.18 = (bf16[256,384]{1,0:T(8,128)(2,1)S(1)}, bf16[256,384]{1,0:T(8,128)(2,1)S(1)}, u32[]{:S(2)}, u32[]{:S(2)}) collective-permute-start(bf16[256,384]{1,0:T(8,128)(2,1)S(1)} %get-tuple-element.73), channel_id=1, source_target_pairs={{0,24},{8,16},{16,8},{24,0},{1,25},{9,17},{17,9},{25,1},{2,26},{10... | collective-permute-start | bytes 589832 | tf_op jit(solution)/shard_map/ppermute | solution.py:325
  47.0 15.4 %collective-permute-start.13 = (bf16[2,64,512]{2,1,0:T(8,128)(2,1)S(1)}, bf16[2,64,512]{2,1,0:T(8,128)(2,1)S(1)}, u32[]{:S(2)}, u32[]{:S(2)}) collective-permute-start(bf16[2,64,512]{2,1,0:T(8,128)(2,1)S(1)} %get-tuple-element.83), channel_id=1, source_target_pairs={{0,8},{8,0},{16,24},{24,16},{1,9},{9,1},{17,25},{25,17},{2,10},{10... | collective-permute-start | bytes 393224 | tf_op jit(solution)/shard_map/ppermute | solution.py:325
  49.0 13.4 %collective-permute-start.14 = (bf16[2,64,512]{2,1,0:T(8,128)(2,1)S(1)}, bf16[2,64,512]{2,1,0:T(8,128)(2,1)S(1)}, u32[]{:S(2)}, u32[]{:S(2)}) collective-permute-start(bf16[2,64,512]{2,1,0:T(8,128)(2,1)S(1)} %get-tuple-element.84), channel_id=1, source_target_pairs={{0,16},{8,24},{16,0},{24,8},{1,17},{9,25},{17,1},{25,9},{2,18},{10... | collective-permute-start | bytes 393224 | tf_op jit(solution)/shard_map/ppermute | solution.py:325
  49.0 13.4 %collective-permute-start.15 = (bf16[2,64,512]{2,1,0:T(8,128)(2,1)S(1)}, bf16[2,64,512]{2,1,0:T(8,128)(2,1)S(1)}, u32[]{:S(2)}, u32[]{:S(2)}) collective-permute-start(bf16[2,64,512]{2,1,0:T(8,128)(2,1)S(1)} %get-tuple-element.85), channel_id=1, source_target_pairs={{0,24},{8,16},{16,8},{24,0},{1,25},{9,17},{17,9},{25,1},{2,26},{10... | collective-permute-start | bytes 393224 | tf_op jit(solution)/shard_map/ppermute | solution.py:325
  55.2 4.7 %collective-permute-start.19 = (bf16[128,384]{1,0:T(8,128)(2,1)S(1)}, bf16[128,384]{1,0:T(8,128)(2,1)S(1)}, u32[]{:S(2)}, u32[]{:S(2)}) collective-permute-start(bf16[128,384]{1,0:T(8,128)(2,1)S(1)} %get-tuple-element.91), channel_id=1, source_target_pairs={{0,2},{1,3},{2,0},{3,1},{4,6},{5,7},{6,4},{7,5},{8,10},{9,11},{10,... | collective-permute-start | bytes 294920 | tf_op jit(solution)/shard_map/ppermute | solution.py:325
  59.9 5.1 %collective-permute-start.20 = (bf16[64,384]{1,0:T(8,128)(2,1)S(1)}, bf16[64,384]{1,0:T(8,128)(2,1)S(1)}, u32[]{:S(2)}, u32[]{:S(2)}) collective-permute-start(bf16[64,384]{1,0:T(8,128)(2,1)S(1)} %get-tuple-element.93), channel_id=1, source_target_pairs={{0,4},{1,5},{2,6},{3,7},{4,0},{5,1},{6,2},{7,3},{8,12},{9,13},{10,... | collective-permute-start | bytes 147464 | tf_op jit(solution)/shard_map/ppermute | solution.py:325

commit v13 on v10

--- a/solution.py
+++ b/solution.py
@@ -343,15 +343,15 @@
         send[rows] = jnp.where(lower, high, low).astype(BF)
 
 
-def sum_kernel(z, *refs):
-    out, wide = refs[-1], z.c // z.n
-    total = sum(part[...].astype(F32) for part in refs[:-1])
+def add_up(z, kept_ref, got_ref, out):
+    wide = z.c // z.n
+    total = kept_ref[...] + got_ref[...].astype(F32)
     for k in range(3):
         out[k] = total[:, k * wide : (k + 1) * wide]
 
 
-def join_kernel(z, *refs):
-    parts, (out, whole, sem) = refs[: z.n], refs[z.n :]
+def join_kernel(z, kept_ref, got_ref, *refs):
+    parts, (out, grad, whole, sem) = refs[: z.n], refs[z.n :]
     me = lax.axis_index("tm")
     copies = []
     for f in range(z.fl):
@@ -360,17 +360,19 @@
             whole[f, :, cols] = parts[k][:, f * z.wc : (f + 1) * z.wc]
         copies.append(pltpu.make_async_copy(whole.at[f], out.at[f], sem.at[f]))
         copies[f].start()
+    add_up(z, kept_ref, got_ref, grad)
     for copy in copies:
         copy.wait()
 
 
-def joined(z, back):
+def joined(z, back, kept, got):
+    grad = shape((3, kept.shape[0], z.c // z.n), F32)
     if z.wc % 16 == 0:
         return pl.pallas_call(
             functools.partial(join_kernel, z),
-            out_shape=shape((z.fl, z.r, z.w, z.c)),
-            in_specs=[VMEM] * z.n,
-            out_specs=pl.BlockSpec(memory_space=pl.ANY),
+            out_shape=(shape((z.fl, z.r, z.w, z.c)), grad),
+            in_specs=[VMEM] * (2 + z.n),
+            out_specs=(pl.BlockSpec(memory_space=pl.ANY), VMEM),
             scratch_shapes=[
                 pltpu.VMEM((z.fl, z.r, z.w, z.c), BF),
                 pltpu.SemaphoreType.DMA((z.fl,)),
@@ -379,12 +381,13 @@
             cost_estimate=pl.CostEstimate(
                 flops=0, bytes_accessed=8 * z.n * z.main * z.c, transcendentals=0
             ),
-        )(*back)
+        )(kept, got, *back)
     whole = jnp.zeros((z.fl, z.r, z.n, z.wc, z.c), BF)
     for k in range(z.n):
         rows = back[k].reshape(z.r, z.fl, 1, z.wc, z.c).transpose(1, 0, 2, 3, 4)
         whole = lax.dynamic_update_slice_in_dim(whole, rows, lax.axis_index("tm") ^ k, 2)
-    return whole.reshape(z.fl, z.r, z.w, z.c)
+    (grad,) = call(functools.partial(add_up, z), [grad], kept, got)
+    return whole.reshape(z.fl, z.r, z.w, z.c), grad
 
 
 def on_device(frames_in, spatial, temporal, gain, q_w, k_w, v_w, o_w, cotangent):
@@ -510,10 +513,8 @@
         )
         pieces = (keep, swap(send, "space", 2 << bit))
         bit += 1
-    (kernel_grad,) = call(
-        functools.partial(sum_kernel, z), [shape((3, width, wide), F32)], *pieces
-    )
-    return joined(z, back), kernel_grad.transpose(0, 2, 1)
+    encoded, kernel_grad = joined(z, back, *pieces)
+    return encoded, kernel_grad.transpose(0, 2, 1)
 
 
 def solution(mesh):

time: 61.2 us -> 61.4 us (level); the launches traced: 60.2 us -> 61.2 us
  waiting for transfers between devices: 7.28 us -> 8.21 us
    ppermute x15, waiting for transfers between devices: 7.27 us -> 8.2 us  [swap(): return lax.ppermute(value, axis, [(i, i ^ k) for i in range(count)])]
    pallas_call x14 -> x13, Pallas kernels: 21.5 us -> 20.9 us  [call(): pl.pallas_call(kernel, out_shape=tuple(outs), in_specs=[VMEM] * len(args)...]
    pallas_call x1, Pallas kernels: 1.02 us -> 1.66 us  [joined(): pl.pallas_call(functools.partial(join_kernel, z), out_shape=(shape((z.fl,...]
  transfers between devices with their start and end apart: 18 -> 18, of which waited for: 4 -> 5; matrix products, arithmetic and copies ran while one was open for 0% -> 0% of each run, Pallas kernels for 34% -> 32%
where the time goes in v13:
time: 61.4 us; the launch traced here: 61.2 us
  starting transfers between devices  28.1 us (46%)
  Pallas kernels  22.5 us (37%)
  waiting for transfers between devices  8.21 us (13%)
  local copies, waits for them, and re-layouts  1.32 us (2%)
  between operations  1.07 us (2%)
    ppermute x15, starting transfers between devices, swap(): return lax.ppermute(value, axis, [(i, i ^ k) for i in range(count)])  25.7 us
    pallas_call x13, Pallas kernels, call(): pl.pallas_call(kernel, out_shape=tuple(outs), in_specs=[VMEM] * len(args)...  20.9 us
    ppermute x15, waiting for transfers between devices, swap(): return lax.ppermute(value, axis, [(i, i ^ k) for i in range(count)])  8.2 us
    ppermute x3, starting transfers between devices, swap_both(): far = lax.ppermute(far, axis, pairs + [(b, a) for a, b in pairs])  2.33 us
    pallas_call x1, Pallas kernels, joined(): pl.pallas_call(functools.partial(join_kernel, z), out_shape=(shape((z.fl,...  1.66 us
    unnamed x20, local copies, waits for them, and re-layouts  1.32 us
  transfers between devices with their start and end apart: 18, of which 5 were waited for; matrix products, arithmetic and copies ran while one was open for 0% of the time, Pallas kernels for 32%

profile of v13, /device:TPU:0, one launch (start us, length us, event | category | flops | bytes accessed | tf_op | source)
XLA Modules:
  0.0 61.2 jit_solution(5875641887746297294)
XLA Ops:
  0.6 1.2 %copy-done.1 = bf16[4,4,64,512]{3,2,1,0:T(8,128)(2,1)S(1)} copy-done((bf16[4,4,64,512]{3,2,1,0:T(8,128)(2,1)S(1)}, bf16[4,4,64,512]{3,2,1,0:T(8,128)(2,1)}, u32[]{:S(2)}) %copy-start.1) | copy-done | bytes 1048600
  1.9 0.6 shard_map.105
  2.4 3.0 %collective-permute-start.4 = (bf16[288,512]{1,0:T(8,128)(2,1)S(1)}, bf16[288,512]{1,0:T(8,128)(2,1)S(1)}, u32[]{:S(2)}, u32[]{:S(2)}) collective-permute-start(bf16[288,512]{1,0:T(8,128)(2,1)S(1)} %get-tuple-element.53), channel_id=1, source_target_pairs={{0,8},{8,0},{16,24},{24,16},{1,9},{9,1},{17,25},{25,17},{2,10},{10... | collective-permute-start | bytes 884744 | tf_op jit(solution)/shard_map/ppermute | solution.py:325
  5.4 1.5 %collective-permute-start.5 = (bf16[288,512]{1,0:T(8,128)(2,1)S(1)}, bf16[288,512]{1,0:T(8,128)(2,1)S(1)}, u32[]{:S(2)}, u32[]{:S(2)}) collective-permute-start(bf16[288,512]{1,0:T(8,128)(2,1)S(1)} %get-tuple-element.54), channel_id=1, source_target_pairs={{0,16},{8,24},{16,0},{24,8},{1,17},{9,25},{17,1},{25,9},{2,18},{10... | collective-permute-start | bytes 884744 | tf_op jit(solution)/shard_map/ppermute | solution.py:325
  7.0 0.0 collective-permute-start.6
  7.0 0.1 shard_map.106
  7.0 0.1 collective-permute-start
  7.1 0.0 copy-start
  7.1 0.8 %collective-permute-start.1 = (bf16[256,512]{1,0:T(8,128)(2,1)S(1)}, bf16[256,512]{1,0:T(8,128)(2,1)S(1)}, u32[]{:S(2)}, u32[]{:S(2)}) collective-permute-start(bf16[256,512]{1,0:T(8,128)(2,1)S(1)} %get-tuple-element.49), channel_id=1, source_target_pairs={{1,2},{3,4},{5,6},{2,1},{4,3},{6,5},{9,10},{11,12},{13,14},{10,9},... | collective-permute-start | bytes 786440 | tf_op jit(solution)/shard_map/ppermute | solution.py:330
  8.0 0.1 slice-done.1
  8.0 4.8 %shard_map.104.part_ref = f32[4,256,512]{2,1,0:T(8,128)S(1)} custom-call(bf16[4,4,64,512]{3,2,1,0:T(8,128)(2,1)S(1)} %copy-done.1, bf16[3,3,512,512]{3,2,1,0:T(8,128)(2,1)S(1)} %bitcast.3), custom_call_target="tpu_custom_call" | custom-call | flops 4294967296 | bytes 7864320 | tf_op jit(solution)/shard_map/pallas_call | solution.py:18
  12.8 0.0 collective-permute-done.near_ref
  12.8 0.0 collective-permute-done.1.far_ref
  12.8 1.9 %shard_map.107 = (bf16[4,4,64,512]{3,2,1,0:T(8,128)(2,1)S(1)}, bf16[4,64,512]{2,1,0:T(8,128)(2,1)S(1)}, bf16[4,64,512]{2,1,0:T(8,128)(2,1)S(1)}) custom-call(f32[4,256,512]{2,1,0:T(8,128)S(1)} %shard_map.104.part_ref, bf16[256,512]{1,0:T(8,128)(2,1)S(1)} %collective-permute-done.near_ref, bf16[256,512]{1,0:T(8,128)(2,1)S(1)} %collective-permute-done.1.far_ref, ...), custom_call_target="tpu_custom_call" | custom-call | flops 1610612736 | bytes 9961472 | tf_op jit(solution)/shard_map/pallas_call | solution.py:18
  14.7 2.0 %collective-permute-start.2 = (bf16[4,64,512]{2,1,0:T(8,128)(2,1)S(1)}, bf16[4,64,512]{2,1,0:T(8,128)(2,1)S(1)}, u32[]{:S(2)}, u32[]{:S(2)}) collective-permute-start(bf16[4,64,512]{2,1,0:T(8,128)(2,1)S(1)} %get-tuple-element.51), channel_id=1, source_target_pairs={{0,8},{8,0},{16,24},{24,16},{1,9},{9,1},{17,25},{25,17},{2,10},{10... | collective-permute-start | bytes 786440 | tf_op jit(solution)/shard_map/ppermute | solution.py:325
  16.7 0.7 %collective-permute-start.3 = (bf16[4,64,512]{2,1,0:T(8,128)(2,1)S(1)}, bf16[4,64,512]{2,1,0:T(8,128)(2,1)S(1)}, u32[]{:S(2)}, u32[]{:S(2)}) collective-permute-start(bf16[4,64,512]{2,1,0:T(8,128)(2,1)S(1)} %get-tuple-element.52), channel_id=1, source_target_pairs={{8,16},{16,8},{9,17},{17,9},{10,18},{18,10},{11,19},{19,11},{12,20... | collective-permute-start | bytes 786440 | tf_op jit(solution)/shard_map/ppermute | solution.py:330
  17.4 0.0 collective-permute-done.4.refs_1_
  17.4 2.8 %collective-permute-done.5.refs_2_ = bf16[288,512]{1,0:T(8,128)(2,1)S(1)} collective-permute-done((bf16[288,512]{1,0:T(8,128)(2,1)S(1)}, bf16[288,512]{1,0:T(8,128)(2,1)S(1)}, u32[]{:S(2)}, u32[]{:S(2)}) %collective-permute-start.5) | collective-permute-done | bytes 294944 | tf_op jit(solution)/shard_map/ppermute | solution.py:325
  20.2 0.5 shard_map.109
  20.7 0.1 collective-permute-start.7
  20.8 0.9 %collective-permute-start.8 = (bf16[288,512]{1,0:T(8,128)(2,1)S(1)}, bf16[288,512]{1,0:T(8,128)(2,1)S(1)}, u32[]{:S(2)}, u32[]{:S(2)}) collective-permute-start(bf16[288,512]{1,0:T(8,128)(2,1)S(1)} %get-tuple-element.58), channel_id=1, source_target_pairs={{1,2},{3,4},{5,6},{2,1},{4,3},{6,5},{9,10},{11,12},{13,14},{10,9},... | collective-permute-start | bytes 884744 | tf_op jit(solution)/shard_map/ppermute | solution.py:330
  21.7 1.4 %shard_map.108.part_ref = f32[512,1536]{1,0:T(8,128)S(1)} custom-call(bf16[4,4,64,512]{3,2,1,0:T(8,128)(2,1)S(1)} %get-tuple-element.50.act_ref, bf16[4,4,64,512]{3,2,1,0:T(8,128)(2,1)S(1)} %copy-done), custom_call_target="tpu_custom_call" | custom-call | flops 1207959552 | bytes 5242880 | tf_op jit(solution)/shard_map/pallas_call | solution.py:18
  23.1 2.7 %shard_map.110.middle_ref = bf16[2,256,512]{2,1,0:T(8,128)(2,1)S(1)} custom-call(bf16[4,288,512]{2,1,0:T(8,128)(2,1)S(1)} %get-tuple-element.62.x_ref, bf16[3,3,512,512]{3,2,1,0:T(8,128)(2,1)S(1)} %bitcast.3), custom_call_target="tpu_custom_call" | custom-call | flops 2415919104 | bytes 6422528 | tf_op jit(solution)/shard_map/pallas_call | solution.py:18
  25.8 0.0 collective-permute-done.2.near_ref
  25.8 0.0 collective-permute-done.7.near_ref
  25.8 0.0 collective-permute-done.8.far_ref
  25.8 0.7 %shard_map.111 = (f32[256,1536]{1,0:T(8,128)S(1)}, bf16[256,1536]{1,0:T(8,128)(2,1)S(1)}) custom-call(f32[512,1536]{1,0:T(8,128)S(1)} %shard_map.108.part_ref, bf16[4,64,512]{2,1,0:T(8,128)(2,1)S(1)} %collective-permute-done.2.near_ref, bf16[4,64,512]{2,1,0:T(8,128)(2,1)S(1)} %collective-permute-done.3.far_ref, ...), custom_call_target="tpu_custom_call" | custom-call | flops 402653184 | bytes 8126464 | tf_op jit(solution)/shard_map/pallas_call | solution.py:18
  26.5 3.6 %collective-permute-start.9 = (bf16[256,1536]{1,0:T(8,128)(2,1)S(1)}, bf16[256,1536]{1,0:T(8,128)(2,1)S(1)}, u32[]{:S(2)}, u32[]{:S(2)}) collective-permute-start(bf16[256,1536]{1,0:T(8,128)(2,1)S(1)} %get-tuple-element.61), channel_id=1, source_target_pairs={{0,1},{1,0},{2,3},{3,2},{4,5},{5,4},{6,7},{7,6},{8,9},{9,8},{10,11... | collective-permute-start | bytes 2359304 | tf_op jit(solution)/shard_map/ppermute | solution.py:325
  30.0 2.7 %shard_map.112.border_ref = bf16[2,256,512]{2,1,0:T(8,128)(2,1)S(1)} custom-call(bf16[4,288,512]{2,1,0:T(8,128)(2,1)S(1)} %get-tuple-element.62.x_ref, bf16[288,512]{1,0:T(8,128)(2,1)S(1)} %collective-permute-done.7.near_ref, bf16[288,512]{1,0:T(8,128)(2,1)S(1)} %collective-permute-done.8.far_ref, bf16[3,3,512,512]{3,2,1,0:T(8,128)(2,1)S(1)} %bitcast.3), custom_call_target="tpu_custom_call" | custom-call | flops 2415919104 | bytes 7012352 | tf_op jit(solution)/shard_map/pallas_call | solution.py:18
  32.7 0.0 copy-start.2
  32.7 0.0 copy-start.3
  32.8 0.0 copy-start.7
  32.8 0.3 shard_map.113
  33.1 3.3 %collective-permute-start.10 = (bf16[256,384]{1,0:T(8,128)(2,1)S(1)}, bf16[256,384]{1,0:T(8,128)(2,1)S(1)}, u32[]{:S(2)}, u32[]{:S(2)}) collective-permute-start(bf16[256,384]{1,0:T(8,128)(2,1)S(1)} %get-tuple-element.73), channel_id=1, source_target_pairs={{0,8},{8,0},{16,24},{24,16},{1,9},{9,1},{17,25},{25,17},{2,10},{10... | collective-permute-start | bytes 589832 | tf_op jit(solution)/shard_map/ppermute | solution.py:325
  36.4 0.0 collective-permute-start.11
  36.4 1.5 %collective-permute-start.12 = (bf16[256,384]{1,0:T(8,128)(2,1)S(1)}, bf16[256,384]{1,0:T(8,128)(2,1)S(1)}, u32[]{:S(2)}, u32[]{:S(2)}) collective-permute-start(bf16[256,384]{1,0:T(8,128)(2,1)S(1)} %get-tuple-element.75), channel_id=1, source_target_pairs={{0,24},{8,16},{16,8},{24,0},{1,25},{9,17},{17,9},{25,1},{2,26},{10... | collective-permute-start | bytes 589832 | tf_op jit(solution)/shard_map/ppermute | solution.py:325
  38.0 5.3 %shard_map.114 = (bf16[4,64,512]{2,1,0:T(8,128)(2,1)S(1)}, bf16[4,64,512]{2,1,0:T(8,128)(2,1)S(1)}, bf16[4,64,512]{2,1,0:T(8,128)(2,1)S(1)}, bf16[4,64,512]{2,1,0:T(8,128)(2,1)S(1)}) custom-call(bf16[2,256,512]{2,1,0:T(8,128)(2,1)S(1)} %shard_map.110.middle_ref, bf16[2,256,512]{2,1,0:T(8,128)(2,1)S(1)} %shard_map.112.border_ref, ...), custom_call_target="tpu_custom_call" | custom-call | flops 4831838208 | bytes 6948864 | tf_op jit(solution)/shard_map/pallas_call | solution.py:18
  43.3 2.0 %collective-permute-start.15 = (bf16[4,64,512]{2,1,0:T(8,128)(2,1)S(1)}, bf16[4,64,512]{2,1,0:T(8,128)(2,1)S(1)}, u32[]{:S(2)}, u32[]{:S(2)}) collective-permute-start(bf16[4,64,512]{2,1,0:T(8,128)(2,1)S(1)} %get-tuple-element.79), channel_id=1, source_target_pairs={{0,8},{8,0},{16,24},{24,16},{1,9},{9,1},{17,25},{25,17},{2,10},{10... | collective-permute-start | bytes 786440 | tf_op jit(solution)/shard_map/ppermute | solution.py:325
  45.3 0.0 collective-permute-start.16
  45.3 1.5 %collective-permute-start.17 = (bf16[4,64,512]{2,1,0:T(8,128)(2,1)S(1)}, bf16[4,64,512]{2,1,0:T(8,128)(2,1)S(1)}, u32[]{:S(2)}, u32[]{:S(2)}) collective-permute-start(bf16[4,64,512]{2,1,0:T(8,128)(2,1)S(1)} %get-tuple-element.81), channel_id=1, source_target_pairs={{0,24},{8,16},{16,8},{24,0},{1,25},{9,17},{17,9},{25,1},{2,26},{10... | collective-permute-start | bytes 786440 | tf_op jit(solution)/shard_map/ppermute | solution.py:325
  46.9 0.7 %collective-permute-done.11.refs_2_ = bf16[256,384]{1,0:T(8,128)(2,1)S(1)} collective-permute-done((bf16[256,384]{1,0:T(8,128)(2,1)S(1)}, bf16[256,384]{1,0:T(8,128)(2,1)S(1)}, u32[]{:S(2)}, u32[]{:S(2)}) %collective-permute-start.11) | collective-permute-done | bytes 196640 | tf_op jit(solution)/shard_map/ppermute | solution.py:325
  47.5 0.1 shard_map.115
  47.7 3.9 %collective-permute-start.13 = (bf16[128,384]{1,0:T(8,128)(2,1)S(1)}, bf16[128,384]{1,0:T(8,128)(2,1)S(1)}, u32[]{:S(2)}, u32[]{:S(2)}) collective-permute-start(bf16[128,384]{1,0:T(8,128)(2,1)S(1)} %get-tuple-element.87), channel_id=1, source_target_pairs={{0,2},{1,3},{2,0},{3,1},{4,6},{5,7},{6,4},{7,5},{8,10},{9,11},{10,... | collective-permute-start | bytes 294920 | tf_op jit(solution)/shard_map/ppermute | solution.py:325
  51.6 2.6 %collective-permute-done.13.refs_1_ = bf16[128,384]{1,0:T(8,128)(2,1)S(1)} collective-permute-done((bf16[128,384]{1,0:T(8,128)(2,1)S(1)}, bf16[128,384]{1,0:T(8,128)(2,1)S(1)}, u32[]{:S(2)}, u32[]{:S(2)}) %collective-permute-start.13) | collective-permute-done | bytes 98336 | tf_op jit(solution)/shard_map/ppermute | solution.py:325
  54.2 3.1 %collective-permute-start.14 = (bf16[64,384]{1,0:T(8,128)(2,1)S(1)}, bf16[64,384]{1,0:T(8,128)(2,1)S(1)}, u32[]{:S(2)}, u32[]{:S(2)}) collective-permute-start(bf16[64,384]{1,0:T(8,128)(2,1)S(1)} %get-tuple-element.89), channel_id=1, source_target_pairs={{0,4},{1,5},{2,6},{3,7},{4,0},{5,1},{6,2},{7,3},{8,12},{9,13},{10,... | collective-permute-start | bytes 147464 | tf_op jit(solution)/shard_map/ppermute | solution.py:325
  57.3 1.1 %collective-permute-done.16.refs_2_ = bf16[4,64,512]{2,1,0:T(8,128)(2,1)S(1)} collective-permute-done((bf16[4,64,512]{2,1,0:T(8,128)(2,1)S(1)}, bf16[4,64,512]{2,1,0:T(8,128)(2,1)S(1)}, u32[]{:S(2)}, u32[]{:S(2)}) %collective-permute-start.16) | collective-permute-done | bytes 262176 | tf_op jit(solution)/shard_map/ppermute | solution.py:325
  58.5 0.9 %collective-permute-done.14.got_ref = bf16[64,384]{1,0:T(8,128)(2,1)S(1)} collective-permute-done((bf16[64,384]{1,0:T(8,128)(2,1)S(1)}, bf16[64,384]{1,0:T(8,128)(2,1)S(1)}, u32[]{:S(2)}, u32[]{:S(2)}) %collective-permute-start.14) | collective-permute-done | bytes 49184 | tf_op jit(solution)/shard_map/ppermute | solution.py:325
  59.4 1.7 %shard_map.117 = (bf16[4,4,64,512]{3,2,1,0:T(8,128)(2,1)}, f32[3,64,128]{2,1,0:T(8,128)}) custom-call(f32[64,384]{1,0:T(8,128)S(1)} %get-tuple-element.88.kept_ref, bf16[64,384]{1,0:T(8,128)(2,1)S(1)} %collective-permute-done.14.got_ref, bf16[4,64,512]{2,1,0:T(8,128)(2,1)S(1)} %get-tuple-element.78.refs_0_, ...), custom_call_target="tpu_custom_call" | custom-call | bytes 4194304 | tf_op jit(solution)/shard_map/pallas_call | solution.py:371
  (23 shorter events, 0.1 us)
Async XLA Ops:
  0.6 1.2 %copy-start.1 = (bf16[4,4,64,512]{3,2,1,0:T(8,128)(2,1)S(1)}, bf16[4,4,64,512]{3,2,1,0:T(8,128)(2,1)}, u32[]{:S(2)}) copy-start(bf16[4,4,64,512]{3,2,1,0:T(8,128)(2,1)} %x_ref.5) | copy-start | bytes 3145732
  1.9 6.1 %slice-start = ((s8[4718592]{0:T(1024)(128)(4,1)}), s8[4194304]{0:T(1024)(128)(4,1)S(1)}, s32[]{:S(2)}) async-start(s8[4718592]{0:T(1024)(128)(4,1)} %bitcast.2), calls=%async_computation | async-start | bytes 8388608
  2.4 15.0 %collective-permute-start.4 = (bf16[288,512]{1,0:T(8,128)(2,1)S(1)}, bf16[288,512]{1,0:T(8,128)(2,1)S(1)}, u32[]{:S(2)}, u32[]{:S(2)}) collective-permute-start(bf16[288,512]{1,0:T(8,128)(2,1)S(1)} %get-tuple-element.53), channel_id=1, source_target_pairs={{0,8},{8,0},{16,24},{24,16},{1,9},{9,1},{17,25},{25,17},{2,10},{10... | collective-permute-start | bytes 884744 | tf_op jit(solution)/shard_map/ppermute | solution.py:325
  5.4 14.8 %collective-permute-start.5 = (bf16[288,512]{1,0:T(8,128)(2,1)S(1)}, bf16[288,512]{1,0:T(8,128)(2,1)S(1)}, u32[]{:S(2)}, u32[]{:S(2)}) collective-permute-start(bf16[288,512]{1,0:T(8,128)(2,1)S(1)} %get-tuple-element.54), channel_id=1, source_target_pairs={{0,16},{8,24},{16,0},{24,8},{1,17},{9,25},{17,1},{25,9},{2,18},{10... | collective-permute-start | bytes 884744 | tf_op jit(solution)/shard_map/ppermute | solution.py:325
  7.0 13.3 %collective-permute-start.6 = (bf16[288,512]{1,0:T(8,128)(2,1)S(1)}, bf16[288,512]{1,0:T(8,128)(2,1)S(1)}, u32[]{:S(2)}, u32[]{:S(2)}) collective-permute-start(bf16[288,512]{1,0:T(8,128)(2,1)S(1)} %get-tuple-element.55), channel_id=1, source_target_pairs={{0,24},{8,16},{16,8},{24,0},{1,25},{9,17},{17,9},{25,1},{2,26},{10... | collective-permute-start | bytes 884744 | tf_op jit(solution)/shard_map/ppermute | solution.py:325
  7.0 1.0 %slice-start.1 = ((s8[4718592]{0:T(1024)(128)(4,1)}), s8[524288]{0:T(1024)(128)(4,1)S(1)}, s32[]{:S(2)}) async-start(s8[4718592]{0:T(1024)(128)(4,1)} %bitcast.2), calls=%async_computation.1 | async-start | bytes 1048576
  7.0 5.7 %collective-permute-start = (bf16[256,512]{1,0:T(8,128)(2,1)S(1)}, bf16[256,512]{1,0:T(8,128)(2,1)S(1)}, u32[]{:S(2)}, u32[]{:S(2)}) collective-permute-start(bf16[256,512]{1,0:T(8,128)(2,1)S(1)} %get-tuple-element.48), channel_id=1, source_target_pairs={{0,1},{1,0},{2,3},{3,2},{4,5},{5,4},{6,7},{7,6},{8,9},{9,8},{10,11... | collective-permute-start | bytes 786440 | tf_op jit(solution)/shard_map/ppermute | solution.py:325
  7.1 5.7 %copy-start = (bf16[4,4,64,512]{3,2,1,0:T(8,128)(2,1)S(1)}, bf16[4,4,64,512]{3,2,1,0:T(8,128)(2,1)}, u32[]{:S(2)}) copy-start(bf16[4,4,64,512]{3,2,1,0:T(8,128)(2,1)} %cot_ref.5) | copy-start | bytes 3145732
  7.1 5.7 %collective-permute-start.1 = (bf16[256,512]{1,0:T(8,128)(2,1)S(1)}, bf16[256,512]{1,0:T(8,128)(2,1)S(1)}, u32[]{:S(2)}, u32[]{:S(2)}) collective-permute-start(bf16[256,512]{1,0:T(8,128)(2,1)S(1)} %get-tuple-element.49), channel_id=1, source_target_pairs={{1,2},{3,4},{5,6},{2,1},{4,3},{6,5},{9,10},{11,12},{13,14},{10,9},... | collective-permute-start | bytes 786440 | tf_op jit(solution)/shard_map/ppermute | solution.py:330
  14.7 11.1 %collective-permute-start.2 = (bf16[4,64,512]{2,1,0:T(8,128)(2,1)S(1)}, bf16[4,64,512]{2,1,0:T(8,128)(2,1)S(1)}, u32[]{:S(2)}, u32[]{:S(2)}) collective-permute-start(bf16[4,64,512]{2,1,0:T(8,128)(2,1)S(1)} %get-tuple-element.51), channel_id=1, source_target_pairs={{0,8},{8,0},{16,24},{24,16},{1,9},{9,1},{17,25},{25,17},{2,10},{10... | collective-permute-start | bytes 786440 | tf_op jit(solution)/shard_map/ppermute | solution.py:325
  16.7 9.1 %collective-permute-start.3 = (bf16[4,64,512]{2,1,0:T(8,128)(2,1)S(1)}, bf16[4,64,512]{2,1,0:T(8,128)(2,1)S(1)}, u32[]{:S(2)}, u32[]{:S(2)}) collective-permute-start(bf16[4,64,512]{2,1,0:T(8,128)(2,1)S(1)} %get-tuple-element.52), channel_id=1, source_target_pairs={{8,16},{16,8},{9,17},{17,9},{10,18},{18,10},{11,19},{19,11},{12,20... | collective-permute-start | bytes 786440 | tf_op jit(solution)/shard_map/ppermute | solution.py:330
  20.7 5.1 %collective-permute-start.7 = (bf16[288,512]{1,0:T(8,128)(2,1)S(1)}, bf16[288,512]{1,0:T(8,128)(2,1)S(1)}, u32[]{:S(2)}, u32[]{:S(2)}) collective-permute-start(bf16[288,512]{1,0:T(8,128)(2,1)S(1)} %get-tuple-element.57), channel_id=1, source_target_pairs={{0,1},{1,0},{2,3},{3,2},{4,5},{5,4},{6,7},{7,6},{8,9},{9,8},{10,11... | collective-permute-start | bytes 884744 | tf_op jit(solution)/shard_map/ppermute | solution.py:325
  20.8 5.0 %collective-permute-start.8 = (bf16[288,512]{1,0:T(8,128)(2,1)S(1)}, bf16[288,512]{1,0:T(8,128)(2,1)S(1)}, u32[]{:S(2)}, u32[]{:S(2)}) collective-permute-start(bf16[288,512]{1,0:T(8,128)(2,1)S(1)} %get-tuple-element.58), channel_id=1, source_target_pairs={{1,2},{3,4},{5,6},{2,1},{4,3},{6,5},{9,10},{11,12},{13,14},{10,9},... | collective-permute-start | bytes 884744 | tf_op jit(solution)/shard_map/ppermute | solution.py:330
  26.5 6.3 %collective-permute-start.9 = (bf16[256,1536]{1,0:T(8,128)(2,1)S(1)}, bf16[256,1536]{1,0:T(8,128)(2,1)S(1)}, u32[]{:S(2)}, u32[]{:S(2)}) collective-permute-start(bf16[256,1536]{1,0:T(8,128)(2,1)S(1)} %get-tuple-element.61), channel_id=1, source_target_pairs={{0,1},{1,0},{2,3},{3,2},{4,5},{5,4},{6,7},{7,6},{8,9},{9,8},{10,11... | collective-permute-start | bytes 2359304 | tf_op jit(solution)/shard_map/ppermute | solution.py:325
  30.0 7.9 %copy-start.4 = (bf16[512,512]{1,0:T(8,128)(2,1)S(1)}, bf16[512,512]{1,0:T(8,128)(2,1)}, u32[]{:S(2)}) copy-start(bf16[512,512]{1,0:T(8,128)(2,1)} %k_ref.1) | copy-start | bytes 1572868
  30.0 7.9 %copy-start.5 = (bf16[512,512]{1,0:T(8,128)(2,1)S(1)}, bf16[512,512]{1,0:T(8,128)(2,1)}, u32[]{:S(2)}) copy-start(bf16[512,512]{1,0:T(8,128)(2,1)} %v_ref.1) | copy-start | bytes 1572868
  30.0 7.9 %copy-start.6 = (bf16[512,512]{1,0:T(8,128)(2,1)S(1)}, bf16[512,512]{1,0:T(8,128)(2,1)}, u32[]{:S(2)}) copy-start(bf16[512,512]{1,0:T(8,128)(2,1)} %o_ref.1) | copy-start | bytes 1572868
  32.7 5.3 %copy-start.2 = (bf16[3,512,512]{2,1,0:T(8,128)(2,1)S(1)}, bf16[3,512,512]{2,1,0:T(8,128)(2,1)}, u32[]{:S(2)}) copy-start(bf16[3,512,512]{2,1,0:T(8,128)(2,1)} %t_ref.1) | copy-start | bytes 4718596
  32.7 5.3 %copy-start.3 = (bf16[512,512]{1,0:T(8,128)(2,1)S(1)}, bf16[512,512]{1,0:T(8,128)(2,1)}, u32[]{:S(2)}) copy-start(bf16[512,512]{1,0:T(8,128)(2,1)} %q_ref.1) | copy-start | bytes 1572868
  32.8 5.2 %copy-start.7 = (f32[512]{0:T(512)S(1)}, f32[512]{0:T(512)}, u32[]{:S(2)}) copy-start(f32[512]{0:T(512)} %param.12) | copy-start | bytes 6148
  33.1 12.2 %collective-permute-start.10 = (bf16[256,384]{1,0:T(8,128)(2,1)S(1)}, bf16[256,384]{1,0:T(8,128)(2,1)S(1)}, u32[]{:S(2)}, u32[]{:S(2)}) collective-permute-start(bf16[256,384]{1,0:T(8,128)(2,1)S(1)} %get-tuple-element.73), channel_id=1, source_target_pairs={{0,8},{8,0},{16,24},{24,16},{1,9},{9,1},{17,25},{25,17},{2,10},{10... | collective-permute-start | bytes 589832 | tf_op jit(solution)/shard_map/ppermute | solution.py:325
  36.4 11.1 %collective-permute-start.11 = (bf16[256,384]{1,0:T(8,128)(2,1)S(1)}, bf16[256,384]{1,0:T(8,128)(2,1)S(1)}, u32[]{:S(2)}, u32[]{:S(2)}) collective-permute-start(bf16[256,384]{1,0:T(8,128)(2,1)S(1)} %get-tuple-element.74), channel_id=1, source_target_pairs={{0,16},{8,24},{16,0},{24,8},{1,17},{9,25},{17,1},{25,9},{2,18},{10... | collective-permute-start | bytes 589832 | tf_op jit(solution)/shard_map/ppermute | solution.py:325
  36.4 11.1 %collective-permute-start.12 = (bf16[256,384]{1,0:T(8,128)(2,1)S(1)}, bf16[256,384]{1,0:T(8,128)(2,1)S(1)}, u32[]{:S(2)}, u32[]{:S(2)}) collective-permute-start(bf16[256,384]{1,0:T(8,128)(2,1)S(1)} %get-tuple-element.75), channel_id=1, source_target_pairs={{0,24},{8,16},{16,8},{24,0},{1,25},{9,17},{17,9},{25,1},{2,26},{10... | collective-permute-start | bytes 589832 | tf_op jit(solution)/shard_map/ppermute | solution.py:325
  43.3 14.0 %collective-permute-start.15 = (bf16[4,64,512]{2,1,0:T(8,128)(2,1)S(1)}, bf16[4,64,512]{2,1,0:T(8,128)(2,1)S(1)}, u32[]{:S(2)}, u32[]{:S(2)}) collective-permute-start(bf16[4,64,512]{2,1,0:T(8,128)(2,1)S(1)} %get-tuple-element.79), channel_id=1, source_target_pairs={{0,8},{8,0},{16,24},{24,16},{1,9},{9,1},{17,25},{25,17},{2,10},{10... | collective-permute-start | bytes 786440 | tf_op jit(solution)/shard_map/ppermute | solution.py:325
  45.3 13.1 %collective-permute-start.16 = (bf16[4,64,512]{2,1,0:T(8,128)(2,1)S(1)}, bf16[4,64,512]{2,1,0:T(8,128)(2,1)S(1)}, u32[]{:S(2)}, u32[]{:S(2)}) collective-permute-start(bf16[4,64,512]{2,1,0:T(8,128)(2,1)S(1)} %get-tuple-element.80), channel_id=1, source_target_pairs={{0,16},{8,24},{16,0},{24,8},{1,17},{9,25},{17,1},{25,9},{2,18},{10... | collective-permute-start | bytes 786440 | tf_op jit(solution)/shard_map/ppermute | solution.py:325
  45.3 13.1 %collective-permute-start.17 = (bf16[4,64,512]{2,1,0:T(8,128)(2,1)S(1)}, bf16[4,64,512]{2,1,0:T(8,128)(2,1)S(1)}, u32[]{:S(2)}, u32[]{:S(2)}) collective-permute-start(bf16[4,64,512]{2,1,0:T(8,128)(2,1)S(1)} %get-tuple-element.81), channel_id=1, source_target_pairs={{0,24},{8,16},{16,8},{24,0},{1,25},{9,17},{17,9},{25,1},{2,26},{10... | collective-permute-start | bytes 786440 | tf_op jit(solution)/shard_map/ppermute | solution.py:325
  47.7 6.5 %collective-permute-start.13 = (bf16[128,384]{1,0:T(8,128)(2,1)S(1)}, bf16[128,384]{1,0:T(8,128)(2,1)S(1)}, u32[]{:S(2)}, u32[]{:S(2)}) collective-permute-start(bf16[128,384]{1,0:T(8,128)(2,1)S(1)} %get-tuple-element.87), channel_id=1, source_target_pairs={{0,2},{1,3},{2,0},{3,1},{4,6},{5,7},{6,4},{7,5},{8,10},{9,11},{10,... | collective-permute-start | bytes 294920 | tf_op jit(solution)/shard_map/ppermute | solution.py:325
  54.2 5.2 %collective-permute-start.14 = (bf16[64,384]{1,0:T(8,128)(2,1)S(1)}, bf16[64,384]{1,0:T(8,128)(2,1)S(1)}, u32[]{:S(2)}, u32[]{:S(2)}) collective-permute-start(bf16[64,384]{1,0:T(8,128)(2,1)S(1)} %get-tuple-element.89), channel_id=1, source_target_pairs={{0,4},{1,5},{2,6},{3,7},{4,0},{5,1},{6,2},{7,3},{8,12},{9,13},{10,... | collective-permute-start | bytes 147464 | tf_op jit(solution)/shard_map/ppermute | solution.py:325

commit v14 on v13

--- a/solution.py
+++ b/solution.py
@@ -49,6 +49,13 @@
         self.piece = frames * self.wc
         self.main = rows * self.piece
         self.sides = 2 * rows * frames
+        self.order = sorted(range(count), key=lambda k: -k.bit_count())
+
+    def ordered(self, pieces):
+        return [pieces[k] for k in self.order]
+
+    def by_partner(self, pieces):
+        return [pieces[self.order.index(k)] for k in range(self.n)]
 
 
 def even(axis):
@@ -171,7 +178,7 @@
 
 
 def assemble_kernel(z, *refs):
-    parts, (out, near, far) = refs[: z.n], refs[z.n :]
+    parts, (out, near, far) = z.by_partner(refs[: z.n]), refs[z.n :]
     me = lax.axis_index("tm")
     lower = even("space")
     matrix = gather_matrix(z, me)
@@ -294,8 +301,8 @@
 
     def spread(r):
         encoded = moved(back, held.pop(("e", r)))
-        for k in range(z.n):
-            outs[k][r] = encoded[k * z.piece : (k + 1) * z.piece]
+        for out, k in zip(outs, z.order):
+            out[r] = encoded[k * z.piece : (k + 1) * z.piece]
 
     staged(z, (activate, hide, norm, project, score, weigh, mix, finish, spread))
 
@@ -351,16 +358,17 @@
 
 
 def join_kernel(z, kept_ref, got_ref, *refs):
-    parts, (out, grad, whole, sem) = refs[: z.n], refs[z.n :]
+    parts, (out, grad, whole, total, sem) = z.by_partner(refs[: z.n]), refs[z.n :]
     me = lax.axis_index("tm")
-    copies = []
+    add_up(z, kept_ref, got_ref, total)
+    copies = [pltpu.make_async_copy(total, grad, sem.at[z.fl])]
+    copies[0].start()
     for f in range(z.fl):
         for k in range(z.n):
             cols = pl.ds(pl.multiple_of((me ^ k) * z.wc, z.wc), z.wc)
             whole[f, :, cols] = parts[k][:, f * z.wc : (f + 1) * z.wc]
         copies.append(pltpu.make_async_copy(whole.at[f], out.at[f], sem.at[f]))
-        copies[f].start()
-    add_up(z, kept_ref, got_ref, grad)
+        copies[-1].start()
     for copy in copies:
         copy.wait()
 
@@ -372,16 +380,17 @@
             functools.partial(join_kernel, z),
             out_shape=(shape((z.fl, z.r, z.w, z.c)), grad),
             in_specs=[VMEM] * (2 + z.n),
-            out_specs=(pl.BlockSpec(memory_space=pl.ANY), VMEM),
+            out_specs=(pl.BlockSpec(memory_space=pl.ANY),) * 2,
             scratch_shapes=[
                 pltpu.VMEM((z.fl, z.r, z.w, z.c), BF),
-                pltpu.SemaphoreType.DMA((z.fl,)),
+                pltpu.VMEM(grad.shape, F32),
+                pltpu.SemaphoreType.DMA((z.fl + 1,)),
             ],
             compiler_params=pltpu.CompilerParams(vmem_limit_bytes=16 * 2**20),
             cost_estimate=pl.CostEstimate(
                 flops=0, bytes_accessed=8 * z.n * z.main * z.c, transcendentals=0
             ),
-        )(kept, got, *back)
+        )(kept, got, *z.ordered(back))
     whole = jnp.zeros((z.fl, z.r, z.n, z.wc, z.c), BF)
     for k in range(z.n):
         rows = back[k].reshape(z.r, z.fl, 1, z.wc, z.c).transpose(1, 0, 2, 3, 4)
@@ -395,12 +404,11 @@
     space = lax.axis_size("space")
     z = Sizes(n, *frames_in.shape)
     one = 2 * z.r * z.block * z.c * z.c
-    others = sorted(range(1, n), key=lambda k: -k.bit_count())
     width, wide = z.c // space, z.c // n
 
     def exchange(pieces):
         pieces = list(pieces)
-        for k in others:
+        for k in z.order[:-1]:
             pieces[k] = swap(pieces[k], "tm", k)
         return pieces
 
@@ -446,7 +454,7 @@
     x, close, apart = call(
         functools.partial(assemble_kernel, z),
         [shape((z.r, line, z.c)), shape((line, z.c)), shape((line, z.c))],
-        *got,
+        *z.ordered(got),
     )
     close, apart = swap_both(close, apart, "space")
     (middle,) = call(
@@ -489,7 +497,7 @@
     )
     border, *pieces = lax.optimization_barrier((border, *pieces))
     pieces = exchange(pieces)
-    encoded = call(
+    encoded = z.by_partner(call(
         functools.partial(main_kernel, z),
         [shape((z.r, z.piece, z.c))] * n,
         middle,
@@ -502,9 +510,9 @@
         v_w,
         o_w,
         flops=9 * one,
-    )
+    ))
     back = exchange(encoded)
-    pieces = lax.optimization_barrier((*pieces, *encoded))[:n]
+    pieces = lax.optimization_barrier((*z.ordered(pieces), *z.ordered(encoded)))[:n]
     bit = 0
     while 2 << bit < space:
         half = (pieces[0].shape[0] // 2, 3 * wide)

time: 61.4 us -> 60.5 us (0.985); the launches traced: 61.2 us -> 59.4 us
  starting transfers between devices: 28.1 us -> 27.3 us
    ppermute x15, starting transfers between devices: 25.7 us -> 25 us  [swap(): return lax.ppermute(value, axis, [(i, i ^ k) for i in range(count)])]
  transfers between devices with their start and end apart: 18 -> 18, of which waited for: 5 -> 4; matrix products, arithmetic and copies ran while one was open for 0% -> 0% of each run, Pallas kernels for 32% -> 33%
where the time goes in v14:
time: 60.5 us; the launch traced here: 59.4 us
  starting transfers between devices  27.3 us (45%)
  Pallas kernels  21.9 us (36%)
  waiting for transfers between devices  7.83 us (13%)
  local copies, waits for them, and re-layouts  1.32 us (2%)
  between operations  1.06 us (2%)
    ppermute x15, starting transfers between devices, swap(): return lax.ppermute(value, axis, [(i, i ^ k) for i in range(count)])  25 us
    pallas_call x13, Pallas kernels, call(): pl.pallas_call(kernel, out_shape=tuple(outs), in_specs=[VMEM] * len(args)...  20.9 us
    ppermute x15, waiting for transfers between devices, swap(): return lax.ppermute(value, axis, [(i, i ^ k) for i in range(count)])  7.83 us
    ppermute x3, starting transfers between devices, swap_both(): far = lax.ppermute(far, axis, pairs + [(b, a) for a, b in pairs])  2.32 us
    unnamed x20, local copies, waits for them, and re-layouts  1.32 us
  transfers between devices with their start and end apart: 18, of which 4 were waited for; matrix products, arithmetic and copies ran while one was open for 0% of the time, Pallas kernels for 33%

profile of v14, /device:TPU:0, one launch (start us, length us, event | category | flops | bytes accessed | tf_op | source)
XLA Modules:
  0.0 59.4 jit_solution(7693827757796323645)
XLA Ops:
  0.6 1.2 %copy-done.1 = bf16[4,4,64,512]{3,2,1,0:T(8,128)(2,1)S(1)} copy-done((bf16[4,4,64,512]{3,2,1,0:T(8,128)(2,1)S(1)}, bf16[4,4,64,512]{3,2,1,0:T(8,128)(2,1)}, u32[]{:S(2)}) %copy-start.1) | copy-done | bytes 1048600
  1.9 0.6 shard_map.105
  2.4 4.0 %collective-permute-start.4 = (bf16[288,512]{1,0:T(8,128)(2,1)S(1)}, bf16[288,512]{1,0:T(8,128)(2,1)S(1)}, u32[]{:S(2)}, u32[]{:S(2)}) collective-permute-start(bf16[288,512]{1,0:T(8,128)(2,1)S(1)} %get-tuple-element.53), channel_id=1, source_target_pairs={{0,24},{8,16},{16,8},{24,0},{1,25},{9,17},{17,9},{25,1},{2,26},{10... | collective-permute-start | bytes 884744 | tf_op jit(solution)/shard_map/ppermute | solution.py:332
  6.4 0.5 collective-permute-start.5
  6.9 0.1 collective-permute-start.6
  7.0 0.1 shard_map.106
  7.1 0.1 collective-permute-start
  7.2 0.0 copy-start
  7.2 0.8 %collective-permute-start.1 = (bf16[256,512]{1,0:T(8,128)(2,1)S(1)}, bf16[256,512]{1,0:T(8,128)(2,1)S(1)}, u32[]{:S(2)}, u32[]{:S(2)}) collective-permute-start(bf16[256,512]{1,0:T(8,128)(2,1)S(1)} %get-tuple-element.49), channel_id=1, source_target_pairs={{1,2},{3,4},{5,6},{2,1},{4,3},{6,5},{9,10},{11,12},{13,14},{10,9},... | collective-permute-start | bytes 786440 | tf_op jit(solution)/shard_map/ppermute | solution.py:337
  8.0 0.1 slice-done.1
  8.1 4.8 %shard_map.104.part_ref = f32[4,256,512]{2,1,0:T(8,128)S(1)} custom-call(bf16[4,4,64,512]{3,2,1,0:T(8,128)(2,1)S(1)} %copy-done.1, bf16[3,3,512,512]{3,2,1,0:T(8,128)(2,1)S(1)} %bitcast.3), custom_call_target="tpu_custom_call" | custom-call | flops 4294967296 | bytes 7864320 | tf_op jit(solution)/shard_map/pallas_call | solution.py:18
  12.8 0.0 collective-permute-done.near_ref
  12.9 0.0 collective-permute-done.1.far_ref
  12.9 1.9 %shard_map.107 = (bf16[4,4,64,512]{3,2,1,0:T(8,128)(2,1)S(1)}, bf16[4,64,512]{2,1,0:T(8,128)(2,1)S(1)}, bf16[4,64,512]{2,1,0:T(8,128)(2,1)S(1)}) custom-call(f32[4,256,512]{2,1,0:T(8,128)S(1)} %shard_map.104.part_ref, bf16[256,512]{1,0:T(8,128)(2,1)S(1)} %collective-permute-done.near_ref, bf16[256,512]{1,0:T(8,128)(2,1)S(1)} %collective-permute-done.1.far_ref, ...), custom_call_target="tpu_custom_call" | custom-call | flops 1610612736 | bytes 9961472 | tf_op jit(solution)/shard_map/pallas_call | solution.py:18
  14.8 2.0 %collective-permute-start.2 = (bf16[4,64,512]{2,1,0:T(8,128)(2,1)S(1)}, bf16[4,64,512]{2,1,0:T(8,128)(2,1)S(1)}, u32[]{:S(2)}, u32[]{:S(2)}) collective-permute-start(bf16[4,64,512]{2,1,0:T(8,128)(2,1)S(1)} %get-tuple-element.51), channel_id=1, source_target_pairs={{0,8},{8,0},{16,24},{24,16},{1,9},{9,1},{17,25},{25,17},{2,10},{10... | collective-permute-start | bytes 786440 | tf_op jit(solution)/shard_map/ppermute | solution.py:332
  16.7 0.7 %collective-permute-start.3 = (bf16[4,64,512]{2,1,0:T(8,128)(2,1)S(1)}, bf16[4,64,512]{2,1,0:T(8,128)(2,1)S(1)}, u32[]{:S(2)}, u32[]{:S(2)}) collective-permute-start(bf16[4,64,512]{2,1,0:T(8,128)(2,1)S(1)} %get-tuple-element.52), channel_id=1, source_target_pairs={{8,16},{16,8},{9,17},{17,9},{10,18},{18,10},{11,19},{19,11},{12,20... | collective-permute-start | bytes 786440 | tf_op jit(solution)/shard_map/ppermute | solution.py:337
  17.4 0.0 collective-permute-done.4.refs_0_
  17.4 2.6 %collective-permute-done.5.refs_1_ = bf16[288,512]{1,0:T(8,128)(2,1)S(1)} collective-permute-done((bf16[288,512]{1,0:T(8,128)(2,1)S(1)}, bf16[288,512]{1,0:T(8,128)(2,1)S(1)}, u32[]{:S(2)}, u32[]{:S(2)}) %collective-permute-start.5) | collective-permute-done | bytes 294944 | tf_op jit(solution)/shard_map/ppermute | solution.py:332
  20.0 0.5 shard_map.109
  20.5 0.1 collective-permute-start.7
  20.6 0.8 %collective-permute-start.8 = (bf16[288,512]{1,0:T(8,128)(2,1)S(1)}, bf16[288,512]{1,0:T(8,128)(2,1)S(1)}, u32[]{:S(2)}, u32[]{:S(2)}) collective-permute-start(bf16[288,512]{1,0:T(8,128)(2,1)S(1)} %get-tuple-element.58), channel_id=1, source_target_pairs={{1,2},{3,4},{5,6},{2,1},{4,3},{6,5},{9,10},{11,12},{13,14},{10,9},... | collective-permute-start | bytes 884744 | tf_op jit(solution)/shard_map/ppermute | solution.py:337
  21.5 1.4 %shard_map.108.part_ref = f32[512,1536]{1,0:T(8,128)S(1)} custom-call(bf16[4,4,64,512]{3,2,1,0:T(8,128)(2,1)S(1)} %get-tuple-element.50.act_ref, bf16[4,4,64,512]{3,2,1,0:T(8,128)(2,1)S(1)} %copy-done), custom_call_target="tpu_custom_call" | custom-call | flops 1207959552 | bytes 5242880 | tf_op jit(solution)/shard_map/pallas_call | solution.py:18
  22.9 2.7 %shard_map.110.middle_ref = bf16[2,256,512]{2,1,0:T(8,128)(2,1)S(1)} custom-call(bf16[4,288,512]{2,1,0:T(8,128)(2,1)S(1)} %get-tuple-element.62.x_ref, bf16[3,3,512,512]{3,2,1,0:T(8,128)(2,1)S(1)} %bitcast.3), custom_call_target="tpu_custom_call" | custom-call | flops 2415919104 | bytes 6422528 | tf_op jit(solution)/shard_map/pallas_call | solution.py:18
  25.6 0.0 collective-permute-done.2.near_ref
  25.6 0.0 collective-permute-done.3.far_ref
  25.6 0.0 collective-permute-done.8.far_ref
  25.6 0.6 %shard_map.111 = (f32[256,1536]{1,0:T(8,128)S(1)}, bf16[256,1536]{1,0:T(8,128)(2,1)S(1)}) custom-call(f32[512,1536]{1,0:T(8,128)S(1)} %shard_map.108.part_ref, bf16[4,64,512]{2,1,0:T(8,128)(2,1)S(1)} %collective-permute-done.2.near_ref, bf16[4,64,512]{2,1,0:T(8,128)(2,1)S(1)} %collective-permute-done.3.far_ref, ...), custom_call_target="tpu_custom_call" | custom-call | flops 402653184 | bytes 8126464 | tf_op jit(solution)/shard_map/pallas_call | solution.py:18
  26.3 3.6 %collective-permute-start.9 = (bf16[256,1536]{1,0:T(8,128)(2,1)S(1)}, bf16[256,1536]{1,0:T(8,128)(2,1)S(1)}, u32[]{:S(2)}, u32[]{:S(2)}) collective-permute-start(bf16[256,1536]{1,0:T(8,128)(2,1)S(1)} %get-tuple-element.61), channel_id=1, source_target_pairs={{0,1},{1,0},{2,3},{3,2},{4,5},{5,4},{6,7},{7,6},{8,9},{9,8},{10,11... | collective-permute-start | bytes 2359304 | tf_op jit(solution)/shard_map/ppermute | solution.py:332
  29.8 2.7 %shard_map.112.border_ref = bf16[2,256,512]{2,1,0:T(8,128)(2,1)S(1)} custom-call(bf16[4,288,512]{2,1,0:T(8,128)(2,1)S(1)} %get-tuple-element.62.x_ref, bf16[288,512]{1,0:T(8,128)(2,1)S(1)} %collective-permute-done.7.near_ref, bf16[288,512]{1,0:T(8,128)(2,1)S(1)} %collective-permute-done.8.far_ref, bf16[3,3,512,512]{3,2,1,0:T(8,128)(2,1)S(1)} %bitcast.3), custom_call_target="tpu_custom_call" | custom-call | flops 2415919104 | bytes 7012352 | tf_op jit(solution)/shard_map/pallas_call | solution.py:18
  32.5 0.0 copy-start.2
  32.5 0.0 copy-start.3
  32.5 0.0 copy-start.7
  32.6 0.3 shard_map.113
  32.9 2.4 %collective-permute-start.10 = (bf16[256,384]{1,0:T(8,128)(2,1)S(1)}, bf16[256,384]{1,0:T(8,128)(2,1)S(1)}, u32[]{:S(2)}, u32[]{:S(2)}) collective-permute-start(bf16[256,384]{1,0:T(8,128)(2,1)S(1)} %get-tuple-element.72), channel_id=1, source_target_pairs={{0,24},{8,16},{16,8},{24,0},{1,25},{9,17},{17,9},{25,1},{2,26},{10... | collective-permute-start | bytes 589832 | tf_op jit(solution)/shard_map/ppermute | solution.py:332
  35.3 2.5 %collective-permute-start.11 = (bf16[256,384]{1,0:T(8,128)(2,1)S(1)}, bf16[256,384]{1,0:T(8,128)(2,1)S(1)}, u32[]{:S(2)}, u32[]{:S(2)}) collective-permute-start(bf16[256,384]{1,0:T(8,128)(2,1)S(1)} %get-tuple-element.73), channel_id=1, source_target_pairs={{0,8},{8,0},{16,24},{24,16},{1,9},{9,1},{17,25},{25,17},{2,10},{10... | collective-permute-start | bytes 589832 | tf_op jit(solution)/shard_map/ppermute | solution.py:332
  37.9 0.0 collective-permute-start.12
  37.9 5.3 %shard_map.114 = (bf16[4,64,512]{2,1,0:T(8,128)(2,1)S(1)}, bf16[4,64,512]{2,1,0:T(8,128)(2,1)S(1)}, bf16[4,64,512]{2,1,0:T(8,128)(2,1)S(1)}, bf16[4,64,512]{2,1,0:T(8,128)(2,1)S(1)}) custom-call(bf16[2,256,512]{2,1,0:T(8,128)(2,1)S(1)} %shard_map.110.middle_ref, bf16[2,256,512]{2,1,0:T(8,128)(2,1)S(1)} %shard_map.112.border_ref, ...), custom_call_target="tpu_custom_call" | custom-call | flops 4831838208 | bytes 6948864 | tf_op jit(solution)/shard_map/pallas_call | solution.py:18
  43.2 1.5 %collective-permute-start.15 = (bf16[4,64,512]{2,1,0:T(8,128)(2,1)S(1)}, bf16[4,64,512]{2,1,0:T(8,128)(2,1)S(1)}, u32[]{:S(2)}, u32[]{:S(2)}) collective-permute-start(bf16[4,64,512]{2,1,0:T(8,128)(2,1)S(1)} %get-tuple-element.78), channel_id=1, source_target_pairs={{0,24},{8,16},{16,8},{24,0},{1,25},{9,17},{17,9},{25,1},{2,26},{10... | collective-permute-start | bytes 786440 | tf_op jit(solution)/shard_map/ppermute | solution.py:332
  44.8 2.0 %collective-permute-start.16 = (bf16[4,64,512]{2,1,0:T(8,128)(2,1)S(1)}, bf16[4,64,512]{2,1,0:T(8,128)(2,1)S(1)}, u32[]{:S(2)}, u32[]{:S(2)}) collective-permute-start(bf16[4,64,512]{2,1,0:T(8,128)(2,1)S(1)} %get-tuple-element.79), channel_id=1, source_target_pairs={{0,8},{8,0},{16,24},{24,16},{1,9},{9,1},{17,25},{25,17},{2,10},{10... | collective-permute-start | bytes 786440 | tf_op jit(solution)/shard_map/ppermute | solution.py:332
  46.7 0.0 collective-permute-done.10.refs_0_
  46.7 0.0 collective-permute-start.17
  46.8 0.5 collective-permute-done.11.refs_1_
  47.3 0.1 shard_map.115
  47.4 3.0 %collective-permute-start.13 = (bf16[128,384]{1,0:T(8,128)(2,1)S(1)}, bf16[128,384]{1,0:T(8,128)(2,1)S(1)}, u32[]{:S(2)}, u32[]{:S(2)}) collective-permute-start(bf16[128,384]{1,0:T(8,128)(2,1)S(1)} %get-tuple-element.87), channel_id=1, source_target_pairs={{0,2},{1,3},{2,0},{3,1},{4,6},{5,7},{6,4},{7,5},{8,10},{9,11},{10,... | collective-permute-start | bytes 294920 | tf_op jit(solution)/shard_map/ppermute | solution.py:332
  50.4 2.6 %collective-permute-done.13.refs_1_ = bf16[128,384]{1,0:T(8,128)(2,1)S(1)} collective-permute-done((bf16[128,384]{1,0:T(8,128)(2,1)S(1)}, bf16[128,384]{1,0:T(8,128)(2,1)S(1)}, u32[]{:S(2)}, u32[]{:S(2)}) %collective-permute-start.13) | collective-permute-done | bytes 98336 | tf_op jit(solution)/shard_map/ppermute | solution.py:332
  53.0 3.1 %collective-permute-start.14 = (bf16[64,384]{1,0:T(8,128)(2,1)S(1)}, bf16[64,384]{1,0:T(8,128)(2,1)S(1)}, u32[]{:S(2)}, u32[]{:S(2)}) collective-permute-start(bf16[64,384]{1,0:T(8,128)(2,1)S(1)} %get-tuple-element.89), channel_id=1, source_target_pairs={{0,4},{1,5},{2,6},{3,7},{4,0},{5,1},{6,2},{7,3},{8,12},{9,13},{10,... | collective-permute-start | bytes 147464 | tf_op jit(solution)/shard_map/ppermute | solution.py:332
  56.1 2.1 %collective-permute-done.16.refs_1_ = bf16[4,64,512]{2,1,0:T(8,128)(2,1)S(1)} collective-permute-done((bf16[4,64,512]{2,1,0:T(8,128)(2,1)S(1)}, bf16[4,64,512]{2,1,0:T(8,128)(2,1)S(1)}, u32[]{:S(2)}, u32[]{:S(2)}) %collective-permute-start.16) | collective-permute-done | bytes 262176 | tf_op jit(solution)/shard_map/ppermute | solution.py:332
  58.2 1.1 %shard_map.117 = (bf16[4,4,64,512]{3,2,1,0:T(8,128)(2,1)}, f32[3,64,128]{2,1,0:T(8,128)}) custom-call(f32[64,384]{1,0:T(8,128)S(1)} %get-tuple-element.88.kept_ref, bf16[64,384]{1,0:T(8,128)(2,1)S(1)} %collective-permute-done.14.got_ref, bf16[4,64,512]{2,1,0:T(8,128)(2,1)S(1)} %collective-permute-done.15.refs_0_, ...), custom_call_target="tpu_custom_call" | custom-call | bytes 4194304 | tf_op jit(solution)/shard_map/pallas_call | solution.py:379
  (23 shorter events, 0.1 us)
Async XLA Ops:
  0.6 1.2 %copy-start.1 = (bf16[4,4,64,512]{3,2,1,0:T(8,128)(2,1)S(1)}, bf16[4,4,64,512]{3,2,1,0:T(8,128)(2,1)}, u32[]{:S(2)}) copy-start(bf16[4,4,64,512]{3,2,1,0:T(8,128)(2,1)} %x_ref.5) | copy-start | bytes 3145732
  1.9 6.2 %slice-start = ((s8[4718592]{0:T(1024)(128)(4,1)}), s8[4194304]{0:T(1024)(128)(4,1)S(1)}, s32[]{:S(2)}) async-start(s8[4718592]{0:T(1024)(128)(4,1)} %bitcast.2), calls=%async_computation | async-start | bytes 8388608
  2.4 15.0 %collective-permute-start.4 = (bf16[288,512]{1,0:T(8,128)(2,1)S(1)}, bf16[288,512]{1,0:T(8,128)(2,1)S(1)}, u32[]{:S(2)}, u32[]{:S(2)}) collective-permute-start(bf16[288,512]{1,0:T(8,128)(2,1)S(1)} %get-tuple-element.53), channel_id=1, source_target_pairs={{0,24},{8,16},{16,8},{24,0},{1,25},{9,17},{17,9},{25,1},{2,26},{10... | collective-permute-start | bytes 884744 | tf_op jit(solution)/shard_map/ppermute | solution.py:332
  6.4 13.6 %collective-permute-start.5 = (bf16[288,512]{1,0:T(8,128)(2,1)S(1)}, bf16[288,512]{1,0:T(8,128)(2,1)S(1)}, u32[]{:S(2)}, u32[]{:S(2)}) collective-permute-start(bf16[288,512]{1,0:T(8,128)(2,1)S(1)} %get-tuple-element.54), channel_id=1, source_target_pairs={{0,8},{8,0},{16,24},{24,16},{1,9},{9,1},{17,25},{25,17},{2,10},{10... | collective-permute-start | bytes 884744 | tf_op jit(solution)/shard_map/ppermute | solution.py:332
  6.9 13.1 %collective-permute-start.6 = (bf16[288,512]{1,0:T(8,128)(2,1)S(1)}, bf16[288,512]{1,0:T(8,128)(2,1)S(1)}, u32[]{:S(2)}, u32[]{:S(2)}) collective-permute-start(bf16[288,512]{1,0:T(8,128)(2,1)S(1)} %get-tuple-element.55), channel_id=1, source_target_pairs={{0,16},{8,24},{16,0},{24,8},{1,17},{9,25},{17,1},{25,9},{2,18},{10... | collective-permute-start | bytes 884744 | tf_op jit(solution)/shard_map/ppermute | solution.py:332
  7.0 1.0 %slice-start.1 = ((s8[4718592]{0:T(1024)(128)(4,1)}), s8[524288]{0:T(1024)(128)(4,1)S(1)}, s32[]{:S(2)}) async-start(s8[4718592]{0:T(1024)(128)(4,1)} %bitcast.2), calls=%async_computation.1 | async-start | bytes 1048576
  7.1 5.7 %collective-permute-start = (bf16[256,512]{1,0:T(8,128)(2,1)S(1)}, bf16[256,512]{1,0:T(8,128)(2,1)S(1)}, u32[]{:S(2)}, u32[]{:S(2)}) collective-permute-start(bf16[256,512]{1,0:T(8,128)(2,1)S(1)} %get-tuple-element.48), channel_id=1, source_target_pairs={{0,1},{1,0},{2,3},{3,2},{4,5},{5,4},{6,7},{7,6},{8,9},{9,8},{10,11... | collective-permute-start | bytes 786440 | tf_op jit(solution)/shard_map/ppermute | solution.py:332
  7.2 5.7 %copy-start = (bf16[4,4,64,512]{3,2,1,0:T(8,128)(2,1)S(1)}, bf16[4,4,64,512]{3,2,1,0:T(8,128)(2,1)}, u32[]{:S(2)}) copy-start(bf16[4,4,64,512]{3,2,1,0:T(8,128)(2,1)} %cot_ref.5) | copy-start | bytes 3145732
  7.2 5.7 %collective-permute-start.1 = (bf16[256,512]{1,0:T(8,128)(2,1)S(1)}, bf16[256,512]{1,0:T(8,128)(2,1)S(1)}, u32[]{:S(2)}, u32[]{:S(2)}) collective-permute-start(bf16[256,512]{1,0:T(8,128)(2,1)S(1)} %get-tuple-element.49), channel_id=1, source_target_pairs={{1,2},{3,4},{5,6},{2,1},{4,3},{6,5},{9,10},{11,12},{13,14},{10,9},... | collective-permute-start | bytes 786440 | tf_op jit(solution)/shard_map/ppermute | solution.py:337
  14.8 10.8 %collective-permute-start.2 = (bf16[4,64,512]{2,1,0:T(8,128)(2,1)S(1)}, bf16[4,64,512]{2,1,0:T(8,128)(2,1)S(1)}, u32[]{:S(2)}, u32[]{:S(2)}) collective-permute-start(bf16[4,64,512]{2,1,0:T(8,128)(2,1)S(1)} %get-tuple-element.51), channel_id=1, source_target_pairs={{0,8},{8,0},{16,24},{24,16},{1,9},{9,1},{17,25},{25,17},{2,10},{10... | collective-permute-start | bytes 786440 | tf_op jit(solution)/shard_map/ppermute | solution.py:332
  16.7 8.9 %collective-permute-start.3 = (bf16[4,64,512]{2,1,0:T(8,128)(2,1)S(1)}, bf16[4,64,512]{2,1,0:T(8,128)(2,1)S(1)}, u32[]{:S(2)}, u32[]{:S(2)}) collective-permute-start(bf16[4,64,512]{2,1,0:T(8,128)(2,1)S(1)} %get-tuple-element.52), channel_id=1, source_target_pairs={{8,16},{16,8},{9,17},{17,9},{10,18},{18,10},{11,19},{19,11},{12,20... | collective-permute-start | bytes 786440 | tf_op jit(solution)/shard_map/ppermute | solution.py:337
  20.5 5.1 %collective-permute-start.7 = (bf16[288,512]{1,0:T(8,128)(2,1)S(1)}, bf16[288,512]{1,0:T(8,128)(2,1)S(1)}, u32[]{:S(2)}, u32[]{:S(2)}) collective-permute-start(bf16[288,512]{1,0:T(8,128)(2,1)S(1)} %get-tuple-element.57), channel_id=1, source_target_pairs={{0,1},{1,0},{2,3},{3,2},{4,5},{5,4},{6,7},{7,6},{8,9},{9,8},{10,11... | collective-permute-start | bytes 884744 | tf_op jit(solution)/shard_map/ppermute | solution.py:332
  20.6 5.0 %collective-permute-start.8 = (bf16[288,512]{1,0:T(8,128)(2,1)S(1)}, bf16[288,512]{1,0:T(8,128)(2,1)S(1)}, u32[]{:S(2)}, u32[]{:S(2)}) collective-permute-start(bf16[288,512]{1,0:T(8,128)(2,1)S(1)} %get-tuple-element.58), channel_id=1, source_target_pairs={{1,2},{3,4},{5,6},{2,1},{4,3},{6,5},{9,10},{11,12},{13,14},{10,9},... | collective-permute-start | bytes 884744 | tf_op jit(solution)/shard_map/ppermute | solution.py:337
  26.3 6.3 %collective-permute-start.9 = (bf16[256,1536]{1,0:T(8,128)(2,1)S(1)}, bf16[256,1536]{1,0:T(8,128)(2,1)S(1)}, u32[]{:S(2)}, u32[]{:S(2)}) collective-permute-start(bf16[256,1536]{1,0:T(8,128)(2,1)S(1)} %get-tuple-element.61), channel_id=1, source_target_pairs={{0,1},{1,0},{2,3},{3,2},{4,5},{5,4},{6,7},{7,6},{8,9},{9,8},{10,11... | collective-permute-start | bytes 2359304 | tf_op jit(solution)/shard_map/ppermute | solution.py:332
  29.8 8.1 %copy-start.4 = (bf16[512,512]{1,0:T(8,128)(2,1)S(1)}, bf16[512,512]{1,0:T(8,128)(2,1)}, u32[]{:S(2)}) copy-start(bf16[512,512]{1,0:T(8,128)(2,1)} %k_ref.1) | copy-start | bytes 1572868
  29.8 8.1 %copy-start.5 = (bf16[512,512]{1,0:T(8,128)(2,1)S(1)}, bf16[512,512]{1,0:T(8,128)(2,1)}, u32[]{:S(2)}) copy-start(bf16[512,512]{1,0:T(8,128)(2,1)} %v_ref.1) | copy-start | bytes 1572868
  29.8 8.1 %copy-start.6 = (bf16[512,512]{1,0:T(8,128)(2,1)S(1)}, bf16[512,512]{1,0:T(8,128)(2,1)}, u32[]{:S(2)}) copy-start(bf16[512,512]{1,0:T(8,128)(2,1)} %o_ref.1) | copy-start | bytes 1572868
  32.5 5.4 %copy-start.2 = (bf16[3,512,512]{2,1,0:T(8,128)(2,1)S(1)}, bf16[3,512,512]{2,1,0:T(8,128)(2,1)}, u32[]{:S(2)}) copy-start(bf16[3,512,512]{2,1,0:T(8,128)(2,1)} %t_ref.1) | copy-start | bytes 4718596
  32.5 5.4 %copy-start.3 = (bf16[512,512]{1,0:T(8,128)(2,1)S(1)}, bf16[512,512]{1,0:T(8,128)(2,1)}, u32[]{:S(2)}) copy-start(bf16[512,512]{1,0:T(8,128)(2,1)} %q_ref.1) | copy-start | bytes 1572868
  32.5 5.4 %copy-start.7 = (f32[512]{0:T(512)S(1)}, f32[512]{0:T(512)}, u32[]{:S(2)}) copy-start(f32[512]{0:T(512)} %param.12) | copy-start | bytes 6148
  32.9 13.8 %collective-permute-start.10 = (bf16[256,384]{1,0:T(8,128)(2,1)S(1)}, bf16[256,384]{1,0:T(8,128)(2,1)S(1)}, u32[]{:S(2)}, u32[]{:S(2)}) collective-permute-start(bf16[256,384]{1,0:T(8,128)(2,1)S(1)} %get-tuple-element.72), channel_id=1, source_target_pairs={{0,24},{8,16},{16,8},{24,0},{1,25},{9,17},{17,9},{25,1},{2,26},{10... | collective-permute-start | bytes 589832 | tf_op jit(solution)/shard_map/ppermute | solution.py:332
  35.3 12.0 %collective-permute-start.11 = (bf16[256,384]{1,0:T(8,128)(2,1)S(1)}, bf16[256,384]{1,0:T(8,128)(2,1)S(1)}, u32[]{:S(2)}, u32[]{:S(2)}) collective-permute-start(bf16[256,384]{1,0:T(8,128)(2,1)S(1)} %get-tuple-element.73), channel_id=1, source_target_pairs={{0,8},{8,0},{16,24},{24,16},{1,9},{9,1},{17,25},{25,17},{2,10},{10... | collective-permute-start | bytes 589832 | tf_op jit(solution)/shard_map/ppermute | solution.py:332
  37.9 9.4 %collective-permute-start.12 = (bf16[256,384]{1,0:T(8,128)(2,1)S(1)}, bf16[256,384]{1,0:T(8,128)(2,1)S(1)}, u32[]{:S(2)}, u32[]{:S(2)}) collective-permute-start(bf16[256,384]{1,0:T(8,128)(2,1)S(1)} %get-tuple-element.74), channel_id=1, source_target_pairs={{0,16},{8,24},{16,0},{24,8},{1,17},{9,25},{17,1},{25,9},{2,18},{10... | collective-permute-start | bytes 589832 | tf_op jit(solution)/shard_map/ppermute | solution.py:332
  43.2 12.9 %collective-permute-start.15 = (bf16[4,64,512]{2,1,0:T(8,128)(2,1)S(1)}, bf16[4,64,512]{2,1,0:T(8,128)(2,1)S(1)}, u32[]{:S(2)}, u32[]{:S(2)}) collective-permute-start(bf16[4,64,512]{2,1,0:T(8,128)(2,1)S(1)} %get-tuple-element.78), channel_id=1, source_target_pairs={{0,24},{8,16},{16,8},{24,0},{1,25},{9,17},{17,9},{25,1},{2,26},{10... | collective-permute-start | bytes 786440 | tf_op jit(solution)/shard_map/ppermute | solution.py:332
  44.8 13.4 %collective-permute-start.16 = (bf16[4,64,512]{2,1,0:T(8,128)(2,1)S(1)}, bf16[4,64,512]{2,1,0:T(8,128)(2,1)S(1)}, u32[]{:S(2)}, u32[]{:S(2)}) collective-permute-start(bf16[4,64,512]{2,1,0:T(8,128)(2,1)S(1)} %get-tuple-element.79), channel_id=1, source_target_pairs={{0,8},{8,0},{16,24},{24,16},{1,9},{9,1},{17,25},{25,17},{2,10},{10... | collective-permute-start | bytes 786440 | tf_op jit(solution)/shard_map/ppermute | solution.py:332
  46.7 11.5 %collective-permute-start.17 = (bf16[4,64,512]{2,1,0:T(8,128)(2,1)S(1)}, bf16[4,64,512]{2,1,0:T(8,128)(2,1)S(1)}, u32[]{:S(2)}, u32[]{:S(2)}) collective-permute-start(bf16[4,64,512]{2,1,0:T(8,128)(2,1)S(1)} %get-tuple-element.80), channel_id=1, source_target_pairs={{0,16},{8,24},{16,0},{24,8},{1,17},{9,25},{17,1},{25,9},{2,18},{10... | collective-permute-start | bytes 786440 | tf_op jit(solution)/shard_map/ppermute | solution.py:332
  47.4 5.6 %collective-permute-start.13 = (bf16[128,384]{1,0:T(8,128)(2,1)S(1)}, bf16[128,384]{1,0:T(8,128)(2,1)S(1)}, u32[]{:S(2)}, u32[]{:S(2)}) collective-permute-start(bf16[128,384]{1,0:T(8,128)(2,1)S(1)} %get-tuple-element.87), channel_id=1, source_target_pairs={{0,2},{1,3},{2,0},{3,1},{4,6},{5,7},{6,4},{7,5},{8,10},{9,11},{10,... | collective-permute-start | bytes 294920 | tf_op jit(solution)/shard_map/ppermute | solution.py:332
  53.0 5.2 %collective-permute-start.14 = (bf16[64,384]{1,0:T(8,128)(2,1)S(1)}, bf16[64,384]{1,0:T(8,128)(2,1)S(1)}, u32[]{:S(2)}, u32[]{:S(2)}) collective-permute-start(bf16[64,384]{1,0:T(8,128)(2,1)S(1)} %get-tuple-element.89), channel_id=1, source_target_pairs={{0,4},{1,5},{2,6},{3,7},{4,0},{5,1},{6,2},{7,3},{8,12},{9,13},{10,... | collective-permute-start | bytes 147464 | tf_op jit(solution)/shard_map/ppermute | solution.py:332

commit v15 on v14

--- a/solution.py
+++ b/solution.py
@@ -12,7 +12,7 @@
 VMEM = pl.BlockSpec(memory_space=pltpu.VMEM)
 
 
-def call(kernel, outs, *args, flops=0, scratch=(), limit=16):
+def call(kernel, outs, *args, flops=0, scratch=(), limit=16, light=False):
     moved = sum(a.size * a.dtype.itemsize for a in args)
     moved += sum(o.size * o.dtype.itemsize for o in outs)
     return pl.pallas_call(
@@ -22,7 +22,7 @@
         out_specs=tuple(VMEM for _ in outs),
         scratch_shapes=scratch,
         compiler_params=pltpu.CompilerParams(vmem_limit_bytes=limit * 2**20),
-        cost_estimate=pl.CostEstimate(flops=flops, bytes_accessed=moved, transcendentals=0),
+        cost_estimate=pl.CostEstimate(flops=flops, bytes_accessed=0 if light else moved, transcendentals=0),
     )(*args)
 
 
@@ -233,20 +233,9 @@
                 stage(step - late)
 
 
-def main_kernel(
-    z, middle_ref, border_ref, x_ref, t_ref, gain_ref, q_ref, k_ref, v_ref, o_ref, *outs
+def norm_kernel(
+    z, middle_ref, border_ref, x_ref, t_ref, gain_ref, hidden_ref, normed_ref
 ):
-    me = lax.axis_index("tm")
-    a = lax.broadcasted_iota(jnp.int32, (z.block, z.block), 0)
-    b = lax.broadcasted_iota(jnp.int32, (z.block, z.block), 1)
-    allowed = (a // z.f == b // z.f) & (b % z.f <= a % z.f)
-    scale = float(z.c) ** -0.5
-
-    def source(q):
-        t = ((me ^ (q // z.piece)) * z.fl) + q % z.piece // z.wc
-        return q % z.wc * z.f + t
-
-    back = chooser(z.block, z.block, source)
     frame = lax.broadcasted_iota(jnp.int32, (z.block, z.c), 0) % z.f
     held = {}
 
@@ -260,15 +249,33 @@
     def hide(r):
         temporal = taps(held.pop(("a", r)), t_ref[...])
         hidden = (x_ref[r, z.f : z.f + z.block].astype(F32) + temporal).astype(BF)
+        hidden_ref[r] = hidden
         held["h", r] = hidden
 
     def norm(r):
-        wide = held["h", r].astype(F32)
+        wide = held.pop(("h", r)).astype(F32)
         mean = jnp.mean(wide * wide, axis=1, keepdims=True)
-        held["n", r] = (wide * (1.0 / jnp.sqrt(mean + 1e-06)) * gain_ref[...]).astype(BF)
+        normed_ref[r] = (wide * (1.0 / jnp.sqrt(mean + 1e-06)) * gain_ref[...]).astype(BF)
+
+    staged(z, (activate, hide, norm))
+
+
+def attend_kernel(z, hidden_ref, normed_ref, q_ref, k_ref, v_ref, o_ref, *outs):
+    me = lax.axis_index("tm")
+    a = lax.broadcasted_iota(jnp.int32, (z.block, z.block), 0)
+    b = lax.broadcasted_iota(jnp.int32, (z.block, z.block), 1)
+    allowed = (a // z.f == b // z.f) & (b % z.f <= a % z.f)
+    scale = float(z.c) ** -0.5
+
+    def source(q):
+        t = ((me ^ (q // z.piece)) * z.fl) + q % z.piece // z.wc
+        return q % z.wc * z.f + t
+
+    back = chooser(z.block, z.block, source)
+    held = {}
 
     def project(r):
-        rows = held.pop(("n", r))
+        rows = normed_ref[r]
         held["q", r], held["k", r], held["v", r] = (
             jnp.dot(rows, w[...], preferred_element_type=F32).astype(BF)
             for w in (q_ref, k_ref, v_ref)
@@ -294,7 +301,7 @@
         held["a", r] = (mixed * held.pop(("t", r))).astype(BF)
 
     def finish(r):
-        encoded = held.pop(("h", r)).astype(F32) + jnp.dot(
+        encoded = hidden_ref[r].astype(F32) + jnp.dot(
             held.pop(("a", r)), o_ref[...], preferred_element_type=F32
         )
         held["e", r] = encoded.astype(BF)
@@ -304,7 +311,7 @@
         for out, k in zip(outs, z.order):
             out[r] = encoded[k * z.piece : (k + 1) * z.piece]
 
-    staged(z, (activate, hide, norm, project, score, weigh, mix, finish, spread))
+    staged(z, (project, score, weigh, mix, finish, spread))
 
 
 def split_kernel(z, keep_ref, got_ref, *outs):
@@ -464,8 +471,17 @@
         spatial,
         flops=9 * one * (z.r - 2) // z.r,
     )
-    tied = lax.optimization_barrier((near, far, middle, close, apart))
-    near, far, middle, close, apart = tied
+    (border,) = call(
+        functools.partial(border_kernel, z),
+        [shape((2, z.block, z.c))],
+        x,
+        close,
+        apart,
+        spatial,
+        light=True,
+        scratch=[pltpu.VMEM((2, line, z.c), BF)],
+    )
+    near, far, border, middle = lax.optimization_barrier((near, far, border, middle))
     keep, send = call(
         functools.partial(cross_kernel, z, width),
         [shape((z.c // 2, 3 * z.c), F32), shape((z.c // 2, 3 * z.c))],
@@ -477,40 +493,37 @@
         flops=3 * one // 4,
     )
     other = swap(send, "space", 1)
-    x, _ = lax.optimization_barrier((x, send))
-    (border,) = call(
-        functools.partial(border_kernel, z),
-        [shape((2, z.block, z.c))],
+    border, _ = lax.optimization_barrier((border, send))
+    hidden, normed = call(
+        functools.partial(norm_kernel, z),
+        [shape((z.r, z.block, z.c))] * 2,
+        middle,
+        border,
         x,
-        close,
-        apart,
-        spatial,
-        flops=18 * one // z.r,
-        scratch=[pltpu.VMEM((2, line, z.c), BF)],
-    )
-    other, border = lax.optimization_barrier((other, border))
+        temporal,
+        gain.reshape(1, z.c),
+        flops=3 * one,
+    )
     pieces = call(
         functools.partial(split_kernel, z),
         [shape((z.c // 2, 3 * wide), F32)] + [shape((z.c // 2, 3 * wide))] * (n - 1),
         keep,
         other,
     )
-    border, *pieces = lax.optimization_barrier((border, *pieces))
+    normed, *pieces = lax.optimization_barrier((normed, *pieces))
     pieces = exchange(pieces)
-    encoded = z.by_partner(call(
-        functools.partial(main_kernel, z),
+    encoded = call(
+        functools.partial(attend_kernel, z),
         [shape((z.r, z.piece, z.c))] * n,
-        middle,
-        border,
-        x,
-        temporal,
-        gain.reshape(1, z.c),
+        hidden,
+        normed,
         q_w,
         k_w,
         v_w,
         o_w,
-        flops=9 * one,
-    ))
+        flops=5 * one,
+    )
+    encoded = z.by_partner(encoded)
     back = exchange(encoded)
     pieces = lax.optimization_barrier((*z.ordered(pieces), *z.ordered(encoded)))[:n]
     bit = 0

time: 60.5 us -> 61.9 us (1.023); the launches traced: 59.4 us -> 61.7 us
  waiting for transfers between devices: 7.83 us -> 10.8 us
  starting transfers between devices: 27.3 us -> 26 us
    ppermute x15, waiting for transfers between devices: 7.83 us -> 10.8 us  [swap(): return lax.ppermute(value, axis, [(i, i ^ k) for i in range(count)])]
    ppermute x15, starting transfers between devices: 25 us -> 23.7 us  [swap(): return lax.ppermute(value, axis, [(i, i ^ k) for i in range(count)])]
    pallas_call x13 -> x14, Pallas kernels: 20.9 us -> 21.4 us  [call(): pl.pallas_call(kernel, out_shape=tuple(outs), in_specs=[VMEM] * len(args)...]
  transfers between devices with their start and end apart: 18 -> 18, of which waited for: 4 -> 4; matrix products, arithmetic and copies ran while one was open for 0% -> 0% of each run, Pallas kernels for 33% -> 32%
where the time goes in v15:
time: 61.9 us; the launch traced here: 61.7 us
  starting transfers between devices  26 us (42%)
  Pallas kernels  22.4 us (36%)
  waiting for transfers between devices  10.8 us (17%)
  local copies, waits for them, and re-layouts  1.33 us (2%)
  between operations  1.07 us (2%)
    ppermute x15, starting transfers between devices, swap(): return lax.ppermute(value, axis, [(i, i ^ k) for i in range(count)])  23.7 us
    pallas_call x14, Pallas kernels, call(): pl.pallas_call(kernel, out_shape=tuple(outs), in_specs=[VMEM] * len(args)...  21.4 us
    ppermute x15, waiting for transfers between devices, swap(): return lax.ppermute(value, axis, [(i, i ^ k) for i in range(count)])  10.8 us
    ppermute x3, starting transfers between devices, swap_both(): far = lax.ppermute(far, axis, pairs + [(b, a) for a, b in pairs])  2.32 us
    unnamed x20, local copies, waits for them, and re-layouts  1.33 us
  transfers between devices with their start and end apart: 18, of which 4 were waited for; matrix products, arithmetic and copies ran while one was open for 0% of the time, Pallas kernels for 32%

profile of v15, /device:TPU:0, one launch (start us, length us, event | category | flops | bytes accessed | tf_op | source)
XLA Modules:
  0.0 61.7 jit_solution(13822622257796644780)
XLA Ops:
  0.6 1.2 %copy-done.1 = bf16[4,4,64,512]{3,2,1,0:T(8,128)(2,1)S(1)} copy-done((bf16[4,4,64,512]{3,2,1,0:T(8,128)(2,1)S(1)}, bf16[4,4,64,512]{3,2,1,0:T(8,128)(2,1)}, u32[]{:S(2)}) %copy-start.1) | copy-done | bytes 1048600
  1.9 0.6 shard_map.105
  2.4 4.0 %collective-permute-start.4 = (bf16[288,512]{1,0:T(8,128)(2,1)S(1)}, bf16[288,512]{1,0:T(8,128)(2,1)S(1)}, u32[]{:S(2)}, u32[]{:S(2)}) collective-permute-start(bf16[288,512]{1,0:T(8,128)(2,1)S(1)} %get-tuple-element.51), channel_id=1, source_target_pairs={{0,24},{8,16},{16,8},{24,0},{1,25},{9,17},{17,9},{25,1},{2,26},{10... | collective-permute-start | bytes 884744 | tf_op jit(solution)/shard_map/ppermute | solution.py:339
  6.4 0.5 collective-permute-start.5
  6.9 0.1 collective-permute-start.6
  7.0 0.1 shard_map.106
  7.1 0.1 collective-permute-start
  7.2 0.0 copy-start
  7.2 0.8 %collective-permute-start.1 = (bf16[256,512]{1,0:T(8,128)(2,1)S(1)}, bf16[256,512]{1,0:T(8,128)(2,1)S(1)}, u32[]{:S(2)}, u32[]{:S(2)}) collective-permute-start(bf16[256,512]{1,0:T(8,128)(2,1)S(1)} %get-tuple-element.48), channel_id=1, source_target_pairs={{1,2},{3,4},{5,6},{2,1},{4,3},{6,5},{9,10},{11,12},{13,14},{10,9},... | collective-permute-start | bytes 786440 | tf_op jit(solution)/shard_map/ppermute | solution.py:344
  8.0 0.1 slice-done.1
  8.1 4.8 %shard_map.104.part_ref = f32[4,256,512]{2,1,0:T(8,128)S(1)} custom-call(bf16[4,4,64,512]{3,2,1,0:T(8,128)(2,1)S(1)} %copy-done.1, bf16[3,3,512,512]{3,2,1,0:T(8,128)(2,1)S(1)} %bitcast.3), custom_call_target="tpu_custom_call" | custom-call | flops 4294967296 | bytes 7864320 | tf_op jit(solution)/shard_map/pallas_call | solution.py:18
  12.8 0.0 collective-permute-done.near_ref
  12.9 1.9 %shard_map.107 = (bf16[4,4,64,512]{3,2,1,0:T(8,128)(2,1)S(1)}, bf16[4,64,512]{2,1,0:T(8,128)(2,1)S(1)}, bf16[4,64,512]{2,1,0:T(8,128)(2,1)S(1)}) custom-call(f32[4,256,512]{2,1,0:T(8,128)S(1)} %shard_map.104.part_ref, bf16[256,512]{1,0:T(8,128)(2,1)S(1)} %collective-permute-done.near_ref, bf16[256,512]{1,0:T(8,128)(2,1)S(1)} %collective-permute-done.1.far_ref, ...), custom_call_target="tpu_custom_call" | custom-call | flops 1610612736 | bytes 9961472 | tf_op jit(solution)/shard_map/pallas_call | solution.py:18
  14.8 2.0 %collective-permute-start.2 = (bf16[4,64,512]{2,1,0:T(8,128)(2,1)S(1)}, bf16[4,64,512]{2,1,0:T(8,128)(2,1)S(1)}, u32[]{:S(2)}, u32[]{:S(2)}) collective-permute-start(bf16[4,64,512]{2,1,0:T(8,128)(2,1)S(1)} %get-tuple-element.49), channel_id=1, source_target_pairs={{0,8},{8,0},{16,24},{24,16},{1,9},{9,1},{17,25},{25,17},{2,10},{10... | collective-permute-start | bytes 786440 | tf_op jit(solution)/shard_map/ppermute | solution.py:339
  16.7 0.7 %collective-permute-start.3 = (bf16[4,64,512]{2,1,0:T(8,128)(2,1)S(1)}, bf16[4,64,512]{2,1,0:T(8,128)(2,1)S(1)}, u32[]{:S(2)}, u32[]{:S(2)}) collective-permute-start(bf16[4,64,512]{2,1,0:T(8,128)(2,1)S(1)} %get-tuple-element.50), channel_id=1, source_target_pairs={{8,16},{16,8},{9,17},{17,9},{10,18},{18,10},{11,19},{19,11},{12,20... | collective-permute-start | bytes 786440 | tf_op jit(solution)/shard_map/ppermute | solution.py:344
  17.4 0.0 collective-permute-done.4.refs_0_
  17.4 2.6 %collective-permute-done.5.refs_1_ = bf16[288,512]{1,0:T(8,128)(2,1)S(1)} collective-permute-done((bf16[288,512]{1,0:T(8,128)(2,1)S(1)}, bf16[288,512]{1,0:T(8,128)(2,1)S(1)}, u32[]{:S(2)}, u32[]{:S(2)}) %collective-permute-start.5) | collective-permute-done | bytes 294944 | tf_op jit(solution)/shard_map/ppermute | solution.py:339
  20.0 0.5 shard_map.108
  20.5 0.1 collective-permute-start.7
  20.6 0.8 %collective-permute-start.8 = (bf16[288,512]{1,0:T(8,128)(2,1)S(1)}, bf16[288,512]{1,0:T(8,128)(2,1)S(1)}, u32[]{:S(2)}, u32[]{:S(2)}) collective-permute-start(bf16[288,512]{1,0:T(8,128)(2,1)S(1)} %get-tuple-element.56), channel_id=1, source_target_pairs={{1,2},{3,4},{5,6},{2,1},{4,3},{6,5},{9,10},{11,12},{13,14},{10,9},... | collective-permute-start | bytes 884744 | tf_op jit(solution)/shard_map/ppermute | solution.py:344
  21.5 1.4 %shard_map.111.part_ref = f32[512,1536]{1,0:T(8,128)S(1)} custom-call(bf16[4,4,64,512]{3,2,1,0:T(8,128)(2,1)S(1)} %get-tuple-element.59.act_ref, bf16[4,4,64,512]{3,2,1,0:T(8,128)(2,1)S(1)} %copy-done), custom_call_target="tpu_custom_call" | custom-call | flops 1207959552 | bytes 5242880 | tf_op jit(solution)/shard_map/pallas_call | solution.py:18
  22.9 2.7 %shard_map.110.middle_ref = bf16[2,256,512]{2,1,0:T(8,128)(2,1)S(1)} custom-call(bf16[4,288,512]{2,1,0:T(8,128)(2,1)S(1)} %get-tuple-element.54.x_ref, bf16[3,3,512,512]{3,2,1,0:T(8,128)(2,1)S(1)} %bitcast.3), custom_call_target="tpu_custom_call" | custom-call | flops 2415919104 | bytes 6422528 | tf_op jit(solution)/shard_map/pallas_call | solution.py:18
  25.6 0.0 collective-permute-done.7.near_ref
  25.6 2.7 %shard_map.109.border_ref = bf16[2,256,512]{2,1,0:T(8,128)(2,1)S(1)} custom-call(bf16[4,288,512]{2,1,0:T(8,128)(2,1)S(1)} %get-tuple-element.54.x_ref, bf16[288,512]{1,0:T(8,128)(2,1)S(1)} %collective-permute-done.7.near_ref, bf16[288,512]{1,0:T(8,128)(2,1)S(1)} %collective-permute-done.8.far_ref, bf16[3,3,512,512]{3,2,1,0:T(8,128)(2,1)S(1)} %bitcast.3), custom_call_target="tpu_custom_call" | custom-call | tf_op jit(solution)/shard_map/pallas_call | solution.py:18
  28.3 0.0 copy-start.2
  28.3 0.0 copy-start.7
  28.3 0.7 %shard_map.112 = (f32[256,1536]{1,0:T(8,128)S(1)}, bf16[256,1536]{1,0:T(8,128)(2,1)S(1)}) custom-call(f32[512,1536]{1,0:T(8,128)S(1)} %shard_map.111.part_ref, bf16[4,64,512]{2,1,0:T(8,128)(2,1)S(1)} %collective-permute-done.2.near_ref, bf16[4,64,512]{2,1,0:T(8,128)(2,1)S(1)} %collective-permute-done.3.far_ref, ...), custom_call_target="tpu_custom_call" | custom-call | flops 402653184 | bytes 8126464 | tf_op jit(solution)/shard_map/pallas_call | solution.py:18
  29.0 3.6 %collective-permute-start.9 = (bf16[256,1536]{1,0:T(8,128)(2,1)S(1)}, bf16[256,1536]{1,0:T(8,128)(2,1)S(1)}, u32[]{:S(2)}, u32[]{:S(2)}) collective-permute-start(bf16[256,1536]{1,0:T(8,128)(2,1)S(1)} %get-tuple-element.62), channel_id=1, source_target_pairs={{0,1},{1,0},{2,3},{3,2},{4,5},{5,4},{6,7},{7,6},{8,9},{9,8},{10,11... | collective-permute-start | bytes 2359304 | tf_op jit(solution)/shard_map/ppermute | solution.py:339
  32.6 2.3 %shard_map.113 = (bf16[4,256,512]{2,1,0:T(8,128)(2,1)S(1)}, bf16[4,256,512]{2,1,0:T(8,128)(2,1)S(1)}) custom-call(bf16[2,256,512]{2,1,0:T(8,128)(2,1)S(1)} %shard_map.110.middle_ref, bf16[2,256,512]{2,1,0:T(8,128)(2,1)S(1)} %shard_map.109.border_ref, bf16[4,288,512]{2,1,0:T(8,128)(2,1)S(1)} %get-tuple-element.54.x_ref, bf16[3,512,512]{2,1,0:T(8,128)(2,1)S(1)} %copy-done.2, ...), custom_call_target="tpu_custom_call" | custom-call | flops 1610612736 | bytes 5900288 | tf_op jit(solution)/shard_map/pallas_call | solution.py:18
  34.8 0.0 copy-start.3
  34.9 0.0 copy-start.4
  34.9 0.0 copy-start.5
  34.9 0.0 copy-start.6
  34.9 0.3 shard_map.114
  35.2 2.4 %collective-permute-start.10 = (bf16[256,384]{1,0:T(8,128)(2,1)S(1)}, bf16[256,384]{1,0:T(8,128)(2,1)S(1)}, u32[]{:S(2)}, u32[]{:S(2)}) collective-permute-start(bf16[256,384]{1,0:T(8,128)(2,1)S(1)} %get-tuple-element.70), channel_id=1, source_target_pairs={{0,24},{8,16},{16,8},{24,0},{1,25},{9,17},{17,9},{25,1},{2,26},{10... | collective-permute-start | bytes 589832 | tf_op jit(solution)/shard_map/ppermute | solution.py:339
  37.6 1.9 %collective-permute-start.11 = (bf16[256,384]{1,0:T(8,128)(2,1)S(1)}, bf16[256,384]{1,0:T(8,128)(2,1)S(1)}, u32[]{:S(2)}, u32[]{:S(2)}) collective-permute-start(bf16[256,384]{1,0:T(8,128)(2,1)S(1)} %get-tuple-element.71), channel_id=1, source_target_pairs={{0,8},{8,0},{16,24},{24,16},{1,9},{9,1},{17,25},{25,17},{2,10},{10... | collective-permute-start | bytes 589832 | tf_op jit(solution)/shard_map/ppermute | solution.py:339
  39.5 0.7 %collective-permute-start.12 = (bf16[256,384]{1,0:T(8,128)(2,1)S(1)}, bf16[256,384]{1,0:T(8,128)(2,1)S(1)}, u32[]{:S(2)}, u32[]{:S(2)}) collective-permute-start(bf16[256,384]{1,0:T(8,128)(2,1)S(1)} %get-tuple-element.72), channel_id=1, source_target_pairs={{0,16},{8,24},{16,0},{24,8},{1,17},{9,25},{17,1},{25,9},{2,18},{10... | collective-permute-start | bytes 589832 | tf_op jit(solution)/shard_map/ppermute | solution.py:339
  40.3 3.5 %shard_map.115 = (bf16[4,64,512]{2,1,0:T(8,128)(2,1)S(1)}, bf16[4,64,512]{2,1,0:T(8,128)(2,1)S(1)}, bf16[4,64,512]{2,1,0:T(8,128)(2,1)S(1)}, bf16[4,64,512]{2,1,0:T(8,128)(2,1)S(1)}) custom-call(bf16[4,256,512]{2,1,0:T(8,128)(2,1)S(1)} %get-tuple-element.74.hidden_ref, bf16[4,256,512]{2,1,0:T(8,128)(2,1)S(1)} %get-tuple-element.75.normed_ref, ...), custom_call_target="tpu_custom_call" | custom-call | flops 2684354560 | bytes 5242880 | tf_op jit(solution)/shard_map/pallas_call | solution.py:18
  43.8 1.5 %collective-permute-start.15 = (bf16[4,64,512]{2,1,0:T(8,128)(2,1)S(1)}, bf16[4,64,512]{2,1,0:T(8,128)(2,1)S(1)}, u32[]{:S(2)}, u32[]{:S(2)}) collective-permute-start(bf16[4,64,512]{2,1,0:T(8,128)(2,1)S(1)} %get-tuple-element.76), channel_id=1, source_target_pairs={{0,24},{8,16},{16,8},{24,0},{1,25},{9,17},{17,9},{25,1},{2,26},{10... | collective-permute-start | bytes 786440 | tf_op jit(solution)/shard_map/ppermute | solution.py:339
  45.3 1.3 %collective-permute-start.16 = (bf16[4,64,512]{2,1,0:T(8,128)(2,1)S(1)}, bf16[4,64,512]{2,1,0:T(8,128)(2,1)S(1)}, u32[]{:S(2)}, u32[]{:S(2)}) collective-permute-start(bf16[4,64,512]{2,1,0:T(8,128)(2,1)S(1)} %get-tuple-element.77), channel_id=1, source_target_pairs={{0,8},{8,0},{16,24},{24,16},{1,9},{9,1},{17,25},{25,17},{2,10},{10... | collective-permute-start | bytes 786440 | tf_op jit(solution)/shard_map/ppermute | solution.py:339
  46.6 0.7 %collective-permute-start.17 = (bf16[4,64,512]{2,1,0:T(8,128)(2,1)S(1)}, bf16[4,64,512]{2,1,0:T(8,128)(2,1)S(1)}, u32[]{:S(2)}, u32[]{:S(2)}) collective-permute-start(bf16[4,64,512]{2,1,0:T(8,128)(2,1)S(1)} %get-tuple-element.78), channel_id=1, source_target_pairs={{0,16},{8,24},{16,0},{24,8},{1,17},{9,25},{17,1},{25,9},{2,18},{10... | collective-permute-start | bytes 786440 | tf_op jit(solution)/shard_map/ppermute | solution.py:339
  47.3 2.2 %collective-permute-done.11.refs_1_ = bf16[256,384]{1,0:T(8,128)(2,1)S(1)} collective-permute-done((bf16[256,384]{1,0:T(8,128)(2,1)S(1)}, bf16[256,384]{1,0:T(8,128)(2,1)S(1)}, u32[]{:S(2)}, u32[]{:S(2)}) %collective-permute-start.11) | collective-permute-done | bytes 196640 | tf_op jit(solution)/shard_map/ppermute | solution.py:339
  49.5 0.1 shard_map.116
  49.6 1.9 %collective-permute-start.13 = (bf16[128,384]{1,0:T(8,128)(2,1)S(1)}, bf16[128,384]{1,0:T(8,128)(2,1)S(1)}, u32[]{:S(2)}, u32[]{:S(2)}) collective-permute-start(bf16[128,384]{1,0:T(8,128)(2,1)S(1)} %get-tuple-element.85), channel_id=1, source_target_pairs={{0,2},{1,3},{2,0},{3,1},{4,6},{5,7},{6,4},{7,5},{8,10},{9,11},{10,... | collective-permute-start | bytes 294920 | tf_op jit(solution)/shard_map/ppermute | solution.py:339
  51.5 2.8 %collective-permute-done.13.refs_1_ = bf16[128,384]{1,0:T(8,128)(2,1)S(1)} collective-permute-done((bf16[128,384]{1,0:T(8,128)(2,1)S(1)}, bf16[128,384]{1,0:T(8,128)(2,1)S(1)}, u32[]{:S(2)}, u32[]{:S(2)}) %collective-permute-start.13) | collective-permute-done | bytes 98336 | tf_op jit(solution)/shard_map/ppermute | solution.py:339
  54.3 2.9 %collective-permute-start.14 = (bf16[64,384]{1,0:T(8,128)(2,1)S(1)}, bf16[64,384]{1,0:T(8,128)(2,1)S(1)}, u32[]{:S(2)}, u32[]{:S(2)}) collective-permute-start(bf16[64,384]{1,0:T(8,128)(2,1)S(1)} %get-tuple-element.87), channel_id=1, source_target_pairs={{0,4},{1,5},{2,6},{3,7},{4,0},{5,1},{6,2},{7,3},{8,12},{9,13},{10,... | collective-permute-start | bytes 147464 | tf_op jit(solution)/shard_map/ppermute | solution.py:339
  57.3 3.2 %collective-permute-done.16.refs_1_ = bf16[4,64,512]{2,1,0:T(8,128)(2,1)S(1)} collective-permute-done((bf16[4,64,512]{2,1,0:T(8,128)(2,1)S(1)}, bf16[4,64,512]{2,1,0:T(8,128)(2,1)S(1)}, u32[]{:S(2)}, u32[]{:S(2)}) %collective-permute-start.16) | collective-permute-done | bytes 262176 | tf_op jit(solution)/shard_map/ppermute | solution.py:339
  60.5 1.1 %shard_map.118 = (bf16[4,4,64,512]{3,2,1,0:T(8,128)(2,1)}, f32[3,64,128]{2,1,0:T(8,128)}) custom-call(f32[64,384]{1,0:T(8,128)S(1)} %get-tuple-element.86.kept_ref, bf16[64,384]{1,0:T(8,128)(2,1)S(1)} %collective-permute-done.14.got_ref, bf16[4,64,512]{2,1,0:T(8,128)(2,1)S(1)} %collective-permute-done.15.refs_0_, ...), custom_call_target="tpu_custom_call" | custom-call | bytes 4194304 | tf_op jit(solution)/shard_map/pallas_call | solution.py:386
  (24 shorter events, 0.1 us)
Async XLA Ops:
  0.6 1.2 %copy-start.1 = (bf16[4,4,64,512]{3,2,1,0:T(8,128)(2,1)S(1)}, bf16[4,4,64,512]{3,2,1,0:T(8,128)(2,1)}, u32[]{:S(2)}) copy-start(bf16[4,4,64,512]{3,2,1,0:T(8,128)(2,1)} %x_ref.5) | copy-start | bytes 3145732
  1.9 6.2 %slice-start = ((s8[4718592]{0:T(1024)(128)(4,1)}), s8[4194304]{0:T(1024)(128)(4,1)S(1)}, s32[]{:S(2)}) async-start(s8[4718592]{0:T(1024)(128)(4,1)} %bitcast.2), calls=%async_computation | async-start | bytes 8388608
  2.4 15.0 %collective-permute-start.4 = (bf16[288,512]{1,0:T(8,128)(2,1)S(1)}, bf16[288,512]{1,0:T(8,128)(2,1)S(1)}, u32[]{:S(2)}, u32[]{:S(2)}) collective-permute-start(bf16[288,512]{1,0:T(8,128)(2,1)S(1)} %get-tuple-element.51), channel_id=1, source_target_pairs={{0,24},{8,16},{16,8},{24,0},{1,25},{9,17},{17,9},{25,1},{2,26},{10... | collective-permute-start | bytes 884744 | tf_op jit(solution)/shard_map/ppermute | solution.py:339
  6.4 13.6 %collective-permute-start.5 = (bf16[288,512]{1,0:T(8,128)(2,1)S(1)}, bf16[288,512]{1,0:T(8,128)(2,1)S(1)}, u32[]{:S(2)}, u32[]{:S(2)}) collective-permute-start(bf16[288,512]{1,0:T(8,128)(2,1)S(1)} %get-tuple-element.52), channel_id=1, source_target_pairs={{0,8},{8,0},{16,24},{24,16},{1,9},{9,1},{17,25},{25,17},{2,10},{10... | collective-permute-start | bytes 884744 | tf_op jit(solution)/shard_map/ppermute | solution.py:339
  6.9 13.1 %collective-permute-start.6 = (bf16[288,512]{1,0:T(8,128)(2,1)S(1)}, bf16[288,512]{1,0:T(8,128)(2,1)S(1)}, u32[]{:S(2)}, u32[]{:S(2)}) collective-permute-start(bf16[288,512]{1,0:T(8,128)(2,1)S(1)} %get-tuple-element.53), channel_id=1, source_target_pairs={{0,16},{8,24},{16,0},{24,8},{1,17},{9,25},{17,1},{25,9},{2,18},{10... | collective-permute-start | bytes 884744 | tf_op jit(solution)/shard_map/ppermute | solution.py:339
  7.0 1.0 %slice-start.1 = ((s8[4718592]{0:T(1024)(128)(4,1)}), s8[524288]{0:T(1024)(128)(4,1)S(1)}, s32[]{:S(2)}) async-start(s8[4718592]{0:T(1024)(128)(4,1)} %bitcast.2), calls=%async_computation.1 | async-start | bytes 1048576
  7.1 5.7 %collective-permute-start = (bf16[256,512]{1,0:T(8,128)(2,1)S(1)}, bf16[256,512]{1,0:T(8,128)(2,1)S(1)}, u32[]{:S(2)}, u32[]{:S(2)}) collective-permute-start(bf16[256,512]{1,0:T(8,128)(2,1)S(1)} %get-tuple-element.47), channel_id=1, source_target_pairs={{0,1},{1,0},{2,3},{3,2},{4,5},{5,4},{6,7},{7,6},{8,9},{9,8},{10,11... | collective-permute-start | bytes 786440 | tf_op jit(solution)/shard_map/ppermute | solution.py:339
  7.2 5.7 %copy-start = (bf16[4,4,64,512]{3,2,1,0:T(8,128)(2,1)S(1)}, bf16[4,4,64,512]{3,2,1,0:T(8,128)(2,1)}, u32[]{:S(2)}) copy-start(bf16[4,4,64,512]{3,2,1,0:T(8,128)(2,1)} %cot_ref.5) | copy-start | bytes 3145732
  7.2 5.7 %collective-permute-start.1 = (bf16[256,512]{1,0:T(8,128)(2,1)S(1)}, bf16[256,512]{1,0:T(8,128)(2,1)S(1)}, u32[]{:S(2)}, u32[]{:S(2)}) collective-permute-start(bf16[256,512]{1,0:T(8,128)(2,1)S(1)} %get-tuple-element.48), channel_id=1, source_target_pairs={{1,2},{3,4},{5,6},{2,1},{4,3},{6,5},{9,10},{11,12},{13,14},{10,9},... | collective-permute-start | bytes 786440 | tf_op jit(solution)/shard_map/ppermute | solution.py:344
  14.8 13.5 %collective-permute-start.2 = (bf16[4,64,512]{2,1,0:T(8,128)(2,1)S(1)}, bf16[4,64,512]{2,1,0:T(8,128)(2,1)S(1)}, u32[]{:S(2)}, u32[]{:S(2)}) collective-permute-start(bf16[4,64,512]{2,1,0:T(8,128)(2,1)S(1)} %get-tuple-element.49), channel_id=1, source_target_pairs={{0,8},{8,0},{16,24},{24,16},{1,9},{9,1},{17,25},{25,17},{2,10},{10... | collective-permute-start | bytes 786440 | tf_op jit(solution)/shard_map/ppermute | solution.py:339
  16.7 11.6 %collective-permute-start.3 = (bf16[4,64,512]{2,1,0:T(8,128)(2,1)S(1)}, bf16[4,64,512]{2,1,0:T(8,128)(2,1)S(1)}, u32[]{:S(2)}, u32[]{:S(2)}) collective-permute-start(bf16[4,64,512]{2,1,0:T(8,128)(2,1)S(1)} %get-tuple-element.50), channel_id=1, source_target_pairs={{8,16},{16,8},{9,17},{17,9},{10,18},{18,10},{11,19},{19,11},{12,20... | collective-permute-start | bytes 786440 | tf_op jit(solution)/shard_map/ppermute | solution.py:344
  20.5 5.0 %collective-permute-start.7 = (bf16[288,512]{1,0:T(8,128)(2,1)S(1)}, bf16[288,512]{1,0:T(8,128)(2,1)S(1)}, u32[]{:S(2)}, u32[]{:S(2)}) collective-permute-start(bf16[288,512]{1,0:T(8,128)(2,1)S(1)} %get-tuple-element.55), channel_id=1, source_target_pairs={{0,1},{1,0},{2,3},{3,2},{4,5},{5,4},{6,7},{7,6},{8,9},{9,8},{10,11... | collective-permute-start | bytes 884744 | tf_op jit(solution)/shard_map/ppermute | solution.py:339
  20.6 5.0 %collective-permute-start.8 = (bf16[288,512]{1,0:T(8,128)(2,1)S(1)}, bf16[288,512]{1,0:T(8,128)(2,1)S(1)}, u32[]{:S(2)}, u32[]{:S(2)}) collective-permute-start(bf16[288,512]{1,0:T(8,128)(2,1)S(1)} %get-tuple-element.56), channel_id=1, source_target_pairs={{1,2},{3,4},{5,6},{2,1},{4,3},{6,5},{9,10},{11,12},{13,14},{10,9},... | collective-permute-start | bytes 884744 | tf_op jit(solution)/shard_map/ppermute | solution.py:344
  28.3 4.3 %copy-start.2 = (bf16[3,512,512]{2,1,0:T(8,128)(2,1)S(1)}, bf16[3,512,512]{2,1,0:T(8,128)(2,1)}, u32[]{:S(2)}) copy-start(bf16[3,512,512]{2,1,0:T(8,128)(2,1)} %t_ref.1) | copy-start | bytes 4718596
  28.3 4.3 %copy-start.7 = (f32[512]{0:T(512)S(1)}, f32[512]{0:T(512)}, u32[]{:S(2)}) copy-start(f32[512]{0:T(512)} %param.12) | copy-start | bytes 6148
  29.0 5.9 %collective-permute-start.9 = (bf16[256,1536]{1,0:T(8,128)(2,1)S(1)}, bf16[256,1536]{1,0:T(8,128)(2,1)S(1)}, u32[]{:S(2)}, u32[]{:S(2)}) collective-permute-start(bf16[256,1536]{1,0:T(8,128)(2,1)S(1)} %get-tuple-element.62), channel_id=1, source_target_pairs={{0,1},{1,0},{2,3},{3,2},{4,5},{5,4},{6,7},{7,6},{8,9},{9,8},{10,11... | collective-permute-start | bytes 2359304 | tf_op jit(solution)/shard_map/ppermute | solution.py:339
  34.8 5.4 %copy-start.3 = (bf16[512,512]{1,0:T(8,128)(2,1)S(1)}, bf16[512,512]{1,0:T(8,128)(2,1)}, u32[]{:S(2)}) copy-start(bf16[512,512]{1,0:T(8,128)(2,1)} %q_ref.1) | copy-start | bytes 1572868
  34.9 5.4 %copy-start.4 = (bf16[512,512]{1,0:T(8,128)(2,1)S(1)}, bf16[512,512]{1,0:T(8,128)(2,1)}, u32[]{:S(2)}) copy-start(bf16[512,512]{1,0:T(8,128)(2,1)} %k_ref.1) | copy-start | bytes 1572868
  34.9 5.4 %copy-start.5 = (bf16[512,512]{1,0:T(8,128)(2,1)S(1)}, bf16[512,512]{1,0:T(8,128)(2,1)}, u32[]{:S(2)}) copy-start(bf16[512,512]{1,0:T(8,128)(2,1)} %v_ref.1) | copy-start | bytes 1572868
  34.9 5.4 %copy-start.6 = (bf16[512,512]{1,0:T(8,128)(2,1)S(1)}, bf16[512,512]{1,0:T(8,128)(2,1)}, u32[]{:S(2)}) copy-start(bf16[512,512]{1,0:T(8,128)(2,1)} %o_ref.1) | copy-start | bytes 1572868
  35.2 11.4 %collective-permute-start.10 = (bf16[256,384]{1,0:T(8,128)(2,1)S(1)}, bf16[256,384]{1,0:T(8,128)(2,1)S(1)}, u32[]{:S(2)}, u32[]{:S(2)}) collective-permute-start(bf16[256,384]{1,0:T(8,128)(2,1)S(1)} %get-tuple-element.70), channel_id=1, source_target_pairs={{0,24},{8,16},{16,8},{24,0},{1,25},{9,17},{17,9},{25,1},{2,26},{10... | collective-permute-start | bytes 589832 | tf_op jit(solution)/shard_map/ppermute | solution.py:339
  37.6 11.9 %collective-permute-start.11 = (bf16[256,384]{1,0:T(8,128)(2,1)S(1)}, bf16[256,384]{1,0:T(8,128)(2,1)S(1)}, u32[]{:S(2)}, u32[]{:S(2)}) collective-permute-start(bf16[256,384]{1,0:T(8,128)(2,1)S(1)} %get-tuple-element.71), channel_id=1, source_target_pairs={{0,8},{8,0},{16,24},{24,16},{1,9},{9,1},{17,25},{25,17},{2,10},{10... | collective-permute-start | bytes 589832 | tf_op jit(solution)/shard_map/ppermute | solution.py:339
  39.5 10.0 %collective-permute-start.12 = (bf16[256,384]{1,0:T(8,128)(2,1)S(1)}, bf16[256,384]{1,0:T(8,128)(2,1)S(1)}, u32[]{:S(2)}, u32[]{:S(2)}) collective-permute-start(bf16[256,384]{1,0:T(8,128)(2,1)S(1)} %get-tuple-element.72), channel_id=1, source_target_pairs={{0,16},{8,24},{16,0},{24,8},{1,17},{9,25},{17,1},{25,9},{2,18},{10... | collective-permute-start | bytes 589832 | tf_op jit(solution)/shard_map/ppermute | solution.py:339
  43.8 13.5 %collective-permute-start.15 = (bf16[4,64,512]{2,1,0:T(8,128)(2,1)S(1)}, bf16[4,64,512]{2,1,0:T(8,128)(2,1)S(1)}, u32[]{:S(2)}, u32[]{:S(2)}) collective-permute-start(bf16[4,64,512]{2,1,0:T(8,128)(2,1)S(1)} %get-tuple-element.76), channel_id=1, source_target_pairs={{0,24},{8,16},{16,8},{24,0},{1,25},{9,17},{17,9},{25,1},{2,26},{10... | collective-permute-start | bytes 786440 | tf_op jit(solution)/shard_map/ppermute | solution.py:339
  45.3 15.2 %collective-permute-start.16 = (bf16[4,64,512]{2,1,0:T(8,128)(2,1)S(1)}, bf16[4,64,512]{2,1,0:T(8,128)(2,1)S(1)}, u32[]{:S(2)}, u32[]{:S(2)}) collective-permute-start(bf16[4,64,512]{2,1,0:T(8,128)(2,1)S(1)} %get-tuple-element.77), channel_id=1, source_target_pairs={{0,8},{8,0},{16,24},{24,16},{1,9},{9,1},{17,25},{25,17},{2,10},{10... | collective-permute-start | bytes 786440 | tf_op jit(solution)/shard_map/ppermute | solution.py:339
  46.6 13.9 %collective-permute-start.17 = (bf16[4,64,512]{2,1,0:T(8,128)(2,1)S(1)}, bf16[4,64,512]{2,1,0:T(8,128)(2,1)S(1)}, u32[]{:S(2)}, u32[]{:S(2)}) collective-permute-start(bf16[4,64,512]{2,1,0:T(8,128)(2,1)S(1)} %get-tuple-element.78), channel_id=1, source_target_pairs={{0,16},{8,24},{16,0},{24,8},{1,17},{9,25},{17,1},{25,9},{2,18},{10... | collective-permute-start | bytes 786440 | tf_op jit(solution)/shard_map/ppermute | solution.py:339
  49.6 4.7 %collective-permute-start.13 = (bf16[128,384]{1,0:T(8,128)(2,1)S(1)}, bf16[128,384]{1,0:T(8,128)(2,1)S(1)}, u32[]{:S(2)}, u32[]{:S(2)}) collective-permute-start(bf16[128,384]{1,0:T(8,128)(2,1)S(1)} %get-tuple-element.85), channel_id=1, source_target_pairs={{0,2},{1,3},{2,0},{3,1},{4,6},{5,7},{6,4},{7,5},{8,10},{9,11},{10,... | collective-permute-start | bytes 294920 | tf_op jit(solution)/shard_map/ppermute | solution.py:339
  54.3 6.1 %collective-permute-start.14 = (bf16[64,384]{1,0:T(8,128)(2,1)S(1)}, bf16[64,384]{1,0:T(8,128)(2,1)S(1)}, u32[]{:S(2)}, u32[]{:S(2)}) collective-permute-start(bf16[64,384]{1,0:T(8,128)(2,1)S(1)} %get-tuple-element.87), channel_id=1, source_target_pairs={{0,4},{1,5},{2,6},{3,7},{4,0},{5,1},{6,2},{7,3},{8,12},{9,13},{10,... | collective-permute-start | bytes 147464 | tf_op jit(solution)/shard_map/ppermute | solution.py:339

commit v16 on v14

--- a/solution.py
+++ b/solution.py
@@ -132,7 +132,8 @@
 
 
 def silu(total):
-    return (total / (1.0 + jnp.exp(-total))).astype(BF)
+    half = 0.5 * total
+    return (half + half * jnp.tanh(half)).astype(BF)
 
 
 def flat(value):
@@ -265,7 +266,7 @@
     def norm(r):
         wide = held["h", r].astype(F32)
         mean = jnp.mean(wide * wide, axis=1, keepdims=True)
-        held["n", r] = (wide * (1.0 / jnp.sqrt(mean + 1e-06)) * gain_ref[...]).astype(BF)
+        held["n", r] = (wide * lax.rsqrt(mean + 1e-06) * gain_ref[...]).astype(BF)
 
     def project(r):
         rows = held.pop(("n", r))

time: 60.5 us -> 60.3 us (level)
  transfers between devices with their start and end apart: 18 -> 18, of which waited for: 4 -> 4; matrix products, arithmetic and copies ran while one was open for 0% -> 0% of each run, Pallas kernels for 33% -> 32%
where the time goes in v16:
time: 60.3 us; the launch traced here: 59.4 us
  starting transfers between devices  27.2 us (45%)
  Pallas kernels  21.7 us (36%)
  waiting for transfers between devices  8.05 us (13%)
  local copies, waits for them, and re-layouts  1.32 us (2%)
  between operations  1.08 us (2%)
    ppermute x15, starting transfers between devices, swap(): return lax.ppermute(value, axis, [(i, i ^ k) for i in range(count)])  24.9 us
    pallas_call x13, Pallas kernels, call(): pl.pallas_call(kernel, out_shape=tuple(outs), in_specs=[VMEM] * len(args)...  20.6 us
    ppermute x15, waiting for transfers between devices, swap(): return lax.ppermute(value, axis, [(i, i ^ k) for i in range(count)])  8.04 us
    ppermute x3, starting transfers between devices, swap_both(): far = lax.ppermute(far, axis, pairs + [(b, a) for a, b in pairs])  2.33 us
    unnamed x20, local copies, waits for them, and re-layouts  1.32 us
  transfers between devices with their start and end apart: 18, of which 4 were waited for; matrix products, arithmetic and copies ran while one was open for 0% of the time, Pallas kernels for 32%

profile of v16, /device:TPU:0, one launch (start us, length us, event | category | flops | bytes accessed | tf_op | source)
XLA Modules:
  0.0 59.4 jit_solution(3868791604142537963)
XLA Ops:
  0.6 1.2 %copy-done.1 = bf16[4,4,64,512]{3,2,1,0:T(8,128)(2,1)S(1)} copy-done((bf16[4,4,64,512]{3,2,1,0:T(8,128)(2,1)S(1)}, bf16[4,4,64,512]{3,2,1,0:T(8,128)(2,1)}, u32[]{:S(2)}) %copy-start.1) | copy-done | bytes 1048600
  1.9 0.6 shard_map.105
  2.4 4.0 %collective-permute-start.4 = (bf16[288,512]{1,0:T(8,128)(2,1)S(1)}, bf16[288,512]{1,0:T(8,128)(2,1)S(1)}, u32[]{:S(2)}, u32[]{:S(2)}) collective-permute-start(bf16[288,512]{1,0:T(8,128)(2,1)S(1)} %get-tuple-element.53), channel_id=1, source_target_pairs={{0,24},{8,16},{16,8},{24,0},{1,25},{9,17},{17,9},{25,1},{2,26},{10... | collective-permute-start | bytes 884744 | tf_op jit(solution)/shard_map/ppermute | solution.py:333
  6.4 0.5 collective-permute-start.5
  6.9 0.1 collective-permute-start.6
  7.0 0.1 shard_map.106
  7.1 0.1 collective-permute-start
  7.2 0.0 copy-start
  7.2 0.8 %collective-permute-start.1 = (bf16[256,512]{1,0:T(8,128)(2,1)S(1)}, bf16[256,512]{1,0:T(8,128)(2,1)S(1)}, u32[]{:S(2)}, u32[]{:S(2)}) collective-permute-start(bf16[256,512]{1,0:T(8,128)(2,1)S(1)} %get-tuple-element.49), channel_id=1, source_target_pairs={{1,2},{3,4},{5,6},{2,1},{4,3},{6,5},{9,10},{11,12},{13,14},{10,9},... | collective-permute-start | bytes 786440 | tf_op jit(solution)/shard_map/ppermute | solution.py:338
  8.0 0.1 slice-done.1
  8.1 4.8 %shard_map.104.part_ref = f32[4,256,512]{2,1,0:T(8,128)S(1)} custom-call(bf16[4,4,64,512]{3,2,1,0:T(8,128)(2,1)S(1)} %copy-done.1, bf16[3,3,512,512]{3,2,1,0:T(8,128)(2,1)S(1)} %bitcast.3), custom_call_target="tpu_custom_call" | custom-call | flops 4294967296 | bytes 7864320 | tf_op jit(solution)/shard_map/pallas_call | solution.py:18
  12.8 0.0 collective-permute-done.near_ref
  12.9 0.0 collective-permute-done.1.far_ref
  12.9 1.8 %shard_map.107 = (bf16[4,4,64,512]{3,2,1,0:T(8,128)(2,1)S(1)}, bf16[4,64,512]{2,1,0:T(8,128)(2,1)S(1)}, bf16[4,64,512]{2,1,0:T(8,128)(2,1)S(1)}) custom-call(f32[4,256,512]{2,1,0:T(8,128)S(1)} %shard_map.104.part_ref, bf16[256,512]{1,0:T(8,128)(2,1)S(1)} %collective-permute-done.near_ref, bf16[256,512]{1,0:T(8,128)(2,1)S(1)} %collective-permute-done.1.far_ref, ...), custom_call_target="tpu_custom_call" | custom-call | flops 1610612736 | bytes 9961472 | tf_op jit(solution)/shard_map/pallas_call | solution.py:18
  14.7 2.0 %collective-permute-start.2 = (bf16[4,64,512]{2,1,0:T(8,128)(2,1)S(1)}, bf16[4,64,512]{2,1,0:T(8,128)(2,1)S(1)}, u32[]{:S(2)}, u32[]{:S(2)}) collective-permute-start(bf16[4,64,512]{2,1,0:T(8,128)(2,1)S(1)} %get-tuple-element.51), channel_id=1, source_target_pairs={{0,8},{8,0},{16,24},{24,16},{1,9},{9,1},{17,25},{25,17},{2,10},{10... | collective-permute-start | bytes 786440 | tf_op jit(solution)/shard_map/ppermute | solution.py:333
  16.6 0.7 %collective-permute-start.3 = (bf16[4,64,512]{2,1,0:T(8,128)(2,1)S(1)}, bf16[4,64,512]{2,1,0:T(8,128)(2,1)S(1)}, u32[]{:S(2)}, u32[]{:S(2)}) collective-permute-start(bf16[4,64,512]{2,1,0:T(8,128)(2,1)S(1)} %get-tuple-element.52), channel_id=1, source_target_pairs={{8,16},{16,8},{9,17},{17,9},{10,18},{18,10},{11,19},{19,11},{12,20... | collective-permute-start | bytes 786440 | tf_op jit(solution)/shard_map/ppermute | solution.py:338
  17.3 0.0 collective-permute-done.4.refs_0_
  17.3 2.7 %collective-permute-done.5.refs_1_ = bf16[288,512]{1,0:T(8,128)(2,1)S(1)} collective-permute-done((bf16[288,512]{1,0:T(8,128)(2,1)S(1)}, bf16[288,512]{1,0:T(8,128)(2,1)S(1)}, u32[]{:S(2)}, u32[]{:S(2)}) %collective-permute-start.5) | collective-permute-done | bytes 294944 | tf_op jit(solution)/shard_map/ppermute | solution.py:333
  20.0 0.0 collective-permute-done.6.refs_2_
  20.0 0.5 shard_map.109
  20.5 0.1 collective-permute-start.7
  20.6 0.9 %collective-permute-start.8 = (bf16[288,512]{1,0:T(8,128)(2,1)S(1)}, bf16[288,512]{1,0:T(8,128)(2,1)S(1)}, u32[]{:S(2)}, u32[]{:S(2)}) collective-permute-start(bf16[288,512]{1,0:T(8,128)(2,1)S(1)} %get-tuple-element.58), channel_id=1, source_target_pairs={{1,2},{3,4},{5,6},{2,1},{4,3},{6,5},{9,10},{11,12},{13,14},{10,9},... | collective-permute-start | bytes 884744 | tf_op jit(solution)/shard_map/ppermute | solution.py:338
  21.5 1.4 %shard_map.108.part_ref = f32[512,1536]{1,0:T(8,128)S(1)} custom-call(bf16[4,4,64,512]{3,2,1,0:T(8,128)(2,1)S(1)} %get-tuple-element.50.act_ref, bf16[4,4,64,512]{3,2,1,0:T(8,128)(2,1)S(1)} %copy-done), custom_call_target="tpu_custom_call" | custom-call | flops 1207959552 | bytes 5242880 | tf_op jit(solution)/shard_map/pallas_call | solution.py:18
  22.9 2.6 %shard_map.110.middle_ref = bf16[2,256,512]{2,1,0:T(8,128)(2,1)S(1)} custom-call(bf16[4,288,512]{2,1,0:T(8,128)(2,1)S(1)} %get-tuple-element.62.x_ref, bf16[3,3,512,512]{3,2,1,0:T(8,128)(2,1)S(1)} %bitcast.3), custom_call_target="tpu_custom_call" | custom-call | flops 2415919104 | bytes 6422528 | tf_op jit(solution)/shard_map/pallas_call | solution.py:18
  25.5 0.0 collective-permute-done.7.near_ref
  25.5 0.0 collective-permute-done.8.far_ref
  25.5 0.7 %shard_map.111 = (f32[256,1536]{1,0:T(8,128)S(1)}, bf16[256,1536]{1,0:T(8,128)(2,1)S(1)}) custom-call(f32[512,1536]{1,0:T(8,128)S(1)} %shard_map.108.part_ref, bf16[4,64,512]{2,1,0:T(8,128)(2,1)S(1)} %collective-permute-done.2.near_ref, bf16[4,64,512]{2,1,0:T(8,128)(2,1)S(1)} %collective-permute-done.3.far_ref, ...), custom_call_target="tpu_custom_call" | custom-call | flops 402653184 | bytes 8126464 | tf_op jit(solution)/shard_map/pallas_call | solution.py:18
  26.2 3.6 %collective-permute-start.9 = (bf16[256,1536]{1,0:T(8,128)(2,1)S(1)}, bf16[256,1536]{1,0:T(8,128)(2,1)S(1)}, u32[]{:S(2)}, u32[]{:S(2)}) collective-permute-start(bf16[256,1536]{1,0:T(8,128)(2,1)S(1)} %get-tuple-element.61), channel_id=1, source_target_pairs={{0,1},{1,0},{2,3},{3,2},{4,5},{5,4},{6,7},{7,6},{8,9},{9,8},{10,11... | collective-permute-start | bytes 2359304 | tf_op jit(solution)/shard_map/ppermute | solution.py:333
  29.8 2.6 %shard_map.112.border_ref = bf16[2,256,512]{2,1,0:T(8,128)(2,1)S(1)} custom-call(bf16[4,288,512]{2,1,0:T(8,128)(2,1)S(1)} %get-tuple-element.62.x_ref, bf16[288,512]{1,0:T(8,128)(2,1)S(1)} %collective-permute-done.7.near_ref, bf16[288,512]{1,0:T(8,128)(2,1)S(1)} %collective-permute-done.8.far_ref, bf16[3,3,512,512]{3,2,1,0:T(8,128)(2,1)S(1)} %bitcast.3), custom_call_target="tpu_custom_call" | custom-call | flops 2415919104 | bytes 7012352 | tf_op jit(solution)/shard_map/pallas_call | solution.py:18
  32.5 0.0 copy-start.2
  32.5 0.0 copy-start.3
  32.5 0.0 copy-start.7
  32.5 0.0 collective-permute-done.9.got_ref
  32.5 0.3 shard_map.113
  32.8 2.4 %collective-permute-start.10 = (bf16[256,384]{1,0:T(8,128)(2,1)S(1)}, bf16[256,384]{1,0:T(8,128)(2,1)S(1)}, u32[]{:S(2)}, u32[]{:S(2)}) collective-permute-start(bf16[256,384]{1,0:T(8,128)(2,1)S(1)} %get-tuple-element.72), channel_id=1, source_target_pairs={{0,24},{8,16},{16,8},{24,0},{1,25},{9,17},{17,9},{25,1},{2,26},{10... | collective-permute-start | bytes 589832 | tf_op jit(solution)/shard_map/ppermute | solution.py:333
  35.2 2.5 %collective-permute-start.11 = (bf16[256,384]{1,0:T(8,128)(2,1)S(1)}, bf16[256,384]{1,0:T(8,128)(2,1)S(1)}, u32[]{:S(2)}, u32[]{:S(2)}) collective-permute-start(bf16[256,384]{1,0:T(8,128)(2,1)S(1)} %get-tuple-element.73), channel_id=1, source_target_pairs={{0,8},{8,0},{16,24},{24,16},{1,9},{9,1},{17,25},{25,17},{2,10},{10... | collective-permute-start | bytes 589832 | tf_op jit(solution)/shard_map/ppermute | solution.py:333
  37.8 0.0 collective-permute-start.12
  37.8 5.2 %shard_map.114 = (bf16[4,64,512]{2,1,0:T(8,128)(2,1)S(1)}, bf16[4,64,512]{2,1,0:T(8,128)(2,1)S(1)}, bf16[4,64,512]{2,1,0:T(8,128)(2,1)S(1)}, bf16[4,64,512]{2,1,0:T(8,128)(2,1)S(1)}) custom-call(bf16[2,256,512]{2,1,0:T(8,128)(2,1)S(1)} %shard_map.110.middle_ref, bf16[2,256,512]{2,1,0:T(8,128)(2,1)S(1)} %shard_map.112.border_ref, ...), custom_call_target="tpu_custom_call" | custom-call | flops 4831838208 | bytes 6948864 | tf_op jit(solution)/shard_map/pallas_call | solution.py:18
  43.1 1.5 %collective-permute-start.15 = (bf16[4,64,512]{2,1,0:T(8,128)(2,1)S(1)}, bf16[4,64,512]{2,1,0:T(8,128)(2,1)S(1)}, u32[]{:S(2)}, u32[]{:S(2)}) collective-permute-start(bf16[4,64,512]{2,1,0:T(8,128)(2,1)S(1)} %get-tuple-element.78), channel_id=1, source_target_pairs={{0,24},{8,16},{16,8},{24,0},{1,25},{9,17},{17,9},{25,1},{2,26},{10... | collective-permute-start | bytes 786440 | tf_op jit(solution)/shard_map/ppermute | solution.py:333
  44.6 2.0 %collective-permute-start.16 = (bf16[4,64,512]{2,1,0:T(8,128)(2,1)S(1)}, bf16[4,64,512]{2,1,0:T(8,128)(2,1)S(1)}, u32[]{:S(2)}, u32[]{:S(2)}) collective-permute-start(bf16[4,64,512]{2,1,0:T(8,128)(2,1)S(1)} %get-tuple-element.79), channel_id=1, source_target_pairs={{0,8},{8,0},{16,24},{24,16},{1,9},{9,1},{17,25},{25,17},{2,10},{10... | collective-permute-start | bytes 786440 | tf_op jit(solution)/shard_map/ppermute | solution.py:333
  46.6 0.0 collective-permute-start.17
  46.6 0.6 %collective-permute-done.11.refs_1_ = bf16[256,384]{1,0:T(8,128)(2,1)S(1)} collective-permute-done((bf16[256,384]{1,0:T(8,128)(2,1)S(1)}, bf16[256,384]{1,0:T(8,128)(2,1)S(1)}, u32[]{:S(2)}, u32[]{:S(2)}) %collective-permute-start.11) | collective-permute-done | bytes 196640 | tf_op jit(solution)/shard_map/ppermute | solution.py:333
  47.3 0.1 shard_map.115
  47.4 2.9 %collective-permute-start.13 = (bf16[128,384]{1,0:T(8,128)(2,1)S(1)}, bf16[128,384]{1,0:T(8,128)(2,1)S(1)}, u32[]{:S(2)}, u32[]{:S(2)}) collective-permute-start(bf16[128,384]{1,0:T(8,128)(2,1)S(1)} %get-tuple-element.87), channel_id=1, source_target_pairs={{0,2},{1,3},{2,0},{3,1},{4,6},{5,7},{6,4},{7,5},{8,10},{9,11},{10,... | collective-permute-start | bytes 294920 | tf_op jit(solution)/shard_map/ppermute | solution.py:333
  50.3 2.6 %collective-permute-done.13.refs_1_ = bf16[128,384]{1,0:T(8,128)(2,1)S(1)} collective-permute-done((bf16[128,384]{1,0:T(8,128)(2,1)S(1)}, bf16[128,384]{1,0:T(8,128)(2,1)S(1)}, u32[]{:S(2)}, u32[]{:S(2)}) %collective-permute-start.13) | collective-permute-done | bytes 98336 | tf_op jit(solution)/shard_map/ppermute | solution.py:333
  53.0 3.1 %collective-permute-start.14 = (bf16[64,384]{1,0:T(8,128)(2,1)S(1)}, bf16[64,384]{1,0:T(8,128)(2,1)S(1)}, u32[]{:S(2)}, u32[]{:S(2)}) collective-permute-start(bf16[64,384]{1,0:T(8,128)(2,1)S(1)} %get-tuple-element.89), channel_id=1, source_target_pairs={{0,4},{1,5},{2,6},{3,7},{4,0},{5,1},{6,2},{7,3},{8,12},{9,13},{10,... | collective-permute-start | bytes 147464 | tf_op jit(solution)/shard_map/ppermute | solution.py:333
  56.1 2.1 %collective-permute-done.16.refs_1_ = bf16[4,64,512]{2,1,0:T(8,128)(2,1)S(1)} collective-permute-done((bf16[4,64,512]{2,1,0:T(8,128)(2,1)S(1)}, bf16[4,64,512]{2,1,0:T(8,128)(2,1)S(1)}, u32[]{:S(2)}, u32[]{:S(2)}) %collective-permute-start.16) | collective-permute-done | bytes 262176 | tf_op jit(solution)/shard_map/ppermute | solution.py:333
  58.2 1.1 %shard_map.117 = (bf16[4,4,64,512]{3,2,1,0:T(8,128)(2,1)}, f32[3,64,128]{2,1,0:T(8,128)}) custom-call(f32[64,384]{1,0:T(8,128)S(1)} %get-tuple-element.88.kept_ref, bf16[64,384]{1,0:T(8,128)(2,1)S(1)} %collective-permute-done.14.got_ref, bf16[4,64,512]{2,1,0:T(8,128)(2,1)S(1)} %collective-permute-done.15.refs_0_, ...), custom_call_target="tpu_custom_call" | custom-call | bytes 4194304 | tf_op jit(solution)/shard_map/pallas_call | solution.py:380
  (23 shorter events, 0.1 us)
Async XLA Ops:
  0.6 1.2 %copy-start.1 = (bf16[4,4,64,512]{3,2,1,0:T(8,128)(2,1)S(1)}, bf16[4,4,64,512]{3,2,1,0:T(8,128)(2,1)}, u32[]{:S(2)}) copy-start(bf16[4,4,64,512]{3,2,1,0:T(8,128)(2,1)} %x_ref.5) | copy-start | bytes 3145732
  1.9 6.2 %slice-start = ((s8[4718592]{0:T(1024)(128)(4,1)}), s8[4194304]{0:T(1024)(128)(4,1)S(1)}, s32[]{:S(2)}) async-start(s8[4718592]{0:T(1024)(128)(4,1)} %bitcast.2), calls=%async_computation | async-start | bytes 8388608
  2.4 14.9 %collective-permute-start.4 = (bf16[288,512]{1,0:T(8,128)(2,1)S(1)}, bf16[288,512]{1,0:T(8,128)(2,1)S(1)}, u32[]{:S(2)}, u32[]{:S(2)}) collective-permute-start(bf16[288,512]{1,0:T(8,128)(2,1)S(1)} %get-tuple-element.53), channel_id=1, source_target_pairs={{0,24},{8,16},{16,8},{24,0},{1,25},{9,17},{17,9},{25,1},{2,26},{10... | collective-permute-start | bytes 884744 | tf_op jit(solution)/shard_map/ppermute | solution.py:333
  6.4 13.6 %collective-permute-start.5 = (bf16[288,512]{1,0:T(8,128)(2,1)S(1)}, bf16[288,512]{1,0:T(8,128)(2,1)S(1)}, u32[]{:S(2)}, u32[]{:S(2)}) collective-permute-start(bf16[288,512]{1,0:T(8,128)(2,1)S(1)} %get-tuple-element.54), channel_id=1, source_target_pairs={{0,8},{8,0},{16,24},{24,16},{1,9},{9,1},{17,25},{25,17},{2,10},{10... | collective-permute-start | bytes 884744 | tf_op jit(solution)/shard_map/ppermute | solution.py:333
  6.9 13.1 %collective-permute-start.6 = (bf16[288,512]{1,0:T(8,128)(2,1)S(1)}, bf16[288,512]{1,0:T(8,128)(2,1)S(1)}, u32[]{:S(2)}, u32[]{:S(2)}) collective-permute-start(bf16[288,512]{1,0:T(8,128)(2,1)S(1)} %get-tuple-element.55), channel_id=1, source_target_pairs={{0,16},{8,24},{16,0},{24,8},{1,17},{9,25},{17,1},{25,9},{2,18},{10... | collective-permute-start | bytes 884744 | tf_op jit(solution)/shard_map/ppermute | solution.py:333
  7.0 1.0 %slice-start.1 = ((s8[4718592]{0:T(1024)(128)(4,1)}), s8[524288]{0:T(1024)(128)(4,1)S(1)}, s32[]{:S(2)}) async-start(s8[4718592]{0:T(1024)(128)(4,1)} %bitcast.2), calls=%async_computation.1 | async-start | bytes 1048576
  7.1 5.7 %collective-permute-start = (bf16[256,512]{1,0:T(8,128)(2,1)S(1)}, bf16[256,512]{1,0:T(8,128)(2,1)S(1)}, u32[]{:S(2)}, u32[]{:S(2)}) collective-permute-start(bf16[256,512]{1,0:T(8,128)(2,1)S(1)} %get-tuple-element.48), channel_id=1, source_target_pairs={{0,1},{1,0},{2,3},{3,2},{4,5},{5,4},{6,7},{7,6},{8,9},{9,8},{10,11... | collective-permute-start | bytes 786440 | tf_op jit(solution)/shard_map/ppermute | solution.py:333
  7.2 5.7 %copy-start = (bf16[4,4,64,512]{3,2,1,0:T(8,128)(2,1)S(1)}, bf16[4,4,64,512]{3,2,1,0:T(8,128)(2,1)}, u32[]{:S(2)}) copy-start(bf16[4,4,64,512]{3,2,1,0:T(8,128)(2,1)} %cot_ref.5) | copy-start | bytes 3145732
  7.2 5.7 %collective-permute-start.1 = (bf16[256,512]{1,0:T(8,128)(2,1)S(1)}, bf16[256,512]{1,0:T(8,128)(2,1)S(1)}, u32[]{:S(2)}, u32[]{:S(2)}) collective-permute-start(bf16[256,512]{1,0:T(8,128)(2,1)S(1)} %get-tuple-element.49), channel_id=1, source_target_pairs={{1,2},{3,4},{5,6},{2,1},{4,3},{6,5},{9,10},{11,12},{13,14},{10,9},... | collective-permute-start | bytes 786440 | tf_op jit(solution)/shard_map/ppermute | solution.py:338
  14.7 10.8 %collective-permute-start.2 = (bf16[4,64,512]{2,1,0:T(8,128)(2,1)S(1)}, bf16[4,64,512]{2,1,0:T(8,128)(2,1)S(1)}, u32[]{:S(2)}, u32[]{:S(2)}) collective-permute-start(bf16[4,64,512]{2,1,0:T(8,128)(2,1)S(1)} %get-tuple-element.51), channel_id=1, source_target_pairs={{0,8},{8,0},{16,24},{24,16},{1,9},{9,1},{17,25},{25,17},{2,10},{10... | collective-permute-start | bytes 786440 | tf_op jit(solution)/shard_map/ppermute | solution.py:333
  16.6 8.9 %collective-permute-start.3 = (bf16[4,64,512]{2,1,0:T(8,128)(2,1)S(1)}, bf16[4,64,512]{2,1,0:T(8,128)(2,1)S(1)}, u32[]{:S(2)}, u32[]{:S(2)}) collective-permute-start(bf16[4,64,512]{2,1,0:T(8,128)(2,1)S(1)} %get-tuple-element.52), channel_id=1, source_target_pairs={{8,16},{16,8},{9,17},{17,9},{10,18},{18,10},{11,19},{19,11},{12,20... | collective-permute-start | bytes 786440 | tf_op jit(solution)/shard_map/ppermute | solution.py:338
  20.5 5.0 %collective-permute-start.7 = (bf16[288,512]{1,0:T(8,128)(2,1)S(1)}, bf16[288,512]{1,0:T(8,128)(2,1)S(1)}, u32[]{:S(2)}, u32[]{:S(2)}) collective-permute-start(bf16[288,512]{1,0:T(8,128)(2,1)S(1)} %get-tuple-element.57), channel_id=1, source_target_pairs={{0,1},{1,0},{2,3},{3,2},{4,5},{5,4},{6,7},{7,6},{8,9},{9,8},{10,11... | collective-permute-start | bytes 884744 | tf_op jit(solution)/shard_map/ppermute | solution.py:333
  20.6 4.9 %collective-permute-start.8 = (bf16[288,512]{1,0:T(8,128)(2,1)S(1)}, bf16[288,512]{1,0:T(8,128)(2,1)S(1)}, u32[]{:S(2)}, u32[]{:S(2)}) collective-permute-start(bf16[288,512]{1,0:T(8,128)(2,1)S(1)} %get-tuple-element.58), channel_id=1, source_target_pairs={{1,2},{3,4},{5,6},{2,1},{4,3},{6,5},{9,10},{11,12},{13,14},{10,9},... | collective-permute-start | bytes 884744 | tf_op jit(solution)/shard_map/ppermute | solution.py:338
  26.2 6.3 %collective-permute-start.9 = (bf16[256,1536]{1,0:T(8,128)(2,1)S(1)}, bf16[256,1536]{1,0:T(8,128)(2,1)S(1)}, u32[]{:S(2)}, u32[]{:S(2)}) collective-permute-start(bf16[256,1536]{1,0:T(8,128)(2,1)S(1)} %get-tuple-element.61), channel_id=1, source_target_pairs={{0,1},{1,0},{2,3},{3,2},{4,5},{5,4},{6,7},{7,6},{8,9},{9,8},{10,11... | collective-permute-start | bytes 2359304 | tf_op jit(solution)/shard_map/ppermute | solution.py:333
  29.8 8.0 %copy-start.4 = (bf16[512,512]{1,0:T(8,128)(2,1)S(1)}, bf16[512,512]{1,0:T(8,128)(2,1)}, u32[]{:S(2)}) copy-start(bf16[512,512]{1,0:T(8,128)(2,1)} %k_ref.1) | copy-start | bytes 1572868
  29.8 8.0 %copy-start.5 = (bf16[512,512]{1,0:T(8,128)(2,1)S(1)}, bf16[512,512]{1,0:T(8,128)(2,1)}, u32[]{:S(2)}) copy-start(bf16[512,512]{1,0:T(8,128)(2,1)} %v_ref.1) | copy-start | bytes 1572868
  29.8 8.0 %copy-start.6 = (bf16[512,512]{1,0:T(8,128)(2,1)S(1)}, bf16[512,512]{1,0:T(8,128)(2,1)}, u32[]{:S(2)}) copy-start(bf16[512,512]{1,0:T(8,128)(2,1)} %o_ref.1) | copy-start | bytes 1572868
  32.5 5.4 %copy-start.2 = (bf16[3,512,512]{2,1,0:T(8,128)(2,1)S(1)}, bf16[3,512,512]{2,1,0:T(8,128)(2,1)}, u32[]{:S(2)}) copy-start(bf16[3,512,512]{2,1,0:T(8,128)(2,1)} %t_ref.1) | copy-start | bytes 4718596
  32.5 5.4 %copy-start.3 = (bf16[512,512]{1,0:T(8,128)(2,1)S(1)}, bf16[512,512]{1,0:T(8,128)(2,1)}, u32[]{:S(2)}) copy-start(bf16[512,512]{1,0:T(8,128)(2,1)} %q_ref.1) | copy-start | bytes 1572868
  32.5 5.4 %copy-start.7 = (f32[512]{0:T(512)S(1)}, f32[512]{0:T(512)}, u32[]{:S(2)}) copy-start(f32[512]{0:T(512)} %param.12) | copy-start | bytes 6148
  32.8 13.8 %collective-permute-start.10 = (bf16[256,384]{1,0:T(8,128)(2,1)S(1)}, bf16[256,384]{1,0:T(8,128)(2,1)S(1)}, u32[]{:S(2)}, u32[]{:S(2)}) collective-permute-start(bf16[256,384]{1,0:T(8,128)(2,1)S(1)} %get-tuple-element.72), channel_id=1, source_target_pairs={{0,24},{8,16},{16,8},{24,0},{1,25},{9,17},{17,9},{25,1},{2,26},{10... | collective-permute-start | bytes 589832 | tf_op jit(solution)/shard_map/ppermute | solution.py:333
  35.2 12.0 %collective-permute-start.11 = (bf16[256,384]{1,0:T(8,128)(2,1)S(1)}, bf16[256,384]{1,0:T(8,128)(2,1)S(1)}, u32[]{:S(2)}, u32[]{:S(2)}) collective-permute-start(bf16[256,384]{1,0:T(8,128)(2,1)S(1)} %get-tuple-element.73), channel_id=1, source_target_pairs={{0,8},{8,0},{16,24},{24,16},{1,9},{9,1},{17,25},{25,17},{2,10},{10... | collective-permute-start | bytes 589832 | tf_op jit(solution)/shard_map/ppermute | solution.py:333
  37.8 9.5 %collective-permute-start.12 = (bf16[256,384]{1,0:T(8,128)(2,1)S(1)}, bf16[256,384]{1,0:T(8,128)(2,1)S(1)}, u32[]{:S(2)}, u32[]{:S(2)}) collective-permute-start(bf16[256,384]{1,0:T(8,128)(2,1)S(1)} %get-tuple-element.74), channel_id=1, source_target_pairs={{0,16},{8,24},{16,0},{24,8},{1,17},{9,25},{17,1},{25,9},{2,18},{10... | collective-permute-start | bytes 589832 | tf_op jit(solution)/shard_map/ppermute | solution.py:333
  43.1 13.0 %collective-permute-start.15 = (bf16[4,64,512]{2,1,0:T(8,128)(2,1)S(1)}, bf16[4,64,512]{2,1,0:T(8,128)(2,1)S(1)}, u32[]{:S(2)}, u32[]{:S(2)}) collective-permute-start(bf16[4,64,512]{2,1,0:T(8,128)(2,1)S(1)} %get-tuple-element.78), channel_id=1, source_target_pairs={{0,24},{8,16},{16,8},{24,0},{1,25},{9,17},{17,9},{25,1},{2,26},{10... | collective-permute-start | bytes 786440 | tf_op jit(solution)/shard_map/ppermute | solution.py:333
  44.6 13.6 %collective-permute-start.16 = (bf16[4,64,512]{2,1,0:T(8,128)(2,1)S(1)}, bf16[4,64,512]{2,1,0:T(8,128)(2,1)S(1)}, u32[]{:S(2)}, u32[]{:S(2)}) collective-permute-start(bf16[4,64,512]{2,1,0:T(8,128)(2,1)S(1)} %get-tuple-element.79), channel_id=1, source_target_pairs={{0,8},{8,0},{16,24},{24,16},{1,9},{9,1},{17,25},{25,17},{2,10},{10... | collective-permute-start | bytes 786440 | tf_op jit(solution)/shard_map/ppermute | solution.py:333
  46.6 11.5 %collective-permute-start.17 = (bf16[4,64,512]{2,1,0:T(8,128)(2,1)S(1)}, bf16[4,64,512]{2,1,0:T(8,128)(2,1)S(1)}, u32[]{:S(2)}, u32[]{:S(2)}) collective-permute-start(bf16[4,64,512]{2,1,0:T(8,128)(2,1)S(1)} %get-tuple-element.80), channel_id=1, source_target_pairs={{0,16},{8,24},{16,0},{24,8},{1,17},{9,25},{17,1},{25,9},{2,18},{10... | collective-permute-start | bytes 786440 | tf_op jit(solution)/shard_map/ppermute | solution.py:333
  47.4 5.5 %collective-permute-start.13 = (bf16[128,384]{1,0:T(8,128)(2,1)S(1)}, bf16[128,384]{1,0:T(8,128)(2,1)S(1)}, u32[]{:S(2)}, u32[]{:S(2)}) collective-permute-start(bf16[128,384]{1,0:T(8,128)(2,1)S(1)} %get-tuple-element.87), channel_id=1, source_target_pairs={{0,2},{1,3},{2,0},{3,1},{4,6},{5,7},{6,4},{7,5},{8,10},{9,11},{10,... | collective-permute-start | bytes 294920 | tf_op jit(solution)/shard_map/ppermute | solution.py:333
  53.0 5.2 %collective-permute-start.14 = (bf16[64,384]{1,0:T(8,128)(2,1)S(1)}, bf16[64,384]{1,0:T(8,128)(2,1)S(1)}, u32[]{:S(2)}, u32[]{:S(2)}) collective-permute-start(bf16[64,384]{1,0:T(8,128)(2,1)S(1)} %get-tuple-element.89), channel_id=1, source_target_pairs={{0,4},{1,5},{2,6},{3,7},{4,0},{5,1},{6,2},{7,3},{8,12},{9,13},{10,... | collective-permute-start | bytes 147464 | tf_op jit(solution)/shard_map/ppermute | solution.py:333

commit v17 on v14

--- a/solution.py
+++ b/solution.py
@@ -115,7 +115,7 @@
         out[r] = taps(pieces, w_ref[low:high])
 
 
-def own_act_kernel(z, part_ref, near_ref, far_ref, w_ref, cot_ref, out, near, far):
+def own_act_kernel(z, part_ref, near_ref, far_ref, w_ref, cot_ref, out, far, near):
     lower = even("space")
     first = even("tm")
     for r in range(z.r):
@@ -150,7 +150,7 @@
         out[:, k * z.c : (k + 1) * z.c] = outer(cot_ref[k:], act_ref[: z.fl - k])
 
 
-def cross_kernel(z, width, part_ref, near_ref, far_ref, act_ref, cot_ref, keep, send):
+def cross_kernel(z, width, part_ref, far_ref, near_ref, act_ref, cot_ref, keep, send):
     mine = even("space")
     before = jnp.where(even("tm"), far_ref[...], near_ref[...])
     after = jnp.where(even("tm"), near_ref[...], far_ref[...])
@@ -432,7 +432,7 @@
         flops=8 * one,
         scratch=[pltpu.VMEM((3, z.r, z.fl * z.w, z.c), BF)],
     )
-    own_act, near, far = call(
+    own_act, far, near = call(
         functools.partial(own_act_kernel, z),
         [shape(frames_in.shape), shape((z.r, z.w, z.c)), shape((z.r, z.w, z.c))],
         own,
@@ -464,14 +464,14 @@
         spatial,
         flops=9 * one * (z.r - 2) // z.r,
     )
-    tied = lax.optimization_barrier((near, far, middle, close, apart))
-    near, far, middle, close, apart = tied
+    tied = lax.optimization_barrier((far, near, middle, close, apart))
+    far, near, middle, close, apart = tied
     keep, send = call(
         functools.partial(cross_kernel, z, width),
         [shape((z.c // 2, 3 * z.c), F32), shape((z.c // 2, 3 * z.c))],
         own_grad,
+        far,
         near,
-        far,
         own_act,
         cotangent,
         flops=3 * one // 4,

time: 60.5 us -> 62.5 us (1.033); the launches traced: 59.4 us -> 62.3 us
  starting transfers between devices: 27.3 us -> 30.2 us
    ppermute x15, starting transfers between devices: 25 us -> 27.9 us  [swap(): return lax.ppermute(value, axis, [(i, i ^ k) for i in range(count)])]
  transfers between devices with their start and end apart: 18 -> 18, of which waited for: 4 -> 5; matrix products, arithmetic and copies ran while one was open for 0% -> 0% of each run, Pallas kernels for 33% -> 31%
where the time goes in v17:
time: 62.5 us; the launch traced here: 62.3 us
  starting transfers between devices  30.2 us (48%)
  Pallas kernels  21.9 us (35%)
  waiting for transfers between devices  7.83 us (13%)
  local copies, waits for them, and re-layouts  1.32 us (2%)
  between operations  1.03 us (2%)
    ppermute x15, starting transfers between devices, swap(): return lax.ppermute(value, axis, [(i, i ^ k) for i in range(count)])  27.9 us
    pallas_call x13, Pallas kernels, call(): pl.pallas_call(kernel, out_shape=tuple(outs), in_specs=[VMEM] * len(args)...  20.9 us
    ppermute x15, waiting for transfers between devices, swap(): return lax.ppermute(value, axis, [(i, i ^ k) for i in range(count)])  7.82 us
    ppermute x3, starting transfers between devices, swap_both(): far = lax.ppermute(far, axis, pairs + [(b, a) for a, b in pairs])  2.33 us
    unnamed x20, local copies, waits for them, and re-layouts  1.32 us
  transfers between devices with their start and end apart: 18, of which 5 were waited for; matrix products, arithmetic and copies ran while one was open for 0% of the time, Pallas kernels for 31%

profile of v17, /device:TPU:0, one launch (start us, length us, event | category | flops | bytes accessed | tf_op | source)
XLA Modules:
  0.0 62.3 jit_solution(2436033570729711094)
XLA Ops:
  0.6 1.2 %copy-done.1 = bf16[4,4,64,512]{3,2,1,0:T(8,128)(2,1)S(1)} copy-done((bf16[4,4,64,512]{3,2,1,0:T(8,128)(2,1)S(1)}, bf16[4,4,64,512]{3,2,1,0:T(8,128)(2,1)}, u32[]{:S(2)}) %copy-start.1) | copy-done | bytes 1048600
  1.9 0.6 shard_map.105
  2.4 4.0 %collective-permute-start.4 = (bf16[288,512]{1,0:T(8,128)(2,1)S(1)}, bf16[288,512]{1,0:T(8,128)(2,1)S(1)}, u32[]{:S(2)}, u32[]{:S(2)}) collective-permute-start(bf16[288,512]{1,0:T(8,128)(2,1)S(1)} %get-tuple-element.53), channel_id=1, source_target_pairs={{0,24},{8,16},{16,8},{24,0},{1,25},{9,17},{17,9},{25,1},{2,26},{10... | collective-permute-start | bytes 884744 | tf_op jit(solution)/shard_map/ppermute | solution.py:332
  6.4 0.5 collective-permute-start.5
  6.9 0.1 collective-permute-start.6
  7.0 0.1 shard_map.106
  7.1 0.1 collective-permute-start
  7.2 0.0 copy-start
  7.2 0.8 %collective-permute-start.1 = (bf16[256,512]{1,0:T(8,128)(2,1)S(1)}, bf16[256,512]{1,0:T(8,128)(2,1)S(1)}, u32[]{:S(2)}, u32[]{:S(2)}) collective-permute-start(bf16[256,512]{1,0:T(8,128)(2,1)S(1)} %get-tuple-element.49), channel_id=1, source_target_pairs={{1,2},{3,4},{5,6},{2,1},{4,3},{6,5},{9,10},{11,12},{13,14},{10,9},... | collective-permute-start | bytes 786440 | tf_op jit(solution)/shard_map/ppermute | solution.py:337
  8.0 0.1 slice-done.1
  8.1 4.8 %shard_map.104.part_ref = f32[4,256,512]{2,1,0:T(8,128)S(1)} custom-call(bf16[4,4,64,512]{3,2,1,0:T(8,128)(2,1)S(1)} %copy-done.1, bf16[3,3,512,512]{3,2,1,0:T(8,128)(2,1)S(1)} %bitcast.3), custom_call_target="tpu_custom_call" | custom-call | flops 4294967296 | bytes 7864320 | tf_op jit(solution)/shard_map/pallas_call | solution.py:18
  12.8 0.0 collective-permute-done.near_ref
  12.9 1.9 %shard_map.107 = (bf16[4,4,64,512]{3,2,1,0:T(8,128)(2,1)S(1)}, bf16[4,64,512]{2,1,0:T(8,128)(2,1)S(1)}, bf16[4,64,512]{2,1,0:T(8,128)(2,1)S(1)}) custom-call(f32[4,256,512]{2,1,0:T(8,128)S(1)} %shard_map.104.part_ref, bf16[256,512]{1,0:T(8,128)(2,1)S(1)} %collective-permute-done.near_ref, bf16[256,512]{1,0:T(8,128)(2,1)S(1)} %collective-permute-done.1.far_ref, ...), custom_call_target="tpu_custom_call" | custom-call | flops 1610612736 | bytes 9961472 | tf_op jit(solution)/shard_map/pallas_call | solution.py:18
  14.8 0.7 %collective-permute-start.2 = (bf16[4,64,512]{2,1,0:T(8,128)(2,1)S(1)}, bf16[4,64,512]{2,1,0:T(8,128)(2,1)S(1)}, u32[]{:S(2)}, u32[]{:S(2)}) collective-permute-start(bf16[4,64,512]{2,1,0:T(8,128)(2,1)S(1)} %get-tuple-element.51), channel_id=1, source_target_pairs={{8,16},{16,8},{9,17},{17,9},{10,18},{18,10},{11,19},{19,11},{12,20... | collective-permute-start | bytes 786440 | tf_op jit(solution)/shard_map/ppermute | solution.py:337
  15.4 4.7 %collective-permute-start.3 = (bf16[4,64,512]{2,1,0:T(8,128)(2,1)S(1)}, bf16[4,64,512]{2,1,0:T(8,128)(2,1)S(1)}, u32[]{:S(2)}, u32[]{:S(2)}) collective-permute-start(bf16[4,64,512]{2,1,0:T(8,128)(2,1)S(1)} %get-tuple-element.52), channel_id=1, source_target_pairs={{0,8},{8,0},{16,24},{24,16},{1,9},{9,1},{17,25},{25,17},{2,10},{10... | collective-permute-start | bytes 786440 | tf_op jit(solution)/shard_map/ppermute | solution.py:332
  20.1 0.0 collective-permute-done.5.refs_1_
  20.1 0.0 collective-permute-done.6.refs_2_
  20.1 0.5 shard_map.109
  20.6 2.4 %collective-permute-start.7 = (bf16[288,512]{1,0:T(8,128)(2,1)S(1)}, bf16[288,512]{1,0:T(8,128)(2,1)S(1)}, u32[]{:S(2)}, u32[]{:S(2)}) collective-permute-start(bf16[288,512]{1,0:T(8,128)(2,1)S(1)} %get-tuple-element.57), channel_id=1, source_target_pairs={{0,1},{1,0},{2,3},{3,2},{4,5},{5,4},{6,7},{7,6},{8,9},{9,8},{10,11... | collective-permute-start | bytes 884744 | tf_op jit(solution)/shard_map/ppermute | solution.py:332
  23.0 0.8 %collective-permute-start.8 = (bf16[288,512]{1,0:T(8,128)(2,1)S(1)}, bf16[288,512]{1,0:T(8,128)(2,1)S(1)}, u32[]{:S(2)}, u32[]{:S(2)}) collective-permute-start(bf16[288,512]{1,0:T(8,128)(2,1)S(1)} %get-tuple-element.58), channel_id=1, source_target_pairs={{1,2},{3,4},{5,6},{2,1},{4,3},{6,5},{9,10},{11,12},{13,14},{10,9},... | collective-permute-start | bytes 884744 | tf_op jit(solution)/shard_map/ppermute | solution.py:337
  23.9 1.4 %shard_map.108.part_ref = f32[512,1536]{1,0:T(8,128)S(1)} custom-call(bf16[4,4,64,512]{3,2,1,0:T(8,128)(2,1)S(1)} %get-tuple-element.50.act_ref, bf16[4,4,64,512]{3,2,1,0:T(8,128)(2,1)S(1)} %copy-done), custom_call_target="tpu_custom_call" | custom-call | flops 1207959552 | bytes 5242880 | tf_op jit(solution)/shard_map/pallas_call | solution.py:18
  25.3 2.7 %shard_map.110.middle_ref = bf16[2,256,512]{2,1,0:T(8,128)(2,1)S(1)} custom-call(bf16[4,288,512]{2,1,0:T(8,128)(2,1)S(1)} %get-tuple-element.62.x_ref, bf16[3,3,512,512]{3,2,1,0:T(8,128)(2,1)S(1)} %bitcast.3), custom_call_target="tpu_custom_call" | custom-call | flops 2415919104 | bytes 6422528 | tf_op jit(solution)/shard_map/pallas_call | solution.py:18
  28.0 2.8 %collective-permute-done.3.near_ref = bf16[4,64,512]{2,1,0:T(8,128)(2,1)S(1)} collective-permute-done((bf16[4,64,512]{2,1,0:T(8,128)(2,1)S(1)}, bf16[4,64,512]{2,1,0:T(8,128)(2,1)S(1)}, u32[]{:S(2)}, u32[]{:S(2)}) %collective-permute-start.3) | collective-permute-done | bytes 262176 | tf_op jit(solution)/shard_map/ppermute | solution.py:332
  30.8 0.0 collective-permute-done.7.near_ref
  30.8 0.7 %shard_map.111 = (f32[256,1536]{1,0:T(8,128)S(1)}, bf16[256,1536]{1,0:T(8,128)(2,1)S(1)}) custom-call(f32[512,1536]{1,0:T(8,128)S(1)} %shard_map.108.part_ref, bf16[4,64,512]{2,1,0:T(8,128)(2,1)S(1)} %collective-permute-done.2.far_ref, bf16[4,64,512]{2,1,0:T(8,128)(2,1)S(1)} %collective-permute-done.3.near_ref, ...), custom_call_target="tpu_custom_call" | custom-call | flops 402653184 | bytes 8126464 | tf_op jit(solution)/shard_map/pallas_call | solution.py:18
  31.5 1.9 %collective-permute-start.9 = (bf16[256,1536]{1,0:T(8,128)(2,1)S(1)}, bf16[256,1536]{1,0:T(8,128)(2,1)S(1)}, u32[]{:S(2)}, u32[]{:S(2)}) collective-permute-start(bf16[256,1536]{1,0:T(8,128)(2,1)S(1)} %get-tuple-element.61), channel_id=1, source_target_pairs={{0,1},{1,0},{2,3},{3,2},{4,5},{5,4},{6,7},{7,6},{8,9},{9,8},{10,11... | collective-permute-start | bytes 2359304 | tf_op jit(solution)/shard_map/ppermute | solution.py:332
  33.4 2.7 %shard_map.112.border_ref = bf16[2,256,512]{2,1,0:T(8,128)(2,1)S(1)} custom-call(bf16[4,288,512]{2,1,0:T(8,128)(2,1)S(1)} %get-tuple-element.62.x_ref, bf16[288,512]{1,0:T(8,128)(2,1)S(1)} %collective-permute-done.7.near_ref, bf16[288,512]{1,0:T(8,128)(2,1)S(1)} %collective-permute-done.8.far_ref, bf16[3,3,512,512]{3,2,1,0:T(8,128)(2,1)S(1)} %bitcast.3), custom_call_target="tpu_custom_call" | custom-call | flops 2415919104 | bytes 7012352 | tf_op jit(solution)/shard_map/pallas_call | solution.py:18
  36.0 0.0 copy-start.2
  36.1 0.0 copy-start.3
  36.1 0.0 copy-start.7
  36.1 0.3 shard_map.113
  36.4 1.5 %collective-permute-start.10 = (bf16[256,384]{1,0:T(8,128)(2,1)S(1)}, bf16[256,384]{1,0:T(8,128)(2,1)S(1)}, u32[]{:S(2)}, u32[]{:S(2)}) collective-permute-start(bf16[256,384]{1,0:T(8,128)(2,1)S(1)} %get-tuple-element.72), channel_id=1, source_target_pairs={{0,24},{8,16},{16,8},{24,0},{1,25},{9,17},{17,9},{25,1},{2,26},{10... | collective-permute-start | bytes 589832 | tf_op jit(solution)/shard_map/ppermute | solution.py:332
  37.9 2.0 %collective-permute-start.12 = (bf16[256,384]{1,0:T(8,128)(2,1)S(1)}, bf16[256,384]{1,0:T(8,128)(2,1)S(1)}, u32[]{:S(2)}, u32[]{:S(2)}) collective-permute-start(bf16[256,384]{1,0:T(8,128)(2,1)S(1)} %get-tuple-element.74), channel_id=1, source_target_pairs={{0,16},{8,24},{16,0},{24,8},{1,17},{9,25},{17,1},{25,9},{2,18},{10... | collective-permute-start | bytes 589832 | tf_op jit(solution)/shard_map/ppermute | solution.py:332
  40.0 5.3 %shard_map.114 = (bf16[4,64,512]{2,1,0:T(8,128)(2,1)S(1)}, bf16[4,64,512]{2,1,0:T(8,128)(2,1)S(1)}, bf16[4,64,512]{2,1,0:T(8,128)(2,1)S(1)}, bf16[4,64,512]{2,1,0:T(8,128)(2,1)S(1)}) custom-call(bf16[2,256,512]{2,1,0:T(8,128)(2,1)S(1)} %shard_map.110.middle_ref, bf16[2,256,512]{2,1,0:T(8,128)(2,1)S(1)} %shard_map.112.border_ref, ...), custom_call_target="tpu_custom_call" | custom-call | flops 4831838208 | bytes 6948864 | tf_op jit(solution)/shard_map/pallas_call | solution.py:18
  45.3 1.5 %collective-permute-start.15 = (bf16[4,64,512]{2,1,0:T(8,128)(2,1)S(1)}, bf16[4,64,512]{2,1,0:T(8,128)(2,1)S(1)}, u32[]{:S(2)}, u32[]{:S(2)}) collective-permute-start(bf16[4,64,512]{2,1,0:T(8,128)(2,1)S(1)} %get-tuple-element.78), channel_id=1, source_target_pairs={{0,24},{8,16},{16,8},{24,0},{1,25},{9,17},{17,9},{25,1},{2,26},{10... | collective-permute-start | bytes 786440 | tf_op jit(solution)/shard_map/ppermute | solution.py:332
  46.8 0.0 collective-permute-start.16
  46.8 0.0 collective-permute-done.10.refs_0_
  46.8 2.0 %collective-permute-start.17 = (bf16[4,64,512]{2,1,0:T(8,128)(2,1)S(1)}, bf16[4,64,512]{2,1,0:T(8,128)(2,1)S(1)}, u32[]{:S(2)}, u32[]{:S(2)}) collective-permute-start(bf16[4,64,512]{2,1,0:T(8,128)(2,1)S(1)} %get-tuple-element.80), channel_id=1, source_target_pairs={{0,16},{8,24},{16,0},{24,8},{1,17},{9,25},{17,1},{25,9},{2,18},{10... | collective-permute-start | bytes 786440 | tf_op jit(solution)/shard_map/ppermute | solution.py:332
  48.9 0.1 collective-permute-done.12.refs_2_
  48.9 0.1 shard_map.115
  49.0 4.2 %collective-permute-start.13 = (bf16[128,384]{1,0:T(8,128)(2,1)S(1)}, bf16[128,384]{1,0:T(8,128)(2,1)S(1)}, u32[]{:S(2)}, u32[]{:S(2)}) collective-permute-start(bf16[128,384]{1,0:T(8,128)(2,1)S(1)} %get-tuple-element.87), channel_id=1, source_target_pairs={{0,2},{1,3},{2,0},{3,1},{4,6},{5,7},{6,4},{7,5},{8,10},{9,11},{10,... | collective-permute-start | bytes 294920 | tf_op jit(solution)/shard_map/ppermute | solution.py:332
  53.2 2.8 %collective-permute-done.13.refs_1_ = bf16[128,384]{1,0:T(8,128)(2,1)S(1)} collective-permute-done((bf16[128,384]{1,0:T(8,128)(2,1)S(1)}, bf16[128,384]{1,0:T(8,128)(2,1)S(1)}, u32[]{:S(2)}, u32[]{:S(2)}) %collective-permute-start.13) | collective-permute-done | bytes 98336 | tf_op jit(solution)/shard_map/ppermute | solution.py:332
  56.0 2.9 %collective-permute-start.14 = (bf16[64,384]{1,0:T(8,128)(2,1)S(1)}, bf16[64,384]{1,0:T(8,128)(2,1)S(1)}, u32[]{:S(2)}, u32[]{:S(2)}) collective-permute-start(bf16[64,384]{1,0:T(8,128)(2,1)S(1)} %get-tuple-element.89), channel_id=1, source_target_pairs={{0,4},{1,5},{2,6},{3,7},{4,0},{5,1},{6,2},{7,3},{8,12},{9,13},{10,... | collective-permute-start | bytes 147464 | tf_op jit(solution)/shard_map/ppermute | solution.py:332
  58.9 0.0 collective-permute-done.15.refs_0_
  58.9 0.0 collective-permute-done.16.refs_1_
  59.0 0.7 %collective-permute-done.17.refs_2_ = bf16[4,64,512]{2,1,0:T(8,128)(2,1)S(1)} collective-permute-done((bf16[4,64,512]{2,1,0:T(8,128)(2,1)S(1)}, bf16[4,64,512]{2,1,0:T(8,128)(2,1)S(1)}, u32[]{:S(2)}, u32[]{:S(2)}) %collective-permute-start.17) | collective-permute-done | bytes 262176 | tf_op jit(solution)/shard_map/ppermute | solution.py:332
  59.7 1.4 %collective-permute-done.14.got_ref = bf16[64,384]{1,0:T(8,128)(2,1)S(1)} collective-permute-done((bf16[64,384]{1,0:T(8,128)(2,1)S(1)}, bf16[64,384]{1,0:T(8,128)(2,1)S(1)}, u32[]{:S(2)}, u32[]{:S(2)}) %collective-permute-start.14) | collective-permute-done | bytes 49184 | tf_op jit(solution)/shard_map/ppermute | solution.py:332
  61.1 1.1 %shard_map.117 = (bf16[4,4,64,512]{3,2,1,0:T(8,128)(2,1)}, f32[3,64,128]{2,1,0:T(8,128)}) custom-call(f32[64,384]{1,0:T(8,128)S(1)} %get-tuple-element.88.kept_ref, bf16[64,384]{1,0:T(8,128)(2,1)S(1)} %collective-permute-done.14.got_ref, bf16[4,64,512]{2,1,0:T(8,128)(2,1)S(1)} %collective-permute-done.15.refs_0_, ...), custom_call_target="tpu_custom_call" | custom-call | bytes 4194304 | tf_op jit(solution)/shard_map/pallas_call | solution.py:379
  (23 shorter events, 0.1 us)
Async XLA Ops:
  0.6 1.2 %copy-start.1 = (bf16[4,4,64,512]{3,2,1,0:T(8,128)(2,1)S(1)}, bf16[4,4,64,512]{3,2,1,0:T(8,128)(2,1)}, u32[]{:S(2)}) copy-start(bf16[4,4,64,512]{3,2,1,0:T(8,128)(2,1)} %x_ref.5) | copy-start | bytes 3145732
  1.9 6.2 %slice-start = ((s8[4718592]{0:T(1024)(128)(4,1)}), s8[4194304]{0:T(1024)(128)(4,1)S(1)}, s32[]{:S(2)}) async-start(s8[4718592]{0:T(1024)(128)(4,1)} %bitcast.2), calls=%async_computation | async-start | bytes 8388608
  2.4 17.7 %collective-permute-start.4 = (bf16[288,512]{1,0:T(8,128)(2,1)S(1)}, bf16[288,512]{1,0:T(8,128)(2,1)S(1)}, u32[]{:S(2)}, u32[]{:S(2)}) collective-permute-start(bf16[288,512]{1,0:T(8,128)(2,1)S(1)} %get-tuple-element.53), channel_id=1, source_target_pairs={{0,24},{8,16},{16,8},{24,0},{1,25},{9,17},{17,9},{25,1},{2,26},{10... | collective-permute-start | bytes 884744 | tf_op jit(solution)/shard_map/ppermute | solution.py:332
  6.4 13.7 %collective-permute-start.5 = (bf16[288,512]{1,0:T(8,128)(2,1)S(1)}, bf16[288,512]{1,0:T(8,128)(2,1)S(1)}, u32[]{:S(2)}, u32[]{:S(2)}) collective-permute-start(bf16[288,512]{1,0:T(8,128)(2,1)S(1)} %get-tuple-element.54), channel_id=1, source_target_pairs={{0,8},{8,0},{16,24},{24,16},{1,9},{9,1},{17,25},{25,17},{2,10},{10... | collective-permute-start | bytes 884744 | tf_op jit(solution)/shard_map/ppermute | solution.py:332
  6.9 13.2 %collective-permute-start.6 = (bf16[288,512]{1,0:T(8,128)(2,1)S(1)}, bf16[288,512]{1,0:T(8,128)(2,1)S(1)}, u32[]{:S(2)}, u32[]{:S(2)}) collective-permute-start(bf16[288,512]{1,0:T(8,128)(2,1)S(1)} %get-tuple-element.55), channel_id=1, source_target_pairs={{0,16},{8,24},{16,0},{24,8},{1,17},{9,25},{17,1},{25,9},{2,18},{10... | collective-permute-start | bytes 884744 | tf_op jit(solution)/shard_map/ppermute | solution.py:332
  7.0 1.0 %slice-start.1 = ((s8[4718592]{0:T(1024)(128)(4,1)}), s8[524288]{0:T(1024)(128)(4,1)S(1)}, s32[]{:S(2)}) async-start(s8[4718592]{0:T(1024)(128)(4,1)} %bitcast.2), calls=%async_computation.1 | async-start | bytes 1048576
  7.1 5.7 %collective-permute-start = (bf16[256,512]{1,0:T(8,128)(2,1)S(1)}, bf16[256,512]{1,0:T(8,128)(2,1)S(1)}, u32[]{:S(2)}, u32[]{:S(2)}) collective-permute-start(bf16[256,512]{1,0:T(8,128)(2,1)S(1)} %get-tuple-element.48), channel_id=1, source_target_pairs={{0,1},{1,0},{2,3},{3,2},{4,5},{5,4},{6,7},{7,6},{8,9},{9,8},{10,11... | collective-permute-start | bytes 786440 | tf_op jit(solution)/shard_map/ppermute | solution.py:332
  7.2 5.7 %copy-start = (bf16[4,4,64,512]{3,2,1,0:T(8,128)(2,1)S(1)}, bf16[4,4,64,512]{3,2,1,0:T(8,128)(2,1)}, u32[]{:S(2)}) copy-start(bf16[4,4,64,512]{3,2,1,0:T(8,128)(2,1)} %cot_ref.5) | copy-start | bytes 3145732
  7.2 5.7 %collective-permute-start.1 = (bf16[256,512]{1,0:T(8,128)(2,1)S(1)}, bf16[256,512]{1,0:T(8,128)(2,1)S(1)}, u32[]{:S(2)}, u32[]{:S(2)}) collective-permute-start(bf16[256,512]{1,0:T(8,128)(2,1)S(1)} %get-tuple-element.49), channel_id=1, source_target_pairs={{1,2},{3,4},{5,6},{2,1},{4,3},{6,5},{9,10},{11,12},{13,14},{10,9},... | collective-permute-start | bytes 786440 | tf_op jit(solution)/shard_map/ppermute | solution.py:337
  14.8 13.2 %collective-permute-start.2 = (bf16[4,64,512]{2,1,0:T(8,128)(2,1)S(1)}, bf16[4,64,512]{2,1,0:T(8,128)(2,1)S(1)}, u32[]{:S(2)}, u32[]{:S(2)}) collective-permute-start(bf16[4,64,512]{2,1,0:T(8,128)(2,1)S(1)} %get-tuple-element.51), channel_id=1, source_target_pairs={{8,16},{16,8},{9,17},{17,9},{10,18},{18,10},{11,19},{19,11},{12,20... | collective-permute-start | bytes 786440 | tf_op jit(solution)/shard_map/ppermute | solution.py:337
  15.4 15.4 %collective-permute-start.3 = (bf16[4,64,512]{2,1,0:T(8,128)(2,1)S(1)}, bf16[4,64,512]{2,1,0:T(8,128)(2,1)S(1)}, u32[]{:S(2)}, u32[]{:S(2)}) collective-permute-start(bf16[4,64,512]{2,1,0:T(8,128)(2,1)S(1)} %get-tuple-element.52), channel_id=1, source_target_pairs={{0,8},{8,0},{16,24},{24,16},{1,9},{9,1},{17,25},{25,17},{2,10},{10... | collective-permute-start | bytes 786440 | tf_op jit(solution)/shard_map/ppermute | solution.py:332
  20.6 10.2 %collective-permute-start.7 = (bf16[288,512]{1,0:T(8,128)(2,1)S(1)}, bf16[288,512]{1,0:T(8,128)(2,1)S(1)}, u32[]{:S(2)}, u32[]{:S(2)}) collective-permute-start(bf16[288,512]{1,0:T(8,128)(2,1)S(1)} %get-tuple-element.57), channel_id=1, source_target_pairs={{0,1},{1,0},{2,3},{3,2},{4,5},{5,4},{6,7},{7,6},{8,9},{9,8},{10,11... | collective-permute-start | bytes 884744 | tf_op jit(solution)/shard_map/ppermute | solution.py:332
  23.0 7.8 %collective-permute-start.8 = (bf16[288,512]{1,0:T(8,128)(2,1)S(1)}, bf16[288,512]{1,0:T(8,128)(2,1)S(1)}, u32[]{:S(2)}, u32[]{:S(2)}) collective-permute-start(bf16[288,512]{1,0:T(8,128)(2,1)S(1)} %get-tuple-element.58), channel_id=1, source_target_pairs={{1,2},{3,4},{5,6},{2,1},{4,3},{6,5},{9,10},{11,12},{13,14},{10,9},... | collective-permute-start | bytes 884744 | tf_op jit(solution)/shard_map/ppermute | solution.py:337
  31.5 4.6 %collective-permute-start.9 = (bf16[256,1536]{1,0:T(8,128)(2,1)S(1)}, bf16[256,1536]{1,0:T(8,128)(2,1)S(1)}, u32[]{:S(2)}, u32[]{:S(2)}) collective-permute-start(bf16[256,1536]{1,0:T(8,128)(2,1)S(1)} %get-tuple-element.61), channel_id=1, source_target_pairs={{0,1},{1,0},{2,3},{3,2},{4,5},{5,4},{6,7},{7,6},{8,9},{9,8},{10,11... | collective-permute-start | bytes 2359304 | tf_op jit(solution)/shard_map/ppermute | solution.py:332
  33.4 6.6 %copy-start.4 = (bf16[512,512]{1,0:T(8,128)(2,1)S(1)}, bf16[512,512]{1,0:T(8,128)(2,1)}, u32[]{:S(2)}) copy-start(bf16[512,512]{1,0:T(8,128)(2,1)} %k_ref.1) | copy-start | bytes 1572868
  33.4 6.6 %copy-start.5 = (bf16[512,512]{1,0:T(8,128)(2,1)S(1)}, bf16[512,512]{1,0:T(8,128)(2,1)}, u32[]{:S(2)}) copy-start(bf16[512,512]{1,0:T(8,128)(2,1)} %v_ref.1) | copy-start | bytes 1572868
  33.4 6.6 %copy-start.6 = (bf16[512,512]{1,0:T(8,128)(2,1)S(1)}, bf16[512,512]{1,0:T(8,128)(2,1)}, u32[]{:S(2)}) copy-start(bf16[512,512]{1,0:T(8,128)(2,1)} %o_ref.1) | copy-start | bytes 1572868
  36.0 3.9 %copy-start.2 = (bf16[3,512,512]{2,1,0:T(8,128)(2,1)S(1)}, bf16[3,512,512]{2,1,0:T(8,128)(2,1)}, u32[]{:S(2)}) copy-start(bf16[3,512,512]{2,1,0:T(8,128)(2,1)} %t_ref.1) | copy-start | bytes 4718596
  36.1 3.9 %copy-start.3 = (bf16[512,512]{1,0:T(8,128)(2,1)S(1)}, bf16[512,512]{1,0:T(8,128)(2,1)}, u32[]{:S(2)}) copy-start(bf16[512,512]{1,0:T(8,128)(2,1)} %q_ref.1) | copy-start | bytes 1572868
  36.1 3.9 %copy-start.7 = (f32[512]{0:T(512)S(1)}, f32[512]{0:T(512)}, u32[]{:S(2)}) copy-start(f32[512]{0:T(512)} %param.12) | copy-start | bytes 6148
  36.4 10.4 %collective-permute-start.10 = (bf16[256,384]{1,0:T(8,128)(2,1)S(1)}, bf16[256,384]{1,0:T(8,128)(2,1)S(1)}, u32[]{:S(2)}, u32[]{:S(2)}) collective-permute-start(bf16[256,384]{1,0:T(8,128)(2,1)S(1)} %get-tuple-element.72), channel_id=1, source_target_pairs={{0,24},{8,16},{16,8},{24,0},{1,25},{9,17},{17,9},{25,1},{2,26},{10... | collective-permute-start | bytes 589832 | tf_op jit(solution)/shard_map/ppermute | solution.py:332
  37.9 10.9 %collective-permute-start.11 = (bf16[256,384]{1,0:T(8,128)(2,1)S(1)}, bf16[256,384]{1,0:T(8,128)(2,1)S(1)}, u32[]{:S(2)}, u32[]{:S(2)}) collective-permute-start(bf16[256,384]{1,0:T(8,128)(2,1)S(1)} %get-tuple-element.73), channel_id=1, source_target_pairs={{0,8},{8,0},{16,24},{24,16},{1,9},{9,1},{17,25},{25,17},{2,10},{10... | collective-permute-start | bytes 589832 | tf_op jit(solution)/shard_map/ppermute | solution.py:332
  37.9 11.0 %collective-permute-start.12 = (bf16[256,384]{1,0:T(8,128)(2,1)S(1)}, bf16[256,384]{1,0:T(8,128)(2,1)S(1)}, u32[]{:S(2)}, u32[]{:S(2)}) collective-permute-start(bf16[256,384]{1,0:T(8,128)(2,1)S(1)} %get-tuple-element.74), channel_id=1, source_target_pairs={{0,16},{8,24},{16,0},{24,8},{1,17},{9,25},{17,1},{25,9},{2,18},{10... | collective-permute-start | bytes 589832 | tf_op jit(solution)/shard_map/ppermute | solution.py:332
  45.3 13.7 %collective-permute-start.15 = (bf16[4,64,512]{2,1,0:T(8,128)(2,1)S(1)}, bf16[4,64,512]{2,1,0:T(8,128)(2,1)S(1)}, u32[]{:S(2)}, u32[]{:S(2)}) collective-permute-start(bf16[4,64,512]{2,1,0:T(8,128)(2,1)S(1)} %get-tuple-element.78), channel_id=1, source_target_pairs={{0,24},{8,16},{16,8},{24,0},{1,25},{9,17},{17,9},{25,1},{2,26},{10... | collective-permute-start | bytes 786440 | tf_op jit(solution)/shard_map/ppermute | solution.py:332
  46.8 12.2 %collective-permute-start.16 = (bf16[4,64,512]{2,1,0:T(8,128)(2,1)S(1)}, bf16[4,64,512]{2,1,0:T(8,128)(2,1)S(1)}, u32[]{:S(2)}, u32[]{:S(2)}) collective-permute-start(bf16[4,64,512]{2,1,0:T(8,128)(2,1)S(1)} %get-tuple-element.79), channel_id=1, source_target_pairs={{0,8},{8,0},{16,24},{24,16},{1,9},{9,1},{17,25},{25,17},{2,10},{10... | collective-permute-start | bytes 786440 | tf_op jit(solution)/shard_map/ppermute | solution.py:332
  46.8 12.8 %collective-permute-start.17 = (bf16[4,64,512]{2,1,0:T(8,128)(2,1)S(1)}, bf16[4,64,512]{2,1,0:T(8,128)(2,1)S(1)}, u32[]{:S(2)}, u32[]{:S(2)}) collective-permute-start(bf16[4,64,512]{2,1,0:T(8,128)(2,1)S(1)} %get-tuple-element.80), channel_id=1, source_target_pairs={{0,16},{8,24},{16,0},{24,8},{1,17},{9,25},{17,1},{25,9},{2,18},{10... | collective-permute-start | bytes 786440 | tf_op jit(solution)/shard_map/ppermute | solution.py:332
  49.0 7.0 %collective-permute-start.13 = (bf16[128,384]{1,0:T(8,128)(2,1)S(1)}, bf16[128,384]{1,0:T(8,128)(2,1)S(1)}, u32[]{:S(2)}, u32[]{:S(2)}) collective-permute-start(bf16[128,384]{1,0:T(8,128)(2,1)S(1)} %get-tuple-element.87), channel_id=1, source_target_pairs={{0,2},{1,3},{2,0},{3,1},{4,6},{5,7},{6,4},{7,5},{8,10},{9,11},{10,... | collective-permute-start | bytes 294920 | tf_op jit(solution)/shard_map/ppermute | solution.py:332
  56.0 5.1 %collective-permute-start.14 = (bf16[64,384]{1,0:T(8,128)(2,1)S(1)}, bf16[64,384]{1,0:T(8,128)(2,1)S(1)}, u32[]{:S(2)}, u32[]{:S(2)}) collective-permute-start(bf16[64,384]{1,0:T(8,128)(2,1)S(1)} %get-tuple-element.89), channel_id=1, source_target_pairs={{0,4},{1,5},{2,6},{3,7},{4,0},{5,1},{6,2},{7,3},{8,12},{9,13},{10,... | collective-permute-start | bytes 147464 | tf_op jit(solution)/shard_map/ppermute | solution.py:332

commit v18 on v14

--- a/solution.py
+++ b/solution.py
@@ -115,7 +115,7 @@
         out[r] = taps(pieces, w_ref[low:high])
 
 
-def own_act_kernel(z, part_ref, near_ref, far_ref, w_ref, cot_ref, out, near, far):
+def own_act_kernel(z, part_ref, far_ref, near_ref, w_ref, cot_ref, out, near, far):
     lower = even("space")
     first = even("tm")
     for r in range(z.r):
@@ -218,7 +218,7 @@
         out[r - 1] = conv_row(z, w_ref, [x_ref.at[r + di] for di in (-1, 0, 1)])
 
 
-def border_kernel(z, x_ref, near_ref, far_ref, w_ref, out, edges):
+def border_kernel(z, x_ref, far_ref, near_ref, w_ref, out, edges):
     lower = even("space")
     edges[0] = jnp.where(lower, far_ref[...], near_ref[...])
     edges[1] = jnp.where(lower, near_ref[...], far_ref[...])
@@ -436,8 +436,8 @@
         functools.partial(own_act_kernel, z),
         [shape(frames_in.shape), shape((z.r, z.w, z.c)), shape((z.r, z.w, z.c))],
         own,
+        far,
         near,
-        far,
         spatial,
         cotangent,
         flops=3 * one,
@@ -464,8 +464,8 @@
         spatial,
         flops=9 * one * (z.r - 2) // z.r,
     )
-    tied = lax.optimization_barrier((near, far, middle, close, apart))
-    near, far, middle, close, apart = tied
+    tied = lax.optimization_barrier((near, far, middle, apart, close))
+    near, far, middle, apart, close = tied
     keep, send = call(
         functools.partial(cross_kernel, z, width),
         [shape((z.c // 2, 3 * z.c), F32), shape((z.c // 2, 3 * z.c))],
@@ -482,8 +482,8 @@
         functools.partial(border_kernel, z),
         [shape((2, z.block, z.c))],
         x,
+        apart,
         close,
-        apart,
         spatial,
         flops=18 * one // z.r,
         scratch=[pltpu.VMEM((2, line, z.c), BF)],

time: 60.5 us -> 61.2 us (1.012); the launches traced: 59.4 us -> 61 us
  starting transfers between devices: 27.3 us -> 29.9 us
  waiting for transfers between devices: 7.83 us -> 6.76 us
    ppermute x15, starting transfers between devices: 25 us -> 27.6 us  [swap(): return lax.ppermute(value, axis, [(i, i ^ k) for i in range(count)])]
    ppermute x15, waiting for transfers between devices: 7.83 us -> 6.75 us  [swap(): return lax.ppermute(value, axis, [(i, i ^ k) for i in range(count)])]
  transfers between devices with their start and end apart: 18 -> 18, of which waited for: 4 -> 3; matrix products, arithmetic and copies ran while one was open for 0% -> 0% of each run, Pallas kernels for 33% -> 32%
where the time goes in v18:
time: 61.2 us; the launch traced here: 61 us
  starting transfers between devices  29.9 us (49%)
  Pallas kernels  21.9 us (36%)
  waiting for transfers between devices  6.76 us (11%)
  local copies, waits for them, and re-layouts  1.27 us (2%)
  between operations  1.08 us (2%)
    ppermute x15, starting transfers between devices, swap(): return lax.ppermute(value, axis, [(i, i ^ k) for i in range(count)])  27.6 us
    pallas_call x13, Pallas kernels, call(): pl.pallas_call(kernel, out_shape=tuple(outs), in_specs=[VMEM] * len(args)...  20.9 us
    ppermute x15, waiting for transfers between devices, swap(): return lax.ppermute(value, axis, [(i, i ^ k) for i in range(count)])  6.75 us
    ppermute x3, starting transfers between devices, swap_both(): far = lax.ppermute(far, axis, pairs + [(b, a) for a, b in pairs])  2.33 us
    unnamed x20, local copies, waits for them, and re-layouts  1.27 us
  transfers between devices with their start and end apart: 18, of which 3 were waited for; matrix products, arithmetic and copies ran while one was open for 0% of the time, Pallas kernels for 32%

profile of v18, /device:TPU:0, one launch (start us, length us, event | category | flops | bytes accessed | tf_op | source)
XLA Modules:
  0.0 61.0 jit_solution(9177941567502416657)
XLA Ops:
  0.6 1.2 %copy-done.1 = bf16[4,4,64,512]{3,2,1,0:T(8,128)(2,1)S(1)} copy-done((bf16[4,4,64,512]{3,2,1,0:T(8,128)(2,1)S(1)}, bf16[4,4,64,512]{3,2,1,0:T(8,128)(2,1)}, u32[]{:S(2)}) %copy-start.1) | copy-done | bytes 1048600
  1.9 0.6 shard_map.105
  2.4 4.0 %collective-permute-start.4 = (bf16[288,512]{1,0:T(8,128)(2,1)S(1)}, bf16[288,512]{1,0:T(8,128)(2,1)S(1)}, u32[]{:S(2)}, u32[]{:S(2)}) collective-permute-start(bf16[288,512]{1,0:T(8,128)(2,1)S(1)} %get-tuple-element.53), channel_id=1, source_target_pairs={{0,24},{8,16},{16,8},{24,0},{1,25},{9,17},{17,9},{25,1},{2,26},{10... | collective-permute-start | bytes 884744 | tf_op jit(solution)/shard_map/ppermute | solution.py:332
  6.4 0.5 collective-permute-start.5
  6.9 0.1 collective-permute-start.6
  7.0 0.1 shard_map.106
  7.1 0.8 %collective-permute-start = (bf16[256,512]{1,0:T(8,128)(2,1)S(1)}, bf16[256,512]{1,0:T(8,128)(2,1)S(1)}, u32[]{:S(2)}, u32[]{:S(2)}) collective-permute-start(bf16[256,512]{1,0:T(8,128)(2,1)S(1)} %get-tuple-element.48), channel_id=1, source_target_pairs={{1,2},{3,4},{5,6},{2,1},{4,3},{6,5},{9,10},{11,12},{13,14},{10,9},... | collective-permute-start | bytes 786440 | tf_op jit(solution)/shard_map/ppermute | solution.py:337
  7.9 0.0 copy-start
  7.9 3.4 %collective-permute-start.1 = (bf16[256,512]{1,0:T(8,128)(2,1)S(1)}, bf16[256,512]{1,0:T(8,128)(2,1)S(1)}, u32[]{:S(2)}, u32[]{:S(2)}) collective-permute-start(bf16[256,512]{1,0:T(8,128)(2,1)S(1)} %get-tuple-element.49), channel_id=1, source_target_pairs={{0,1},{1,0},{2,3},{3,2},{4,5},{5,4},{6,7},{7,6},{8,9},{9,8},{10,11... | collective-permute-start | bytes 786440 | tf_op jit(solution)/shard_map/ppermute | solution.py:332
  11.3 4.8 %shard_map.104.part_ref = f32[4,256,512]{2,1,0:T(8,128)S(1)} custom-call(bf16[4,4,64,512]{3,2,1,0:T(8,128)(2,1)S(1)} %copy-done.1, bf16[3,3,512,512]{3,2,1,0:T(8,128)(2,1)S(1)} %bitcast.3), custom_call_target="tpu_custom_call" | custom-call | flops 4294967296 | bytes 7864320 | tf_op jit(solution)/shard_map/pallas_call | solution.py:18
  16.1 0.0 collective-permute-done.far_ref
  16.1 0.0 collective-permute-done.1.near_ref
  16.1 1.9 %shard_map.107 = (bf16[4,4,64,512]{3,2,1,0:T(8,128)(2,1)S(1)}, bf16[4,64,512]{2,1,0:T(8,128)(2,1)S(1)}, bf16[4,64,512]{2,1,0:T(8,128)(2,1)S(1)}) custom-call(f32[4,256,512]{2,1,0:T(8,128)S(1)} %shard_map.104.part_ref, bf16[256,512]{1,0:T(8,128)(2,1)S(1)} %collective-permute-done.far_ref, bf16[256,512]{1,0:T(8,128)(2,1)S(1)} %collective-permute-done.1.near_ref, ...), custom_call_target="tpu_custom_call" | custom-call | flops 1610612736 | bytes 9961472 | tf_op jit(solution)/shard_map/pallas_call | solution.py:18
  18.0 1.6 %collective-permute-start.2 = (bf16[4,64,512]{2,1,0:T(8,128)(2,1)S(1)}, bf16[4,64,512]{2,1,0:T(8,128)(2,1)S(1)}, u32[]{:S(2)}, u32[]{:S(2)}) collective-permute-start(bf16[4,64,512]{2,1,0:T(8,128)(2,1)S(1)} %get-tuple-element.51), channel_id=1, source_target_pairs={{0,8},{8,0},{16,24},{24,16},{1,9},{9,1},{17,25},{25,17},{2,10},{10... | collective-permute-start | bytes 786440 | tf_op jit(solution)/shard_map/ppermute | solution.py:332
  19.6 0.7 %collective-permute-start.3 = (bf16[4,64,512]{2,1,0:T(8,128)(2,1)S(1)}, bf16[4,64,512]{2,1,0:T(8,128)(2,1)S(1)}, u32[]{:S(2)}, u32[]{:S(2)}) collective-permute-start(bf16[4,64,512]{2,1,0:T(8,128)(2,1)S(1)} %get-tuple-element.52), channel_id=1, source_target_pairs={{8,16},{16,8},{9,17},{17,9},{10,18},{18,10},{11,19},{19,11},{12,20... | collective-permute-start | bytes 786440 | tf_op jit(solution)/shard_map/ppermute | solution.py:337
  20.2 0.0 collective-permute-done.4.refs_0_
  20.3 0.0 collective-permute-done.6.refs_2_
  20.3 0.5 shard_map.109
  20.8 0.9 %collective-permute-start.7 = (bf16[288,512]{1,0:T(8,128)(2,1)S(1)}, bf16[288,512]{1,0:T(8,128)(2,1)S(1)}, u32[]{:S(2)}, u32[]{:S(2)}) collective-permute-start(bf16[288,512]{1,0:T(8,128)(2,1)S(1)} %get-tuple-element.57), channel_id=1, source_target_pairs={{1,2},{3,4},{5,6},{2,1},{4,3},{6,5},{9,10},{11,12},{13,14},{10,9},... | collective-permute-start | bytes 884744 | tf_op jit(solution)/shard_map/ppermute | solution.py:337
  21.6 3.0 %collective-permute-start.8 = (bf16[288,512]{1,0:T(8,128)(2,1)S(1)}, bf16[288,512]{1,0:T(8,128)(2,1)S(1)}, u32[]{:S(2)}, u32[]{:S(2)}) collective-permute-start(bf16[288,512]{1,0:T(8,128)(2,1)S(1)} %get-tuple-element.58), channel_id=1, source_target_pairs={{0,1},{1,0},{2,3},{3,2},{4,5},{5,4},{6,7},{7,6},{8,9},{9,8},{10,11... | collective-permute-start | bytes 884744 | tf_op jit(solution)/shard_map/ppermute | solution.py:332
  24.6 1.4 %shard_map.108.part_ref = f32[512,1536]{1,0:T(8,128)S(1)} custom-call(bf16[4,4,64,512]{3,2,1,0:T(8,128)(2,1)S(1)} %get-tuple-element.50.act_ref, bf16[4,4,64,512]{3,2,1,0:T(8,128)(2,1)S(1)} %copy-done), custom_call_target="tpu_custom_call" | custom-call | flops 1207959552 | bytes 5242880 | tf_op jit(solution)/shard_map/pallas_call | solution.py:18
  26.0 2.7 %shard_map.110.middle_ref = bf16[2,256,512]{2,1,0:T(8,128)(2,1)S(1)} custom-call(bf16[4,288,512]{2,1,0:T(8,128)(2,1)S(1)} %get-tuple-element.62.x_ref, bf16[3,3,512,512]{3,2,1,0:T(8,128)(2,1)S(1)} %bitcast.3), custom_call_target="tpu_custom_call" | custom-call | flops 2415919104 | bytes 6422528 | tf_op jit(solution)/shard_map/pallas_call | solution.py:18
  28.7 0.0 collective-permute-done.3.far_ref
  28.7 0.0 collective-permute-done.7.far_ref
  28.8 0.6 %shard_map.111 = (f32[256,1536]{1,0:T(8,128)S(1)}, bf16[256,1536]{1,0:T(8,128)(2,1)S(1)}) custom-call(f32[512,1536]{1,0:T(8,128)S(1)} %shard_map.108.part_ref, bf16[4,64,512]{2,1,0:T(8,128)(2,1)S(1)} %collective-permute-done.2.near_ref, bf16[4,64,512]{2,1,0:T(8,128)(2,1)S(1)} %collective-permute-done.3.far_ref, ...), custom_call_target="tpu_custom_call" | custom-call | flops 402653184 | bytes 8126464 | tf_op jit(solution)/shard_map/pallas_call | solution.py:18
  29.4 0.1 collective-permute-start.9
  29.5 0.0 copy-start.4
  29.5 0.0 copy-start.5
  29.5 0.0 copy-start.6
  29.5 2.7 %shard_map.112.border_ref = bf16[2,256,512]{2,1,0:T(8,128)(2,1)S(1)} custom-call(bf16[4,288,512]{2,1,0:T(8,128)(2,1)S(1)} %get-tuple-element.62.x_ref, bf16[288,512]{1,0:T(8,128)(2,1)S(1)} %collective-permute-done.7.far_ref, bf16[288,512]{1,0:T(8,128)(2,1)S(1)} %collective-permute-done.8.near_ref, bf16[3,3,512,512]{3,2,1,0:T(8,128)(2,1)S(1)} %bitcast.3), custom_call_target="tpu_custom_call" | custom-call | flops 2415919104 | bytes 7012352 | tf_op jit(solution)/shard_map/pallas_call | solution.py:18
  32.2 0.0 copy-start.2
  32.2 0.0 copy-start.3
  32.2 0.0 copy-start.7
  32.3 0.3 shard_map.113
  32.6 2.2 %collective-permute-start.10 = (bf16[256,384]{1,0:T(8,128)(2,1)S(1)}, bf16[256,384]{1,0:T(8,128)(2,1)S(1)}, u32[]{:S(2)}, u32[]{:S(2)}) collective-permute-start(bf16[256,384]{1,0:T(8,128)(2,1)S(1)} %get-tuple-element.72), channel_id=1, source_target_pairs={{0,24},{8,16},{16,8},{24,0},{1,25},{9,17},{17,9},{25,1},{2,26},{10... | collective-permute-start | bytes 589832 | tf_op jit(solution)/shard_map/ppermute | solution.py:332
  34.8 4.0 %collective-permute-start.11 = (bf16[256,384]{1,0:T(8,128)(2,1)S(1)}, bf16[256,384]{1,0:T(8,128)(2,1)S(1)}, u32[]{:S(2)}, u32[]{:S(2)}) collective-permute-start(bf16[256,384]{1,0:T(8,128)(2,1)S(1)} %get-tuple-element.73), channel_id=1, source_target_pairs={{0,8},{8,0},{16,24},{24,16},{1,9},{9,1},{17,25},{25,17},{2,10},{10... | collective-permute-start | bytes 589832 | tf_op jit(solution)/shard_map/ppermute | solution.py:332
  38.8 1.0 %collective-permute-start.12 = (bf16[256,384]{1,0:T(8,128)(2,1)S(1)}, bf16[256,384]{1,0:T(8,128)(2,1)S(1)}, u32[]{:S(2)}, u32[]{:S(2)}) collective-permute-start(bf16[256,384]{1,0:T(8,128)(2,1)S(1)} %get-tuple-element.74), channel_id=1, source_target_pairs={{0,16},{8,24},{16,0},{24,8},{1,17},{9,25},{17,1},{25,9},{2,18},{10... | collective-permute-start | bytes 589832 | tf_op jit(solution)/shard_map/ppermute | solution.py:332
  39.8 5.3 %shard_map.114 = (bf16[4,64,512]{2,1,0:T(8,128)(2,1)S(1)}, bf16[4,64,512]{2,1,0:T(8,128)(2,1)S(1)}, bf16[4,64,512]{2,1,0:T(8,128)(2,1)S(1)}, bf16[4,64,512]{2,1,0:T(8,128)(2,1)S(1)}) custom-call(bf16[2,256,512]{2,1,0:T(8,128)(2,1)S(1)} %shard_map.110.middle_ref, bf16[2,256,512]{2,1,0:T(8,128)(2,1)S(1)} %shard_map.112.border_ref, ...), custom_call_target="tpu_custom_call" | custom-call | flops 4831838208 | bytes 6948864 | tf_op jit(solution)/shard_map/pallas_call | solution.py:18
  45.1 1.5 %collective-permute-start.15 = (bf16[4,64,512]{2,1,0:T(8,128)(2,1)S(1)}, bf16[4,64,512]{2,1,0:T(8,128)(2,1)S(1)}, u32[]{:S(2)}, u32[]{:S(2)}) collective-permute-start(bf16[4,64,512]{2,1,0:T(8,128)(2,1)S(1)} %get-tuple-element.78), channel_id=1, source_target_pairs={{0,24},{8,16},{16,8},{24,0},{1,25},{9,17},{17,9},{25,1},{2,26},{10... | collective-permute-start | bytes 786440 | tf_op jit(solution)/shard_map/ppermute | solution.py:332
  46.6 1.0 %collective-permute-start.16 = (bf16[4,64,512]{2,1,0:T(8,128)(2,1)S(1)}, bf16[4,64,512]{2,1,0:T(8,128)(2,1)S(1)}, u32[]{:S(2)}, u32[]{:S(2)}) collective-permute-start(bf16[4,64,512]{2,1,0:T(8,128)(2,1)S(1)} %get-tuple-element.79), channel_id=1, source_target_pairs={{0,8},{8,0},{16,24},{24,16},{1,9},{9,1},{17,25},{25,17},{2,10},{10... | collective-permute-start | bytes 786440 | tf_op jit(solution)/shard_map/ppermute | solution.py:332
  47.6 1.0 %collective-permute-start.17 = (bf16[4,64,512]{2,1,0:T(8,128)(2,1)S(1)}, bf16[4,64,512]{2,1,0:T(8,128)(2,1)S(1)}, u32[]{:S(2)}, u32[]{:S(2)}) collective-permute-start(bf16[4,64,512]{2,1,0:T(8,128)(2,1)S(1)} %get-tuple-element.80), channel_id=1, source_target_pairs={{0,16},{8,24},{16,0},{24,8},{1,17},{9,25},{17,1},{25,9},{2,18},{10... | collective-permute-start | bytes 786440 | tf_op jit(solution)/shard_map/ppermute | solution.py:332
  48.6 0.1 shard_map.115
  48.7 1.6 %collective-permute-start.13 = (bf16[128,384]{1,0:T(8,128)(2,1)S(1)}, bf16[128,384]{1,0:T(8,128)(2,1)S(1)}, u32[]{:S(2)}, u32[]{:S(2)}) collective-permute-start(bf16[128,384]{1,0:T(8,128)(2,1)S(1)} %get-tuple-element.87), channel_id=1, source_target_pairs={{0,2},{1,3},{2,0},{3,1},{4,6},{5,7},{6,4},{7,5},{8,10},{9,11},{10,... | collective-permute-start | bytes 294920 | tf_op jit(solution)/shard_map/ppermute | solution.py:332
  50.4 3.1 %collective-permute-done.13.refs_1_ = bf16[128,384]{1,0:T(8,128)(2,1)S(1)} collective-permute-done((bf16[128,384]{1,0:T(8,128)(2,1)S(1)}, bf16[128,384]{1,0:T(8,128)(2,1)S(1)}, u32[]{:S(2)}, u32[]{:S(2)}) %collective-permute-start.13) | collective-permute-done | bytes 98336 | tf_op jit(solution)/shard_map/ppermute | solution.py:332
  53.5 2.6 %collective-permute-start.14 = (bf16[64,384]{1,0:T(8,128)(2,1)S(1)}, bf16[64,384]{1,0:T(8,128)(2,1)S(1)}, u32[]{:S(2)}, u32[]{:S(2)}) collective-permute-start(bf16[64,384]{1,0:T(8,128)(2,1)S(1)} %get-tuple-element.89), channel_id=1, source_target_pairs={{0,4},{1,5},{2,6},{3,7},{4,0},{5,1},{6,2},{7,3},{8,12},{9,13},{10,... | collective-permute-start | bytes 147464 | tf_op jit(solution)/shard_map/ppermute | solution.py:332
  56.1 3.4 %collective-permute-done.16.refs_1_ = bf16[4,64,512]{2,1,0:T(8,128)(2,1)S(1)} collective-permute-done((bf16[4,64,512]{2,1,0:T(8,128)(2,1)S(1)}, bf16[4,64,512]{2,1,0:T(8,128)(2,1)S(1)}, u32[]{:S(2)}, u32[]{:S(2)}) %collective-permute-start.16) | collective-permute-done | bytes 262176 | tf_op jit(solution)/shard_map/ppermute | solution.py:332
  59.5 0.2 collective-permute-done.17.refs_2_
  59.8 1.1 %shard_map.117 = (bf16[4,4,64,512]{3,2,1,0:T(8,128)(2,1)}, f32[3,64,128]{2,1,0:T(8,128)}) custom-call(f32[64,384]{1,0:T(8,128)S(1)} %get-tuple-element.88.kept_ref, bf16[64,384]{1,0:T(8,128)(2,1)S(1)} %collective-permute-done.14.got_ref, bf16[4,64,512]{2,1,0:T(8,128)(2,1)S(1)} %collective-permute-done.15.refs_0_, ...), custom_call_target="tpu_custom_call" | custom-call | bytes 4194304 | tf_op jit(solution)/shard_map/pallas_call | solution.py:379
  (23 shorter events, 0.1 us)
Async XLA Ops:
  0.6 1.2 %copy-start.1 = (bf16[4,4,64,512]{3,2,1,0:T(8,128)(2,1)S(1)}, bf16[4,4,64,512]{3,2,1,0:T(8,128)(2,1)}, u32[]{:S(2)}) copy-start(bf16[4,4,64,512]{3,2,1,0:T(8,128)(2,1)} %x_ref.5) | copy-start | bytes 3145732
  1.9 9.5 %slice-start = ((s8[4718592]{0:T(1024)(128)(4,1)}), s8[4194304]{0:T(1024)(128)(4,1)S(1)}, s32[]{:S(2)}) async-start(s8[4718592]{0:T(1024)(128)(4,1)} %bitcast.2), calls=%async_computation | async-start | bytes 8388608
  2.4 17.8 %collective-permute-start.4 = (bf16[288,512]{1,0:T(8,128)(2,1)S(1)}, bf16[288,512]{1,0:T(8,128)(2,1)S(1)}, u32[]{:S(2)}, u32[]{:S(2)}) collective-permute-start(bf16[288,512]{1,0:T(8,128)(2,1)S(1)} %get-tuple-element.53), channel_id=1, source_target_pairs={{0,24},{8,16},{16,8},{24,0},{1,25},{9,17},{17,9},{25,1},{2,26},{10... | collective-permute-start | bytes 884744 | tf_op jit(solution)/shard_map/ppermute | solution.py:332
  6.4 13.8 %collective-permute-start.5 = (bf16[288,512]{1,0:T(8,128)(2,1)S(1)}, bf16[288,512]{1,0:T(8,128)(2,1)S(1)}, u32[]{:S(2)}, u32[]{:S(2)}) collective-permute-start(bf16[288,512]{1,0:T(8,128)(2,1)S(1)} %get-tuple-element.54), channel_id=1, source_target_pairs={{0,8},{8,0},{16,24},{24,16},{1,9},{9,1},{17,25},{25,17},{2,10},{10... | collective-permute-start | bytes 884744 | tf_op jit(solution)/shard_map/ppermute | solution.py:332
  6.9 13.3 %collective-permute-start.6 = (bf16[288,512]{1,0:T(8,128)(2,1)S(1)}, bf16[288,512]{1,0:T(8,128)(2,1)S(1)}, u32[]{:S(2)}, u32[]{:S(2)}) collective-permute-start(bf16[288,512]{1,0:T(8,128)(2,1)S(1)} %get-tuple-element.55), channel_id=1, source_target_pairs={{0,16},{8,24},{16,0},{24,8},{1,17},{9,25},{17,1},{25,9},{2,18},{10... | collective-permute-start | bytes 884744 | tf_op jit(solution)/shard_map/ppermute | solution.py:332
  7.0 4.3 %slice-start.1 = ((s8[4718592]{0:T(1024)(128)(4,1)}), s8[524288]{0:T(1024)(128)(4,1)S(1)}, s32[]{:S(2)}) async-start(s8[4718592]{0:T(1024)(128)(4,1)} %bitcast.2), calls=%async_computation.1 | async-start | bytes 1048576
  7.1 9.0 %collective-permute-start = (bf16[256,512]{1,0:T(8,128)(2,1)S(1)}, bf16[256,512]{1,0:T(8,128)(2,1)S(1)}, u32[]{:S(2)}, u32[]{:S(2)}) collective-permute-start(bf16[256,512]{1,0:T(8,128)(2,1)S(1)} %get-tuple-element.48), channel_id=1, source_target_pairs={{1,2},{3,4},{5,6},{2,1},{4,3},{6,5},{9,10},{11,12},{13,14},{10,9},... | collective-permute-start | bytes 786440 | tf_op jit(solution)/shard_map/ppermute | solution.py:337
  7.9 8.2 %copy-start = (bf16[4,4,64,512]{3,2,1,0:T(8,128)(2,1)S(1)}, bf16[4,4,64,512]{3,2,1,0:T(8,128)(2,1)}, u32[]{:S(2)}) copy-start(bf16[4,4,64,512]{3,2,1,0:T(8,128)(2,1)} %cot_ref.5) | copy-start | bytes 3145732
  7.9 8.2 %collective-permute-start.1 = (bf16[256,512]{1,0:T(8,128)(2,1)S(1)}, bf16[256,512]{1,0:T(8,128)(2,1)S(1)}, u32[]{:S(2)}, u32[]{:S(2)}) collective-permute-start(bf16[256,512]{1,0:T(8,128)(2,1)S(1)} %get-tuple-element.49), channel_id=1, source_target_pairs={{0,1},{1,0},{2,3},{3,2},{4,5},{5,4},{6,7},{7,6},{8,9},{9,8},{10,11... | collective-permute-start | bytes 786440 | tf_op jit(solution)/shard_map/ppermute | solution.py:332
  18.0 10.7 %collective-permute-start.2 = (bf16[4,64,512]{2,1,0:T(8,128)(2,1)S(1)}, bf16[4,64,512]{2,1,0:T(8,128)(2,1)S(1)}, u32[]{:S(2)}, u32[]{:S(2)}) collective-permute-start(bf16[4,64,512]{2,1,0:T(8,128)(2,1)S(1)} %get-tuple-element.51), channel_id=1, source_target_pairs={{0,8},{8,0},{16,24},{24,16},{1,9},{9,1},{17,25},{25,17},{2,10},{10... | collective-permute-start | bytes 786440 | tf_op jit(solution)/shard_map/ppermute | solution.py:332
  19.6 9.2 %collective-permute-start.3 = (bf16[4,64,512]{2,1,0:T(8,128)(2,1)S(1)}, bf16[4,64,512]{2,1,0:T(8,128)(2,1)S(1)}, u32[]{:S(2)}, u32[]{:S(2)}) collective-permute-start(bf16[4,64,512]{2,1,0:T(8,128)(2,1)S(1)} %get-tuple-element.52), channel_id=1, source_target_pairs={{8,16},{16,8},{9,17},{17,9},{10,18},{18,10},{11,19},{19,11},{12,20... | collective-permute-start | bytes 786440 | tf_op jit(solution)/shard_map/ppermute | solution.py:337
  20.8 8.0 %collective-permute-start.7 = (bf16[288,512]{1,0:T(8,128)(2,1)S(1)}, bf16[288,512]{1,0:T(8,128)(2,1)S(1)}, u32[]{:S(2)}, u32[]{:S(2)}) collective-permute-start(bf16[288,512]{1,0:T(8,128)(2,1)S(1)} %get-tuple-element.57), channel_id=1, source_target_pairs={{1,2},{3,4},{5,6},{2,1},{4,3},{6,5},{9,10},{11,12},{13,14},{10,9},... | collective-permute-start | bytes 884744 | tf_op jit(solution)/shard_map/ppermute | solution.py:337
  21.6 7.1 %collective-permute-start.8 = (bf16[288,512]{1,0:T(8,128)(2,1)S(1)}, bf16[288,512]{1,0:T(8,128)(2,1)S(1)}, u32[]{:S(2)}, u32[]{:S(2)}) collective-permute-start(bf16[288,512]{1,0:T(8,128)(2,1)S(1)} %get-tuple-element.58), channel_id=1, source_target_pairs={{0,1},{1,0},{2,3},{3,2},{4,5},{5,4},{6,7},{7,6},{8,9},{9,8},{10,11... | collective-permute-start | bytes 884744 | tf_op jit(solution)/shard_map/ppermute | solution.py:332
  29.4 2.8 %collective-permute-start.9 = (bf16[256,1536]{1,0:T(8,128)(2,1)S(1)}, bf16[256,1536]{1,0:T(8,128)(2,1)S(1)}, u32[]{:S(2)}, u32[]{:S(2)}) collective-permute-start(bf16[256,1536]{1,0:T(8,128)(2,1)S(1)} %get-tuple-element.61), channel_id=1, source_target_pairs={{0,1},{1,0},{2,3},{3,2},{4,5},{5,4},{6,7},{7,6},{8,9},{9,8},{10,11... | collective-permute-start | bytes 2359304 | tf_op jit(solution)/shard_map/ppermute | solution.py:332
  29.5 10.3 %copy-start.4 = (bf16[512,512]{1,0:T(8,128)(2,1)S(1)}, bf16[512,512]{1,0:T(8,128)(2,1)}, u32[]{:S(2)}) copy-start(bf16[512,512]{1,0:T(8,128)(2,1)} %k_ref.1) | copy-start | bytes 1572868
  29.5 10.3 %copy-start.5 = (bf16[512,512]{1,0:T(8,128)(2,1)S(1)}, bf16[512,512]{1,0:T(8,128)(2,1)}, u32[]{:S(2)}) copy-start(bf16[512,512]{1,0:T(8,128)(2,1)} %v_ref.1) | copy-start | bytes 1572868
  29.5 10.2 %copy-start.6 = (bf16[512,512]{1,0:T(8,128)(2,1)S(1)}, bf16[512,512]{1,0:T(8,128)(2,1)}, u32[]{:S(2)}) copy-start(bf16[512,512]{1,0:T(8,128)(2,1)} %o_ref.1) | copy-start | bytes 1572868
  32.2 7.6 %copy-start.2 = (bf16[3,512,512]{2,1,0:T(8,128)(2,1)S(1)}, bf16[3,512,512]{2,1,0:T(8,128)(2,1)}, u32[]{:S(2)}) copy-start(bf16[3,512,512]{2,1,0:T(8,128)(2,1)} %t_ref.1) | copy-start | bytes 4718596
  32.2 7.5 %copy-start.3 = (bf16[512,512]{1,0:T(8,128)(2,1)S(1)}, bf16[512,512]{1,0:T(8,128)(2,1)}, u32[]{:S(2)}) copy-start(bf16[512,512]{1,0:T(8,128)(2,1)} %q_ref.1) | copy-start | bytes 1572868
  32.2 7.5 %copy-start.7 = (f32[512]{0:T(512)S(1)}, f32[512]{0:T(512)}, u32[]{:S(2)}) copy-start(f32[512]{0:T(512)} %param.12) | copy-start | bytes 6148
  32.6 15.1 %collective-permute-start.10 = (bf16[256,384]{1,0:T(8,128)(2,1)S(1)}, bf16[256,384]{1,0:T(8,128)(2,1)S(1)}, u32[]{:S(2)}, u32[]{:S(2)}) collective-permute-start(bf16[256,384]{1,0:T(8,128)(2,1)S(1)} %get-tuple-element.72), channel_id=1, source_target_pairs={{0,24},{8,16},{16,8},{24,0},{1,25},{9,17},{17,9},{25,1},{2,26},{10... | collective-permute-start | bytes 589832 | tf_op jit(solution)/shard_map/ppermute | solution.py:332
  34.8 13.9 %collective-permute-start.11 = (bf16[256,384]{1,0:T(8,128)(2,1)S(1)}, bf16[256,384]{1,0:T(8,128)(2,1)S(1)}, u32[]{:S(2)}, u32[]{:S(2)}) collective-permute-start(bf16[256,384]{1,0:T(8,128)(2,1)S(1)} %get-tuple-element.73), channel_id=1, source_target_pairs={{0,8},{8,0},{16,24},{24,16},{1,9},{9,1},{17,25},{25,17},{2,10},{10... | collective-permute-start | bytes 589832 | tf_op jit(solution)/shard_map/ppermute | solution.py:332
  38.8 9.9 %collective-permute-start.12 = (bf16[256,384]{1,0:T(8,128)(2,1)S(1)}, bf16[256,384]{1,0:T(8,128)(2,1)S(1)}, u32[]{:S(2)}, u32[]{:S(2)}) collective-permute-start(bf16[256,384]{1,0:T(8,128)(2,1)S(1)} %get-tuple-element.74), channel_id=1, source_target_pairs={{0,16},{8,24},{16,0},{24,8},{1,17},{9,25},{17,1},{25,9},{2,18},{10... | collective-permute-start | bytes 589832 | tf_op jit(solution)/shard_map/ppermute | solution.py:332
  45.1 11.0 %collective-permute-start.15 = (bf16[4,64,512]{2,1,0:T(8,128)(2,1)S(1)}, bf16[4,64,512]{2,1,0:T(8,128)(2,1)S(1)}, u32[]{:S(2)}, u32[]{:S(2)}) collective-permute-start(bf16[4,64,512]{2,1,0:T(8,128)(2,1)S(1)} %get-tuple-element.78), channel_id=1, source_target_pairs={{0,24},{8,16},{16,8},{24,0},{1,25},{9,17},{17,9},{25,1},{2,26},{10... | collective-permute-start | bytes 786440 | tf_op jit(solution)/shard_map/ppermute | solution.py:332
  46.6 12.9 %collective-permute-start.16 = (bf16[4,64,512]{2,1,0:T(8,128)(2,1)S(1)}, bf16[4,64,512]{2,1,0:T(8,128)(2,1)S(1)}, u32[]{:S(2)}, u32[]{:S(2)}) collective-permute-start(bf16[4,64,512]{2,1,0:T(8,128)(2,1)S(1)} %get-tuple-element.79), channel_id=1, source_target_pairs={{0,8},{8,0},{16,24},{24,16},{1,9},{9,1},{17,25},{25,17},{2,10},{10... | collective-permute-start | bytes 786440 | tf_op jit(solution)/shard_map/ppermute | solution.py:332
  47.6 12.1 %collective-permute-start.17 = (bf16[4,64,512]{2,1,0:T(8,128)(2,1)S(1)}, bf16[4,64,512]{2,1,0:T(8,128)(2,1)S(1)}, u32[]{:S(2)}, u32[]{:S(2)}) collective-permute-start(bf16[4,64,512]{2,1,0:T(8,128)(2,1)S(1)} %get-tuple-element.80), channel_id=1, source_target_pairs={{0,16},{8,24},{16,0},{24,8},{1,17},{9,25},{17,1},{25,9},{2,18},{10... | collective-permute-start | bytes 786440 | tf_op jit(solution)/shard_map/ppermute | solution.py:332
  48.7 4.7 %collective-permute-start.13 = (bf16[128,384]{1,0:T(8,128)(2,1)S(1)}, bf16[128,384]{1,0:T(8,128)(2,1)S(1)}, u32[]{:S(2)}, u32[]{:S(2)}) collective-permute-start(bf16[128,384]{1,0:T(8,128)(2,1)S(1)} %get-tuple-element.87), channel_id=1, source_target_pairs={{0,2},{1,3},{2,0},{3,1},{4,6},{5,7},{6,4},{7,5},{8,10},{9,11},{10,... | collective-permute-start | bytes 294920 | tf_op jit(solution)/shard_map/ppermute | solution.py:332
  53.5 6.3 %collective-permute-start.14 = (bf16[64,384]{1,0:T(8,128)(2,1)S(1)}, bf16[64,384]{1,0:T(8,128)(2,1)S(1)}, u32[]{:S(2)}, u32[]{:S(2)}) collective-permute-start(bf16[64,384]{1,0:T(8,128)(2,1)S(1)} %get-tuple-element.89), channel_id=1, source_target_pairs={{0,4},{1,5},{2,6},{3,7},{4,0},{5,1},{6,2},{7,3},{8,12},{9,13},{10,... | collective-permute-start | bytes 147464 | tf_op jit(solution)/shard_map/ppermute | solution.py:332
